TPU v7x, 128 devices: a whole 4x4x4 slice. The times are simulated.
128 devices in a mesh: sub: 8 (over x, core), band: 16 (over z, y).
Axes of the slice: x: 4, y: 4, z: 4, core: 2. Of those that a mesh axis runs over, the one named last changes fastest.
Arguments:
- coeffs_in: float32 [32, 128, 1024], P('sub'), may hold values from -6 to 6
- basis: bfloat16 [224, 32], P('band'), may hold values from -0.375 to 0.375
- kernels: float32 [224, 9, 9], P('band'), may hold values from -0.625 to 0.625
- response: bfloat16 [8, 224], P(None, 'band'), may hold values from -1.5 to 1.5
- hs_image: bfloat16 [224, 32, 256], P('band', 'sub'), may hold values from -6 to 6
- ms_image: bfloat16 [8, 128, 1024], P(None, 'sub'), may hold values from -6 to 6
Outputs:
- coeffs: float32 [32, 128, 1024], P('sub')
All inputs are finite; a program needn't handle non-finite values.
Results may differ from a plain program's by a relative error of at most 0.0003.
The roundings to bfloat16 on the way count: a program that leaves them out, or rounds other values in their place, can miss the bound.
Values may be sent and summed in bfloat16 or wider, within the bound.
No kernel may reach another device: no remote copies, remote signals or barrier semaphores. Data moves between devices by JAX's collectives and lax.ppermute only.
A program may use at most 128 MiB of HBM per device.

v0:
```python
import jax
import jax.numpy as jnp
from jax import lax
from jax.sharding import PartitionSpec as P

ITERS = 2


step_scale = 0.15


def padded_2(cells, sides, width):
    for axis, dim in sides:
        count = lax.axis_size(axis)
        ends = count - 1
        head = lax.slice_in_dim(cells, 0, width, axis=dim)
        tail = lax.slice_in_dim(cells, cells.shape[dim] - width, cells.shape[dim], axis=dim)
        cells = jnp.concatenate(
            [
                lax.ppermute(tail, axis, [(i, (i + 1) % count) for i in range(ends)]),
                cells,
                lax.ppermute(head, axis, [((i + 1) % count, i) for i in range(ends)]),
            ],
            axis=dim,
        )
    return cells


def hs_gradient(rounded, basis, kernels, hs_image):
    chans, rows, width = rounded.shape
    bands = basis.shape[0]
    groups = rows // 4
    columns = width // 4
    mixed = jnp.dot(basis, rounded.reshape(chans, -1), preferred_element_type=jnp.float32).astype(
        jnp.bfloat16
    )
    mixed = mixed.reshape(bands, rows, width)
    extended = padded_2(mixed, (("sub", 1),), 4)
    padded = jnp.pad(extended, ((0, 0), (0, 0), (4, 4)))
    phases = padded.reshape(bands, groups + 2, 4, columns + 2, 4).transpose(0, 2, 4, 1, 3)
    blurred = jnp.zeros((bands, groups, columns), jnp.float32)
    for row_tap in range(9):
        row_step, row_phase = divmod(row_tap, 4)
        for col_tap in range(9):
            col_step, col_phase = divmod(col_tap, 4)
            window = phases[
                :, row_phase, col_phase, row_step : row_step + groups, col_step : col_step + columns
            ]
            blurred = blurred + kernels[:, row_tap, col_tap][:, None, None] * window
    misfit = hs_image.astype(jnp.float32) - blurred
    misfit_ext = padded_2(misfit, (("sub", 1),), 1)
    misfit_pad = jnp.pad(misfit_ext, ((0, 0), (0, 0), (1, 1)))
    outer = []
    for row_phase in range(4):
        inner = []
        for col_phase in range(4):
            total = jnp.zeros((bands, groups, columns), jnp.float32)
            for row_step in range(3):
                if 4 * row_step + row_phase > 8:
                    continue
                for col_step in range(3):
                    if 4 * col_step + col_phase > 8:
                        continue
                    weight = kernels[:, 4 * row_step + row_phase, 4 * col_step + col_phase][
                        :, None, None
                    ]
                    window = misfit_pad[
                        :,
                        2 - row_step : 2 - row_step + groups,
                        2 - col_step : 2 - col_step + columns,
                    ]
                    total = total + weight * window
            inner.append(total)
        outer.append(jnp.stack(inner, axis=1))
    back = jnp.stack(outer, axis=1).transpose(0, 3, 1, 4, 2).reshape(bands, rows * width)
    back = back.astype(jnp.bfloat16)
    grad = jnp.einsum("lk,lp->kp", basis, back, preferred_element_type=jnp.float32)
    return grad.reshape(chans, rows, width)


def ms_gradient(rounded, ms_rows, combined):
    chans, rows, width = rounded.shape
    sensors = ms_rows.shape[0]
    predicted = jnp.dot(combined, rounded.reshape(chans, -1), preferred_element_type=jnp.float32)
    ms_misfit = (ms_rows.reshape(sensors, -1).astype(jnp.float32) - predicted).astype(jnp.bfloat16)
    grad = jnp.einsum("mk,mp->kp", combined, ms_misfit, preferred_element_type=jnp.float32)
    return grad.reshape(chans, rows, width)


def per_device(coeffs_in, basis, kernels, response, hs_image, ms_image):
    partial_map = jnp.dot(response, basis, preferred_element_type=jnp.float32)
    combined = lax.psum(partial_map, "band").astype(jnp.bfloat16)
    current = coeffs_in
    for turn in range(ITERS):
        rounded = lax.all_to_all(
            current.astype(jnp.bfloat16), "sub", split_axis=1, concat_axis=0, tiled=True
        )
        hs_part = hs_gradient(rounded, basis, kernels, hs_image)
        hs_total = lax.psum(hs_part, "band")
        update = step_scale * (hs_total + ms_gradient(rounded, ms_image, combined))
        current = current + lax.all_to_all(update, "sub", split_axis=0, concat_axis=1, tiled=True)
    return current


def solution(mesh):
    return jax.shard_map(
        per_device,
        mesh=mesh,
        in_specs=(
            P("sub", None, None),
            P("band", None),
            P("band", None, None),
            P(None, "band"),
            P("band", "sub", None),
            P(None, "sub", None),
        ),
        out_specs=P("sub", None, None),
        check_vma=False,
    )
```

profile of v0, /device:TPU:1, one launch (start us, length us, event | category | flops | bytes accessed | tf_op | source)
XLA Modules:
  0.0 448.6 jit_solution(3410588063902400602)
XLA Ops:
  6.5 3.9 copy.459
  10.5 5.8 %all-to-all-start = ((bf16[4,128,1024]{2,0,1:T(4,128)(2,1)}), bf16[4,128,1024]{2,0,1:T(4,128)(2,1)S(1)}, u32[]{:S(2)}, u32[]{:S(2)}) async-start(bf16[4,128,1024]{2,0,1:T(4,128)(2,1)} %copy.459), calls=%async_computation | async-start | bytes 2097152 | tf_op jit(solution)/shard_map/all_to_all | solution.py:95
  19.6 11.8 %all-to-all-done = bf16[4,128,1024]{2,0,1:T(4,128)(2,1)S(1)} async-done(((bf16[4,128,1024]{2,0,1:T(4,128)(2,1)}), bf16[4,128,1024]{2,0,1:T(4,128)(2,1)S(1)}, u32[]{:S(2)}, u32[]{:S(2)}) %all-to-all-start) | async-done | bytes 1048608 | tf_op jit(solution)/shard_map/all_to_all | solution.py:95
  33.0 2.9 collective-permute-start
  42.4 4.8 %copy.442 = bf16[14,24,1024]{0,2,1:T(8,128)(2,1)} copy(bf16[14,24,1024]{2,1,0:T(8,128)(2,1)S(1)} %pad_maximum_fusion) | data formatting | bytes 1376256
  47.2 7.5 %pad.14.clone = bf16[14,24,1032]{0,2,1:T(8,128)(2,1)} pad(bf16[14,24,1024]{0,2,1:T(8,128)(2,1)} %copy.442, bf16[]{:T(256)} %constant.4.clone.1), padding=0_0x0_0x4_4 | pad | bytes 1381634 | tf_op jit(solution)/shard_map/jit(_pad)/pad | solution.py:39
  54.7 11.1 %copy.392 = bf16[14,6,4,258,4]{3,1,0,4,2:T(8,128)(2,1)S(1)} copy(bf16[14,6,4,258,4]{0,4,3,2,1:T(4,128)(2,1)} %bitcast.1049) | data formatting | bytes 1387008 | tf_op jit(solution)/shard_map/reshape | solution.py:40
  65.8 3.8 convert_subtract_fusion.1
  71.5 2.6 collective-permute-start.3
  86.3 4.9 %copy.413 = bf16[14,4,4,256,4]{0,4,3,2,1:T(4,128)(2,1)} copy(bf16[14,4,4,256,4]{3,1,4,2,0:T(4,128)(2,1)S(1)} %maximum_bitcast_fusion) | data formatting | bytes 917504 | tf_op jit(solution)/shard_map/convert_element_type | solution.py:76
  91.2 3.7 fusion.212
  94.9 2.5 copy.446
  98.9 35.0 %psum.22 = bf16[8,32]{1,0:T(8,128)(2,1)S(1)} all-reduce(f32[8,32]{1,0:T(8,128)S(1)} %fusion.213), channel_id=1, replica_groups=mesh['sub'=8,'band'=16] {'band'}, use_global_device_ids=true, to_apply=%region_1.2 | all-reduce | flops 256 | bytes 1536 | tf_op jit(solution)/shard_map/psum | solution.py:92
  135.7 2.8 copy.448
  138.5 49.4 %all-reduce.7.cloned.1.call-done = f32[32,16,1024]{2,1,0:T(8,128)} async-done(((f32[32,16,1024]{2,1,0:T(8,128)}), f32[32,16,1024]{2,1,0:T(8,128)}) %all-reduce.7.cloned.1.call-update) | async-done | bytes 2097168 | tf_op jit(solution)/shard_map/psum | solution.py:99
  189.8 32.5 %all_to_all.66 = f32[32,16,1024]{2,1,0:T(8,128)S(1)} all-to-all(f32[32,16,1024]{2,1,0:T(8,128)S(1)} %fusion.3), channel_id=1, replica_groups=mesh['sub'=8,'band'=16] {'sub'}, dimensions={0} | all-to-all | bytes 4194304 | tf_op jit(solution)/shard_map/all_to_all | solution.py:101
  225.7 18.5 %all_to_all.67 = bf16[4,128,1024]{2,0,1:T(4,128)(2,1)S(1)} all-to-all(bf16[4,128,1024]{2,0,1:T(4,128)(2,1)S(1)} %fusion.6), channel_id=1, replica_groups=mesh['sub'=8,'band'=16] {'sub'}, dimensions={1} | all-to-all | bytes 2097152 | tf_op jit(solution)/shard_map/all_to_all | solution.py:95
  246.8 3.1 collective-permute-start.4
  252.0 4.1 collective-permute-done.5
  256.4 4.8 %copy.443 = bf16[14,24,1024]{0,2,1:T(8,128)(2,1)} copy(bf16[14,24,1024]{2,1,0:T(8,128)(2,1)S(1)} %pad_maximum_fusion.1) | data formatting | bytes 1376256
  261.2 7.5 %pad.16.clone = bf16[14,24,1032]{0,2,1:T(8,128)(2,1)} pad(bf16[14,24,1024]{0,2,1:T(8,128)(2,1)} %copy.443, bf16[]{:T(256)} %constant.4.clone.1), padding=0_0x0_0x4_4 | pad | bytes 1381634 | tf_op jit(solution)/shard_map/jit(_pad)/pad | solution.py:39
  268.7 11.1 %copy.418 = bf16[14,6,4,258,4]{3,1,0,4,2:T(8,128)(2,1)S(1)} copy(bf16[14,6,4,258,4]{0,4,3,2,1:T(4,128)(2,1)} %bitcast.1048) | data formatting | bytes 1387008 | tf_op jit(solution)/shard_map/reshape | solution.py:40
  280.0 4.2 convert_subtract_fusion
  286.3 2.7 collective-permute-start.7
  301.1 4.9 %copy.439 = bf16[14,4,4,256,4]{0,4,3,2,1:T(4,128)(2,1)} copy(bf16[14,4,4,256,4]{3,1,4,2,0:T(4,128)(2,1)S(1)} %maximum_bitcast_fusion.1) | data formatting | bytes 917504 | tf_op jit(solution)/shard_map/convert_element_type | solution.py:76
  306.0 3.7 fusion.214
  309.7 2.5 copy.451
  313.5 2.9 fusion.4
  316.3 4.1 copy.452
  320.5 79.2 %all-reduce.9.cloned.1.call-done = f32[32,16,1024]{2,1,0:T(8,128)} async-done(((f32[32,16,1024]{2,1,0:T(8,128)}), f32[32,16,1024]{2,1,0:T(8,128)}) %all-reduce.9.cloned.1.call-update) | async-done | bytes 2097168 | tf_op jit(solution)/shard_map/psum | solution.py:99
  399.6 2.7 fusion.2
  402.3 32.5 %all_to_all.68 = f32[32,16,1024]{2,1,0:T(8,128)S(1)} all-to-all(f32[32,16,1024]{2,1,0:T(8,128)S(1)} %fusion.2), channel_id=1, replica_groups=mesh['sub'=8,'band'=16] {'sub'}, dimensions={0} | all-to-all | bytes 4194304 | tf_op jit(solution)/shard_map/all_to_all | solution.py:101
  (258 shorter events, 59.5 us)
Async XLA Ops:
  10.5 20.9 %all-to-all-start = ((bf16[4,128,1024]{2,0,1:T(4,128)(2,1)}), bf16[4,128,1024]{2,0,1:T(4,128)(2,1)S(1)}, u32[]{:S(2)}, u32[]{:S(2)}) async-start(bf16[4,128,1024]{2,0,1:T(4,128)(2,1)} %copy.459), calls=%async_computation | async-start | bytes 2097152 | tf_op jit(solution)/shard_map/all_to_all | solution.py:95
  16.3 171.6 %all-reduce.7.cloned.1.call-start = ((), (), s32[]{:S(2)}) async-start(), calls=%async_computation.4 | async-start | bytes 4194304 | tf_op jit(solution)/shard_map/psum | solution.py:99
  17.3 63.3 %copy-start.56 = (f32[14]{0:T(128)}, f32[14]{0:T(128)S(1)}, u32[]{:S(2)}) copy-start(f32[14]{0:T(128)S(1)} %get-tuple-element.9) | copy-start | bytes 172
  17.3 66.2 %copy-start.22 = (f32[14]{0:T(128)}, f32[14]{0:T(128)S(1)}, u32[]{:S(2)}) copy-start(f32[14]{0:T(128)S(1)} %get-tuple-element.23) | copy-start | bytes 172
  18.3 64.2 %copy-start.48 = (f32[14]{0:T(128)}, f32[14]{0:T(128)S(1)}, u32[]{:S(2)}) copy-start(f32[14]{0:T(128)S(1)} %get-tuple-element.25) | copy-start | bytes 172
  18.4 64.2 %copy-start.50 = (f32[14]{0:T(128)}, f32[14]{0:T(128)S(1)}, u32[]{:S(2)}) copy-start(f32[14]{0:T(128)S(1)} %get-tuple-element.29) | copy-start | bytes 172
  18.4 64.2 %copy-start.52 = (f32[14]{0:T(128)}, f32[14]{0:T(128)S(1)}, u32[]{:S(2)}) copy-start(f32[14]{0:T(128)S(1)} %get-tuple-element.33) | copy-start | bytes 172
  18.4 64.2 %copy-start.54 = (f32[14]{0:T(128)}, f32[14]{0:T(128)S(1)}, u32[]{:S(2)}) copy-start(f32[14]{0:T(128)S(1)} %get-tuple-element.37) | copy-start | bytes 172
  18.4 65.1 %copy-start.38 = (f32[14]{0:T(128)}, f32[14]{0:T(128)S(1)}, u32[]{:S(2)}) copy-start(f32[14]{0:T(128)S(1)} %get-tuple-element.28) | copy-start | bytes 172
  18.4 65.1 %copy-start.40 = (f32[14]{0:T(128)}, f32[14]{0:T(128)S(1)}, u32[]{:S(2)}) copy-start(f32[14]{0:T(128)S(1)} %get-tuple-element.34) | copy-start | bytes 172
  18.4 65.1 %copy-start.42 = (f32[14]{0:T(128)}, f32[14]{0:T(128)S(1)}, u32[]{:S(2)}) copy-start(f32[14]{0:T(128)S(1)} %get-tuple-element.38) | copy-start | bytes 172
  18.4 66.7 %copy-start.24 = (f32[14]{0:T(128)}, f32[14]{0:T(128)S(1)}, u32[]{:S(2)}) copy-start(f32[14]{0:T(128)S(1)} %get-tuple-element.27) | copy-start | bytes 172
  18.4 66.7 %copy-start.26 = (f32[14]{0:T(128)}, f32[14]{0:T(128)S(1)}, u32[]{:S(2)}) copy-start(f32[14]{0:T(128)S(1)} %get-tuple-element.31) | copy-start | bytes 172
  18.4 67.0 %copy-start.12 = (f32[14]{0:T(128)}, f32[14]{0:T(128)S(1)}, u32[]{:S(2)}) copy-start(f32[14]{0:T(128)S(1)} %get-tuple-element.26) | copy-start | bytes 172
  18.4 67.0 %copy-start.14 = (f32[14]{0:T(128)}, f32[14]{0:T(128)S(1)}, u32[]{:S(2)}) copy-start(f32[14]{0:T(128)S(1)} %get-tuple-element.30) | copy-start | bytes 172
  19.5 64.1 %copy-start.64 = (f32[14]{0:T(128)}, f32[14]{0:T(128)S(1)}, u32[]{:S(2)}) copy-start(f32[14]{0:T(128)S(1)} %get-tuple-element.61) | copy-start | bytes 172
  19.5 65.2 %copy-start.16 = (f32[14]{0:T(128)}, f32[14]{0:T(128)S(1)}, u32[]{:S(2)}) copy-start(f32[14]{0:T(128)S(1)} %get-tuple-element.51) | copy-start | bytes 172
  19.5 65.2 %copy-start.18 = (f32[14]{0:T(128)}, f32[14]{0:T(128)S(1)}, u32[]{:S(2)}) copy-start(f32[14]{0:T(128)S(1)} %get-tuple-element.55) | copy-start | bytes 172
  19.5 65.2 %copy-start.20 = (f32[14]{0:T(128)}, f32[14]{0:T(128)S(1)}, u32[]{:S(2)}) copy-start(f32[14]{0:T(128)S(1)} %get-tuple-element.59) | copy-start | bytes 172
  19.5 65.4 %copy-start.10 = (f32[14]{0:T(128)}, f32[14]{0:T(128)S(1)}, u32[]{:S(2)}) copy-start(f32[14]{0:T(128)S(1)} %get-tuple-element.57) | copy-start | bytes 172
  19.5 65.6 %copy-start.36 = (f32[14]{0:T(128)}, f32[14]{0:T(128)S(1)}, u32[]{:S(2)}) copy-start(f32[14]{0:T(128)S(1)} %get-tuple-element.60) | copy-start | bytes 172
  19.5 65.9 %copy-start.28 = (f32[14]{0:T(128)}, f32[14]{0:T(128)S(1)}, u32[]{:S(2)}) copy-start(f32[14]{0:T(128)S(1)} %get-tuple-element.52) | copy-start | bytes 172
  19.5 65.9 %copy-start.30 = (f32[14]{0:T(128)}, f32[14]{0:T(128)S(1)}, u32[]{:S(2)}) copy-start(f32[14]{0:T(128)S(1)} %get-tuple-element.56) | copy-start | bytes 172
  33.0 6.9 %collective-permute-start = (bf16[14,4,1024]{2,1,0:T(4,128)(2,1)S(1)}, bf16[14,4,1024]{2,1,0:T(4,128)(2,1)S(1)}, u32[]{:S(2)}, u32[]{:S(2)}) collective-permute-start(bf16[14,4,1024]{2,1,0:T(4,128)(2,1)S(1)} %get-tuple-element.88), channel_id=1, source_target_pairs={{0,16},{16,32},{32,48},{48,64},{64,80},{80,96},{96,112},{1,17},{17... | collective-permute-start | bytes 344072 | tf_op jit(solution)/shard_map/ppermute | solution.py:20
  36.0 6.1 %collective-permute-start.1 = (bf16[14,4,1024]{2,1,0:T(4,128)(2,1)S(1)}, bf16[14,4,1024]{2,1,0:T(4,128)(2,1)S(1)}, u32[]{:S(2)}, u32[]{:S(2)}) collective-permute-start(bf16[14,4,1024]{2,1,0:T(4,128)(2,1)S(1)} %get-tuple-element.89), channel_id=1, source_target_pairs={{16,0},{32,16},{48,32},{64,48},{80,64},{96,80},{112,96},{17,1},{33... | collective-permute-start | bytes 344072 | tf_op jit(solution)/shard_map/ppermute | solution.py:22
  69.6 4.5 %collective-permute-start.2 = (f32[14,1,256]{2,1,0:T(1,128)S(1)}, f32[14,1,256]{2,1,0:T(1,128)S(1)}, u32[]{:S(2)}, u32[]{:S(2)}) collective-permute-start(f32[14,1,256]{2,1,0:T(1,128)S(1)} %get-tuple-element.108), channel_id=1, source_target_pairs={{0,16},{16,32},{32,48},{48,64},{64,80},{80,96},{96,112},{1,17},{17... | collective-permute-start | bytes 43016 | tf_op jit(solution)/shard_map/ppermute | solution.py:20
  71.5 5.0 %collective-permute-start.3 = (f32[14,1,256]{2,1,0:T(1,128)S(1)}, f32[14,1,256]{2,1,0:T(1,128)S(1)}, u32[]{:S(2)}, u32[]{:S(2)}) collective-permute-start(f32[14,1,256]{2,1,0:T(1,128)S(1)} %get-tuple-element.109), channel_id=1, source_target_pairs={{16,0},{32,16},{48,32},{64,48},{80,64},{96,80},{112,96},{17,1},{33... | collective-permute-start | bytes 43016 | tf_op jit(solution)/shard_map/ppermute | solution.py:22
  97.4 302.2 %all-reduce.9.cloned.1.call-start = ((), (), s32[]{:S(2)}) async-start(), calls=%async_computation.5 | async-start | bytes 4194304 | tf_op jit(solution)/shard_map/psum | solution.py:99
  246.8 5.1 %collective-permute-start.4 = (bf16[14,4,1024]{2,1,0:T(4,128)(2,1)S(1)}, bf16[14,4,1024]{2,1,0:T(4,128)(2,1)S(1)}, u32[]{:S(2)}, u32[]{:S(2)}) collective-permute-start(bf16[14,4,1024]{2,1,0:T(4,128)(2,1)S(1)} %get-tuple-element.86), channel_id=1, source_target_pairs={{0,16},{16,32},{32,48},{48,64},{64,80},{80,96},{96,112},{1,17},{17... | collective-permute-start | bytes 344072 | tf_op jit(solution)/shard_map/ppermute | solution.py:20
  250.0 6.1 %collective-permute-start.5 = (bf16[14,4,1024]{2,1,0:T(4,128)(2,1)S(1)}, bf16[14,4,1024]{2,1,0:T(4,128)(2,1)S(1)}, u32[]{:S(2)}, u32[]{:S(2)}) collective-permute-start(bf16[14,4,1024]{2,1,0:T(4,128)(2,1)S(1)} %get-tuple-element.87), channel_id=1, source_target_pairs={{16,0},{32,16},{48,32},{64,48},{80,64},{96,80},{112,96},{17,1},{33... | collective-permute-start | bytes 344072 | tf_op jit(solution)/shard_map/ppermute | solution.py:22
  284.4 4.6 %collective-permute-start.6 = (f32[14,1,256]{2,1,0:T(1,128)S(1)}, f32[14,1,256]{2,1,0:T(1,128)S(1)}, u32[]{:S(2)}, u32[]{:S(2)}) collective-permute-start(f32[14,1,256]{2,1,0:T(1,128)S(1)} %get-tuple-element.106), channel_id=1, source_target_pairs={{0,16},{16,32},{32,48},{48,64},{64,80},{80,96},{96,112},{1,17},{17... | collective-permute-start | bytes 43016 | tf_op jit(solution)/shard_map/ppermute | solution.py:20
  286.3 5.0 %collective-permute-start.7 = (f32[14,1,256]{2,1,0:T(1,128)S(1)}, f32[14,1,256]{2,1,0:T(1,128)S(1)}, u32[]{:S(2)}, u32[]{:S(2)}) collective-permute-start(f32[14,1,256]{2,1,0:T(1,128)S(1)} %get-tuple-element.107), channel_id=1, source_target_pairs={{16,0},{32,16},{48,32},{64,48},{80,64},{96,80},{112,96},{17,1},{33... | collective-permute-start | bytes 43016 | tf_op jit(solution)/shard_map/ppermute | solution.py:22
  (68 other events, 1749.5 us)
Sparse Core Ops, SparseCore 0:
  97.6 90.2 all-reduce.6
  312.4 87.1 all-reduce.8
where the time goes:
time: 457 us; the launch traced here: 449 us
  waiting for transfers between devices  152 us (33%)
  blocking collectives  118 us (26%)
  local copies, waits for them, and re-layouts  89.6 us (20%)
  other arithmetic  35.7 us (8%)
  starting transfers between devices  24.8 us (5%)
  between operations  15.6 us (3%)
  matrix products  12.7 us (3%)
    psum x2, waiting for transfers between devices, per_device(): hs_total = lax.psum(hs_part, 'band')  129 us
    all_to_all x2, blocking collectives, per_device(): lax.all_to_all(update, 'sub', split_axis=0, concat_axis=1, tiled=True)  65 us
    psum x1, blocking collectives, per_device(): combined = lax.psum(partial_map, 'band').astype(jnp.bfloat16)  35 us
    unnamed x190, local copies, waits for them, and re-layouts  31.5 us
    reshape x2, local copies, waits for them, and re-layouts, hs_gradient(): padded.reshape(bands, groups + 2, 4, columns + 2, 4)  22.2 us
    all_to_all x1, blocking collectives, per_device(): lax.all_to_all(current.astype(jnp.bfloat16), 'sub', split_axis=1, concat_...  18.5 us
    another operation x24, other arithmetic, hs_gradient(): outer.append(jnp.stack(inner, axis=1))  16.7 us
    pad x2, local copies, waits for them, and re-layouts, hs_gradient(): padded = jnp.pad(extended, ((0, 0), (0, 0), (4, 4)))  15 us
  transfers between devices with their start and end apart: 11, of which 7 were waited for; matrix products, arithmetic and copies ran while one was open for 4% of the time, Pallas kernels for 0%

commit v1 on v0

v1 whole, which is shorter than its diff:
```python
import functools

import jax
import jax.numpy as jnp
from jax import lax
from jax.experimental import pallas as pl
from jax.experimental.pallas import tpu as pltpu
from jax.sharding import PartitionSpec as P

STEP = 0.15
TR, TC = 16, 64
TAPS = 9
LANES = 128
CROWS = 48
MROWS = 32
IROWS = 10
JCOLS = 24
ROWS_LO, COLS_LO = 32, 256
f32 = jnp.float32
bf16 = jnp.bfloat16


def rounded(value):
    return value.astype(bf16).astype(f32)


def refine_kernel(pos_ref, c_ref, hp_ref, ms_ref, out_ref, m0, m1, f0, f1, b0, b1, c1_ref, hs0, hs1, w0, w1):
    s = pos_ref[0]
    b = pos_ref[1]
    m = (m0, m1)
    f = (f0, f1)
    bk = (b0, b1)
    hst = (hs0, hs1)
    w = (w0, w1)
    for h in range(2):
        part = hp_ref[h * 128 : h * 128 + 128, :]
        for piece in range(2):
            hst[h][piece * 128 : piece * 128 + 128, :] = part[:, piece * 128 : piece * 128 + 128].T
        w[h][...] = part[:, 256:384].T
    basis = jnp.concatenate([w0[81:113, :], w1[81:113, :]], axis=1).astype(bf16)
    response = jnp.concatenate([w0[113:121, :], w1[113:121, :]], axis=1).astype(bf16)
    combined = lax.dot_general(response, basis, (((1,), (1,)), ((), ())), preferred_element_type=f32).astype(bf16)
    lane = lax.broadcasted_iota(jnp.int32, (1, LANES), 1)
    column = 64 * b - 16 + lane
    in_columns = (column >= 0) & (column < 1024) & (lane >= 8) & (lane < 88)

    def mix(row, value):
        mixed = lax.dot_general(
            value.astype(bf16), basis, (((0,), (0,)), ((), ())), preferred_element_type=f32
        )
        mixed = rounded(mixed)
        for h in range(2):
            m[h][pl.ds(pl.multiple_of(row * LANES, LANES), LANES), :] = mixed[:, h * 128 : h * 128 + 128]

    def blur_row(n, lane0, i_off, j_off):
        jj = lax.broadcasted_iota(jnp.int32, (JCOLS, LANES), 0) + j_off
        i_at = 4 * s + n + i_off - 3
        j_at = 16 * b + jj - 3
        inside = (i_at >= 0) & (i_at < ROWS_LO) & (j_at >= 0) & (j_at < COLS_LO)
        for h in range(2):
            acc = [None, None, None]
            for a in range(TAPS):
                for q in range(4):
                    x = m[h][pl.ds((4 * n + a) * LANES + lane0 + q, JCOLS, stride=4), :]
                    for d in range(3):
                        if 4 * d + q > 8:
                            continue
                        term = w[h][a * 9 + 4 * d + q : a * 9 + 4 * d + q + 1, :] * x
                        acc[d] = term if acc[d] is None else acc[d] + term
            blurred = (
                acc[0]
                + pltpu.roll(acc[1], JCOLS - 1, 0)
                + pltpu.roll(acc[2], JCOLS - 2, 0)
            )
            seen = hst[h][pl.ds((n + i_off) * JCOLS + j_off, JCOLS), :]
            f[h][pl.ds(pl.multiple_of(n * JCOLS, 8), JCOLS), :] = jnp.where(inside, seen - blurred, 0.0)

    def back_rows(u, lane0, width):
        for h in range(2):
            win = [
                [f[h][pl.ds((u + 2 - t) * JCOLS + 2 - tt, width), :] for tt in range(3)]
                for t in range(3)
            ]
            for p in range(4):
                for q in range(4):
                    total = None
                    for t in range(3):
                        for tt in range(3):
                            if p + 4 * t > 8 or q + 4 * tt > 8:
                                continue
                            tap = (p + 4 * t) * 9 + q + 4 * tt
                            term = w[h][tap : tap + 1, :] * win[t][tt]
                            total = term if total is None else total + term
                    bk[h][pl.ds((4 * u + p) * LANES + lane0 + q, width, stride=4), :] = rounded(total)

    def gradient(row, ms_row, now):
        at = pl.ds(pl.multiple_of(row * LANES, LANES), LANES)
        back = jnp.concatenate([b0[at, :], b1[at, :]], axis=1).astype(bf16)
        hs_grad = lax.dot_general(basis, back, (((1,), (1,)), ((), ())), preferred_element_type=f32)
        near = now.astype(bf16)
        predicted = jnp.dot(combined, near, preferred_element_type=f32)
        ms_misfit = (ms_ref[pl.ds(ms_row, 8, stride=MROWS), :] - predicted).astype(bf16)
        ms_grad = lax.dot_general(combined, ms_misfit, (((0,), (0,)), ((), ())), preferred_element_type=f32)
        return now + STEP * (hs_grad + ms_grad)

    def start_row(row):
        return c_ref[pl.ds(row, 32, stride=CROWS), :]

    def loop(count, body):
        def step(n, _):
            body(n)
            return 0

        lax.fori_loop(0, count, step, 0)

    loop(CROWS, lambda r: mix(r, start_row(r)))
    loop(IROWS, lambda n: blur_row(n, 0, 0, 0))
    loop(MROWS // 4, lambda u: back_rows(u, 8, 24))

    def first(r):
        row_at = 16 * s - 8 + r
        value = gradient(r, r, start_row(r + 8))
        value = jnp.where(in_columns & (row_at >= 0) & (row_at < 128), value, 0.0)
        c1_ref[pl.ds(pl.multiple_of(r * 32, 32), 32), :] = value
        mix(r, value)

    loop(MROWS, first)
    loop(6, lambda n: blur_row(n, 8, 2, 2))
    loop(TR // 4, lambda u: back_rows(u, 16, 16))

    def last(r):
        halves = []
        for half in range(2):
            row = r + 8 * half
            now = c1_ref[pl.ds(pl.multiple_of((row + 8) * 32, 32), 32), :]
            value = gradient(row, row + 8, now)
            halves.append(pltpu.roll(value, LANES - 16 if half == 0 else 48, 1))
        out_ref[pl.ds(r, 32, stride=8), :] = jnp.where(lane < 64, halves[0], halves[1])

    loop(8, last)


def refine(pos, c, hp, ms):
    vmem = pl.BlockSpec(memory_space=pltpu.VMEM)
    return pl.pallas_call(
        refine_kernel,
        out_shape=jax.ShapeDtypeStruct((32 * 8, LANES), f32),
        in_specs=[pl.BlockSpec(memory_space=pltpu.SMEM), vmem, vmem, vmem],
        out_specs=vmem,
        scratch_shapes=[
            pltpu.VMEM((CROWS * LANES, LANES), f32),
            pltpu.VMEM((CROWS * LANES, LANES), f32),
            pltpu.VMEM((256, LANES), f32),
            pltpu.VMEM((256, LANES), f32),
            pltpu.VMEM((MROWS * LANES, LANES), f32),
            pltpu.VMEM((MROWS * LANES, LANES), f32),
            pltpu.VMEM((MROWS * 32, LANES), f32),
            pltpu.VMEM((256, LANES), f32),
            pltpu.VMEM((256, LANES), f32),
            pltpu.VMEM((LANES, LANES), f32),
            pltpu.VMEM((LANES, LANES), f32),
        ],
        compiler_params=pltpu.CompilerParams(vmem_limit_bytes=40 * 2**20),
        cost_estimate=pl.CostEstimate(flops=400_000_000, bytes_accessed=2_000_000, transcendentals=0),
        name="refine",
    )(pos, c, hp, ms)


def place_kernel(g_ref, out_ref):
    lane = lax.broadcasted_iota(jnp.int32, (1, LANES), 1)
    low = lane < 64
    for s in range(8):
        for j in range(8):
            even = g_ref[2 * j, s, 0]
            odd = g_ref[2 * j + 1, s, 0]
            at = slice(j * 128, j * 128 + 128)
            out_ref[0, 16 * s : 16 * s + 8, at] = jnp.where(low, even, pltpu.roll(odd, 64, 1))
            out_ref[0, 16 * s + 8 : 16 * s + 16, at] = jnp.where(low, pltpu.roll(even, 64, 1), odd)


def place(gathered):
    return pl.pallas_call(
        place_kernel,
        out_shape=jax.ShapeDtypeStruct((4, 128, 1024), f32),
        grid=(4,),
        in_specs=[pl.BlockSpec((16, 8, 1, 8, LANES), lambda k: (0, 0, k, 0, 0))],
        out_specs=pl.BlockSpec((1, 128, 1024), lambda k: (k, 0, 0)),
        compiler_params=pltpu.CompilerParams(vmem_limit_bytes=32 * 2**20),
        name="place",
    )(gathered)


def per_device(coeffs_in, basis, kernels, response, hs_image, ms_image):
    s = lax.axis_index("sub")
    b = lax.axis_index("band")
    up = [(i, i + 1) for i in range(7)]
    down = [(i + 1, i) for i in range(7)]
    ms_wide = jnp.pad(ms_image, ((0, 0), (0, 0), (16, 48)))
    ms_tile = lax.dynamic_slice(ms_wide, (0, 0, 64 * b), (8, TR, LANES))
    hs_above = lax.ppermute(hs_image[:, 1:, :], "sub", up)
    hs_below = lax.ppermute(hs_image[:, :3, :], "sub", down)
    ms_above = lax.ppermute(ms_tile[:, 8:, :], "sub", up)
    ms_below = lax.ppermute(ms_tile[:, :8, :], "sub", down)
    hs = jnp.concatenate([hs_above, hs_image, hs_below], axis=1)
    ms = jnp.concatenate([ms_above, ms_tile, ms_below], axis=1).astype(f32)
    hs = jnp.pad(hs, ((0, 2), (0, 0), (3, 5))).astype(f32)
    windows = jnp.stack([hs[:, :, 16 * t : 16 * t + JCOLS] for t in range(16)])
    windows = jnp.pad(windows.reshape(16, 16, IROWS * JCOLS), ((0, 0), (0, 0), (0, 16)))
    params = jnp.concatenate(
        [kernels.reshape(14, 81), basis.astype(f32), response.T.astype(f32)], axis=1
    )
    params = jnp.pad(params, ((0, 2), (0, 7)))
    sent = jnp.concatenate([windows, jnp.broadcast_to(params, (16, 16, 128))], axis=2)
    hp = lax.all_to_all(sent, "band", split_axis=0, concat_axis=0, tiled=True).reshape(256, 384)
    wide = jnp.pad(coeffs_in, ((0, 0), (16, 16), (16, 48)))
    wide = lax.dynamic_slice(wide, (0, 0, 64 * b), (4, 160, LANES))
    tiles = jnp.stack([wide[:, 16 * t : 16 * t + CROWS] for t in range(8)])
    c = lax.all_to_all(tiles, "sub", split_axis=0, concat_axis=0, tiled=True).reshape(32 * CROWS, LANES)
    pos = jnp.stack([s, b]).astype(jnp.int32)
    new = refine(pos, c, hp, ms.reshape(8 * MROWS, LANES))
    owned = lax.all_to_all(new.reshape(8, 4, 8, LANES), "sub", split_axis=0, concat_axis=0, tiled=True)
    copies = jnp.broadcast_to(owned[None], (16,) + owned.shape)
    gathered = lax.all_to_all(copies, "band", split_axis=0, concat_axis=0, tiled=True)
    return place(gathered)


def solution(mesh):
    return jax.shard_map(
        per_device,
        mesh=mesh,
        in_specs=(
            P("sub", None, None),
            P("band", None),
            P("band", None, None),
            P(None, "band"),
            P("band", "sub", None),
            P(None, "sub", None),
        ),
        out_specs=P("sub", None, None),
        check_vma=False,
    )
```

time: 457 us -> 142 us (0.31); the launches traced: 449 us -> 140 us
  waiting for transfers between devices: 152 us -> 12.7 us
  blocking collectives: 118 us -> 38.7 us
  local copies, waits for them, and re-layouts: 89.6 us -> 24 us
  Pallas kernels: 0 us -> 36.1 us
  other arithmetic: 35.7 us -> 3.16 us
  between operations: 15.6 us -> 0.22 us
  matrix products: 12.7 us -> 0 us
    psum x2 -> x0, waiting for transfers between devices: 129 us -> none  [per_device(): hs_total = lax.psum(hs_part, 'band')]
    all_to_all x3 -> x2, blocking collectives: 83.5 us -> 38.7 us  [the longest x1 30 us: per_device(): lax.all_to_all(copies, 'band', split_axis=0, concat_axis=0, tiled=True)]
    pallas_call x0 -> x2, Pallas kernels: none -> 36.1 us  [the longest x1 33.6 us: refine(): pl.pallas_call(refine_kernel, out_shape=jax.ShapeDtypeStruct((32 * 8, LAN...]
    psum x1 -> x0, blocking collectives: 35 us -> none  [per_device(): combined = lax.psum(partial_map, 'band').astype(jnp.bfloat16)]
    unnamed x190 -> x28, local copies, waits for them, and re-layouts: 31.5 us -> 9.77 us
    reshape x4 -> x2, local copies, waits for them, and re-layouts: 22.3 us -> 1 us  [per_device(): kernels.reshape(14, 81)]
    another operation x30 -> x1, other arithmetic: 17.4 us -> 0.07 us  [per_device(): pos = jnp.stack([s, b]).astype(jnp.int32)]
    pad x2 -> x0, local copies, waits for them, and re-layouts: 15 us -> none  [hs_gradient(): padded = jnp.pad(extended, ((0, 0), (0, 0), (4, 4)))]
  transfers between devices with their start and end apart: 11 -> 6, of which waited for: 7 -> 4; matrix products, arithmetic and copies ran while one was open for 4% -> 7% of each run, Pallas kernels for 0% -> 0%
where the time goes in v1:
time: 142 us; the launch traced here: 140 us
  blocking collectives  38.7 us (27%)
  Pallas kernels  36.1 us (25%)
  starting transfers between devices  25.5 us (18%)
  local copies, waits for them, and re-layouts  24 us (17%)
  waiting for transfers between devices  12.7 us (9%)
  other arithmetic  3.16 us (2%)
    pallas_call x1, Pallas kernels, refine(): pl.pallas_call(refine_kernel, out_shape=jax.ShapeDtypeStruct((32 * 8, LAN...  33.6 us
    all_to_all x1, blocking collectives, per_device(): lax.all_to_all(copies, 'band', split_axis=0, concat_axis=0, tiled=True)  30 us
    unnamed x28, local copies, waits for them, and re-layouts  9.77 us
    another operation x17, local copies, waits for them, and re-layouts, per_device(): windows = jnp.stack([hs[:, :, 16 * t:16 * t + JCOLS] for t in range(16)])  8.97 us
    all_to_all x1, blocking collectives, per_device(): lax.all_to_all(new.reshape(8, 4, 8, LANES), 'sub', split_axis=0, concat_a...  8.71 us
    all_to_all x1, starting transfers between devices, per_device(): lax.all_to_all(sent, 'band', split_axis=0, concat_axis=0, tiled=True)  7.77 us
    all_to_all x1, waiting for transfers between devices, per_device(): lax.all_to_all(sent, 'band', split_axis=0, concat_axis=0, tiled=True)  6.21 us
    all_to_all x1, starting transfers between devices, per_device(): lax.all_to_all(tiles, 'sub', split_axis=0, concat_axis=0, tiled=True)  5.84 us
  transfers between devices with their start and end apart: 6, of which 4 were waited for; matrix products, arithmetic and copies ran while one was open for 7% of the time, Pallas kernels for 0%

profile of v1, /device:TPU:1, one launch (start us, length us, event | category | flops | bytes accessed | tf_op | source)
XLA Modules:
  0.0 140.4 jit_solution(862895312376421594)
XLA Ops:
  0.0 0.9 fusion.12
  0.9 4.5 %collective-permute-start = (bf16[14,3,256]{2,1,0:T(4,128)(2,1)S(1)}, bf16[14,3,256]{2,1,0:T(4,128)(2,1)S(1)}, u32[]{:S(2)}, u32[]{:S(2)}) collective-permute-start(bf16[14,3,256]{2,1,0:T(4,128)(2,1)S(1)} %get-tuple-element.23), channel_id=1, source_target_pairs={{0,16},{16,32},{32,48},{48,64},{64,80},{80,96},{96,112},{1,17},{17... | collective-permute-start | bytes 64520 | tf_op jit(solution)/shard_map/ppermute | solution.py:200
  5.5 1.9 %collective-permute-start.1 = (bf16[14,3,256]{2,1,0:T(4,128)(2,1)S(1)}, bf16[14,3,256]{2,1,0:T(4,128)(2,1)S(1)}, u32[]{:S(2)}, u32[]{:S(2)}) collective-permute-start(bf16[14,3,256]{2,1,0:T(4,128)(2,1)S(1)} %get-tuple-element.24), channel_id=1, source_target_pairs={{16,0},{32,16},{48,32},{64,48},{80,64},{96,80},{112,96},{17,1},{33... | collective-permute-start | bytes 64520 | tf_op jit(solution)/shard_map/ppermute | solution.py:201
  8.9 0.9 copy.17
  9.9 1.6 %bitcast_dynamic-update-slice_fusion.7 = f32[8,4,48,128]{3,2,1,0:T(8,128)} fusion(s32[]{:T(128)S(6)} %select_n.4, f32[4,128,1024]{2,1,0:T(8,128)} %param.6), kind=kLoop, calls=%fused_computation.34 | loop fusion | bytes 2195460
  11.5 0.7 bitcast_dynamic-update-slice_fusion.6
  12.3 0.7 bitcast_dynamic-update-slice_fusion.5
  13.0 0.7 bitcast_dynamic-update-slice_fusion.4
  14.7 1.4 fusion.11
  16.0 1.0 stack.114
  17.0 1.6 %stack.113 = f32[1,16,240]{2,1,0:T(8,128)} reshape(f32[16,10,24]{2,1,0:T(8,128)} %get-tuple-element.6) | data formatting | bytes 30720 | tf_op jit(solution)/shard_map/stack | solution.py:207
  18.6 1.6 %stack.112 = f32[1,16,240]{2,1,0:T(8,128)} reshape(f32[16,10,24]{2,1,0:T(8,128)} %get-tuple-element.7) | data formatting | bytes 30720 | tf_op jit(solution)/shard_map/stack | solution.py:207
  20.2 1.6 %stack.111 = f32[1,16,240]{2,1,0:T(8,128)} reshape(f32[16,10,24]{2,1,0:T(8,128)} %get-tuple-element.8) | data formatting | bytes 30720 | tf_op jit(solution)/shard_map/stack | solution.py:207
  21.8 1.6 %stack.110 = f32[1,16,240]{2,1,0:T(8,128)} reshape(f32[16,10,24]{2,1,0:T(8,128)} %get-tuple-element.9) | data formatting | bytes 30720 | tf_op jit(solution)/shard_map/stack | solution.py:207
  25.2 0.7 constant_dynamic-update-slice_fusion.5
  29.5 0.8 select_maximum_fusion
  30.2 7.8 %all-to-all-start.1 = ((f32[16,16,384]{2,1,0:T(8,128)}), f32[16,16,384]{2,1,0:T(8,128)S(1)}, u32[]{:S(2)}, u32[]{:S(2)}) async-start(f32[16,16,384]{2,1,0:T(8,128)} %select_maximum_fusion), calls=%async_computation.1 | async-start | bytes 786432 | tf_op jit(solution)/shard_map/all_to_all | solution.py:214
  38.0 0.8 bitcast_dynamic-update-slice_fusion.3
  38.8 0.7 bitcast_dynamic-update-slice_fusion.2
  39.5 0.7 bitcast_dynamic-update-slice_fusion.1
  40.3 0.7 bitcast_dynamic-update-slice_fusion
  41.0 6.2 %all-to-all-done.1 = f32[16,16,384]{2,1,0:T(8,128)S(1)} async-done(((f32[16,16,384]{2,1,0:T(8,128)}), f32[16,16,384]{2,1,0:T(8,128)S(1)}, u32[]{:S(2)}, u32[]{:S(2)}) %all-to-all-start.1) | async-done | bytes 393248 | tf_op jit(solution)/shard_map/all_to_all | solution.py:214
  47.2 5.8 %all-to-all-start = ((f32[8,4,48,128]{3,2,1,0:T(8,128)}), f32[8,4,48,128]{3,2,1,0:T(8,128)S(1)}, u32[]{:S(2)}, u32[]{:S(2)}) async-start(f32[8,4,48,128]{3,2,1,0:T(8,128)} %bitcast_dynamic-update-slice_fusion), calls=%async_computation | async-start | bytes 1572864 | tf_op jit(solution)/shard_map/all_to_all | solution.py:218
  53.2 3.5 %collective-permute-start.2 = (bf16[8,8,128]{2,1,0:T(8,128)(2,1)S(1)}, bf16[8,8,128]{2,1,0:T(8,128)(2,1)S(1)}, u32[]{:S(2)}, u32[]{:S(2)}) collective-permute-start(bf16[8,8,128]{2,1,0:T(8,128)(2,1)S(1)} %get-tuple-element.21), channel_id=1, source_target_pairs={{0,16},{16,32},{32,48},{48,64},{64,80},{80,96},{96,112},{1,17},{17... | collective-permute-start | bytes 49160 | tf_op jit(solution)/shard_map/ppermute | solution.py:202
  56.7 1.9 %collective-permute-start.3 = (bf16[8,8,128]{2,1,0:T(8,128)(2,1)S(1)}, bf16[8,8,128]{2,1,0:T(8,128)(2,1)S(1)}, u32[]{:S(2)}, u32[]{:S(2)}) collective-permute-start(bf16[8,8,128]{2,1,0:T(8,128)(2,1)S(1)} %get-tuple-element.22), channel_id=1, source_target_pairs={{16,0},{32,16},{48,32},{64,48},{80,64},{96,80},{112,96},{17,1},{33... | collective-permute-start | bytes 49160 | tf_op jit(solution)/shard_map/ppermute | solution.py:203
  58.8 3.6 %collective-permute-done.2 = bf16[8,8,128]{2,1,0:T(8,128)(2,1)S(1)} collective-permute-done((bf16[8,8,128]{2,1,0:T(8,128)(2,1)S(1)}, bf16[8,8,128]{2,1,0:T(8,128)(2,1)S(1)}, u32[]{:S(2)}, u32[]{:S(2)}) %collective-permute-start.2) | collective-permute-done | bytes 16416 | tf_op jit(solution)/shard_map/ppermute | solution.py:202
  62.4 2.1 %collective-permute-done.3 = bf16[8,8,128]{2,1,0:T(8,128)(2,1)S(1)} collective-permute-done((bf16[8,8,128]{2,1,0:T(8,128)(2,1)S(1)}, bf16[8,8,128]{2,1,0:T(8,128)(2,1)S(1)}, u32[]{:S(2)}, u32[]{:S(2)}) %collective-permute-start.3) | collective-permute-done | bytes 16416 | tf_op jit(solution)/shard_map/ppermute | solution.py:203
  64.5 0.8 all-to-all-done
  65.3 33.6 %refine.1 = f32[256,128]{1,0:T(8,128)S(1)} custom-call(s32[2]{0:T(128)S(1)} %pad_add_fusion.pos_ref, f32[1536,128]{1,0:T(8,128)S(1)} %bitcast.26, f32[256,384]{1,0:T(8,128)S(1)} %bitcast.27, f32[256,128]{1,0:T(8,128)S(1)} %bitcast_convert_fusion.ms_ref), custom_call_target="tpu_custom_call" | custom-call | flops 400000000 | bytes 2000000 | tf_op jit(solution)/shard_map/refine/pallas_call | solution.py:145
  99.0 8.7 %all_to_all.20 = f32[8,4,8,128]{3,2,1,0:T(8,128)S(1)} all-to-all(f32[8,4,8,128]{3,2,1,0:T(8,128)S(1)} %bitcast.28), channel_id=1, replica_groups=mesh['sub'=8,'band'=16] {'sub'}, dimensions={0} | all-to-all | bytes 262144 | tf_op jit(solution)/shard_map/all_to_all | solution.py:221
  108.0 30.0 %all_to_all.21.g_ref = f32[16,8,4,8,128]{4,3,2,1,0:T(8,128)S(1)} all-to-all(f32[16,8,4,8,128]{4,3,2,1,0:T(8,128)S(1)} %broadcast_in_dim.10), channel_id=1, replica_groups=mesh['sub'=8,'band'=16] {'band'}, dimensions={0} | all-to-all | bytes 4194304 | tf_op jit(solution)/shard_map/all_to_all | solution.py:223
  137.9 2.4 %place.1 = f32[4,128,1024]{2,1,0:T(8,128)} custom-call(f32[16,8,4,8,128]{4,3,2,1,0:T(8,128)S(1)} %all_to_all.21.g_ref), custom_call_target="tpu_custom_call" | custom-call | tf_op jit(solution)/shard_map/place/pallas_call | solution.py:182
  (47 shorter events, 8.3 us)
Async XLA Ops:
  0.0 11.5 %copy-start = (f32[4,128,1024]{2,1,0:T(8,128)S(1)}, f32[4,128,1024]{2,1,0:T(8,128)}, u32[]{:S(2)}) copy-start(f32[4,128,1024]{2,1,0:T(8,128)} %param.6) | copy-start | bytes 6291460
  0.9 13.5 %collective-permute-start = (bf16[14,3,256]{2,1,0:T(4,128)(2,1)S(1)}, bf16[14,3,256]{2,1,0:T(4,128)(2,1)S(1)}, u32[]{:S(2)}, u32[]{:S(2)}) collective-permute-start(bf16[14,3,256]{2,1,0:T(4,128)(2,1)S(1)} %get-tuple-element.23), channel_id=1, source_target_pairs={{0,16},{16,32},{32,48},{48,64},{64,80},{80,96},{96,112},{1,17},{17... | collective-permute-start | bytes 64520 | tf_op jit(solution)/shard_map/ppermute | solution.py:200
  5.5 9.0 %collective-permute-start.1 = (bf16[14,3,256]{2,1,0:T(4,128)(2,1)S(1)}, bf16[14,3,256]{2,1,0:T(4,128)(2,1)S(1)}, u32[]{:S(2)}, u32[]{:S(2)}) collective-permute-start(bf16[14,3,256]{2,1,0:T(4,128)(2,1)S(1)} %get-tuple-element.24), channel_id=1, source_target_pairs={{16,0},{32,16},{48,32},{64,48},{80,64},{96,80},{112,96},{17,1},{33... | collective-permute-start | bytes 64520 | tf_op jit(solution)/shard_map/ppermute | solution.py:201
  12.3 2.2 %copy-start.2 = (bf16[14,4,256]{2,1,0:T(4,128)(2,1)S(1)}, bf16[14,4,256]{2,1,0:T(4,128)(2,1)}, u32[]{:S(2)}) copy-start(bf16[14,4,256]{2,1,0:T(4,128)(2,1)} %param.10) | copy-start | bytes 86020
  30.2 17.0 %all-to-all-start.1 = ((f32[16,16,384]{2,1,0:T(8,128)}), f32[16,16,384]{2,1,0:T(8,128)S(1)}, u32[]{:S(2)}, u32[]{:S(2)}) async-start(f32[16,16,384]{2,1,0:T(8,128)} %select_maximum_fusion), calls=%async_computation.1 | async-start | bytes 786432 | tf_op jit(solution)/shard_map/all_to_all | solution.py:214
  40.3 12.8 %copy-start.1 = (bf16[8,16,1024]{2,1,0:T(8,128)(2,1)S(1)}, bf16[8,16,1024]{2,1,0:T(8,128)(2,1)}, u32[]{:S(2)}) copy-start(bf16[8,16,1024]{2,1,0:T(8,128)(2,1)} %param.11) | copy-start | bytes 786436
  47.2 18.1 %all-to-all-start = ((f32[8,4,48,128]{3,2,1,0:T(8,128)}), f32[8,4,48,128]{3,2,1,0:T(8,128)S(1)}, u32[]{:S(2)}, u32[]{:S(2)}) async-start(f32[8,4,48,128]{3,2,1,0:T(8,128)} %bitcast_dynamic-update-slice_fusion), calls=%async_computation | async-start | bytes 1572864 | tf_op jit(solution)/shard_map/all_to_all | solution.py:218
  53.2 9.2 %collective-permute-start.2 = (bf16[8,8,128]{2,1,0:T(8,128)(2,1)S(1)}, bf16[8,8,128]{2,1,0:T(8,128)(2,1)S(1)}, u32[]{:S(2)}, u32[]{:S(2)}) collective-permute-start(bf16[8,8,128]{2,1,0:T(8,128)(2,1)S(1)} %get-tuple-element.21), channel_id=1, source_target_pairs={{0,16},{16,32},{32,48},{48,64},{64,80},{80,96},{96,112},{1,17},{17... | collective-permute-start | bytes 49160 | tf_op jit(solution)/shard_map/ppermute | solution.py:202
  56.7 7.8 %collective-permute-start.3 = (bf16[8,8,128]{2,1,0:T(8,128)(2,1)S(1)}, bf16[8,8,128]{2,1,0:T(8,128)(2,1)S(1)}, u32[]{:S(2)}, u32[]{:S(2)}) collective-permute-start(bf16[8,8,128]{2,1,0:T(8,128)(2,1)S(1)} %get-tuple-element.22), channel_id=1, source_target_pairs={{16,0},{32,16},{48,32},{64,48},{80,64},{96,80},{112,96},{17,1},{33... | collective-permute-start | bytes 49160 | tf_op jit(solution)/shard_map/ppermute | solution.py:203

commit v2 on v1

v2 whole, which is shorter than its diff:
```python
import functools

import jax
import jax.numpy as jnp
from jax import lax
from jax.experimental import pallas as pl
from jax.experimental.pallas import tpu as pltpu
from jax.sharding import PartitionSpec as P

STEP = 0.15
TR, TC = 16, 64
TAPS = 9
LANES = 128
CROWS = 48
MROWS = 32
IROWS = 10
JCOLS = 24
ROWS_LO, COLS_LO = 32, 256
f32 = jnp.float32
bf16 = jnp.bfloat16


def rounded(value):
    return value.astype(bf16).astype(f32)


def refine_kernel(pos_ref, c_ref, hp_ref, ms_ref, out_ref, m0, m1, f0, f1, b0, b1, c1_ref, g_ref, hs0, hs1, w0, w1):
    s = pos_ref[0]
    b = pos_ref[1]
    m = (m0, m1)
    f = (f0, f1)
    bk = (b0, b1)
    hst = (hs0, hs1)
    w = (w0, w1)
    for h in range(2):
        part = hp_ref[h * 128 : h * 128 + 128, :]
        for piece in range(2):
            hst[h][piece * 128 : piece * 128 + 128, :] = part[:, piece * 128 : piece * 128 + 128].T
        w[h][...] = part[:, 256:384].T
    basis = jnp.concatenate([w0[81:113, :], w1[81:113, :]], axis=1).astype(bf16)
    response = jnp.concatenate([w0[113:121, :], w1[113:121, :]], axis=1).astype(bf16)
    combined = lax.dot_general(response, basis, (((1,), (1,)), ((), ())), preferred_element_type=f32).astype(bf16)
    lane = lax.broadcasted_iota(jnp.int32, (1, LANES), 1)
    group = lane % 32
    column = 64 * b - 16 + 4 * group + lane // 32
    in_columns = (column >= 0) & (column < 1024) & (group >= 2) & (group < 22)

    def mix(row, value, rows):
        mixed = lax.dot_general(value.astype(bf16), basis, (((0,), (0,)), ((), ())), preferred_element_type=f32)
        mixed = rounded(mixed)
        at = pl.ds(pl.multiple_of(row * LANES, LANES), rows * LANES)
        for h in range(2):
            m[h][at, :] = mixed[:, h * 128 : h * 128 + 128]

    def ms_gradient(row, block):
        predicted = jnp.dot(combined, block.astype(bf16), preferred_element_type=f32)
        seen = jnp.concatenate([ms_ref[pl.ds(row - 8 + r, 8, stride=MROWS), :] for r in range(8)], axis=1)
        misfit = (seen - predicted).astype(bf16)
        grad = lax.dot_general(combined, misfit, (((0,), (0,)), ((), ())), preferred_element_type=f32)
        for r in range(8):
            g_ref[pl.ds((row - 8 + r) * 32, 32), :] = grad[:, r * 128 : r * 128 + 128]

    def blur_row(n):
        g = lax.broadcasted_iota(jnp.int32, (JCOLS, LANES), 0)
        i_at = 4 * s + n - 3
        j_at = 16 * b + g - 3
        inside = (i_at >= 0) & (i_at < ROWS_LO) & (j_at >= 0) & (j_at < COLS_LO)
        for h in range(2):
            acc = [None, None, None]
            for a in range(TAPS):
                for q in range(4):
                    at = pl.multiple_of((4 * n + a) * LANES + 32 * q, 32)
                    x = m[h][pl.ds(at, JCOLS), :]
                    for d in range(3):
                        if 4 * d + q > 8:
                            continue
                        tap = a * 9 + 4 * d + q
                        term = w[h][tap : tap + 1, :] * x
                        acc[d] = term if acc[d] is None else acc[d] + term
            blurred = acc[0] + pltpu.roll(acc[1], JCOLS - 1, 0) + pltpu.roll(acc[2], JCOLS - 2, 0)
            seen = hst[h][pl.ds(pl.multiple_of(n * JCOLS, 8), JCOLS), :]
            f[h][pl.ds(pl.multiple_of(8 + n * JCOLS, 8), JCOLS), :] = jnp.where(inside, seen - blurred, 0.0)

    def back_rows(u):
        for h in range(2):
            win = [[f[h][pl.ds(8 + (u - t) * JCOLS - tt, JCOLS), :] for tt in range(3)] for t in range(3)]
            for p in range(4):
                for q in range(4):
                    total = None
                    for t in range(3):
                        for tt in range(3):
                            if p + 4 * t > 8 or q + 4 * tt > 8:
                                continue
                            tap = (p + 4 * t) * 9 + q + 4 * tt
                            term = w[h][tap : tap + 1, :] * win[t][tt]
                            total = term if total is None else total + term
                    at = pl.multiple_of((4 * u - 8 + p) * LANES + 32 * q, 32)
                    bk[h][pl.ds(at, JCOLS), :] = rounded(total)

    def hs_gradient(row, rows):
        at = pl.ds((row - 8) * LANES, rows * LANES)
        back = jnp.concatenate([b0[at, :].astype(bf16), b1[at, :].astype(bf16)], axis=1)
        return lax.dot_general(basis, back, (((1,), (1,)), ((), ())), preferred_element_type=f32)

    def start_row(row):
        return c_ref[pl.ds(row, 32, stride=CROWS), :]

    def loop(low, high, body):
        def step(n, _):
            body(n)
            return 0

        lax.fori_loop(low, high, step, 0)

    for block in range(CROWS // 8):
        value = jnp.concatenate([start_row(block * 8 + r) for r in range(8)], axis=1)
        mix(block * 8, value, 8)
        if 1 <= block < 5:
            ms_gradient(block * 8, value)
    loop(0, IROWS, blur_row)
    loop(2, 10, back_rows)
    for block in range(1, 5):
        grad = hs_gradient(block * 8, 8)
        values = []
        for r in range(8):
            row = block * 8 + r
            now = start_row(row)
            new = now + STEP * (grad[:, r * 128 : r * 128 + 128] + g_ref[pl.ds((row - 8) * 32, 32), :])
            row_at = 16 * s - 16 + row
            new = jnp.where(in_columns & (row_at >= 0) & (row_at < 128), new, 0.0)
            c1_ref[pl.ds((row - 8) * 32, 32), :] = new
            values.append(new)
        value = jnp.concatenate(values, axis=1)
        mix(block * 8, value, 8)
        if 2 <= block < 4:
            ms_gradient(block * 8, value)
    loop(2, 8, blur_row)
    loop(4, 8, back_rows)
    place_at = lax.broadcasted_iota(jnp.int32, (LANES, LANES), 1)
    take = lax.broadcasted_iota(jnp.int32, (LANES, LANES), 0)
    shift = 4 * (take % 32) + take // 32 - 16
    order = [(place_at == shift + 64 * half) & (shift >= 0) & (shift < 64) for half in range(2)]
    order = [jnp.where(o, 1.0, 0.0).astype(bf16) for o in order]
    grads = [hs_gradient(16, 8), hs_gradient(24, 8)]
    for r in range(8):
        total = None
        for half in range(2):
            row = 8 + r + 8 * half
            at = pl.ds(row * 32, 32)
            value = c1_ref[at, :] + STEP * (grads[half][:, r * 128 : r * 128 + 128] + g_ref[at, :])
            rest = jnp.where((group >= 4) & (group < 20), value, 0.0)
            for _ in range(3):
                piece = rest.astype(bf16)
                rest = rest - piece.astype(f32)
                moved = jnp.dot(piece, order[half], preferred_element_type=f32)
                total = moved if total is None else total + moved
        out_ref[pl.ds(r, 32, stride=8), :] = total


def refine(pos, c, hp, ms):
    vmem = pl.BlockSpec(memory_space=pltpu.VMEM)
    return pl.pallas_call(
        refine_kernel,
        out_shape=jax.ShapeDtypeStruct((32 * 8, LANES), f32),
        in_specs=[pl.BlockSpec(memory_space=pltpu.SMEM), vmem, vmem, vmem],
        out_specs=vmem,
        scratch_shapes=[
            pltpu.VMEM((CROWS * LANES, LANES), f32),
            pltpu.VMEM((CROWS * LANES, LANES), f32),
            pltpu.VMEM((256, LANES), f32),
            pltpu.VMEM((256, LANES), f32),
            pltpu.VMEM((MROWS * LANES, LANES), f32),
            pltpu.VMEM((MROWS * LANES, LANES), f32),
            pltpu.VMEM((MROWS * 32, LANES), f32),
            pltpu.VMEM((MROWS * 32, LANES), f32),
            pltpu.VMEM((256, LANES), f32),
            pltpu.VMEM((256, LANES), f32),
            pltpu.VMEM((LANES, LANES), f32),
            pltpu.VMEM((LANES, LANES), f32),
        ],
        compiler_params=pltpu.CompilerParams(vmem_limit_bytes=40 * 2**20),
        cost_estimate=pl.CostEstimate(flops=400_000_000, bytes_accessed=2_000_000, transcendentals=0),
        name="refine",
    )(pos, c, hp, ms)


def pack_kernel(pos_ref, ca_ref, cb_ref, ma_ref, mb_ref, hs_ref, tiles_ref, near_ref):
    b = pos_ref[1]
    off = pos_ref[4]
    lane = lax.broadcasted_iota(jnp.int32, (1, LANES), 1)
    first = lane >= off
    block = (b + 1) // 2 - jnp.where(first, 1, 0)
    keep = (block >= 0) & (block < 8)
    source = lax.broadcasted_iota(jnp.int32, (LANES, LANES), 0)
    target = lax.broadcasted_iota(jnp.int32, (LANES, LANES), 1)
    order = jnp.where(source == (4 * (target % 32) + target // 32 + off) % LANES, 1.0, 0.0).astype(bf16)
    ms = jnp.where(first, ma_ref[...].reshape(128, LANES).astype(f32), mb_ref[...].reshape(128, LANES).astype(f32))
    ms = jnp.where(keep, ms, 0.0).astype(bf16)
    near_ref[0:128, :] = jnp.dot(ms, order, preferred_element_type=f32).astype(bf16)
    near_ref[128:192, :] = hs_ref[:, 0:128]
    near_ref[192:256, :] = hs_ref[:, 128:256]
    edge = jnp.zeros((16, LANES), f32)
    for k in range(4):
        rest = jnp.where(keep, jnp.where(first, ca_ref[k], cb_ref[k]), 0.0)
        total = None
        for _ in range(3):
            piece = rest.astype(bf16)
            rest = rest - piece.astype(f32)
            moved = jnp.dot(piece, order, preferred_element_type=f32)
            total = moved if total is None else total + moved
        for t in range(8):
            low = 16 * t - 16
            tiles_ref[t, k, 16:32] = total[low + 16 : low + 32]
            tiles_ref[t, k, 0:16] = edge if t == 0 else total[low : low + 16]
            tiles_ref[t, k, 32:48] = edge if t == 7 else total[low + 32 : low + 48]


def pack(pos, coeffs_in, ms_image, hs_rows):
    return pl.pallas_call(
        pack_kernel,
        out_shape=(
            jax.ShapeDtypeStruct((8, 4, CROWS, LANES), f32),
            jax.ShapeDtypeStruct((256, LANES), bf16),
        ),
        grid_spec=pltpu.PrefetchScalarGridSpec(
            num_scalar_prefetch=1,
            grid=(1,),
            in_specs=[
                pl.BlockSpec((4, 128, LANES), lambda i, p: (0, 0, p[2])),
                pl.BlockSpec((4, 128, LANES), lambda i, p: (0, 0, p[3])),
                pl.BlockSpec((8, 16, LANES), lambda i, p: (0, 0, p[2])),
                pl.BlockSpec((8, 16, LANES), lambda i, p: (0, 0, p[3])),
                pl.BlockSpec((64, 256), lambda i, p: (0, 0)),
            ],
            out_specs=(
                pl.BlockSpec((8, 4, CROWS, LANES), lambda i, p: (0, 0, 0, 0)),
                pl.BlockSpec((256, LANES), lambda i, p: (0, 0)),
            ),
        ),
        compiler_params=pltpu.CompilerParams(vmem_limit_bytes=32 * 2**20),
        cost_estimate=pl.CostEstimate(flops=100_000_000, bytes_accessed=1_600_000, transcendentals=0),
        name="pack",
    )(pos, coeffs_in, coeffs_in, ms_image, ms_image, hs_rows)


def spread_kernel(above_ref, own_ref, below_ref, k_ref, basis_ref, response_ref, sent_ref, ms_ref):
    for m in range(8):
        at = slice(16 * m, 16 * m + 16)
        ms_ref[32 * m : 32 * m + 8, :] = above_ref[at, :].astype(f32)[8:16]
        ms_ref[32 * m + 8 : 32 * m + 24, :] = own_ref[at, :].astype(f32)
        ms_ref[32 * m + 24 : 32 * m + 32, :] = below_ref[at, :].astype(f32)[0:8]
    lane = lax.broadcasted_iota(jnp.int32, (1, 256), 1)
    rows = []
    for i in range(IROWS):
        ref, r = (above_ref, i + 1) if i < 3 else (own_ref, i - 3) if i < 7 else (below_ref, i - 7)
        row = [ref[128 + 64 * h + 16 * r : 144 + 64 * h + 16 * r, :].astype(f32) for h in range(2)]
        rows.append(jnp.concatenate(row, axis=1))
    sent_ref[:, :, 256:384] = jnp.zeros((16, 16, 128), f32)
    for a in range(9):
        sent_ref[0, 0:14, 256 + 9 * a : 265 + 9 * a] = k_ref[:, a, :]
    sent_ref[0, 0:14, 337:369] = basis_ref[...].astype(f32)
    sent_ref[0, 0:14, 369:377] = response_ref[...].astype(f32).T
    params = sent_ref[0, :, 256:384]
    for t in range(16):
        total = jnp.zeros((16, 256), f32)
        for i in range(IROWS):
            moved = pltpu.roll(rows[i], (24 * i + 3 - 16 * t) % 256, 1)
            total = jnp.where((lane >= 24 * i) & (lane < 24 * i + 24), moved, total)
        sent_ref[t, :, 0:256] = total
        if t:
            sent_ref[t, :, 256:384] = params


def spread(above, own, below, kernels, basis, response):
    vmem = pl.BlockSpec(memory_space=pltpu.VMEM)
    return pl.pallas_call(
        spread_kernel,
        out_shape=(
            jax.ShapeDtypeStruct((16, 16, 384), f32),
            jax.ShapeDtypeStruct((8 * MROWS, LANES), f32),
        ),
        in_specs=[vmem] * 6,
        out_specs=(vmem, vmem),
        compiler_params=pltpu.CompilerParams(vmem_limit_bytes=16 * 2**20),
        cost_estimate=pl.CostEstimate(flops=1_000_000, bytes_accessed=1_000_000, transcendentals=0),
        name="spread",
    )(above, own, below, kernels, basis, response)


def place_kernel(g_ref, out_ref):
    lane = lax.broadcasted_iota(jnp.int32, (1, LANES), 1)
    low = lane < 64
    for s in range(8):
        for j in range(8):
            even = g_ref[2 * j, s, 0]
            odd = g_ref[2 * j + 1, s, 0]
            at = slice(j * 128, j * 128 + 128)
            out_ref[0, 16 * s : 16 * s + 8, at] = jnp.where(low, even, pltpu.roll(odd, 64, 1))
            out_ref[0, 16 * s + 8 : 16 * s + 16, at] = jnp.where(low, pltpu.roll(even, 64, 1), odd)


def place(gathered):
    return pl.pallas_call(
        place_kernel,
        out_shape=jax.ShapeDtypeStruct((4, 128, 1024), f32),
        grid=(4,),
        in_specs=[pl.BlockSpec((16, 8, 1, 8, LANES), lambda k: (0, 0, k, 0, 0))],
        out_specs=pl.BlockSpec((1, 128, 1024), lambda k: (k, 0, 0)),
        compiler_params=pltpu.CompilerParams(vmem_limit_bytes=32 * 2**20),
        name="place",
    )(gathered)


def per_device(coeffs_in, basis, kernels, response, hs_image, ms_image):
    s = lax.axis_index("sub").astype(jnp.int32)
    b = lax.axis_index("band").astype(jnp.int32)
    at = (b + 1) // 2 - 1
    off = jnp.where(b % 2 == 0, 112, 48)
    pos = jnp.stack([s, b, jnp.maximum(at, 0), jnp.minimum(at + 1, 7), off]).astype(jnp.int32)
    hs_rows = jnp.pad(hs_image.transpose(1, 0, 2), ((0, 0), (0, 2), (0, 0))).reshape(64, 256)
    tiles, own = pack(pos, coeffs_in, ms_image, hs_rows)
    above = lax.ppermute(own, "sub", [(i, i + 1) for i in range(7)])
    below = lax.ppermute(own, "sub", [(i + 1, i) for i in range(7)])
    sent, ms = spread(above, own, below, kernels, basis, response)
    hp = lax.all_to_all(sent, "band", split_axis=0, concat_axis=0, tiled=True).reshape(256, 384)
    c = lax.all_to_all(tiles, "sub", split_axis=0, concat_axis=0, tiled=True).reshape(32 * CROWS, LANES)
    new = refine(pos, c, hp, ms)
    owned = lax.all_to_all(new.reshape(8, 4, 8, LANES), "sub", split_axis=0, concat_axis=0, tiled=True)
    copies = jnp.broadcast_to(owned[None], (16,) + owned.shape)
    gathered = lax.all_to_all(copies, "band", split_axis=0, concat_axis=0, tiled=True)
    return place(gathered)


def solution(mesh):
    return jax.shard_map(
        per_device,
        mesh=mesh,
        in_specs=(
            P("sub", None, None),
            P("band", None),
            P("band", None, None),
            P(None, "band"),
            P("band", "sub", None),
            P(None, "sub", None),
        ),
        out_specs=P("sub", None, None),
        check_vma=False,
    )
```

time: 142 us -> 99.3 us (0.70)
  blocking collectives: 38.7 us -> 73.5 us
  Pallas kernels: 36.1 us -> 13.3 us
  local copies, waits for them, and re-layouts: 24 us -> 3.68 us
  starting transfers between devices: 25.5 us -> 6.43 us
  waiting for transfers between devices: 12.7 us -> 1.26 us
  other arithmetic: 3.16 us -> 0 us
    all_to_all x0 -> x2, blocking collectives: none -> 34.9 us  [the longest x1 17.7 us: per_device(): lax.all_to_all(sent, 'band', split_axis=0, concat_axis=0, tiled=True)]
    pallas_call x1, Pallas kernels: 33.6 us -> 9.73 us  [refine(): pl.pallas_call(refine_kernel, out_shape=jax.ShapeDtypeStruct((32 * 8, LAN...]
    all_to_all x2 -> x0, starting transfers between devices: 13.6 us -> none  [the longest x1 7.77 us: per_device(): lax.all_to_all(sent, 'band', split_axis=0, concat_axis=0, tiled=True)]
    another operation x18 -> x1, local copies, waits for them, and re-layouts: 9.71 us -> 0.09 us  [per_device(): jnp.stack([s, b, jnp.maximum(at, 0), jnp.minimum(at + 1, 7), off])]
    all_to_all x2 -> x0, waiting for transfers between devices: 7.02 us -> none  [the longest x1 6.21 us: per_device(): lax.all_to_all(sent, 'band', split_axis=0, concat_axis=0, tiled=True)]
    unnamed x28 -> x12, local copies, waits for them, and re-layouts: 9.77 us -> 3.33 us
    ppermute x4 -> x2, starting transfers between devices: 11.9 us -> 6.43 us  [the longest x1 3.33 us: per_device(): below = lax.ppermute(own, 'sub', [(i + 1, i) for i in range(7)])]
    ppermute x4 -> x2, waiting for transfers between devices: 5.68 us -> 1.26 us  [the longest x1 1.26 us: per_device(): above = lax.ppermute(own, 'sub', [(i, i + 1) for i in range(7)])]
  transfers between devices with their start and end apart: 6 -> 2, of which waited for: 4 -> 1; matrix products, arithmetic and copies ran while one was open for 7% -> 0% of each run, Pallas kernels for 0% -> 0%
where the time goes in v2:
time: 99.3 us; the launch traced here: 98.3 us
  blocking collectives  73.5 us (74%)
  Pallas kernels  13.3 us (13%)
  starting transfers between devices  6.43 us (6%)
  local copies, waits for them, and re-layouts  3.68 us (4%)
  waiting for transfers between devices  1.26 us (1%)
    all_to_all x1, blocking collectives, per_device(): lax.all_to_all(copies, 'band', split_axis=0, concat_axis=0, tiled=True)  30 us
    all_to_all x1, blocking collectives, per_device(): lax.all_to_all(sent, 'band', split_axis=0, concat_axis=0, tiled=True)  17.7 us
    all_to_all x1, blocking collectives, per_device(): lax.all_to_all(tiles, 'sub', split_axis=0, concat_axis=0, tiled=True)  17.2 us
    pallas_call x1, Pallas kernels, refine(): pl.pallas_call(refine_kernel, out_shape=jax.ShapeDtypeStruct((32 * 8, LAN...  9.73 us
    all_to_all x1, blocking collectives, per_device(): lax.all_to_all(new.reshape(8, 4, 8, LANES), 'sub', split_axis=0, concat_a...  8.7 us
    unnamed x12, local copies, waits for them, and re-layouts  3.33 us
    ppermute x1, starting transfers between devices, per_device(): below = lax.ppermute(own, 'sub', [(i + 1, i) for i in range(7)])  3.33 us
    ppermute x1, starting transfers between devices, per_device(): above = lax.ppermute(own, 'sub', [(i, i + 1) for i in range(7)])  3.1 us
  transfers between devices with their start and end apart: 2, of which 1 were waited for; matrix products, arithmetic and copies ran while one was open for 0% of the time, Pallas kernels for 0%

profile of v2, /device:TPU:1, one launch (start us, length us, event | category | flops | bytes accessed | tf_op | source)
XLA Modules:
  0.0 98.3 jit_solution(10855593019855482165)
XLA Ops:
  0.0 0.8 copy.9
  0.8 0.1 stack.23.pos_ref
  0.9 0.0 copy-start
  0.9 1.6 %copy-done = f32[4,128,1024]{2,1,0:T(8,128)S(1)} copy-done((f32[4,128,1024]{2,1,0:T(8,128)S(1)}, f32[4,128,1024]{2,1,0:T(8,128)}, u32[]{:S(2)}) %copy-start) | copy-done | bytes 2097176
  2.5 0.0 copy-start.1
  2.5 0.9 copy-done.1
  3.4 0.0 copy-start.4
  3.4 0.0 copy-start.2
  3.4 0.0 copy-start.3
  3.4 0.9 pack.1
  4.3 3.3 %collective-permute-start.1 = (bf16[256,128]{1,0:T(8,128)(2,1)S(1)}, bf16[256,128]{1,0:T(8,128)(2,1)S(1)}, u32[]{:S(2)}, u32[]{:S(2)}) collective-permute-start(bf16[256,128]{1,0:T(8,128)(2,1)S(1)} %get-tuple-element.10.own_ref), channel_id=1, source_target_pairs={{16,0},{32,16},{48,32},{64,48},{80,64},{96,80},{112,96},{17,1},{33... | collective-permute-start | bytes 196616 | tf_op jit(solution)/shard_map/ppermute | solution.py:323
  7.6 3.1 %collective-permute-start = (bf16[256,128]{1,0:T(8,128)(2,1)S(1)}, bf16[256,128]{1,0:T(8,128)(2,1)S(1)}, u32[]{:S(2)}, u32[]{:S(2)}) collective-permute-start(bf16[256,128]{1,0:T(8,128)(2,1)S(1)} %get-tuple-element.10.own_ref), channel_id=1, source_target_pairs={{0,16},{16,32},{32,48},{48,64},{64,80},{80,96},{96,112},{1,17},{17... | collective-permute-start | bytes 196616 | tf_op jit(solution)/shard_map/ppermute | solution.py:322
  10.7 0.0 copy-done.4
  10.8 0.0 collective-permute-done.1.below_ref
  10.8 1.3 %collective-permute-done.above_ref = bf16[256,128]{1,0:T(8,128)(2,1)S(1)} collective-permute-done((bf16[256,128]{1,0:T(8,128)(2,1)S(1)}, bf16[256,128]{1,0:T(8,128)(2,1)S(1)}, u32[]{:S(2)}, u32[]{:S(2)}) %collective-permute-start) | collective-permute-done | bytes 65568 | tf_op jit(solution)/shard_map/ppermute | solution.py:322
  12.0 0.0 copy-done.2
  12.0 0.0 copy-done.3
  12.0 0.3 spread.1
  12.4 17.7 %all_to_all.20 = f32[16,16,384]{2,1,0:T(8,128)S(1)} all-to-all(f32[16,16,384]{2,1,0:T(8,128)S(1)} %get-tuple-element.11), channel_id=1, replica_groups=mesh['sub'=8,'band'=16] {'band'}, dimensions={0} | all-to-all | bytes 786432 | tf_op jit(solution)/shard_map/all_to_all | solution.py:325
  30.0 17.2 %all_to_all.21 = f32[8,4,48,128]{3,2,1,0:T(8,128)S(1)} all-to-all(f32[8,4,48,128]{3,2,1,0:T(8,128)S(1)} %get-tuple-element.9), channel_id=1, replica_groups=mesh['sub'=8,'band'=16] {'sub'}, dimensions={0} | all-to-all | bytes 1572864 | tf_op jit(solution)/shard_map/all_to_all | solution.py:326
  47.2 9.7 %refine.1 = f32[256,128]{1,0:T(8,128)S(1)} custom-call(s32[5]{0:T(128)S(1)} %stack.23.pos_ref, f32[1536,128]{1,0:T(8,128)S(1)} %bitcast.10, f32[256,384]{1,0:T(8,128)S(1)} %bitcast.11, f32[256,128]{1,0:T(8,128)S(1)} %get-tuple-element.12.ms_ref), custom_call_target="tpu_custom_call" | custom-call | flops 400000000 | bytes 2000000 | tf_op jit(solution)/shard_map/refine/pallas_call | solution.py:162
  56.9 8.7 %all_to_all.22 = f32[8,4,8,128]{3,2,1,0:T(8,128)S(1)} all-to-all(f32[8,4,8,128]{3,2,1,0:T(8,128)S(1)} %bitcast.13), channel_id=1, replica_groups=mesh['sub'=8,'band'=16] {'sub'}, dimensions={0} | all-to-all | bytes 262144 | tf_op jit(solution)/shard_map/all_to_all | solution.py:328
  65.6 0.2 broadcast_in_dim.2
  65.9 30.0 %all_to_all.23.g_ref = f32[16,8,4,8,128]{4,3,2,1,0:T(8,128)S(1)} all-to-all(f32[16,8,4,8,128]{4,3,2,1,0:T(8,128)S(1)} %broadcast_in_dim.2), channel_id=1, replica_groups=mesh['sub'=8,'band'=16] {'band'}, dimensions={0} | all-to-all | bytes 4194304 | tf_op jit(solution)/shard_map/all_to_all | solution.py:330
  95.9 2.4 %place.1 = f32[4,128,1024]{2,1,0:T(8,128)} custom-call(f32[16,8,4,8,128]{4,3,2,1,0:T(8,128)S(1)} %all_to_all.23.g_ref), custom_call_target="tpu_custom_call" | custom-call | tf_op jit(solution)/shard_map/place/pallas_call | solution.py:303
  (2 shorter events, 0.0 us)
Async XLA Ops:
  0.9 1.6 %copy-start = (f32[4,128,1024]{2,1,0:T(8,128)S(1)}, f32[4,128,1024]{2,1,0:T(8,128)}, u32[]{:S(2)}) copy-start(f32[4,128,1024]{2,1,0:T(8,128)} %cb_ref.1) | copy-start | bytes 6291460
  2.5 0.9 copy-start.1
  3.4 7.3 %copy-start.4 = (f32[14,9,9]{2,0,1:T(8,128)S(1)}, f32[14,9,9]{2,0,1:T(8,128)}, u32[]{:S(2)}) copy-start(f32[14,9,9]{2,0,1:T(8,128)} %param.8) | copy-start | bytes 13612
  3.4 8.6 %copy-start.2 = (bf16[14,32]{1,0:T(8,128)(2,1)S(1)}, bf16[14,32]{1,0:T(8,128)(2,1)}, u32[]{:S(2)}) copy-start(bf16[14,32]{1,0:T(8,128)(2,1)} %basis_ref.1) | copy-start | bytes 2692
  3.4 8.6 %copy-start.3 = (bf16[8,14]{1,0:T(8,128)(2,1)S(1)}, bf16[8,14]{1,0:T(8,128)(2,1)}, u32[]{:S(2)}) copy-start(bf16[8,14]{1,0:T(8,128)(2,1)} %response_ref.1) | copy-start | bytes 676
  4.3 6.5 %collective-permute-start.1 = (bf16[256,128]{1,0:T(8,128)(2,1)S(1)}, bf16[256,128]{1,0:T(8,128)(2,1)S(1)}, u32[]{:S(2)}, u32[]{:S(2)}) collective-permute-start(bf16[256,128]{1,0:T(8,128)(2,1)S(1)} %get-tuple-element.10.own_ref), channel_id=1, source_target_pairs={{16,0},{32,16},{48,32},{64,48},{80,64},{96,80},{112,96},{17,1},{33... | collective-permute-start | bytes 196616 | tf_op jit(solution)/shard_map/ppermute | solution.py:323
  7.6 4.4 %collective-permute-start = (bf16[256,128]{1,0:T(8,128)(2,1)S(1)}, bf16[256,128]{1,0:T(8,128)(2,1)S(1)}, u32[]{:S(2)}, u32[]{:S(2)}) collective-permute-start(bf16[256,128]{1,0:T(8,128)(2,1)S(1)} %get-tuple-element.10.own_ref), channel_id=1, source_target_pairs={{0,16},{16,32},{32,48},{48,64},{64,80},{80,96},{96,112},{1,17},{17... | collective-permute-start | bytes 196616 | tf_op jit(solution)/shard_map/ppermute | solution.py:322

commit v3 on v2

--- a/solution.py
+++ b/solution.py
@@ -237,7 +237,7 @@
                 pl.BlockSpec((256, LANES), lambda i, p: (0, 0)),
             ),
         ),
-        compiler_params=pltpu.CompilerParams(vmem_limit_bytes=32 * 2**20),
+        compiler_params=pltpu.CompilerParams(vmem_limit_bytes=60 * 2**20),
         cost_estimate=pl.CostEstimate(flops=100_000_000, bytes_accessed=1_600_000, transcendentals=0),
         name="pack",
     )(pos, coeffs_in, coeffs_in, ms_image, ms_image, hs_rows)
@@ -319,11 +319,12 @@
     pos = jnp.stack([s, b, jnp.maximum(at, 0), jnp.minimum(at + 1, 7), off]).astype(jnp.int32)
     hs_rows = jnp.pad(hs_image.transpose(1, 0, 2), ((0, 0), (0, 2), (0, 0))).reshape(64, 256)
     tiles, own = pack(pos, coeffs_in, ms_image, hs_rows)
+    c = lax.all_to_all(tiles, "sub", split_axis=0, concat_axis=0, tiled=True).reshape(32 * CROWS, LANES)
     above = lax.ppermute(own, "sub", [(i, i + 1) for i in range(7)])
     below = lax.ppermute(own, "sub", [(i + 1, i) for i in range(7)])
     sent, ms = spread(above, own, below, kernels, basis, response)
+    sent, c = lax.optimization_barrier((sent, c))
     hp = lax.all_to_all(sent, "band", split_axis=0, concat_axis=0, tiled=True).reshape(256, 384)
-    c = lax.all_to_all(tiles, "sub", split_axis=0, concat_axis=0, tiled=True).reshape(32 * CROWS, LANES)
     new = refine(pos, c, hp, ms)
     owned = lax.all_to_all(new.reshape(8, 4, 8, LANES), "sub", split_axis=0, concat_axis=0, tiled=True)
     copies = jnp.broadcast_to(owned[None], (16,) + owned.shape)

time: 99.3 us -> 95 us (0.957)
  blocking collectives: 73.5 us -> 57.4 us
  waiting for transfers between devices: 1.26 us -> 6.36 us
  starting transfers between devices: 6.43 us -> 11.5 us
  Pallas kernels: 13.3 us -> 15.5 us
    all_to_all x1 -> x0, blocking collectives: 17.2 us -> none  [per_device(): lax.all_to_all(tiles, 'sub', split_axis=0, concat_axis=0, tiled=True)]
    ppermute x1, waiting for transfers between devices: 0.01 us -> 6.36 us  [per_device(): below = lax.ppermute(own, 'sub', [(i + 1, i) for i in range(7)])]
    all_to_all x0 -> x1, starting transfers between devices: none -> 5.93 us  [per_device(): lax.all_to_all(tiles, 'sub', split_axis=0, concat_axis=0, tiled=True)]
    pallas_call x1, Pallas kernels: 0.85 us -> 3.04 us  [pack(): pl.pallas_call(pack_kernel, out_shape=(jax.ShapeDtypeStruct((8, 4, CROWS,...]
    all_to_all x1, blocking collectives: 8.7 us -> 10.5 us  [per_device(): lax.all_to_all(new.reshape(8, 4, 8, LANES), 'sub', split_axis=0, concat_a...]
    unnamed x12, local copies, waits for them, and re-layouts: 3.33 us -> 1.63 us
    ppermute x1, starting transfers between devices: 3.33 us -> 1.91 us  [per_device(): below = lax.ppermute(own, 'sub', [(i + 1, i) for i in range(7)])]
    ppermute x1, waiting for transfers between devices: 1.26 us -> 0.01 us  [per_device(): above = lax.ppermute(own, 'sub', [(i, i + 1) for i in range(7)])]
  transfers between devices with their start and end apart: 2 -> 3, of which waited for: 1 -> 1; matrix products, arithmetic and copies ran while one was open for 0% -> 0% of each run, Pallas kernels for 0% -> 0%
where the time goes in v3:
time: 95 us; the launch traced here: 93.9 us
  blocking collectives  57.4 us (60%)
  Pallas kernels  15.5 us (16%)
  starting transfers between devices  11.5 us (12%)
  waiting for transfers between devices  6.36 us (7%)
  local copies, waits for them, and re-layouts  3.12 us (3%)
    all_to_all x1, blocking collectives, per_device(): lax.all_to_all(copies, 'band', split_axis=0, concat_axis=0, tiled=True)  30 us
    all_to_all x1, blocking collectives, per_device(): lax.all_to_all(sent, 'band', split_axis=0, concat_axis=0, tiled=True)  17 us
    all_to_all x1, blocking collectives, per_device(): lax.all_to_all(new.reshape(8, 4, 8, LANES), 'sub', split_axis=0, concat_a...  10.5 us
    pallas_call x1, Pallas kernels, refine(): pl.pallas_call(refine_kernel, out_shape=jax.ShapeDtypeStruct((32 * 8, LAN...  9.74 us
    ppermute x1, waiting for transfers between devices, per_device(): below = lax.ppermute(own, 'sub', [(i + 1, i) for i in range(7)])  6.36 us
    all_to_all x1, starting transfers between devices, per_device(): lax.all_to_all(tiles, 'sub', split_axis=0, concat_axis=0, tiled=True)  5.93 us
    ppermute x1, starting transfers between devices, per_device(): above = lax.ppermute(own, 'sub', [(i, i + 1) for i in range(7)])  3.64 us
    pallas_call x1, Pallas kernels, pack(): pl.pallas_call(pack_kernel, out_shape=(jax.ShapeDtypeStruct((8, 4, CROWS,...  3.04 us
  transfers between devices with their start and end apart: 3, of which 1 were waited for; matrix products, arithmetic and copies ran while one was open for 0% of the time, Pallas kernels for 0%

profile of v3, /device:TPU:1, one launch (start us, length us, event | category | flops | bytes accessed | tf_op | source)
XLA Modules:
  0.0 93.9 jit_solution(12401880057839488344)
XLA Ops:
  0.0 0.8 copy.9
  0.8 0.6 pad.4.clone
  1.4 0.6 stack.23.pos_ref
  2.0 0.0 copy-start.4
  2.0 0.0 copy-start.1
  2.0 0.0 copy-start.2
  2.0 3.0 %pack.1 = (f32[8,4,48,128]{3,2,1,0:T(8,128)}, bf16[256,128]{1,0:T(8,128)(2,1)}) custom-call(s32[5]{0:T(128)} %stack.23.pos_ref, f32[4,128,1024]{2,1,0:T(8,128)} %cb_ref.1, f32[4,128,1024]{2,1,0:T(8,128)} %cb_ref.1, bf16[8,16,1024]{2,1,0:T(8,128)(2,1)} %mb_ref.1, bf16[8,16,1024]{2,1,0:T(8,128)(2,1)} %mb_ref.1, bf16[64,256]{1,0:T(8,128)(2,1)} %bitcast.13), custom_call_target="tpu_custom_call" | custom-call | flops 100000000 | bytes 1600000 | tf_op jit(solution)/shard_map/pack/pallas_call | solution.py:219
  5.0 0.0 copy-start.3
  5.0 5.9 %all-to-all-start = ((f32[8,4,48,128]{3,2,1,0:T(8,128)}), f32[8,4,48,128]{3,2,1,0:T(8,128)S(1)}, u32[]{:S(2)}, u32[]{:S(2)}) async-start(f32[8,4,48,128]{3,2,1,0:T(8,128)} %get-tuple-element.13), calls=%async_computation | async-start | bytes 1572864 | tf_op jit(solution)/shard_map/all_to_all | solution.py:322
  11.0 1.9 %collective-permute-start.1 = (bf16[256,128]{1,0:T(8,128)(2,1)}, bf16[256,128]{1,0:T(8,128)(2,1)S(1)}, u32[]{:S(2)}, u32[]{:S(2)}) collective-permute-start(bf16[256,128]{1,0:T(8,128)(2,1)} %get-tuple-element.11.own_ref), channel_id=1, source_target_pairs={{16,0},{32,16},{48,32},{64,48},{80,64},{96,80},{112,96},{17,1},{33... | collective-permute-start | bytes 196616 | tf_op jit(solution)/shard_map/ppermute | solution.py:324
  12.9 3.6 %collective-permute-start = (bf16[256,128]{1,0:T(8,128)(2,1)}, bf16[256,128]{1,0:T(8,128)(2,1)S(1)}, u32[]{:S(2)}, u32[]{:S(2)}) collective-permute-start(bf16[256,128]{1,0:T(8,128)(2,1)} %get-tuple-element.11.own_ref), channel_id=1, source_target_pairs={{0,16},{16,32},{32,48},{48,64},{64,80},{80,96},{96,112},{1,17},{17... | collective-permute-start | bytes 196616 | tf_op jit(solution)/shard_map/ppermute | solution.py:323
  16.5 0.0 copy-done.4
  16.6 6.4 %collective-permute-done.1.below_ref = bf16[256,128]{1,0:T(8,128)(2,1)S(1)} collective-permute-done((bf16[256,128]{1,0:T(8,128)(2,1)}, bf16[256,128]{1,0:T(8,128)(2,1)S(1)}, u32[]{:S(2)}, u32[]{:S(2)}) %collective-permute-start.1) | collective-permute-done | bytes 65568 | tf_op jit(solution)/shard_map/ppermute | solution.py:324
  22.9 0.0 collective-permute-done.above_ref
  22.9 0.0 copy-done.1
  23.0 0.0 copy-done.2
  23.0 0.0 copy-start
  23.0 0.8 copy-done
  23.8 0.3 spread.1
  24.1 0.0 all-to-all-done
  24.1 17.0 %all_to_all.20 = f32[16,16,384]{2,1,0:T(8,128)S(1)} all-to-all(f32[16,16,384]{2,1,0:T(8,128)S(1)} %get-tuple-element.15), channel_id=1, replica_groups=mesh['sub'=8,'band'=16] {'band'}, dimensions={0} | all-to-all | bytes 786432 | tf_op jit(solution)/shard_map/all_to_all | solution.py:327
  41.1 0.0 copy-done.3
  41.1 9.7 %refine.1 = f32[256,128]{1,0:T(8,128)S(1)} custom-call(s32[5]{0:T(128)S(1)} %copy-done.3, f32[1536,128]{1,0:T(8,128)S(1)} %bitcast.10, f32[256,384]{1,0:T(8,128)S(1)} %bitcast.11, f32[256,128]{1,0:T(8,128)S(1)} %get-tuple-element.16.ms_ref), custom_call_target="tpu_custom_call" | custom-call | flops 400000000 | bytes 2000000 | tf_op jit(solution)/shard_map/refine/pallas_call | solution.py:162
  50.8 10.5 %all_to_all.21 = f32[8,4,8,128]{3,2,1,0:T(8,128)S(1)} all-to-all(f32[8,4,8,128]{3,2,1,0:T(8,128)S(1)} %bitcast.12), channel_id=1, replica_groups=mesh['sub'=8,'band'=16] {'sub'}, dimensions={0} | all-to-all | bytes 262144 | tf_op jit(solution)/shard_map/all_to_all | solution.py:329
  61.3 0.2 broadcast_in_dim.2
  61.5 30.0 %all_to_all.22.g_ref = f32[16,8,4,8,128]{4,3,2,1,0:T(8,128)S(1)} all-to-all(f32[16,8,4,8,128]{4,3,2,1,0:T(8,128)S(1)} %broadcast_in_dim.2), channel_id=1, replica_groups=mesh['sub'=8,'band'=16] {'band'}, dimensions={0} | all-to-all | bytes 4194304 | tf_op jit(solution)/shard_map/all_to_all | solution.py:331
  91.5 2.4 %place.1 = f32[4,128,1024]{2,1,0:T(8,128)} custom-call(f32[16,8,4,8,128]{4,3,2,1,0:T(8,128)S(1)} %all_to_all.22.g_ref), custom_call_target="tpu_custom_call" | custom-call | tf_op jit(solution)/shard_map/place/pallas_call | solution.py:303
  (1 shorter events, 0.0 us)
Async XLA Ops:
  2.0 14.6 %copy-start.4 = (f32[14,9,9]{2,0,1:T(8,128)S(1)}, f32[14,9,9]{2,0,1:T(8,128)}, u32[]{:S(2)}) copy-start(f32[14,9,9]{2,0,1:T(8,128)} %param.8) | copy-start | bytes 13612
  2.0 21.0 %copy-start.1 = (bf16[14,32]{1,0:T(8,128)(2,1)S(1)}, bf16[14,32]{1,0:T(8,128)(2,1)}, u32[]{:S(2)}) copy-start(bf16[14,32]{1,0:T(8,128)(2,1)} %basis_ref.1) | copy-start | bytes 2692
  2.0 21.0 %copy-start.2 = (bf16[8,14]{1,0:T(8,128)(2,1)S(1)}, bf16[8,14]{1,0:T(8,128)(2,1)}, u32[]{:S(2)}) copy-start(bf16[8,14]{1,0:T(8,128)(2,1)} %response_ref.1) | copy-start | bytes 676
  5.0 36.0 %copy-start.3 = (s32[5]{0:T(128)S(1)}, s32[5]{0:T(128)}, u32[]{:S(2)}) copy-start(s32[5]{0:T(128)} %stack.23.pos_ref) | copy-start | bytes 64
  5.0 19.1 %all-to-all-start = ((f32[8,4,48,128]{3,2,1,0:T(8,128)}), f32[8,4,48,128]{3,2,1,0:T(8,128)S(1)}, u32[]{:S(2)}, u32[]{:S(2)}) async-start(f32[8,4,48,128]{3,2,1,0:T(8,128)} %get-tuple-element.13), calls=%async_computation | async-start | bytes 1572864 | tf_op jit(solution)/shard_map/all_to_all | solution.py:322
  11.0 12.0 %collective-permute-start.1 = (bf16[256,128]{1,0:T(8,128)(2,1)}, bf16[256,128]{1,0:T(8,128)(2,1)S(1)}, u32[]{:S(2)}, u32[]{:S(2)}) collective-permute-start(bf16[256,128]{1,0:T(8,128)(2,1)} %get-tuple-element.11.own_ref), channel_id=1, source_target_pairs={{16,0},{32,16},{48,32},{64,48},{80,64},{96,80},{112,96},{17,1},{33... | collective-permute-start | bytes 196616 | tf_op jit(solution)/shard_map/ppermute | solution.py:324
  12.9 10.1 %collective-permute-start = (bf16[256,128]{1,0:T(8,128)(2,1)}, bf16[256,128]{1,0:T(8,128)(2,1)S(1)}, u32[]{:S(2)}, u32[]{:S(2)}) collective-permute-start(bf16[256,128]{1,0:T(8,128)(2,1)} %get-tuple-element.11.own_ref), channel_id=1, source_target_pairs={{0,16},{16,32},{32,48},{48,64},{64,80},{80,96},{96,112},{1,17},{17... | collective-permute-start | bytes 196616 | tf_op jit(solution)/shard_map/ppermute | solution.py:323
  23.0 0.8 copy-start

commit v4 on v3

--- a/solution.py
+++ b/solution.py
@@ -24,9 +24,14 @@
     return value.astype(bf16).astype(f32)
 
 
-def refine_kernel(pos_ref, c_ref, hp_ref, ms_ref, out_ref, m0, m1, f0, f1, b0, b1, c1_ref, g_ref, hs0, hs1, w0, w1):
-    s = pos_ref[0]
-    b = pos_ref[1]
+def refine_kernel(pos_ref, *refs):
+    tiles = refs[:8]
+    hp_ref, ms_ref, out_ref, c_ref, m0, m1, f0, f1, b0, b1, c1_ref, g_ref, hs0, hs1, w0, w1 = refs[8:]
+    s = pos_ref[0] // 16
+    b = pos_ref[0] % 16
+    for d in range(8):
+        at = pl.multiple_of((s + 8 - d) % 8 * (4 * CROWS), 4 * CROWS)
+        c_ref[pl.ds(at, 4 * CROWS), :] = tiles[d][...].reshape(4 * CROWS, LANES)
     m = (m0, m1)
     f = (f0, f1)
     bk = (b0, b1)
@@ -157,14 +162,15 @@
         out_ref[pl.ds(r, 32, stride=8), :] = total
 
 
-def refine(pos, c, hp, ms):
+def refine(pos, tiles, hp, ms):
     vmem = pl.BlockSpec(memory_space=pltpu.VMEM)
     return pl.pallas_call(
         refine_kernel,
         out_shape=jax.ShapeDtypeStruct((32 * 8, LANES), f32),
-        in_specs=[pl.BlockSpec(memory_space=pltpu.SMEM), vmem, vmem, vmem],
+        in_specs=[pl.BlockSpec(memory_space=pltpu.SMEM)] + [vmem] * 10,
         out_specs=vmem,
         scratch_shapes=[
+            pltpu.VMEM((32 * CROWS, LANES), f32),
             pltpu.VMEM((CROWS * LANES, LANES), f32),
             pltpu.VMEM((CROWS * LANES, LANES), f32),
             pltpu.VMEM((256, LANES), f32),
@@ -181,12 +187,15 @@
         compiler_params=pltpu.CompilerParams(vmem_limit_bytes=40 * 2**20),
         cost_estimate=pl.CostEstimate(flops=400_000_000, bytes_accessed=2_000_000, transcendentals=0),
         name="refine",
-    )(pos, c, hp, ms)
-
-
-def pack_kernel(pos_ref, ca_ref, cb_ref, ma_ref, mb_ref, hs_ref, tiles_ref, near_ref):
-    b = pos_ref[1]
-    off = pos_ref[4]
+    )(pos, *tiles, hp, ms)
+
+
+def pack_kernel(pos_ref, ca_ref, cb_ref, ma_ref, mb_ref, hs_ref, near_ref, *rest_refs):
+    tile_refs = rest_refs[:8]
+    wide_ref = rest_refs[8]
+    s = pos_ref[0] // 16
+    b = pos_ref[0] % 16
+    off = jnp.where(b % 2 == 0, 112, 48)
     lane = lax.broadcasted_iota(jnp.int32, (1, LANES), 1)
     first = lane >= off
     block = (b + 1) // 2 - jnp.where(first, 1, 0)
@@ -197,8 +206,11 @@
     ms = jnp.where(first, ma_ref[...].reshape(128, LANES).astype(f32), mb_ref[...].reshape(128, LANES).astype(f32))
     ms = jnp.where(keep, ms, 0.0).astype(bf16)
     near_ref[0:128, :] = jnp.dot(ms, order, preferred_element_type=f32).astype(bf16)
-    near_ref[128:192, :] = hs_ref[:, 0:128]
-    near_ref[192:256, :] = hs_ref[:, 128:256]
+    hs = hs_ref[...].astype(f32)
+    for i in range(4):
+        row = jnp.concatenate([hs[:, i, :], jnp.zeros((2, 256), f32)], axis=0).astype(bf16)
+        near_ref[128 + 16 * i : 144 + 16 * i, :] = row[:, 0:128]
+        near_ref[192 + 16 * i : 208 + 16 * i, :] = row[:, 128:256]
     edge = jnp.zeros((16, LANES), f32)
     for k in range(4):
         rest = jnp.where(keep, jnp.where(first, ca_ref[k], cb_ref[k]), 0.0)
@@ -208,39 +220,45 @@
             rest = rest - piece.astype(f32)
             moved = jnp.dot(piece, order, preferred_element_type=f32)
             total = moved if total is None else total + moved
-        for t in range(8):
-            low = 16 * t - 16
-            tiles_ref[t, k, 16:32] = total[low + 16 : low + 32]
-            tiles_ref[t, k, 0:16] = edge if t == 0 else total[low : low + 16]
-            tiles_ref[t, k, 32:48] = edge if t == 7 else total[low + 32 : low + 48]
-
-
-def pack(pos, coeffs_in, ms_image, hs_rows):
+        wide_ref[k, 0:16] = edge
+        wide_ref[k, 16:144] = total
+        wide_ref[k, 144:160] = edge
+    for d in range(8):
+        t = (s + d) % 8
+        at = pl.ds(pl.multiple_of(16 * t, 16), CROWS)
+        for k in range(4):
+            tile_refs[d][k] = wide_ref[k, at, :]
+
+
+def pack(pos, coeffs_in, ms_image, hs_image):
+    def low(i, p):
+        return (0, 0, jnp.maximum((p[0] % 16 + 1) // 2 - 1, 0))
+
+    def high(i, p):
+        return (0, 0, jnp.minimum((p[0] % 16 + 1) // 2, 7))
+
+    tile = jax.ShapeDtypeStruct((4, CROWS, LANES), f32)
     return pl.pallas_call(
         pack_kernel,
-        out_shape=(
-            jax.ShapeDtypeStruct((8, 4, CROWS, LANES), f32),
-            jax.ShapeDtypeStruct((256, LANES), bf16),
-        ),
+        out_shape=(jax.ShapeDtypeStruct((256, LANES), bf16),) + (tile,) * 8,
         grid_spec=pltpu.PrefetchScalarGridSpec(
             num_scalar_prefetch=1,
             grid=(1,),
             in_specs=[
-                pl.BlockSpec((4, 128, LANES), lambda i, p: (0, 0, p[2])),
-                pl.BlockSpec((4, 128, LANES), lambda i, p: (0, 0, p[3])),
-                pl.BlockSpec((8, 16, LANES), lambda i, p: (0, 0, p[2])),
-                pl.BlockSpec((8, 16, LANES), lambda i, p: (0, 0, p[3])),
-                pl.BlockSpec((64, 256), lambda i, p: (0, 0)),
+                pl.BlockSpec((4, 128, LANES), low),
+                pl.BlockSpec((4, 128, LANES), high),
+                pl.BlockSpec((8, 16, LANES), low),
+                pl.BlockSpec((8, 16, LANES), high),
+                pl.BlockSpec((14, 4, 256), lambda i, p: (0, 0, 0)),
             ],
-            out_specs=(
-                pl.BlockSpec((8, 4, CROWS, LANES), lambda i, p: (0, 0, 0, 0)),
-                pl.BlockSpec((256, LANES), lambda i, p: (0, 0)),
-            ),
+            out_specs=(pl.BlockSpec((256, LANES), lambda i, p: (0, 0)),)
+            + (pl.BlockSpec((4, CROWS, LANES), lambda i, p: (0, 0, 0)),) * 8,
+            scratch_shapes=[pltpu.VMEM((4, 160, LANES), f32)],
         ),
         compiler_params=pltpu.CompilerParams(vmem_limit_bytes=60 * 2**20),
         cost_estimate=pl.CostEstimate(flops=100_000_000, bytes_accessed=1_600_000, transcendentals=0),
         name="pack",
-    )(pos, coeffs_in, coeffs_in, ms_image, ms_image, hs_rows)
+    )(pos, coeffs_in, coeffs_in, ms_image, ms_image, hs_image)
 
 
 def spread_kernel(above_ref, own_ref, below_ref, k_ref, basis_ref, response_ref, sent_ref, ms_ref):
@@ -312,20 +330,16 @@
 
 
 def per_device(coeffs_in, basis, kernels, response, hs_image, ms_image):
-    s = lax.axis_index("sub").astype(jnp.int32)
-    b = lax.axis_index("band").astype(jnp.int32)
-    at = (b + 1) // 2 - 1
-    off = jnp.where(b % 2 == 0, 112, 48)
-    pos = jnp.stack([s, b, jnp.maximum(at, 0), jnp.minimum(at + 1, 7), off]).astype(jnp.int32)
-    hs_rows = jnp.pad(hs_image.transpose(1, 0, 2), ((0, 0), (0, 2), (0, 0))).reshape(64, 256)
-    tiles, own = pack(pos, coeffs_in, ms_image, hs_rows)
-    c = lax.all_to_all(tiles, "sub", split_axis=0, concat_axis=0, tiled=True).reshape(32 * CROWS, LANES)
+    pos = (lax.axis_index("sub") * 16 + lax.axis_index("band")).astype(jnp.int32).reshape(1)
+    own, *tiles = pack(pos, coeffs_in, ms_image, hs_image)
     above = lax.ppermute(own, "sub", [(i, i + 1) for i in range(7)])
     below = lax.ppermute(own, "sub", [(i + 1, i) for i in range(7)])
     sent, ms = spread(above, own, below, kernels, basis, response)
-    sent, c = lax.optimization_barrier((sent, c))
     hp = lax.all_to_all(sent, "band", split_axis=0, concat_axis=0, tiled=True).reshape(256, 384)
-    new = refine(pos, c, hp, ms)
+    tiles = [tiles[0]] + [
+        lax.ppermute(tiles[d], "sub", [(i, (i + d) % 8) for i in range(8)]) for d in range(1, 8)
+    ]
+    new = refine(pos, tiles, hp, ms)
     owned = lax.all_to_all(new.reshape(8, 4, 8, LANES), "sub", split_axis=0, concat_axis=0, tiled=True)
     copies = jnp.broadcast_to(owned[None], (16,) + owned.shape)
     gathered = lax.all_to_all(copies, "band", split_axis=0, concat_axis=0, tiled=True)

time: 95 us -> 92.6 us (0.975)
  blocking collectives: 57.4 us -> 43.2 us
  starting transfers between devices: 11.5 us -> 24.3 us
  local copies, waits for them, and re-layouts: 3.12 us -> 2.02 us
    all_to_all x1 -> x0, blocking collectives: 17 us -> none  [per_device(): lax.all_to_all(sent, 'band', split_axis=0, concat_axis=0, tiled=True)]
    ppermute x0 -> x7, starting transfers between devices: none -> 10.2 us  [per_device(): lax.ppermute(tiles[d], 'sub', [(i, (i + d) % 8) for i in range(8)])]
    ppermute x1, waiting for transfers between devices: 6.36 us -> 0.17 us  [per_device(): below = lax.ppermute(own, 'sub', [(i + 1, i) for i in range(7)])]
    ppermute x0 -> x7, waiting for transfers between devices: none -> 5.46 us  [per_device(): lax.ppermute(tiles[d], 'sub', [(i, (i + d) % 8) for i in range(8)])]
    all_to_all x1, blocking collectives: 30 us -> 34 us  [per_device(): lax.all_to_all(copies, 'band', split_axis=0, concat_axis=0, tiled=True)]
    all_to_all x1, starting transfers between devices: 5.93 us -> 7.77 us  [per_device(): lax.all_to_all(sent, 'band', split_axis=0, concat_axis=0, tiled=True)]
    ppermute x1, starting transfers between devices: 1.91 us -> 3.32 us  [per_device(): below = lax.ppermute(own, 'sub', [(i + 1, i) for i in range(7)])]
    ppermute x1, waiting for transfers between devices: 0.01 us -> 1.41 us  [per_device(): above = lax.ppermute(own, 'sub', [(i, i + 1) for i in range(7)])]
  transfers between devices with their start and end apart: 3 -> 10, of which waited for: 1 -> 5; matrix products, arithmetic and copies ran while one was open for 0% -> 0% of each run, Pallas kernels for 0% -> 0%
where the time goes in v4:
time: 92.6 us; the launch traced here: 91.6 us
  blocking collectives  43.2 us (47%)
  starting transfers between devices  24.3 us (26%)
  Pallas kernels  15 us (16%)
  waiting for transfers between devices  7.04 us (8%)
  local copies, waits for them, and re-layouts  2.02 us (2%)
    all_to_all x1, blocking collectives, per_device(): lax.all_to_all(copies, 'band', split_axis=0, concat_axis=0, tiled=True)  34 us
    ppermute x7, starting transfers between devices, per_device(): lax.ppermute(tiles[d], 'sub', [(i, (i + d) % 8) for i in range(8)])  10.2 us
    pallas_call x1, Pallas kernels, refine(): pl.pallas_call(refine_kernel, out_shape=jax.ShapeDtypeStruct((32 * 8, LAN...  9.21 us
    all_to_all x1, blocking collectives, per_device(): lax.all_to_all(new.reshape(8, 4, 8, LANES), 'sub', split_axis=0, concat_a...  9.13 us
    all_to_all x1, starting transfers between devices, per_device(): lax.all_to_all(sent, 'band', split_axis=0, concat_axis=0, tiled=True)  7.77 us
    ppermute x7, waiting for transfers between devices, per_device(): lax.ppermute(tiles[d], 'sub', [(i, (i + d) % 8) for i in range(8)])  5.46 us
    ppermute x1, starting transfers between devices, per_device(): below = lax.ppermute(own, 'sub', [(i + 1, i) for i in range(7)])  3.32 us
    ppermute x1, starting transfers between devices, per_device(): above = lax.ppermute(own, 'sub', [(i, i + 1) for i in range(7)])  3.1 us
  transfers between devices with their start and end apart: 10, of which 5 were waited for; matrix products, arithmetic and copies ran while one was open for 0% of the time, Pallas kernels for 0%

profile of v4, /device:TPU:1, one launch (start us, length us, event | category | flops | bytes accessed | tf_op | source)
XLA Modules:
  0.0 91.6 jit_solution(6539204401525685720)
XLA Ops:
  0.0 2.3 %pack.1 = (bf16[256,128]{1,0:T(8,128)(2,1)}, f32[4,48,128]{2,1,0:T(8,128)}, f32[4,48,128]{2,1,0:T(8,128)}, f32[4,48,128]{2,1,0:T(8,128)}, f32[4,48,128]{2,1,0:T(...) custom-call(s32[1]{0:T(128)} %bitcast.pos_ref, ...), custom_call_target="tpu_custom_call" | custom-call | flops 100000000 | bytes 1600000 | tf_op jit(solution)/shard_map/pack/pallas_call | solution.py:241
  2.3 3.3 %collective-permute-start.8 = (bf16[256,128]{1,0:T(8,128)(2,1)}, bf16[256,128]{1,0:T(8,128)(2,1)S(1)}, u32[]{:S(2)}, u32[]{:S(2)}) collective-permute-start(bf16[256,128]{1,0:T(8,128)(2,1)} %get-tuple-element.24.own_ref), channel_id=1, source_target_pairs={{16,0},{32,16},{48,32},{64,48},{80,64},{96,80},{112,96},{17,1},{33... | collective-permute-start | bytes 196616 | tf_op jit(solution)/shard_map/ppermute | solution.py:336
  5.6 3.1 %collective-permute-start.7 = (bf16[256,128]{1,0:T(8,128)(2,1)}, bf16[256,128]{1,0:T(8,128)(2,1)S(1)}, u32[]{:S(2)}, u32[]{:S(2)}) collective-permute-start(bf16[256,128]{1,0:T(8,128)(2,1)} %get-tuple-element.24.own_ref), channel_id=1, source_target_pairs={{0,16},{16,32},{32,48},{48,64},{64,80},{80,96},{96,112},{1,17},{17... | collective-permute-start | bytes 196616 | tf_op jit(solution)/shard_map/ppermute | solution.py:335
  8.7 0.0 copy-done.4
  8.8 0.2 collective-permute-done.8.below_ref
  8.9 1.4 %collective-permute-done.7.above_ref = bf16[256,128]{1,0:T(8,128)(2,1)S(1)} collective-permute-done((bf16[256,128]{1,0:T(8,128)(2,1)}, bf16[256,128]{1,0:T(8,128)(2,1)S(1)}, u32[]{:S(2)}, u32[]{:S(2)}) %collective-permute-start.7) | collective-permute-done | bytes 65568 | tf_op jit(solution)/shard_map/ppermute | solution.py:335
  10.3 0.0 copy-done.1
  10.3 0.0 copy-done.2
  10.3 0.8 copy-done
  11.2 1.1 %spread.1 = (f32[16,16,384]{2,1,0:T(8,128)}, f32[256,128]{1,0:T(8,128)S(1)}) custom-call(bf16[256,128]{1,0:T(8,128)(2,1)S(1)} %collective-permute-done.7.above_ref, bf16[256,128]{1,0:T(8,128)(2,1)S(1)} %copy-done, bf16[256,128]{1,0:T(8,128)(2,1)S(1)} %collective-permute-done.8.below_ref, f32[14,9,9]{2,1,0:T(8,128)S(1)} %copy.7.k_ref, ...), custom_call_target="tpu_custom_call" | custom-call | flops 1000000 | bytes 1000000 | tf_op jit(solution)/shard_map/spread/pallas_call | solution.py:294
  12.2 7.8 %all-to-all-start = ((f32[16,16,384]{2,1,0:T(8,128)}), f32[16,16,384]{2,1,0:T(8,128)S(1)}, u32[]{:S(2)}, u32[]{:S(2)}) async-start(f32[16,16,384]{2,1,0:T(8,128)} %get-tuple-element.25), calls=%async_computation | async-start | bytes 786432 | tf_op jit(solution)/shard_map/all_to_all | solution.py:338
  20.0 2.5 %collective-permute-start = (f32[4,48,128]{2,1,0:T(8,128)}, f32[4,48,128]{2,1,0:T(8,128)S(1)}, u32[]{:S(2)}, u32[]{:S(2)}) collective-permute-start(f32[4,48,128]{2,1,0:T(8,128)} %get-tuple-element.17), channel_id=1, source_target_pairs={{0,16},{16,32},{32,48},{48,64},{64,80},{80,96},{96,112},{112,0},{1... | collective-permute-start | bytes 294920 | tf_op jit(solution)/shard_map/ppermute | solution.py:340
  22.6 1.2 %collective-permute-start.1 = (f32[4,48,128]{2,1,0:T(8,128)}, f32[4,48,128]{2,1,0:T(8,128)S(1)}, u32[]{:S(2)}, u32[]{:S(2)}) collective-permute-start(f32[4,48,128]{2,1,0:T(8,128)} %get-tuple-element.18), channel_id=1, source_target_pairs={{0,32},{16,48},{32,64},{48,80},{64,96},{80,112},{96,0},{112,16},{1... | collective-permute-start | bytes 294920 | tf_op jit(solution)/shard_map/ppermute | solution.py:340
  23.8 1.9 %collective-permute-start.2 = (f32[4,48,128]{2,1,0:T(8,128)}, f32[4,48,128]{2,1,0:T(8,128)S(1)}, u32[]{:S(2)}, u32[]{:S(2)}) collective-permute-start(f32[4,48,128]{2,1,0:T(8,128)} %get-tuple-element.19), channel_id=1, source_target_pairs={{0,48},{16,64},{32,80},{48,96},{64,112},{80,0},{96,16},{112,32},{1... | collective-permute-start | bytes 294920 | tf_op jit(solution)/shard_map/ppermute | solution.py:340
  25.6 0.3 collective-permute-start.3
  25.9 2.0 %collective-permute-start.4 = (f32[4,48,128]{2,1,0:T(8,128)}, f32[4,48,128]{2,1,0:T(8,128)S(1)}, u32[]{:S(2)}, u32[]{:S(2)}) collective-permute-start(f32[4,48,128]{2,1,0:T(8,128)} %get-tuple-element.21), channel_id=1, source_target_pairs={{0,80},{16,96},{32,112},{48,0},{64,16},{80,32},{96,48},{112,64},{1... | collective-permute-start | bytes 294920 | tf_op jit(solution)/shard_map/ppermute | solution.py:340
  27.9 0.0 collective-permute-done.refs_1_
  27.9 0.8 collective-permute-start.5
  28.8 0.0 collective-permute-done.1.refs_2_
  28.8 1.4 %collective-permute-start.6 = (f32[4,48,128]{2,1,0:T(8,128)}, f32[4,48,128]{2,1,0:T(8,128)S(1)}, u32[]{:S(2)}, u32[]{:S(2)}) collective-permute-start(f32[4,48,128]{2,1,0:T(8,128)} %get-tuple-element.23), channel_id=1, source_target_pairs={{0,112},{16,0},{32,16},{48,32},{64,48},{80,64},{96,80},{112,96},{1... | collective-permute-start | bytes 294920 | tf_op jit(solution)/shard_map/ppermute | solution.py:340
  30.2 0.0 collective-permute-done.2.refs_3_
  30.2 4.1 %collective-permute-done.3.refs_4_ = f32[4,48,128]{2,1,0:T(8,128)S(1)} collective-permute-done((f32[4,48,128]{2,1,0:T(8,128)}, f32[4,48,128]{2,1,0:T(8,128)S(1)}, u32[]{:S(2)}, u32[]{:S(2)}) %collective-permute-start.3) | collective-permute-done | bytes 98336 | tf_op jit(solution)/shard_map/ppermute | solution.py:340
  34.2 0.6 collective-permute-done.4.refs_5_
  34.9 0.0 collective-permute-done.5.refs_6_
  34.9 0.8 collective-permute-done.6.refs_7_
  35.6 0.0 all-to-all-done
  35.6 0.9 copy-done.3
  36.5 9.2 %refine.1 = f32[256,128]{1,0:T(8,128)S(1)} custom-call(s32[1]{0:T(128)} %bitcast.pos_ref, f32[4,48,128]{2,1,0:T(8,128)S(1)} %copy-done.3, f32[4,48,128]{2,1,0:T(8,128)S(1)} %collective-permute-done.refs_1_, f32[4,48,128]{2,1,0:T(8,128)S(1)} %collective-permute-done.1.refs_2_, f32[4,48,128]{2,1,0:T(8,128)S(1)} %collective-permute-done.2.refs_3_, ...), custom_call_target="tpu_custom_call" | custom-call | flops 400000000 | bytes 2000000 | tf_op jit(solution)/shard_map/refine/pallas_call | solution.py:167
  45.7 9.1 %all_to_all.15 = f32[8,4,8,128]{3,2,1,0:T(8,128)S(1)} all-to-all(f32[8,4,8,128]{3,2,1,0:T(8,128)S(1)} %bitcast.4), channel_id=1, replica_groups=mesh['sub'=8,'band'=16] {'sub'}, dimensions={0} | all-to-all | bytes 262144 | tf_op jit(solution)/shard_map/all_to_all | solution.py:343
  54.9 0.2 broadcast_in_dim.2
  55.1 34.0 %all_to_all.16.g_ref = f32[16,8,4,8,128]{4,3,2,1,0:T(8,128)S(1)} all-to-all(f32[16,8,4,8,128]{4,3,2,1,0:T(8,128)S(1)} %broadcast_in_dim.2), channel_id=1, replica_groups=mesh['sub'=8,'band'=16] {'band'}, dimensions={0} | all-to-all | bytes 4194304 | tf_op jit(solution)/shard_map/all_to_all | solution.py:345
  89.2 2.4 %place.1 = f32[4,128,1024]{2,1,0:T(8,128)} custom-call(f32[16,8,4,8,128]{4,3,2,1,0:T(8,128)S(1)} %all_to_all.16.g_ref), custom_call_target="tpu_custom_call" | custom-call | tf_op jit(solution)/shard_map/place/pallas_call | solution.py:321
  (6 shorter events, 0.0 us)
Async XLA Ops:
  0.0 8.7 %copy-start.4 = (f32[14,9,9]{2,0,1:T(8,128)S(1)}, f32[14,9,9]{2,0,1:T(8,128)}, u32[]{:S(2)}) copy-start(f32[14,9,9]{2,0,1:T(8,128)} %param.8) | copy-start | bytes 13612
  0.0 10.3 %copy-start.1 = (bf16[14,32]{1,0:T(8,128)(2,1)S(1)}, bf16[14,32]{1,0:T(8,128)(2,1)}, u32[]{:S(2)}) copy-start(bf16[14,32]{1,0:T(8,128)(2,1)} %basis_ref.1) | copy-start | bytes 2692
  0.0 10.3 %copy-start.2 = (bf16[8,14]{1,0:T(8,128)(2,1)S(1)}, bf16[8,14]{1,0:T(8,128)(2,1)}, u32[]{:S(2)}) copy-start(bf16[8,14]{1,0:T(8,128)(2,1)} %response_ref.1) | copy-start | bytes 676
  2.3 6.7 %collective-permute-start.8 = (bf16[256,128]{1,0:T(8,128)(2,1)}, bf16[256,128]{1,0:T(8,128)(2,1)S(1)}, u32[]{:S(2)}, u32[]{:S(2)}) collective-permute-start(bf16[256,128]{1,0:T(8,128)(2,1)} %get-tuple-element.24.own_ref), channel_id=1, source_target_pairs={{16,0},{32,16},{48,32},{64,48},{80,64},{96,80},{112,96},{17,1},{33... | collective-permute-start | bytes 196616 | tf_op jit(solution)/shard_map/ppermute | solution.py:336
  5.6 4.7 %collective-permute-start.7 = (bf16[256,128]{1,0:T(8,128)(2,1)}, bf16[256,128]{1,0:T(8,128)(2,1)S(1)}, u32[]{:S(2)}, u32[]{:S(2)}) collective-permute-start(bf16[256,128]{1,0:T(8,128)(2,1)} %get-tuple-element.24.own_ref), channel_id=1, source_target_pairs={{0,16},{16,32},{32,48},{48,64},{64,80},{80,96},{96,112},{1,17},{17... | collective-permute-start | bytes 196616 | tf_op jit(solution)/shard_map/ppermute | solution.py:335
  10.3 0.8 copy-start
  12.2 23.4 %all-to-all-start = ((f32[16,16,384]{2,1,0:T(8,128)}), f32[16,16,384]{2,1,0:T(8,128)S(1)}, u32[]{:S(2)}, u32[]{:S(2)}) async-start(f32[16,16,384]{2,1,0:T(8,128)} %get-tuple-element.25), calls=%async_computation | async-start | bytes 786432 | tf_op jit(solution)/shard_map/all_to_all | solution.py:338
  20.0 7.9 %collective-permute-start = (f32[4,48,128]{2,1,0:T(8,128)}, f32[4,48,128]{2,1,0:T(8,128)S(1)}, u32[]{:S(2)}, u32[]{:S(2)}) collective-permute-start(f32[4,48,128]{2,1,0:T(8,128)} %get-tuple-element.17), channel_id=1, source_target_pairs={{0,16},{16,32},{32,48},{48,64},{64,80},{80,96},{96,112},{112,0},{1... | collective-permute-start | bytes 294920 | tf_op jit(solution)/shard_map/ppermute | solution.py:340
  22.6 6.2 %collective-permute-start.1 = (f32[4,48,128]{2,1,0:T(8,128)}, f32[4,48,128]{2,1,0:T(8,128)S(1)}, u32[]{:S(2)}, u32[]{:S(2)}) collective-permute-start(f32[4,48,128]{2,1,0:T(8,128)} %get-tuple-element.18), channel_id=1, source_target_pairs={{0,32},{16,48},{32,64},{48,80},{64,96},{80,112},{96,0},{112,16},{1... | collective-permute-start | bytes 294920 | tf_op jit(solution)/shard_map/ppermute | solution.py:340
  23.8 6.4 %collective-permute-start.2 = (f32[4,48,128]{2,1,0:T(8,128)}, f32[4,48,128]{2,1,0:T(8,128)S(1)}, u32[]{:S(2)}, u32[]{:S(2)}) collective-permute-start(f32[4,48,128]{2,1,0:T(8,128)} %get-tuple-element.19), channel_id=1, source_target_pairs={{0,48},{16,64},{32,80},{48,96},{64,112},{80,0},{96,16},{112,32},{1... | collective-permute-start | bytes 294920 | tf_op jit(solution)/shard_map/ppermute | solution.py:340
  25.6 8.6 %collective-permute-start.3 = (f32[4,48,128]{2,1,0:T(8,128)}, f32[4,48,128]{2,1,0:T(8,128)S(1)}, u32[]{:S(2)}, u32[]{:S(2)}) collective-permute-start(f32[4,48,128]{2,1,0:T(8,128)} %get-tuple-element.20), channel_id=1, source_target_pairs={{0,64},{16,80},{32,96},{48,112},{64,0},{80,16},{96,32},{112,48},{1... | collective-permute-start | bytes 294920 | tf_op jit(solution)/shard_map/ppermute | solution.py:340
  25.9 9.0 %collective-permute-start.4 = (f32[4,48,128]{2,1,0:T(8,128)}, f32[4,48,128]{2,1,0:T(8,128)S(1)}, u32[]{:S(2)}, u32[]{:S(2)}) collective-permute-start(f32[4,48,128]{2,1,0:T(8,128)} %get-tuple-element.21), channel_id=1, source_target_pairs={{0,80},{16,96},{32,112},{48,0},{64,16},{80,32},{96,48},{112,64},{1... | collective-permute-start | bytes 294920 | tf_op jit(solution)/shard_map/ppermute | solution.py:340
  27.9 6.9 %collective-permute-start.5 = (f32[4,48,128]{2,1,0:T(8,128)}, f32[4,48,128]{2,1,0:T(8,128)S(1)}, u32[]{:S(2)}, u32[]{:S(2)}) collective-permute-start(f32[4,48,128]{2,1,0:T(8,128)} %get-tuple-element.22), channel_id=1, source_target_pairs={{0,96},{16,112},{32,0},{48,16},{64,32},{80,48},{96,64},{112,80},{1... | collective-permute-start | bytes 294920 | tf_op jit(solution)/shard_map/ppermute | solution.py:340
  28.8 6.9 %collective-permute-start.6 = (f32[4,48,128]{2,1,0:T(8,128)}, f32[4,48,128]{2,1,0:T(8,128)S(1)}, u32[]{:S(2)}, u32[]{:S(2)}) collective-permute-start(f32[4,48,128]{2,1,0:T(8,128)} %get-tuple-element.23), channel_id=1, source_target_pairs={{0,112},{16,0},{32,16},{48,32},{64,48},{80,64},{96,80},{112,96},{1... | collective-permute-start | bytes 294920 | tf_op jit(solution)/shard_map/ppermute | solution.py:340
  35.6 0.9 copy-start.3

commit v5 on v4

--- a/solution.py
+++ b/solution.py
@@ -10,6 +10,7 @@
 STEP = 0.15
 TR, TC = 16, 64
 TAPS = 9
+SPAN = 250.0
 LANES = 128
 CROWS = 48
 MROWS = 32
@@ -152,7 +153,8 @@
         for half in range(2):
             row = 8 + r + 8 * half
             at = pl.ds(row * 32, 32)
-            value = c1_ref[at, :] + STEP * (grads[half][:, r * 128 : r * 128 + 128] + g_ref[at, :])
+            value = STEP * (grads[half][:, r * 128 : r * 128 + 128] + g_ref[at, :])
+            value = value + (c1_ref[at, :] - start_row(row + 8))
             rest = jnp.where((group >= 4) & (group < 20), value, 0.0)
             for _ in range(3):
                 piece = rest.astype(bf16)
@@ -305,28 +307,68 @@
     )(above, own, below, kernels, basis, response)
 
 
-def place_kernel(g_ref, out_ref):
+def encode_kernel(d_ref, out_ref):
+    scales = []
+    codes = []
+    for k in range(4):
+        part = d_ref[:, k]
+        size = jnp.abs(part)
+        top = jnp.max(size, axis=(0, 1, 2), keepdims=True)
+        scale = rounded(jnp.maximum(top * (1 + 2**-7), 1e-30))
+        code = jnp.exp2(size * (SPAN / scale) - SPAN / 2)
+        codes.append(jnp.where(part < 0, -code, code))
+        scales.append(jnp.broadcast_to(scale[0], (1, LANES)))
+    scales = jnp.concatenate(scales + [jnp.zeros((12, LANES), f32)], axis=0).astype(bf16)
+    for s in range(8):
+        row = jnp.concatenate([codes[k][s] for k in range(4)], axis=0).astype(bf16)
+        for t in range(16):
+            out_ref[t, 32 * s : 32 * s + 32] = row
+    for t in range(16):
+        out_ref[t, 256:272] = scales
+
+
+def encode(owned):
+    vmem = pl.BlockSpec(memory_space=pltpu.VMEM)
+    return pl.pallas_call(
+        encode_kernel,
+        out_shape=jax.ShapeDtypeStruct((16, 272, LANES), bf16),
+        in_specs=[vmem],
+        out_specs=vmem,
+        compiler_params=pltpu.CompilerParams(vmem_limit_bytes=16 * 2**20),
+        name="encode",
+    )(owned)
+
+
+def place_kernel(g_ref, c_ref, out_ref):
     lane = lax.broadcasted_iota(jnp.int32, (1, LANES), 1)
     low = lane < 64
+    scales = [g_ref[e, 256:272].astype(f32) * (1 / SPAN) for e in range(2)]
     for s in range(8):
-        for j in range(8):
-            even = g_ref[2 * j, s, 0]
-            odd = g_ref[2 * j + 1, s, 0]
-            at = slice(j * 128, j * 128 + 128)
-            out_ref[0, 16 * s : 16 * s + 8, at] = jnp.where(low, even, pltpu.roll(odd, 64, 1))
-            out_ref[0, 16 * s + 8 : 16 * s + 16, at] = jnp.where(low, pltpu.roll(even, 64, 1), odd)
-
-
-def place(gathered):
+        pair = []
+        for e in range(2):
+            code = g_ref[e, 32 * s : 32 * s + 32].astype(f32)
+            size = jnp.log2(jnp.abs(code)) + SPAN / 2
+            pair.append(jnp.where(code < 0, -size, size))
+        for k in range(4):
+            even, odd = [pair[e][8 * k : 8 * k + 8] * scales[e][k : k + 1] for e in range(2)]
+            for half, value in enumerate(
+                [jnp.where(low, even, pltpu.roll(odd, 64, 1)), jnp.where(low, pltpu.roll(even, 64, 1), odd)]
+            ):
+                at = slice(16 * s + 8 * half, 16 * s + 8 * half + 8)
+                out_ref[k, at] = c_ref[k, at] + value
+
+
+def place(gathered, coeffs_in):
+    block = pl.BlockSpec((4, 128, LANES), lambda j: (0, 0, j))
     return pl.pallas_call(
         place_kernel,
         out_shape=jax.ShapeDtypeStruct((4, 128, 1024), f32),
-        grid=(4,),
-        in_specs=[pl.BlockSpec((16, 8, 1, 8, LANES), lambda k: (0, 0, k, 0, 0))],
-        out_specs=pl.BlockSpec((1, 128, 1024), lambda k: (k, 0, 0)),
+        grid=(8,),
+        in_specs=[pl.BlockSpec((2, 272, LANES), lambda j: (j, 0, 0)), block],
+        out_specs=block,
         compiler_params=pltpu.CompilerParams(vmem_limit_bytes=32 * 2**20),
         name="place",
-    )(gathered)
+    )(gathered, coeffs_in)
 
 
 def per_device(coeffs_in, basis, kernels, response, hs_image, ms_image):
@@ -341,9 +383,8 @@
     ]
     new = refine(pos, tiles, hp, ms)
     owned = lax.all_to_all(new.reshape(8, 4, 8, LANES), "sub", split_axis=0, concat_axis=0, tiled=True)
-    copies = jnp.broadcast_to(owned[None], (16,) + owned.shape)
-    gathered = lax.all_to_all(copies, "band", split_axis=0, concat_axis=0, tiled=True)
-    return place(gathered)
+    gathered = lax.all_to_all(encode(owned), "band", split_axis=0, concat_axis=0, tiled=True)
+    return place(gathered, coeffs_in)
 
 
 def solution(mesh):

time: 92.6 us -> 83.6 us (0.903)
  blocking collectives: 43.2 us -> 32.7 us
  Pallas kernels: 15 us -> 16.5 us
    all_to_all x1, blocking collectives: 34 us -> 23.5 us  [per_device(): lax.all_to_all(encode(owned), 'band', split_axis=0, concat_axis=0, tiled=...]
    pallas_call x1, Pallas kernels: 2.43 us -> 3.77 us  [place(): pl.pallas_call(place_kernel, out_shape=jax.ShapeDtypeStruct((4, 128, 1024...]
where the time goes in v5:
time: 83.6 us; the launch traced here: 82.5 us
  blocking collectives  32.7 us (39%)
  starting transfers between devices  24.3 us (29%)
  Pallas kernels  16.5 us (20%)
  waiting for transfers between devices  7.04 us (8%)
  local copies, waits for them, and re-layouts  1.77 us (2%)
    all_to_all x1, blocking collectives, per_device(): lax.all_to_all(encode(owned), 'band', split_axis=0, concat_axis=0, tiled=...  23.5 us
    ppermute x7, starting transfers between devices, per_device(): lax.ppermute(tiles[d], 'sub', [(i, (i + d) % 8) for i in range(8)])  10.2 us
    all_to_all x1, blocking collectives, per_device(): lax.all_to_all(new.reshape(8, 4, 8, LANES), 'sub', split_axis=0, concat_a...  9.27 us
    pallas_call x1, Pallas kernels, refine(): pl.pallas_call(refine_kernel, out_shape=jax.ShapeDtypeStruct((32 * 8, LAN...  9.21 us
    all_to_all x1, starting transfers between devices, per_device(): lax.all_to_all(sent, 'band', split_axis=0, concat_axis=0, tiled=True)  7.77 us
    ppermute x7, waiting for transfers between devices, per_device(): lax.ppermute(tiles[d], 'sub', [(i, (i + d) % 8) for i in range(8)])  5.46 us
    pallas_call x1, Pallas kernels, place(): pl.pallas_call(place_kernel, out_shape=jax.ShapeDtypeStruct((4, 128, 1024...  3.77 us
    ppermute x1, starting transfers between devices, per_device(): below = lax.ppermute(own, 'sub', [(i + 1, i) for i in range(7)])  3.32 us
  transfers between devices with their start and end apart: 10, of which 5 were waited for; matrix products, arithmetic and copies ran while one was open for 0% of the time, Pallas kernels for 0%

profile of v5, /device:TPU:1, one launch (start us, length us, event | category | flops | bytes accessed | tf_op | source)
XLA Modules:
  0.0 82.5 jit_solution(6730001391298448734)
XLA Ops:
  0.0 2.3 %pack.1 = (bf16[256,128]{1,0:T(8,128)(2,1)}, f32[4,48,128]{2,1,0:T(8,128)}, f32[4,48,128]{2,1,0:T(8,128)}, f32[4,48,128]{2,1,0:T(8,128)}, f32[4,48,128]{2,1,0:T(...) custom-call(s32[1]{0:T(128)} %bitcast.pos_ref, ...), custom_call_target="tpu_custom_call" | custom-call | flops 100000000 | bytes 1600000 | tf_op jit(solution)/shard_map/pack/pallas_call | solution.py:243
  2.3 3.3 %collective-permute-start.8 = (bf16[256,128]{1,0:T(8,128)(2,1)}, bf16[256,128]{1,0:T(8,128)(2,1)S(1)}, u32[]{:S(2)}, u32[]{:S(2)}) collective-permute-start(bf16[256,128]{1,0:T(8,128)(2,1)} %get-tuple-element.24.own_ref), channel_id=1, source_target_pairs={{16,0},{32,16},{48,32},{64,48},{80,64},{96,80},{112,96},{17,1},{33... | collective-permute-start | bytes 196616 | tf_op jit(solution)/shard_map/ppermute | solution.py:378
  5.6 3.1 %collective-permute-start.7 = (bf16[256,128]{1,0:T(8,128)(2,1)}, bf16[256,128]{1,0:T(8,128)(2,1)S(1)}, u32[]{:S(2)}, u32[]{:S(2)}) collective-permute-start(bf16[256,128]{1,0:T(8,128)(2,1)} %get-tuple-element.24.own_ref), channel_id=1, source_target_pairs={{0,16},{16,32},{32,48},{48,64},{64,80},{80,96},{96,112},{1,17},{17... | collective-permute-start | bytes 196616 | tf_op jit(solution)/shard_map/ppermute | solution.py:377
  8.7 0.0 copy-done.5
  8.8 0.2 collective-permute-done.8.below_ref
  8.9 1.4 %collective-permute-done.7.above_ref = bf16[256,128]{1,0:T(8,128)(2,1)S(1)} collective-permute-done((bf16[256,128]{1,0:T(8,128)(2,1)}, bf16[256,128]{1,0:T(8,128)(2,1)S(1)}, u32[]{:S(2)}, u32[]{:S(2)}) %collective-permute-start.7) | collective-permute-done | bytes 65568 | tf_op jit(solution)/shard_map/ppermute | solution.py:377
  10.3 0.0 copy-done.2
  10.3 0.0 copy-done.3
  10.3 0.8 %copy-done.1 = bf16[256,128]{1,0:T(8,128)(2,1)S(1)} copy-done((bf16[256,128]{1,0:T(8,128)(2,1)S(1)}, bf16[256,128]{1,0:T(8,128)(2,1)}, u32[]{:S(2)}) %copy-start.1) | copy-done | bytes 65560
  11.2 1.1 %spread.1 = (f32[16,16,384]{2,1,0:T(8,128)}, f32[256,128]{1,0:T(8,128)S(1)}) custom-call(bf16[256,128]{1,0:T(8,128)(2,1)S(1)} %collective-permute-done.7.above_ref, bf16[256,128]{1,0:T(8,128)(2,1)S(1)} %copy-done.1, bf16[256,128]{1,0:T(8,128)(2,1)S(1)} %collective-permute-done.8.below_ref, f32[14,9,9]{2,1,0:T(8,128)S(1)} %copy.7.k_ref, ...), custom_call_target="tpu_custom_call" | custom-call | flops 1000000 | bytes 1000000 | tf_op jit(solution)/shard_map/spread/pallas_call | solution.py:296
  12.2 7.8 %all-to-all-start = ((f32[16,16,384]{2,1,0:T(8,128)}), f32[16,16,384]{2,1,0:T(8,128)S(1)}, u32[]{:S(2)}, u32[]{:S(2)}) async-start(f32[16,16,384]{2,1,0:T(8,128)} %get-tuple-element.25), calls=%async_computation | async-start | bytes 786432 | tf_op jit(solution)/shard_map/all_to_all | solution.py:380
  20.0 2.5 %collective-permute-start = (f32[4,48,128]{2,1,0:T(8,128)}, f32[4,48,128]{2,1,0:T(8,128)S(1)}, u32[]{:S(2)}, u32[]{:S(2)}) collective-permute-start(f32[4,48,128]{2,1,0:T(8,128)} %get-tuple-element.17), channel_id=1, source_target_pairs={{0,16},{16,32},{32,48},{48,64},{64,80},{80,96},{96,112},{112,0},{1... | collective-permute-start | bytes 294920 | tf_op jit(solution)/shard_map/ppermute | solution.py:382
  22.6 1.2 %collective-permute-start.1 = (f32[4,48,128]{2,1,0:T(8,128)}, f32[4,48,128]{2,1,0:T(8,128)S(1)}, u32[]{:S(2)}, u32[]{:S(2)}) collective-permute-start(f32[4,48,128]{2,1,0:T(8,128)} %get-tuple-element.18), channel_id=1, source_target_pairs={{0,32},{16,48},{32,64},{48,80},{64,96},{80,112},{96,0},{112,16},{1... | collective-permute-start | bytes 294920 | tf_op jit(solution)/shard_map/ppermute | solution.py:382
  23.8 1.9 %collective-permute-start.2 = (f32[4,48,128]{2,1,0:T(8,128)}, f32[4,48,128]{2,1,0:T(8,128)S(1)}, u32[]{:S(2)}, u32[]{:S(2)}) collective-permute-start(f32[4,48,128]{2,1,0:T(8,128)} %get-tuple-element.19), channel_id=1, source_target_pairs={{0,48},{16,64},{32,80},{48,96},{64,112},{80,0},{96,16},{112,32},{1... | collective-permute-start | bytes 294920 | tf_op jit(solution)/shard_map/ppermute | solution.py:382
  25.6 0.3 collective-permute-start.3
  25.9 2.0 %collective-permute-start.4 = (f32[4,48,128]{2,1,0:T(8,128)}, f32[4,48,128]{2,1,0:T(8,128)S(1)}, u32[]{:S(2)}, u32[]{:S(2)}) collective-permute-start(f32[4,48,128]{2,1,0:T(8,128)} %get-tuple-element.21), channel_id=1, source_target_pairs={{0,80},{16,96},{32,112},{48,0},{64,16},{80,32},{96,48},{112,64},{1... | collective-permute-start | bytes 294920 | tf_op jit(solution)/shard_map/ppermute | solution.py:382
  27.9 0.0 collective-permute-done.refs_1_
  27.9 0.8 %collective-permute-start.5 = (f32[4,48,128]{2,1,0:T(8,128)}, f32[4,48,128]{2,1,0:T(8,128)S(1)}, u32[]{:S(2)}, u32[]{:S(2)}) collective-permute-start(f32[4,48,128]{2,1,0:T(8,128)} %get-tuple-element.22), channel_id=1, source_target_pairs={{0,96},{16,112},{32,0},{48,16},{64,32},{80,48},{96,64},{112,80},{1... | collective-permute-start | bytes 294920 | tf_op jit(solution)/shard_map/ppermute | solution.py:382
  28.8 0.0 collective-permute-done.1.refs_2_
  28.8 1.4 %collective-permute-start.6 = (f32[4,48,128]{2,1,0:T(8,128)}, f32[4,48,128]{2,1,0:T(8,128)S(1)}, u32[]{:S(2)}, u32[]{:S(2)}) collective-permute-start(f32[4,48,128]{2,1,0:T(8,128)} %get-tuple-element.23), channel_id=1, source_target_pairs={{0,112},{16,0},{32,16},{48,32},{64,48},{80,64},{96,80},{112,96},{1... | collective-permute-start | bytes 294920 | tf_op jit(solution)/shard_map/ppermute | solution.py:382
  30.2 0.0 collective-permute-done.2.refs_3_
  30.2 4.1 %collective-permute-done.3.refs_4_ = f32[4,48,128]{2,1,0:T(8,128)S(1)} collective-permute-done((f32[4,48,128]{2,1,0:T(8,128)}, f32[4,48,128]{2,1,0:T(8,128)S(1)}, u32[]{:S(2)}, u32[]{:S(2)}) %collective-permute-start.3) | collective-permute-done | bytes 98336 | tf_op jit(solution)/shard_map/ppermute | solution.py:382
  34.2 0.6 collective-permute-done.4.refs_5_
  34.9 0.0 collective-permute-done.5.refs_6_
  34.9 0.8 collective-permute-done.6.refs_7_
  35.6 0.0 all-to-all-done
  35.6 0.9 %copy-done.4 = f32[4,48,128]{2,1,0:T(8,128)S(1)} copy-done((f32[4,48,128]{2,1,0:T(8,128)S(1)}, f32[4,48,128]{2,1,0:T(8,128)}, u32[]{:S(2)}) %copy-start.4) | copy-done | bytes 98328
  36.5 9.2 %refine.1 = f32[256,128]{1,0:T(8,128)S(1)} custom-call(s32[1]{0:T(128)} %bitcast.pos_ref, f32[4,48,128]{2,1,0:T(8,128)S(1)} %copy-done.4, f32[4,48,128]{2,1,0:T(8,128)S(1)} %collective-permute-done.refs_1_, f32[4,48,128]{2,1,0:T(8,128)S(1)} %collective-permute-done.1.refs_2_, f32[4,48,128]{2,1,0:T(8,128)S(1)} %collective-permute-done.2.refs_3_, ...), custom_call_target="tpu_custom_call" | custom-call | flops 400000000 | bytes 2000000 | tf_op jit(solution)/shard_map/refine/pallas_call | solution.py:169
  45.8 9.3 %all_to_all.15.d_ref = f32[8,4,8,128]{3,2,1,0:T(8,128)S(1)} all-to-all(f32[8,4,8,128]{3,2,1,0:T(8,128)S(1)} %bitcast.4), channel_id=1, replica_groups=mesh['sub'=8,'band'=16] {'sub'}, dimensions={0} | all-to-all | bytes 262144 | tf_op jit(solution)/shard_map/all_to_all | solution.py:385
  55.0 0.2 encode.1
  55.2 23.5 %all_to_all.16.g_ref = bf16[16,272,128]{2,1,0:T(8,128)(2,1)S(1)} all-to-all(bf16[16,272,128]{2,1,0:T(8,128)(2,1)S(1)} %encode.1), channel_id=1, replica_groups=mesh['sub'=8,'band'=16] {'band'}, dimensions={0} | all-to-all | bytes 2228224 | tf_op jit(solution)/shard_map/all_to_all | solution.py:386
  78.7 3.8 %place.1 = f32[4,128,1024]{2,1,0:T(8,128)} custom-call(bf16[16,272,128]{2,1,0:T(8,128)(2,1)S(1)} %all_to_all.16.g_ref, f32[4,128,1024]{2,1,0:T(8,128)S(1)} %copy-done), custom_call_target="tpu_custom_call" | custom-call | tf_op jit(solution)/shard_map/place/pallas_call | solution.py:363
  (8 shorter events, 0.0 us)
Async XLA Ops:
  0.0 8.7 %copy-start.5 = (f32[14,9,9]{2,0,1:T(8,128)S(1)}, f32[14,9,9]{2,0,1:T(8,128)}, u32[]{:S(2)}) copy-start(f32[14,9,9]{2,0,1:T(8,128)} %param.8) | copy-start | bytes 13612
  0.0 10.3 %copy-start.2 = (bf16[14,32]{1,0:T(8,128)(2,1)S(1)}, bf16[14,32]{1,0:T(8,128)(2,1)}, u32[]{:S(2)}) copy-start(bf16[14,32]{1,0:T(8,128)(2,1)} %basis_ref.1) | copy-start | bytes 2692
  0.0 10.3 %copy-start.3 = (bf16[8,14]{1,0:T(8,128)(2,1)S(1)}, bf16[8,14]{1,0:T(8,128)(2,1)}, u32[]{:S(2)}) copy-start(bf16[8,14]{1,0:T(8,128)(2,1)} %response_ref.1) | copy-start | bytes 676
  2.3 6.7 %collective-permute-start.8 = (bf16[256,128]{1,0:T(8,128)(2,1)}, bf16[256,128]{1,0:T(8,128)(2,1)S(1)}, u32[]{:S(2)}, u32[]{:S(2)}) collective-permute-start(bf16[256,128]{1,0:T(8,128)(2,1)} %get-tuple-element.24.own_ref), channel_id=1, source_target_pairs={{16,0},{32,16},{48,32},{64,48},{80,64},{96,80},{112,96},{17,1},{33... | collective-permute-start | bytes 196616 | tf_op jit(solution)/shard_map/ppermute | solution.py:378
  5.6 4.7 %collective-permute-start.7 = (bf16[256,128]{1,0:T(8,128)(2,1)}, bf16[256,128]{1,0:T(8,128)(2,1)S(1)}, u32[]{:S(2)}, u32[]{:S(2)}) collective-permute-start(bf16[256,128]{1,0:T(8,128)(2,1)} %get-tuple-element.24.own_ref), channel_id=1, source_target_pairs={{0,16},{16,32},{32,48},{48,64},{64,80},{80,96},{96,112},{1,17},{17... | collective-permute-start | bytes 196616 | tf_op jit(solution)/shard_map/ppermute | solution.py:377
  10.3 0.8 %copy-start.1 = (bf16[256,128]{1,0:T(8,128)(2,1)S(1)}, bf16[256,128]{1,0:T(8,128)(2,1)}, u32[]{:S(2)}) copy-start(bf16[256,128]{1,0:T(8,128)(2,1)} %get-tuple-element.24.own_ref) | copy-start | bytes 196612
  12.2 23.4 %all-to-all-start = ((f32[16,16,384]{2,1,0:T(8,128)}), f32[16,16,384]{2,1,0:T(8,128)S(1)}, u32[]{:S(2)}, u32[]{:S(2)}) async-start(f32[16,16,384]{2,1,0:T(8,128)} %get-tuple-element.25), calls=%async_computation | async-start | bytes 786432 | tf_op jit(solution)/shard_map/all_to_all | solution.py:380
  20.0 7.9 %collective-permute-start = (f32[4,48,128]{2,1,0:T(8,128)}, f32[4,48,128]{2,1,0:T(8,128)S(1)}, u32[]{:S(2)}, u32[]{:S(2)}) collective-permute-start(f32[4,48,128]{2,1,0:T(8,128)} %get-tuple-element.17), channel_id=1, source_target_pairs={{0,16},{16,32},{32,48},{48,64},{64,80},{80,96},{96,112},{112,0},{1... | collective-permute-start | bytes 294920 | tf_op jit(solution)/shard_map/ppermute | solution.py:382
  22.6 6.2 %collective-permute-start.1 = (f32[4,48,128]{2,1,0:T(8,128)}, f32[4,48,128]{2,1,0:T(8,128)S(1)}, u32[]{:S(2)}, u32[]{:S(2)}) collective-permute-start(f32[4,48,128]{2,1,0:T(8,128)} %get-tuple-element.18), channel_id=1, source_target_pairs={{0,32},{16,48},{32,64},{48,80},{64,96},{80,112},{96,0},{112,16},{1... | collective-permute-start | bytes 294920 | tf_op jit(solution)/shard_map/ppermute | solution.py:382
  23.8 6.4 %collective-permute-start.2 = (f32[4,48,128]{2,1,0:T(8,128)}, f32[4,48,128]{2,1,0:T(8,128)S(1)}, u32[]{:S(2)}, u32[]{:S(2)}) collective-permute-start(f32[4,48,128]{2,1,0:T(8,128)} %get-tuple-element.19), channel_id=1, source_target_pairs={{0,48},{16,64},{32,80},{48,96},{64,112},{80,0},{96,16},{112,32},{1... | collective-permute-start | bytes 294920 | tf_op jit(solution)/shard_map/ppermute | solution.py:382
  25.6 8.6 %collective-permute-start.3 = (f32[4,48,128]{2,1,0:T(8,128)}, f32[4,48,128]{2,1,0:T(8,128)S(1)}, u32[]{:S(2)}, u32[]{:S(2)}) collective-permute-start(f32[4,48,128]{2,1,0:T(8,128)} %get-tuple-element.20), channel_id=1, source_target_pairs={{0,64},{16,80},{32,96},{48,112},{64,0},{80,16},{96,32},{112,48},{1... | collective-permute-start | bytes 294920 | tf_op jit(solution)/shard_map/ppermute | solution.py:382
  25.9 9.0 %collective-permute-start.4 = (f32[4,48,128]{2,1,0:T(8,128)}, f32[4,48,128]{2,1,0:T(8,128)S(1)}, u32[]{:S(2)}, u32[]{:S(2)}) collective-permute-start(f32[4,48,128]{2,1,0:T(8,128)} %get-tuple-element.21), channel_id=1, source_target_pairs={{0,80},{16,96},{32,112},{48,0},{64,16},{80,32},{96,48},{112,64},{1... | collective-permute-start | bytes 294920 | tf_op jit(solution)/shard_map/ppermute | solution.py:382
  27.9 6.9 %collective-permute-start.5 = (f32[4,48,128]{2,1,0:T(8,128)}, f32[4,48,128]{2,1,0:T(8,128)S(1)}, u32[]{:S(2)}, u32[]{:S(2)}) collective-permute-start(f32[4,48,128]{2,1,0:T(8,128)} %get-tuple-element.22), channel_id=1, source_target_pairs={{0,96},{16,112},{32,0},{48,16},{64,32},{80,48},{96,64},{112,80},{1... | collective-permute-start | bytes 294920 | tf_op jit(solution)/shard_map/ppermute | solution.py:382
  28.8 6.9 %collective-permute-start.6 = (f32[4,48,128]{2,1,0:T(8,128)}, f32[4,48,128]{2,1,0:T(8,128)S(1)}, u32[]{:S(2)}, u32[]{:S(2)}) collective-permute-start(f32[4,48,128]{2,1,0:T(8,128)} %get-tuple-element.23), channel_id=1, source_target_pairs={{0,112},{16,0},{32,16},{48,32},{64,48},{80,64},{96,80},{112,96},{1... | collective-permute-start | bytes 294920 | tf_op jit(solution)/shard_map/ppermute | solution.py:382
  35.6 0.9 %copy-start.4 = (f32[4,48,128]{2,1,0:T(8,128)S(1)}, f32[4,48,128]{2,1,0:T(8,128)}, u32[]{:S(2)}) copy-start(f32[4,48,128]{2,1,0:T(8,128)} %get-tuple-element.16.refs_0_) | copy-start | bytes 294916
  45.8 33.0 %copy-start = (f32[4,128,1024]{2,1,0:T(8,128)S(1)}, f32[4,128,1024]{2,1,0:T(8,128)}, u32[]{:S(2)}) copy-start(f32[4,128,1024]{2,1,0:T(8,128)} %c_ref.1) | copy-start | bytes 6291460

commit v6 on v5

--- a/solution.py
+++ b/solution.py
@@ -27,22 +27,27 @@
 
 def refine_kernel(pos_ref, *refs):
     tiles = refs[:8]
-    hp_ref, ms_ref, out_ref, c_ref, m0, m1, f0, f1, b0, b1, c1_ref, g_ref, hs0, hs1, w0, w1 = refs[8:]
+    ms_own_ref, hp_ref, above_ref, below_ref, out_ref, c_ref, ms_ref, m0, m1, f0, f1, b0, b1, c1_ref, g_ref, hs0, hs1, w0, w1 = refs[8:]
     s = pos_ref[0] // 16
     b = pos_ref[0] % 16
     for d in range(8):
         at = pl.multiple_of((s + 8 - d) % 8 * (4 * CROWS), 4 * CROWS)
-        c_ref[pl.ds(at, 4 * CROWS), :] = tiles[d][...].reshape(4 * CROWS, LANES)
+        c_ref[pl.ds(at, 4 * CROWS), :] = tiles[d][0 : 4 * CROWS]
+    for k in range(8):
+        ms_ref[32 * k : 32 * k + 8, :] = tiles[1][4 * CROWS + 8 * k : 4 * CROWS + 8 * k + 8]
+        ms_ref[32 * k + 8 : 32 * k + 24, :] = ms_own_ref[16 * k : 16 * k + 16, :]
+        ms_ref[32 * k + 24 : 32 * k + 32, :] = tiles[7][4 * CROWS + 8 * k : 4 * CROWS + 8 * k + 8]
+    bk = (b0, b1)
     m = (m0, m1)
     f = (f0, f1)
-    bk = (b0, b1)
     hst = (hs0, hs1)
     w = (w0, w1)
     for h in range(2):
-        part = hp_ref[h * 128 : h * 128 + 128, :]
-        for piece in range(2):
-            hst[h][piece * 128 : piece * 128 + 128, :] = part[:, piece * 128 : piece * 128 + 128].T
-        w[h][...] = part[:, 256:384].T
+        at = slice(h * 128, h * 128 + 128)
+        hst[h][0:72, :] = above_ref[at, :].astype(f32).T[24:96]
+        hst[h][72:168, :] = hp_ref[at, 0:128].T[0:96]
+        hst[h][168:240, :] = below_ref[at, :].astype(f32).T[0:72]
+        w[h][...] = hp_ref[at, 128:256].T
     basis = jnp.concatenate([w0[81:113, :], w1[81:113, :]], axis=1).astype(bf16)
     response = jnp.concatenate([w0[113:121, :], w1[113:121, :]], axis=1).astype(bf16)
     combined = lax.dot_general(response, basis, (((1,), (1,)), ((), ())), preferred_element_type=f32).astype(bf16)
@@ -164,15 +169,16 @@
         out_ref[pl.ds(r, 32, stride=8), :] = total
 
 
-def refine(pos, tiles, hp, ms):
+def refine(pos, tiles, ms, hp, above, below):
     vmem = pl.BlockSpec(memory_space=pltpu.VMEM)
     return pl.pallas_call(
         refine_kernel,
         out_shape=jax.ShapeDtypeStruct((32 * 8, LANES), f32),
-        in_specs=[pl.BlockSpec(memory_space=pltpu.SMEM)] + [vmem] * 10,
+        in_specs=[pl.BlockSpec(memory_space=pltpu.SMEM)] + [vmem] * 12,
         out_specs=vmem,
         scratch_shapes=[
             pltpu.VMEM((32 * CROWS, LANES), f32),
+            pltpu.VMEM((8 * MROWS, LANES), f32),
             pltpu.VMEM((CROWS * LANES, LANES), f32),
             pltpu.VMEM((CROWS * LANES, LANES), f32),
             pltpu.VMEM((256, LANES), f32),
@@ -189,10 +195,10 @@
         compiler_params=pltpu.CompilerParams(vmem_limit_bytes=40 * 2**20),
         cost_estimate=pl.CostEstimate(flops=400_000_000, bytes_accessed=2_000_000, transcendentals=0),
         name="refine",
-    )(pos, *tiles, hp, ms)
-
-
-def pack_kernel(pos_ref, ca_ref, cb_ref, ma_ref, mb_ref, hs_ref, near_ref, *rest_refs):
+    )(pos, *tiles, ms, hp, above, below)
+
+
+def pack_kernel(pos_ref, ca_ref, cb_ref, ma_ref, mb_ref, ms_ref, *rest_refs):
     tile_refs = rest_refs[:8]
     wide_ref = rest_refs[8]
     s = pos_ref[0] // 16
@@ -207,12 +213,12 @@
     order = jnp.where(source == (4 * (target % 32) + target // 32 + off) % LANES, 1.0, 0.0).astype(bf16)
     ms = jnp.where(first, ma_ref[...].reshape(128, LANES).astype(f32), mb_ref[...].reshape(128, LANES).astype(f32))
     ms = jnp.where(keep, ms, 0.0).astype(bf16)
-    near_ref[0:128, :] = jnp.dot(ms, order, preferred_element_type=f32).astype(bf16)
-    hs = hs_ref[...].astype(f32)
-    for i in range(4):
-        row = jnp.concatenate([hs[:, i, :], jnp.zeros((2, 256), f32)], axis=0).astype(bf16)
-        near_ref[128 + 16 * i : 144 + 16 * i, :] = row[:, 0:128]
-        near_ref[192 + 16 * i : 208 + 16 * i, :] = row[:, 128:256]
+    ms = jnp.dot(ms, order, preferred_element_type=f32)
+    ms_ref[...] = ms
+    for k in range(8):
+        at = slice(4 * CROWS + 8 * k, 4 * CROWS + 8 * k + 8)
+        tile_refs[1][at] = ms[16 * k + 8 : 16 * k + 16]
+        tile_refs[7][at] = ms[16 * k : 16 * k + 8]
     edge = jnp.zeros((16, LANES), f32)
     for k in range(4):
         rest = jnp.where(keep, jnp.where(first, ca_ref[k], cb_ref[k]), 0.0)
@@ -229,20 +235,20 @@
         t = (s + d) % 8
         at = pl.ds(pl.multiple_of(16 * t, 16), CROWS)
         for k in range(4):
-            tile_refs[d][k] = wide_ref[k, at, :]
-
-
-def pack(pos, coeffs_in, ms_image, hs_image):
+            tile_refs[d][k * CROWS : k * CROWS + CROWS] = wide_ref[k, at, :]
+
+
+def pack(pos, coeffs_in, ms_image):
     def low(i, p):
         return (0, 0, jnp.maximum((p[0] % 16 + 1) // 2 - 1, 0))
 
     def high(i, p):
         return (0, 0, jnp.minimum((p[0] % 16 + 1) // 2, 7))
 
-    tile = jax.ShapeDtypeStruct((4, CROWS, LANES), f32)
+    rows = [128] + [4 * CROWS + (64 if d in (1, 7) else 0) for d in range(8)]
     return pl.pallas_call(
         pack_kernel,
-        out_shape=(jax.ShapeDtypeStruct((256, LANES), bf16),) + (tile,) * 8,
+        out_shape=tuple(jax.ShapeDtypeStruct((count, LANES), f32) for count in rows),
         grid_spec=pltpu.PrefetchScalarGridSpec(
             num_scalar_prefetch=1,
             grid=(1,),
@@ -251,60 +257,47 @@
                 pl.BlockSpec((4, 128, LANES), high),
                 pl.BlockSpec((8, 16, LANES), low),
                 pl.BlockSpec((8, 16, LANES), high),
-                pl.BlockSpec((14, 4, 256), lambda i, p: (0, 0, 0)),
             ],
-            out_specs=(pl.BlockSpec((256, LANES), lambda i, p: (0, 0)),)
-            + (pl.BlockSpec((4, CROWS, LANES), lambda i, p: (0, 0, 0)),) * 8,
+            out_specs=tuple(pl.BlockSpec((count, LANES), lambda i, p: (0, 0)) for count in rows),
             scratch_shapes=[pltpu.VMEM((4, 160, LANES), f32)],
         ),
         compiler_params=pltpu.CompilerParams(vmem_limit_bytes=60 * 2**20),
         cost_estimate=pl.CostEstimate(flops=100_000_000, bytes_accessed=1_600_000, transcendentals=0),
         name="pack",
-    )(pos, coeffs_in, coeffs_in, ms_image, ms_image, hs_image)
-
-
-def spread_kernel(above_ref, own_ref, below_ref, k_ref, basis_ref, response_ref, sent_ref, ms_ref):
-    for m in range(8):
-        at = slice(16 * m, 16 * m + 16)
-        ms_ref[32 * m : 32 * m + 8, :] = above_ref[at, :].astype(f32)[8:16]
-        ms_ref[32 * m + 8 : 32 * m + 24, :] = own_ref[at, :].astype(f32)
-        ms_ref[32 * m + 24 : 32 * m + 32, :] = below_ref[at, :].astype(f32)[0:8]
-    lane = lax.broadcasted_iota(jnp.int32, (1, 256), 1)
-    rows = []
-    for i in range(IROWS):
-        ref, r = (above_ref, i + 1) if i < 3 else (own_ref, i - 3) if i < 7 else (below_ref, i - 7)
-        row = [ref[128 + 64 * h + 16 * r : 144 + 64 * h + 16 * r, :].astype(f32) for h in range(2)]
-        rows.append(jnp.concatenate(row, axis=1))
-    sent_ref[:, :, 256:384] = jnp.zeros((16, 16, 128), f32)
+    )(pos, coeffs_in, coeffs_in, ms_image, ms_image)
+
+
+def spread_kernel(hs_ref, k_ref, basis_ref, response_ref, sent_ref):
+    lane = lax.broadcasted_iota(jnp.int32, (1, LANES), 1)
+    hs = hs_ref[...].astype(f32)
+    rows = [jnp.concatenate([hs[:, i, :], jnp.zeros((2, 256), f32)], axis=0) for i in range(4)]
+    sent_ref[0, :, 128:256] = jnp.zeros((16, 128), f32)
     for a in range(9):
-        sent_ref[0, 0:14, 256 + 9 * a : 265 + 9 * a] = k_ref[:, a, :]
-    sent_ref[0, 0:14, 337:369] = basis_ref[...].astype(f32)
-    sent_ref[0, 0:14, 369:377] = response_ref[...].astype(f32).T
-    params = sent_ref[0, :, 256:384]
+        sent_ref[0, 0:14, 128 + 9 * a : 137 + 9 * a] = k_ref[:, a, :]
+    sent_ref[0, 0:14, 209:241] = basis_ref[...].astype(f32)
+    sent_ref[0, 0:14, 241:249] = response_ref[...].astype(f32).T
+    params = sent_ref[0, :, 128:256]
     for t in range(16):
-        total = jnp.zeros((16, 256), f32)
-        for i in range(IROWS):
-            moved = pltpu.roll(rows[i], (24 * i + 3 - 16 * t) % 256, 1)
+        total = jnp.zeros((16, LANES), f32)
+        for i in range(4):
+            moved = pltpu.roll(rows[i], (24 * i + 3 - 16 * t) % 256, 1)[:, 0:128]
             total = jnp.where((lane >= 24 * i) & (lane < 24 * i + 24), moved, total)
-        sent_ref[t, :, 0:256] = total
+        sent_ref[t, :, 0:128] = total
         if t:
-            sent_ref[t, :, 256:384] = params
-
-
-def spread(above, own, below, kernels, basis, response):
+            sent_ref[t, :, 128:256] = params
+
+
+def spread(hs_image, kernels, basis, response):
     vmem = pl.BlockSpec(memory_space=pltpu.VMEM)
     return pl.pallas_call(
         spread_kernel,
-        out_shape=(
-            jax.ShapeDtypeStruct((16, 16, 384), f32),
-            jax.ShapeDtypeStruct((8 * MROWS, LANES), f32),
-        ),
-        in_specs=[vmem] * 6,
-        out_specs=(vmem, vmem),
+        out_shape=jax.ShapeDtypeStruct((16, 16, 256), f32),
+        in_specs=[vmem] * 4,
+        out_specs=vmem,
         compiler_params=pltpu.CompilerParams(vmem_limit_bytes=16 * 2**20),
         cost_estimate=pl.CostEstimate(flops=1_000_000, bytes_accessed=1_000_000, transcendentals=0),
         name="spread",
-    )(above, own, below, kernels, basis, response)
+    )(hs_image, kernels, basis, response)
 
 
 def encode_kernel(d_ref, out_ref):
@@ -373,15 +366,16 @@
 
 def per_device(coeffs_in, basis, kernels, response, hs_image, ms_image):
     pos = (lax.axis_index("sub") * 16 + lax.axis_index("band")).astype(jnp.int32).reshape(1)
-    own, *tiles = pack(pos, coeffs_in, ms_image, hs_image)
-    above = lax.ppermute(own, "sub", [(i, i + 1) for i in range(7)])
-    below = lax.ppermute(own, "sub", [(i + 1, i) for i in range(7)])
-    sent, ms = spread(above, own, below, kernels, basis, response)
-    hp = lax.all_to_all(sent, "band", split_axis=0, concat_axis=0, tiled=True).reshape(256, 384)
+    sent = spread(hs_image, kernels, basis, response)
+    hp = lax.all_to_all(sent, "band", split_axis=0, concat_axis=0, tiled=True).reshape(256, 256)
+    ms, *tiles = pack(pos, coeffs_in, ms_image)
     tiles = [tiles[0]] + [
         lax.ppermute(tiles[d], "sub", [(i, (i + d) % 8) for i in range(8)]) for d in range(1, 8)
     ]
-    new = refine(pos, tiles, hp, ms)
+    seen = hp[:, 0:128].astype(bf16)
+    above = lax.ppermute(seen, "sub", [(i, i + 1) for i in range(7)])
+    below = lax.ppermute(seen, "sub", [(i + 1, i) for i in range(7)])
+    new = refine(pos, tiles, ms, hp, above, below)
     owned = lax.all_to_all(new.reshape(8, 4, 8, LANES), "sub", split_axis=0, concat_axis=0, tiled=True)
     gathered = lax.all_to_all(encode(owned), "band", split_axis=0, concat_axis=0, tiled=True)
     return place(gathered, coeffs_in)

time: 83.6 us -> 81.8 us (0.978)
  local copies, waits for them, and re-layouts: 1.77 us -> 4.77 us
  waiting for transfers between devices: 7.04 us -> 4.57 us
  blocking collectives: 32.7 us -> 30.4 us
    ppermute x7, waiting for transfers between devices: 5.46 us -> 0.95 us  [per_device(): lax.ppermute(tiles[d], 'sub', [(i, (i + d) % 8) for i in range(8)])]
    unnamed x13, local copies, waits for them, and re-layouts: 1.77 us -> 4.75 us
    all_to_all x1, blocking collectives: 9.27 us -> 6.99 us  [per_device(): lax.all_to_all(new.reshape(8, 4, 8, LANES), 'sub', split_axis=0, concat_a...]
    ppermute x2, waiting for transfers between devices: 1.58 us -> 3.62 us  [the longest x1 3.61 us: per_device(): below = lax.ppermute(seen, 'sub', [(i + 1, i) for i in range(7)])]
    ppermute x2, starting transfers between devices: 6.42 us -> 5.23 us  [the longest x1 3.31 us: per_device(): above = lax.ppermute(seen, 'sub', [(i, i + 1) for i in range(7)])]
  transfers between devices with their start and end apart: 10 -> 10, of which waited for: 5 -> 3; matrix products, arithmetic and copies ran while one was open for 0% -> 0% of each run, Pallas kernels for 0% -> 3%
where the time goes in v6:
time: 81.8 us; the launch traced here: 80.6 us
  blocking collectives  30.4 us (37%)
  starting transfers between devices  24.2 us (30%)
  Pallas kernels  16.4 us (20%)
  local copies, waits for them, and re-layouts  4.77 us (6%)
  waiting for transfers between devices  4.57 us (6%)
    all_to_all x1, blocking collectives, per_device(): lax.all_to_all(encode(owned), 'band', split_axis=0, concat_axis=0, tiled=...  23.5 us
    ppermute x7, starting transfers between devices, per_device(): lax.ppermute(tiles[d], 'sub', [(i, (i + d) % 8) for i in range(8)])  10.4 us
    pallas_call x1, Pallas kernels, refine(): pl.pallas_call(refine_kernel, out_shape=jax.ShapeDtypeStruct((32 * 8, LAN...  9.21 us
    all_to_all x1, starting transfers between devices, per_device(): lax.all_to_all(sent, 'band', split_axis=0, concat_axis=0, tiled=True)  8.6 us
    all_to_all x1, blocking collectives, per_device(): lax.all_to_all(new.reshape(8, 4, 8, LANES), 'sub', split_axis=0, concat_a...  6.99 us
    unnamed x13, local copies, waits for them, and re-layouts  4.75 us
    pallas_call x1, Pallas kernels, place(): pl.pallas_call(place_kernel, out_shape=jax.ShapeDtypeStruct((4, 128, 1024...  3.77 us
    ppermute x1, waiting for transfers between devices, per_device(): below = lax.ppermute(seen, 'sub', [(i + 1, i) for i in range(7)])  3.61 us
  transfers between devices with their start and end apart: 10, of which 3 were waited for; matrix products, arithmetic and copies ran while one was open for 0% of the time, Pallas kernels for 3%

profile of v6, /device:TPU:1, one launch (start us, length us, event | category | flops | bytes accessed | tf_op | source)
XLA Modules:
  0.0 80.6 jit_solution(9046295170075280528)
XLA Ops:
  0.0 0.9 %copy.7.k_ref = f32[14,9,9]{2,1,0:T(8,128)S(1)} copy(f32[14,9,9]{2,0,1:T(8,128)} %param.8) | data formatting | bytes 9072 | tf_op args[2]
  0.9 0.0 copy-start.1
  0.9 0.7 copy-done.1
  1.7 0.7 copy-done.2
  2.4 0.7 copy-done.3
  3.0 1.0 %spread.1 = f32[16,16,256]{2,1,0:T(8,128)} custom-call(bf16[14,4,256]{2,1,0:T(4,128)(2,1)S(1)} %copy-done.1, f32[14,9,9]{2,1,0:T(8,128)S(1)} %copy.7.k_ref, bf16[14,32]{1,0:T(8,128)(2,1)S(1)} %copy-done.2, bf16[8,14]{1,0:T(8,128)(2,1)S(1)} %copy-done.3), custom_call_target="tpu_custom_call" | custom-call | flops 1000000 | bytes 1000000 | tf_op jit(solution)/shard_map/spread/pallas_call | solution.py:292
  4.0 8.6 %all-to-all-start = ((f32[16,16,256]{2,1,0:T(8,128)}), f32[16,16,256]{2,1,0:T(8,128)S(1)}, u32[]{:S(2)}, u32[]{:S(2)}) async-start(f32[16,16,256]{2,1,0:T(8,128)} %spread.1), calls=%async_computation | async-start | bytes 524288 | tf_op jit(solution)/shard_map/all_to_all | solution.py:370
  12.6 2.3 %pack.1 = (f32[128,128]{1,0:T(8,128)}, f32[192,128]{1,0:T(8,128)}, f32[256,128]{1,0:T(8,128)}, f32[192,128]{1,0:T(8,128)}, f32[192,128]{1,0:T(8,128)}, /*index=5...) custom-call(s32[1]{0:T(128)} %bitcast.pos_ref, f32[4,128,1024]{2,1,0:T(8,128)} %c_ref.1, ...), custom_call_target="tpu_custom_call" | custom-call | flops 100000000 | bytes 1600000 | tf_op jit(solution)/shard_map/pack/pallas_call | solution.py:249
  14.9 1.2 %collective-permute-start.1 = (f32[192,128]{1,0:T(8,128)}, f32[192,128]{1,0:T(8,128)S(1)}, u32[]{:S(2)}, u32[]{:S(2)}) collective-permute-start(f32[192,128]{1,0:T(8,128)} %get-tuple-element.16), channel_id=1, source_target_pairs={{0,32},{16,48},{32,64},{48,80},{64,96},{80,112},{96,0},{112,16},{1... | collective-permute-start | bytes 294920 | tf_op jit(solution)/shard_map/ppermute | solution.py:373
  16.1 3.6 %collective-permute-start.2 = (f32[192,128]{1,0:T(8,128)}, f32[192,128]{1,0:T(8,128)S(1)}, u32[]{:S(2)}, u32[]{:S(2)}) collective-permute-start(f32[192,128]{1,0:T(8,128)} %get-tuple-element.17), channel_id=1, source_target_pairs={{0,48},{16,64},{32,80},{48,96},{64,112},{80,0},{96,16},{112,32},{1... | collective-permute-start | bytes 294920 | tf_op jit(solution)/shard_map/ppermute | solution.py:373
  19.7 0.5 collective-permute-start.3
  20.2 1.0 %collective-permute-start.4 = (f32[192,128]{1,0:T(8,128)}, f32[192,128]{1,0:T(8,128)S(1)}, u32[]{:S(2)}, u32[]{:S(2)}) collective-permute-start(f32[192,128]{1,0:T(8,128)} %get-tuple-element.19), channel_id=1, source_target_pairs={{0,80},{16,96},{32,112},{48,0},{64,16},{80,32},{96,48},{112,64},{1... | collective-permute-start | bytes 294920 | tf_op jit(solution)/shard_map/ppermute | solution.py:373
  21.2 1.3 %collective-permute-start = (f32[256,128]{1,0:T(8,128)}, f32[256,128]{1,0:T(8,128)S(1)}, u32[]{:S(2)}, u32[]{:S(2)}) collective-permute-start(f32[256,128]{1,0:T(8,128)} %get-tuple-element.15), channel_id=1, source_target_pairs={{0,16},{16,32},{32,48},{48,64},{64,80},{80,96},{96,112},{112,0},{1... | collective-permute-start | bytes 393224 | tf_op jit(solution)/shard_map/ppermute | solution.py:373
  22.5 0.0 collective-permute-done.1.refs_2_
  22.5 0.5 collective-permute-start.6
  23.1 0.4 collective-permute-done.2.refs_3_
  23.4 2.3 %collective-permute-start.5 = (f32[192,128]{1,0:T(8,128)}, f32[192,128]{1,0:T(8,128)S(1)}, u32[]{:S(2)}, u32[]{:S(2)}) collective-permute-start(f32[192,128]{1,0:T(8,128)} %get-tuple-element.20), channel_id=1, source_target_pairs={{0,96},{16,112},{32,0},{48,16},{64,32},{80,48},{96,64},{112,80},{1... | collective-permute-start | bytes 294920 | tf_op jit(solution)/shard_map/ppermute | solution.py:373
  25.7 0.0 all-to-all-done
  25.7 0.6 collective-permute-done.3.refs_4_
  26.3 3.3 %collective-permute-start.7 = (bf16[256,128]{1,0:T(8,128)(2,1)S(1)}, bf16[256,128]{1,0:T(8,128)(2,1)S(1)}, u32[]{:S(2)}, u32[]{:S(2)}) collective-permute-start(bf16[256,128]{1,0:T(8,128)(2,1)S(1)} %slice.7), channel_id=1, source_target_pairs={{0,16},{16,32},{32,48},{48,64},{64,80},{80,96},{96,112},{1,17},{17... | collective-permute-start | bytes 196616 | tf_op jit(solution)/shard_map/ppermute | solution.py:376
  29.6 0.0 collective-permute-done.4.refs_5_
  29.6 1.9 %collective-permute-start.8 = (bf16[256,128]{1,0:T(8,128)(2,1)S(1)}, bf16[256,128]{1,0:T(8,128)(2,1)S(1)}, u32[]{:S(2)}, u32[]{:S(2)}) collective-permute-start(bf16[256,128]{1,0:T(8,128)(2,1)S(1)} %slice.7), channel_id=1, source_target_pairs={{16,0},{32,16},{48,32},{64,48},{80,64},{96,80},{112,96},{17,1},{33... | collective-permute-start | bytes 196616 | tf_op jit(solution)/shard_map/ppermute | solution.py:377
  31.5 0.0 collective-permute-done.5.refs_6_
  31.6 0.0 collective-permute-done.7.refs_10_
  31.6 3.6 %collective-permute-done.8.refs_11_ = bf16[256,128]{1,0:T(8,128)(2,1)S(1)} collective-permute-done((bf16[256,128]{1,0:T(8,128)(2,1)S(1)}, bf16[256,128]{1,0:T(8,128)(2,1)S(1)}, u32[]{:S(2)}, u32[]{:S(2)}) %collective-permute-start.8) | collective-permute-done | bytes 65568 | tf_op jit(solution)/shard_map/ppermute | solution.py:377
  35.2 0.9 %copy-done.4 = f32[192,128]{1,0:T(8,128)S(1)} copy-done((f32[192,128]{1,0:T(8,128)S(1)}, f32[192,128]{1,0:T(8,128)}, u32[]{:S(2)}) %copy-start.4) | copy-done | bytes 98328
  36.1 0.8 %copy-done.5 = f32[128,128]{1,0:T(8,128)S(1)} copy-done((f32[128,128]{1,0:T(8,128)S(1)}, f32[128,128]{1,0:T(8,128)}, u32[]{:S(2)}) %copy-start.5) | copy-done | bytes 65560
  36.9 9.2 %refine.1 = f32[256,128]{1,0:T(8,128)S(1)} custom-call(s32[1]{0:T(128)} %bitcast.pos_ref, f32[192,128]{1,0:T(8,128)S(1)} %copy-done.4, f32[256,128]{1,0:T(8,128)S(1)} %collective-permute-done.refs_1_, f32[192,128]{1,0:T(8,128)S(1)} %collective-permute-done.1.refs_2_, f32[192,128]{1,0:T(8,128)S(1)} %collective-permute-done.2.refs_3_, ...), custom_call_target="tpu_custom_call" | custom-call | flops 400000000 | bytes 2000000 | tf_op jit(solution)/shard_map/refine/pallas_call | solution.py:174
  46.1 7.0 %all_to_all.15.d_ref = f32[8,4,8,128]{3,2,1,0:T(8,128)S(1)} all-to-all(f32[8,4,8,128]{3,2,1,0:T(8,128)S(1)} %bitcast.5), channel_id=1, replica_groups=mesh['sub'=8,'band'=16] {'sub'}, dimensions={0} | all-to-all | bytes 262144 | tf_op jit(solution)/shard_map/all_to_all | solution.py:379
  53.1 0.2 encode.1
  53.3 23.5 %all_to_all.16.g_ref = bf16[16,272,128]{2,1,0:T(8,128)(2,1)S(1)} all-to-all(bf16[16,272,128]{2,1,0:T(8,128)(2,1)S(1)} %encode.1), channel_id=1, replica_groups=mesh['sub'=8,'band'=16] {'band'}, dimensions={0} | all-to-all | bytes 2228224 | tf_op jit(solution)/shard_map/all_to_all | solution.py:380
  76.8 3.8 %place.1 = f32[4,128,1024]{2,1,0:T(8,128)} custom-call(bf16[16,272,128]{2,1,0:T(8,128)(2,1)S(1)} %all_to_all.16.g_ref, f32[4,128,1024]{2,1,0:T(8,128)S(1)} %copy-done), custom_call_target="tpu_custom_call" | custom-call | tf_op jit(solution)/shard_map/place/pallas_call | solution.py:356
  (9 shorter events, 0.0 us)
Async XLA Ops:
  0.9 0.8 copy-start.1
  1.7 0.7 copy-start.2
  2.4 0.7 copy-start.3
  4.0 21.7 %all-to-all-start = ((f32[16,16,256]{2,1,0:T(8,128)}), f32[16,16,256]{2,1,0:T(8,128)S(1)}, u32[]{:S(2)}, u32[]{:S(2)}) async-start(f32[16,16,256]{2,1,0:T(8,128)} %spread.1), calls=%async_computation | async-start | bytes 524288 | tf_op jit(solution)/shard_map/all_to_all | solution.py:370
  14.9 7.6 %collective-permute-start.1 = (f32[192,128]{1,0:T(8,128)}, f32[192,128]{1,0:T(8,128)S(1)}, u32[]{:S(2)}, u32[]{:S(2)}) collective-permute-start(f32[192,128]{1,0:T(8,128)} %get-tuple-element.16), channel_id=1, source_target_pairs={{0,32},{16,48},{32,64},{48,80},{64,96},{80,112},{96,0},{112,16},{1... | collective-permute-start | bytes 294920 | tf_op jit(solution)/shard_map/ppermute | solution.py:373
  16.1 7.3 %collective-permute-start.2 = (f32[192,128]{1,0:T(8,128)}, f32[192,128]{1,0:T(8,128)S(1)}, u32[]{:S(2)}, u32[]{:S(2)}) collective-permute-start(f32[192,128]{1,0:T(8,128)} %get-tuple-element.17), channel_id=1, source_target_pairs={{0,48},{16,64},{32,80},{48,96},{64,112},{80,0},{96,16},{112,32},{1... | collective-permute-start | bytes 294920 | tf_op jit(solution)/shard_map/ppermute | solution.py:373
  19.7 6.6 %collective-permute-start.3 = (f32[192,128]{1,0:T(8,128)}, f32[192,128]{1,0:T(8,128)S(1)}, u32[]{:S(2)}, u32[]{:S(2)}) collective-permute-start(f32[192,128]{1,0:T(8,128)} %get-tuple-element.18), channel_id=1, source_target_pairs={{0,64},{16,80},{32,96},{48,112},{64,0},{80,16},{96,32},{112,48},{1... | collective-permute-start | bytes 294920 | tf_op jit(solution)/shard_map/ppermute | solution.py:373
  20.2 9.4 %collective-permute-start.4 = (f32[192,128]{1,0:T(8,128)}, f32[192,128]{1,0:T(8,128)S(1)}, u32[]{:S(2)}, u32[]{:S(2)}) collective-permute-start(f32[192,128]{1,0:T(8,128)} %get-tuple-element.19), channel_id=1, source_target_pairs={{0,80},{16,96},{32,112},{48,0},{64,16},{80,32},{96,48},{112,64},{1... | collective-permute-start | bytes 294920 | tf_op jit(solution)/shard_map/ppermute | solution.py:373
  21.2 10.4 %collective-permute-start = (f32[256,128]{1,0:T(8,128)}, f32[256,128]{1,0:T(8,128)S(1)}, u32[]{:S(2)}, u32[]{:S(2)}) collective-permute-start(f32[256,128]{1,0:T(8,128)} %get-tuple-element.15), channel_id=1, source_target_pairs={{0,16},{16,32},{32,48},{48,64},{64,80},{80,96},{96,112},{112,0},{1... | collective-permute-start | bytes 393224 | tf_op jit(solution)/shard_map/ppermute | solution.py:373
  22.5 9.0 %collective-permute-start.6 = (f32[256,128]{1,0:T(8,128)}, f32[256,128]{1,0:T(8,128)S(1)}, u32[]{:S(2)}, u32[]{:S(2)}) collective-permute-start(f32[256,128]{1,0:T(8,128)} %get-tuple-element.21), channel_id=1, source_target_pairs={{0,112},{16,0},{32,16},{48,32},{64,48},{80,64},{96,80},{112,96},{1... | collective-permute-start | bytes 393224 | tf_op jit(solution)/shard_map/ppermute | solution.py:373
  23.4 8.1 %collective-permute-start.5 = (f32[192,128]{1,0:T(8,128)}, f32[192,128]{1,0:T(8,128)S(1)}, u32[]{:S(2)}, u32[]{:S(2)}) collective-permute-start(f32[192,128]{1,0:T(8,128)} %get-tuple-element.20), channel_id=1, source_target_pairs={{0,96},{16,112},{32,0},{48,16},{64,32},{80,48},{96,64},{112,80},{1... | collective-permute-start | bytes 294920 | tf_op jit(solution)/shard_map/ppermute | solution.py:373
  26.3 5.3 %collective-permute-start.7 = (bf16[256,128]{1,0:T(8,128)(2,1)S(1)}, bf16[256,128]{1,0:T(8,128)(2,1)S(1)}, u32[]{:S(2)}, u32[]{:S(2)}) collective-permute-start(bf16[256,128]{1,0:T(8,128)(2,1)S(1)} %slice.7), channel_id=1, source_target_pairs={{0,16},{16,32},{32,48},{48,64},{64,80},{80,96},{96,112},{1,17},{17... | collective-permute-start | bytes 196616 | tf_op jit(solution)/shard_map/ppermute | solution.py:376
  29.6 5.6 %collective-permute-start.8 = (bf16[256,128]{1,0:T(8,128)(2,1)S(1)}, bf16[256,128]{1,0:T(8,128)(2,1)S(1)}, u32[]{:S(2)}, u32[]{:S(2)}) collective-permute-start(bf16[256,128]{1,0:T(8,128)(2,1)S(1)} %slice.7), channel_id=1, source_target_pairs={{16,0},{32,16},{48,32},{64,48},{80,64},{96,80},{112,96},{17,1},{33... | collective-permute-start | bytes 196616 | tf_op jit(solution)/shard_map/ppermute | solution.py:377
  35.2 0.9 %copy-start.4 = (f32[192,128]{1,0:T(8,128)S(1)}, f32[192,128]{1,0:T(8,128)}, u32[]{:S(2)}) copy-start(f32[192,128]{1,0:T(8,128)} %get-tuple-element.14.refs_0_) | copy-start | bytes 294916
  36.1 0.8 %copy-start.5 = (f32[128,128]{1,0:T(8,128)S(1)}, f32[128,128]{1,0:T(8,128)}, u32[]{:S(2)}) copy-start(f32[128,128]{1,0:T(8,128)} %get-tuple-element.22.refs_8_) | copy-start | bytes 196612
  46.1 30.7 %copy-start = (f32[4,128,1024]{2,1,0:T(8,128)S(1)}, f32[4,128,1024]{2,1,0:T(8,128)}, u32[]{:S(2)}) copy-start(f32[4,128,1024]{2,1,0:T(8,128)} %c_ref.1) | copy-start | bytes 6291460

commit v7 on v6

--- a/solution.py
+++ b/solution.py
@@ -27,7 +27,7 @@
 
 def refine_kernel(pos_ref, *refs):
     tiles = refs[:8]
-    ms_own_ref, hp_ref, above_ref, below_ref, out_ref, c_ref, ms_ref, m0, m1, f0, f1, b0, b1, c1_ref, g_ref, hs0, hs1, w0, w1 = refs[8:]
+    hp_ref, above_ref, below_ref, out_ref, c_ref, ms_ref, m0, m1, f0, f1, b0, b1, c1_ref, g_ref, hs0, hs1, w0, w1 = refs[8:]
     s = pos_ref[0] // 16
     b = pos_ref[0] % 16
     for d in range(8):
@@ -35,7 +35,7 @@
         c_ref[pl.ds(at, 4 * CROWS), :] = tiles[d][0 : 4 * CROWS]
     for k in range(8):
         ms_ref[32 * k : 32 * k + 8, :] = tiles[1][4 * CROWS + 8 * k : 4 * CROWS + 8 * k + 8]
-        ms_ref[32 * k + 8 : 32 * k + 24, :] = ms_own_ref[16 * k : 16 * k + 16, :]
+        ms_ref[32 * k + 8 : 32 * k + 24, :] = tiles[0][4 * CROWS + 16 * k : 4 * CROWS + 16 * k + 16]
         ms_ref[32 * k + 24 : 32 * k + 32, :] = tiles[7][4 * CROWS + 8 * k : 4 * CROWS + 8 * k + 8]
     bk = (b0, b1)
     m = (m0, m1)
@@ -169,12 +169,12 @@
         out_ref[pl.ds(r, 32, stride=8), :] = total
 
 
-def refine(pos, tiles, ms, hp, above, below):
+def refine(pos, tiles, hp, above, below):
     vmem = pl.BlockSpec(memory_space=pltpu.VMEM)
     return pl.pallas_call(
         refine_kernel,
         out_shape=jax.ShapeDtypeStruct((32 * 8, LANES), f32),
-        in_specs=[pl.BlockSpec(memory_space=pltpu.SMEM)] + [vmem] * 12,
+        in_specs=[pl.BlockSpec(memory_space=pltpu.SMEM)] + [vmem] * 11,
         out_specs=vmem,
         scratch_shapes=[
             pltpu.VMEM((32 * CROWS, LANES), f32),
@@ -195,10 +195,10 @@
         compiler_params=pltpu.CompilerParams(vmem_limit_bytes=40 * 2**20),
         cost_estimate=pl.CostEstimate(flops=400_000_000, bytes_accessed=2_000_000, transcendentals=0),
         name="refine",
-    )(pos, *tiles, ms, hp, above, below)
-
-
-def pack_kernel(pos_ref, ca_ref, cb_ref, ma_ref, mb_ref, ms_ref, *rest_refs):
+    )(pos, *tiles, hp, above, below)
+
+
+def pack_kernel(pos_ref, ca_ref, cb_ref, ma_ref, mb_ref, *rest_refs):
     tile_refs = rest_refs[:8]
     wide_ref = rest_refs[8]
     s = pos_ref[0] // 16
@@ -214,7 +214,7 @@
     ms = jnp.where(first, ma_ref[...].reshape(128, LANES).astype(f32), mb_ref[...].reshape(128, LANES).astype(f32))
     ms = jnp.where(keep, ms, 0.0).astype(bf16)
     ms = jnp.dot(ms, order, preferred_element_type=f32)
-    ms_ref[...] = ms
+    tile_refs[0][4 * CROWS : 4 * CROWS + 128] = ms
     for k in range(8):
         at = slice(4 * CROWS + 8 * k, 4 * CROWS + 8 * k + 8)
         tile_refs[1][at] = ms[16 * k + 8 : 16 * k + 16]
@@ -245,7 +245,7 @@
     def high(i, p):
         return (0, 0, jnp.minimum((p[0] % 16 + 1) // 2, 7))
 
-    rows = [128] + [4 * CROWS + (64 if d in (1, 7) else 0) for d in range(8)]
+    rows = [4 * CROWS + {0: 128, 1: 64, 7: 64}.get(d, 0) for d in range(8)]
     return pl.pallas_call(
         pack_kernel,
         out_shape=tuple(jax.ShapeDtypeStruct((count, LANES), f32) for count in rows),
@@ -273,7 +273,7 @@
     rows = [jnp.concatenate([hs[:, i, :], jnp.zeros((2, 256), f32)], axis=0) for i in range(4)]
     sent_ref[0, :, 128:256] = jnp.zeros((16, 128), f32)
     for a in range(9):
-        sent_ref[0, 0:14, 128 + 9 * a : 137 + 9 * a] = k_ref[:, a, :]
+        sent_ref[0, 0:14, 128 + 9 * a : 137 + 9 * a] = k_ref[a]
     sent_ref[0, 0:14, 209:241] = basis_ref[...].astype(f32)
     sent_ref[0, 0:14, 241:249] = response_ref[...].astype(f32).T
     params = sent_ref[0, :, 128:256]
@@ -294,7 +294,7 @@
         out_shape=jax.ShapeDtypeStruct((16, 16, 256), f32),
         in_specs=[vmem] * 4,
         out_specs=vmem,
-        compiler_params=pltpu.CompilerParams(vmem_limit_bytes=16 * 2**20),
+        compiler_params=pltpu.CompilerParams(vmem_limit_bytes=60 * 2**20),
         cost_estimate=pl.CostEstimate(flops=1_000_000, bytes_accessed=1_000_000, transcendentals=0),
         name="spread",
     )(hs_image, kernels, basis, response)
@@ -366,16 +366,16 @@
 
 def per_device(coeffs_in, basis, kernels, response, hs_image, ms_image):
     pos = (lax.axis_index("sub") * 16 + lax.axis_index("band")).astype(jnp.int32).reshape(1)
-    sent = spread(hs_image, kernels, basis, response)
+    sent = spread(hs_image, kernels.transpose(1, 0, 2), basis, response)
     hp = lax.all_to_all(sent, "band", split_axis=0, concat_axis=0, tiled=True).reshape(256, 256)
-    ms, *tiles = pack(pos, coeffs_in, ms_image)
+    tiles = pack(pos, coeffs_in, ms_image)
     tiles = [tiles[0]] + [
         lax.ppermute(tiles[d], "sub", [(i, (i + d) % 8) for i in range(8)]) for d in range(1, 8)
     ]
     seen = hp[:, 0:128].astype(bf16)
     above = lax.ppermute(seen, "sub", [(i, i + 1) for i in range(7)])
     below = lax.ppermute(seen, "sub", [(i + 1, i) for i in range(7)])
-    new = refine(pos, tiles, ms, hp, above, below)
+    new = refine(pos, tiles, hp, above, below)
     owned = lax.all_to_all(new.reshape(8, 4, 8, LANES), "sub", split_axis=0, concat_axis=0, tiled=True)
     gathered = lax.all_to_all(encode(owned), "band", split_axis=0, concat_axis=0, tiled=True)
     return place(gathered, coeffs_in)

time: 81.8 us -> 78.7 us (0.962)
  local copies, waits for them, and re-layouts: 4.77 us -> 0.93 us
  Pallas kernels: 16.4 us -> 17.4 us
    unnamed x13 -> x4, local copies, waits for them, and re-layouts: 4.75 us -> 0.92 us
    pallas_call x1, Pallas kernels: 0.98 us -> 1.86 us  [spread(): pl.pallas_call(spread_kernel, out_shape=jax.ShapeDtypeStruct((16, 16, 256...]
where the time goes in v7:
time: 78.7 us; the launch traced here: 77.6 us
  blocking collectives  30.4 us (39%)
  starting transfers between devices  24.2 us (31%)
  Pallas kernels  17.4 us (22%)
  waiting for transfers between devices  4.58 us (6%)
  local copies, waits for them, and re-layouts  0.93 us (1%)
    all_to_all x1, blocking collectives, per_device(): lax.all_to_all(encode(owned), 'band', split_axis=0, concat_axis=0, tiled=...  23.5 us
    ppermute x7, starting transfers between devices, per_device(): lax.ppermute(tiles[d], 'sub', [(i, (i + d) % 8) for i in range(8)])  10.4 us
    pallas_call x1, Pallas kernels, refine(): pl.pallas_call(refine_kernel, out_shape=jax.ShapeDtypeStruct((32 * 8, LAN...  9.21 us
    all_to_all x1, starting transfers between devices, per_device(): lax.all_to_all(sent, 'band', split_axis=0, concat_axis=0, tiled=True)  8.6 us
    all_to_all x1, blocking collectives, per_device(): lax.all_to_all(new.reshape(8, 4, 8, LANES), 'sub', split_axis=0, concat_a...  6.99 us
    pallas_call x1, Pallas kernels, place(): pl.pallas_call(place_kernel, out_shape=jax.ShapeDtypeStruct((4, 128, 1024...  3.77 us
    ppermute x1, waiting for transfers between devices, per_device(): below = lax.ppermute(seen, 'sub', [(i + 1, i) for i in range(7)])  3.61 us
    ppermute x1, starting transfers between devices, per_device(): above = lax.ppermute(seen, 'sub', [(i, i + 1) for i in range(7)])  3.31 us
  transfers between devices with their start and end apart: 10, of which 3 were waited for; matrix products, arithmetic and copies ran while one was open for 0% of the time, Pallas kernels for 3%

profile of v7, /device:TPU:1, one launch (start us, length us, event | category | flops | bytes accessed | tf_op | source)
XLA Modules:
  0.0 77.6 jit_solution(9174551422630670967)
XLA Ops:
  0.0 1.9 %spread.1 = f32[16,16,256]{2,1,0:T(8,128)} custom-call(bf16[14,4,256]{2,1,0:T(4,128)(2,1)} %hs_ref.1, f32[9,14,9]{2,1,0:T(8,128)} %bitcast.7, bf16[14,32]{1,0:T(8,128)(2,1)} %basis_ref.1, bf16[8,14]{1,0:T(8,128)(2,1)} %response_ref.1), custom_call_target="tpu_custom_call" | custom-call | flops 1000000 | bytes 1000000 | tf_op jit(solution)/shard_map/spread/pallas_call | solution.py:292
  1.9 8.6 %all-to-all-start = ((f32[16,16,256]{2,1,0:T(8,128)}), f32[16,16,256]{2,1,0:T(8,128)S(1)}, u32[]{:S(2)}, u32[]{:S(2)}) async-start(f32[16,16,256]{2,1,0:T(8,128)} %spread.1), calls=%async_computation | async-start | bytes 524288 | tf_op jit(solution)/shard_map/all_to_all | solution.py:370
  10.5 2.3 %pack.1 = (f32[320,128]{1,0:T(8,128)}, f32[256,128]{1,0:T(8,128)}, f32[192,128]{1,0:T(8,128)}, f32[192,128]{1,0:T(8,128)}, f32[192,128]{1,0:T(8,128)}, /*index=5...) custom-call(s32[1]{0:T(128)} %bitcast.pos_ref, f32[4,128,1024]{2,1,0:T(8,128)} %c_ref.1, f32[4,128,1024]{2,1,0:T(8,128)} %c_ref.1, ...), custom_call_target="tpu_custom_call" | custom-call | flops 100000000 | bytes 1600000 | tf_op jit(solution)/shard_map/pack/pallas_call | solution.py:249
  12.8 1.2 %collective-permute-start.1 = (f32[192,128]{1,0:T(8,128)}, f32[192,128]{1,0:T(8,128)S(1)}, u32[]{:S(2)}, u32[]{:S(2)}) collective-permute-start(f32[192,128]{1,0:T(8,128)} %get-tuple-element.15), channel_id=1, source_target_pairs={{0,32},{16,48},{32,64},{48,80},{64,96},{80,112},{96,0},{112,16},{1... | collective-permute-start | bytes 294920 | tf_op jit(solution)/shard_map/ppermute | solution.py:373
  14.0 3.6 %collective-permute-start.2 = (f32[192,128]{1,0:T(8,128)}, f32[192,128]{1,0:T(8,128)S(1)}, u32[]{:S(2)}, u32[]{:S(2)}) collective-permute-start(f32[192,128]{1,0:T(8,128)} %get-tuple-element.16), channel_id=1, source_target_pairs={{0,48},{16,64},{32,80},{48,96},{64,112},{80,0},{96,16},{112,32},{1... | collective-permute-start | bytes 294920 | tf_op jit(solution)/shard_map/ppermute | solution.py:373
  17.6 0.5 collective-permute-start.3
  18.1 1.0 %collective-permute-start.4 = (f32[192,128]{1,0:T(8,128)}, f32[192,128]{1,0:T(8,128)S(1)}, u32[]{:S(2)}, u32[]{:S(2)}) collective-permute-start(f32[192,128]{1,0:T(8,128)} %get-tuple-element.18), channel_id=1, source_target_pairs={{0,80},{16,96},{32,112},{48,0},{64,16},{80,32},{96,48},{112,64},{1... | collective-permute-start | bytes 294920 | tf_op jit(solution)/shard_map/ppermute | solution.py:373
  19.1 1.3 %collective-permute-start = (f32[256,128]{1,0:T(8,128)}, f32[256,128]{1,0:T(8,128)S(1)}, u32[]{:S(2)}, u32[]{:S(2)}) collective-permute-start(f32[256,128]{1,0:T(8,128)} %get-tuple-element.14), channel_id=1, source_target_pairs={{0,16},{16,32},{32,48},{48,64},{64,80},{80,96},{96,112},{112,0},{1... | collective-permute-start | bytes 393224 | tf_op jit(solution)/shard_map/ppermute | solution.py:373
  20.4 0.0 collective-permute-done.1.refs_2_
  20.4 0.5 collective-permute-start.6
  21.0 0.4 collective-permute-done.2.refs_3_
  21.3 2.3 %collective-permute-start.5 = (f32[192,128]{1,0:T(8,128)}, f32[192,128]{1,0:T(8,128)S(1)}, u32[]{:S(2)}, u32[]{:S(2)}) collective-permute-start(f32[192,128]{1,0:T(8,128)} %get-tuple-element.19), channel_id=1, source_target_pairs={{0,96},{16,112},{32,0},{48,16},{64,32},{80,48},{96,64},{112,80},{1... | collective-permute-start | bytes 294920 | tf_op jit(solution)/shard_map/ppermute | solution.py:373
  23.6 0.0 all-to-all-done
  23.6 0.6 collective-permute-done.3.refs_4_
  24.2 3.3 %collective-permute-start.7 = (bf16[256,128]{1,0:T(8,128)(2,1)S(1)}, bf16[256,128]{1,0:T(8,128)(2,1)S(1)}, u32[]{:S(2)}, u32[]{:S(2)}) collective-permute-start(bf16[256,128]{1,0:T(8,128)(2,1)S(1)} %slice.7), channel_id=1, source_target_pairs={{0,16},{16,32},{32,48},{48,64},{64,80},{80,96},{96,112},{1,17},{17... | collective-permute-start | bytes 196616 | tf_op jit(solution)/shard_map/ppermute | solution.py:376
  27.5 0.0 collective-permute-done.4.refs_5_
  27.5 1.9 %collective-permute-start.8 = (bf16[256,128]{1,0:T(8,128)(2,1)S(1)}, bf16[256,128]{1,0:T(8,128)(2,1)S(1)}, u32[]{:S(2)}, u32[]{:S(2)}) collective-permute-start(bf16[256,128]{1,0:T(8,128)(2,1)S(1)} %slice.7), channel_id=1, source_target_pairs={{16,0},{32,16},{48,32},{64,48},{80,64},{96,80},{112,96},{17,1},{33... | collective-permute-start | bytes 196616 | tf_op jit(solution)/shard_map/ppermute | solution.py:377
  29.4 0.0 collective-permute-done.5.refs_6_
  29.4 0.0 collective-permute-done.refs_1_
  29.4 0.0 collective-permute-done.6.refs_7_
  29.5 0.0 collective-permute-done.7.refs_9_
  29.5 3.6 %collective-permute-done.8.refs_10_ = bf16[256,128]{1,0:T(8,128)(2,1)S(1)} collective-permute-done((bf16[256,128]{1,0:T(8,128)(2,1)S(1)}, bf16[256,128]{1,0:T(8,128)(2,1)S(1)}, u32[]{:S(2)}, u32[]{:S(2)}) %collective-permute-start.8) | collective-permute-done | bytes 65568 | tf_op jit(solution)/shard_map/ppermute | solution.py:377
  33.1 0.0 copy-start.1
  33.1 0.9 %copy-done.1 = f32[320,128]{1,0:T(8,128)S(1)} copy-done((f32[320,128]{1,0:T(8,128)S(1)}, f32[320,128]{1,0:T(8,128)}, u32[]{:S(2)}) %copy-start.1) | copy-done | bytes 163864
  34.0 9.2 %refine.1 = f32[256,128]{1,0:T(8,128)S(1)} custom-call(s32[1]{0:T(128)} %bitcast.pos_ref, f32[320,128]{1,0:T(8,128)S(1)} %copy-done.1, f32[256,128]{1,0:T(8,128)S(1)} %collective-permute-done.refs_1_, f32[192,128]{1,0:T(8,128)S(1)} %collective-permute-done.1.refs_2_, f32[192,128]{1,0:T(8,128)S(1)} %collective-permute-done.2.refs_3_, ...), custom_call_target="tpu_custom_call" | custom-call | flops 400000000 | bytes 2000000 | tf_op jit(solution)/shard_map/refine/pallas_call | solution.py:174
  43.2 0.0 copy-start
  43.2 7.0 %all_to_all.15.d_ref = f32[8,4,8,128]{3,2,1,0:T(8,128)S(1)} all-to-all(f32[8,4,8,128]{3,2,1,0:T(8,128)S(1)} %bitcast.6), channel_id=1, replica_groups=mesh['sub'=8,'band'=16] {'sub'}, dimensions={0} | all-to-all | bytes 262144 | tf_op jit(solution)/shard_map/all_to_all | solution.py:379
  50.2 0.2 encode.1
  50.4 23.5 %all_to_all.16.g_ref = bf16[16,272,128]{2,1,0:T(8,128)(2,1)S(1)} all-to-all(bf16[16,272,128]{2,1,0:T(8,128)(2,1)S(1)} %encode.1), channel_id=1, replica_groups=mesh['sub'=8,'band'=16] {'band'}, dimensions={0} | all-to-all | bytes 2228224 | tf_op jit(solution)/shard_map/all_to_all | solution.py:380
  73.9 0.0 copy-done
  73.9 3.8 %place.1 = f32[4,128,1024]{2,1,0:T(8,128)} custom-call(bf16[16,272,128]{2,1,0:T(8,128)(2,1)S(1)} %all_to_all.16.g_ref, f32[4,128,1024]{2,1,0:T(8,128)S(1)} %copy-done), custom_call_target="tpu_custom_call" | custom-call | tf_op jit(solution)/shard_map/place/pallas_call | solution.py:356
  (1 shorter events, 0.0 us)
Async XLA Ops:
  1.9 21.7 %all-to-all-start = ((f32[16,16,256]{2,1,0:T(8,128)}), f32[16,16,256]{2,1,0:T(8,128)S(1)}, u32[]{:S(2)}, u32[]{:S(2)}) async-start(f32[16,16,256]{2,1,0:T(8,128)} %spread.1), calls=%async_computation | async-start | bytes 524288 | tf_op jit(solution)/shard_map/all_to_all | solution.py:370
  12.8 7.6 %collective-permute-start.1 = (f32[192,128]{1,0:T(8,128)}, f32[192,128]{1,0:T(8,128)S(1)}, u32[]{:S(2)}, u32[]{:S(2)}) collective-permute-start(f32[192,128]{1,0:T(8,128)} %get-tuple-element.15), channel_id=1, source_target_pairs={{0,32},{16,48},{32,64},{48,80},{64,96},{80,112},{96,0},{112,16},{1... | collective-permute-start | bytes 294920 | tf_op jit(solution)/shard_map/ppermute | solution.py:373
  14.0 7.3 %collective-permute-start.2 = (f32[192,128]{1,0:T(8,128)}, f32[192,128]{1,0:T(8,128)S(1)}, u32[]{:S(2)}, u32[]{:S(2)}) collective-permute-start(f32[192,128]{1,0:T(8,128)} %get-tuple-element.16), channel_id=1, source_target_pairs={{0,48},{16,64},{32,80},{48,96},{64,112},{80,0},{96,16},{112,32},{1... | collective-permute-start | bytes 294920 | tf_op jit(solution)/shard_map/ppermute | solution.py:373
  17.6 6.6 %collective-permute-start.3 = (f32[192,128]{1,0:T(8,128)}, f32[192,128]{1,0:T(8,128)S(1)}, u32[]{:S(2)}, u32[]{:S(2)}) collective-permute-start(f32[192,128]{1,0:T(8,128)} %get-tuple-element.17), channel_id=1, source_target_pairs={{0,64},{16,80},{32,96},{48,112},{64,0},{80,16},{96,32},{112,48},{1... | collective-permute-start | bytes 294920 | tf_op jit(solution)/shard_map/ppermute | solution.py:373
  18.1 9.4 %collective-permute-start.4 = (f32[192,128]{1,0:T(8,128)}, f32[192,128]{1,0:T(8,128)S(1)}, u32[]{:S(2)}, u32[]{:S(2)}) collective-permute-start(f32[192,128]{1,0:T(8,128)} %get-tuple-element.18), channel_id=1, source_target_pairs={{0,80},{16,96},{32,112},{48,0},{64,16},{80,32},{96,48},{112,64},{1... | collective-permute-start | bytes 294920 | tf_op jit(solution)/shard_map/ppermute | solution.py:373
  19.1 10.3 %collective-permute-start = (f32[256,128]{1,0:T(8,128)}, f32[256,128]{1,0:T(8,128)S(1)}, u32[]{:S(2)}, u32[]{:S(2)}) collective-permute-start(f32[256,128]{1,0:T(8,128)} %get-tuple-element.14), channel_id=1, source_target_pairs={{0,16},{16,32},{32,48},{48,64},{64,80},{80,96},{96,112},{112,0},{1... | collective-permute-start | bytes 393224 | tf_op jit(solution)/shard_map/ppermute | solution.py:373
  20.4 9.0 %collective-permute-start.6 = (f32[256,128]{1,0:T(8,128)}, f32[256,128]{1,0:T(8,128)S(1)}, u32[]{:S(2)}, u32[]{:S(2)}) collective-permute-start(f32[256,128]{1,0:T(8,128)} %get-tuple-element.20), channel_id=1, source_target_pairs={{0,112},{16,0},{32,16},{48,32},{64,48},{80,64},{96,80},{112,96},{1... | collective-permute-start | bytes 393224 | tf_op jit(solution)/shard_map/ppermute | solution.py:373
  21.3 8.1 %collective-permute-start.5 = (f32[192,128]{1,0:T(8,128)}, f32[192,128]{1,0:T(8,128)S(1)}, u32[]{:S(2)}, u32[]{:S(2)}) collective-permute-start(f32[192,128]{1,0:T(8,128)} %get-tuple-element.19), channel_id=1, source_target_pairs={{0,96},{16,112},{32,0},{48,16},{64,32},{80,48},{96,64},{112,80},{1... | collective-permute-start | bytes 294920 | tf_op jit(solution)/shard_map/ppermute | solution.py:373
  24.2 5.3 %collective-permute-start.7 = (bf16[256,128]{1,0:T(8,128)(2,1)S(1)}, bf16[256,128]{1,0:T(8,128)(2,1)S(1)}, u32[]{:S(2)}, u32[]{:S(2)}) collective-permute-start(bf16[256,128]{1,0:T(8,128)(2,1)S(1)} %slice.7), channel_id=1, source_target_pairs={{0,16},{16,32},{32,48},{48,64},{64,80},{80,96},{96,112},{1,17},{17... | collective-permute-start | bytes 196616 | tf_op jit(solution)/shard_map/ppermute | solution.py:376
  27.5 5.6 %collective-permute-start.8 = (bf16[256,128]{1,0:T(8,128)(2,1)S(1)}, bf16[256,128]{1,0:T(8,128)(2,1)S(1)}, u32[]{:S(2)}, u32[]{:S(2)}) collective-permute-start(bf16[256,128]{1,0:T(8,128)(2,1)S(1)} %slice.7), channel_id=1, source_target_pairs={{16,0},{32,16},{48,32},{64,48},{80,64},{96,80},{112,96},{17,1},{33... | collective-permute-start | bytes 196616 | tf_op jit(solution)/shard_map/ppermute | solution.py:377
  33.1 0.9 %copy-start.1 = (f32[320,128]{1,0:T(8,128)S(1)}, f32[320,128]{1,0:T(8,128)}, u32[]{:S(2)}) copy-start(f32[320,128]{1,0:T(8,128)} %get-tuple-element.13.refs_0_) | copy-start | bytes 491524
  43.2 30.7 %copy-start = (f32[4,128,1024]{2,1,0:T(8,128)S(1)}, f32[4,128,1024]{2,1,0:T(8,128)}, u32[]{:S(2)}) copy-start(f32[4,128,1024]{2,1,0:T(8,128)} %c_ref.1) | copy-start | bytes 6291460

commit v8 on v7

--- a/solution.py
+++ b/solution.py
@@ -150,7 +150,7 @@
     place_at = lax.broadcasted_iota(jnp.int32, (LANES, LANES), 1)
     take = lax.broadcasted_iota(jnp.int32, (LANES, LANES), 0)
     shift = 4 * (take % 32) + take // 32 - 16
-    order = [(place_at == shift + 64 * half) & (shift >= 0) & (shift < 64) for half in range(2)]
+    order = [(place_at == shift + 64 * ((half + b) % 2)) & (shift >= 0) & (shift < 64) for half in range(2)]
     order = [jnp.where(o, 1.0, 0.0).astype(bf16) for o in order]
     grads = [hs_gradient(16, 8), hs_gradient(24, 8)]
     for r in range(8):
@@ -335,29 +335,31 @@
 def place_kernel(g_ref, c_ref, out_ref):
     lane = lax.broadcasted_iota(jnp.int32, (1, LANES), 1)
     low = lane < 64
-    scales = [g_ref[e, 256:272].astype(f32) * (1 / SPAN) for e in range(2)]
-    for s in range(8):
-        pair = []
-        for e in range(2):
-            code = g_ref[e, 32 * s : 32 * s + 32].astype(f32)
-            size = jnp.log2(jnp.abs(code)) + SPAN / 2
-            pair.append(jnp.where(code < 0, -size, size))
-        for k in range(4):
-            even, odd = [pair[e][8 * k : 8 * k + 8] * scales[e][k : k + 1] for e in range(2)]
-            for half, value in enumerate(
-                [jnp.where(low, even, pltpu.roll(odd, 64, 1)), jnp.where(low, pltpu.roll(even, 64, 1), odd)]
-            ):
-                at = slice(16 * s + 8 * half, 16 * s + 8 * half + 8)
-                out_ref[k, at] = c_ref[k, at] + value
+    count = g_ref.shape[0] // 2
+    for j in range(count):
+        even, odd = [g_ref[2 * j + e, 256:272].astype(f32) * (1 / SPAN) for e in range(2)]
+        scales = (jnp.where(low, even, odd), jnp.where(low, odd, even))
+        columns = slice(j * LANES, j * LANES + LANES)
+        for s in range(8):
+            even, odd = [g_ref[2 * j + e, 32 * s : 32 * s + 32].astype(f32) for e in range(2)]
+            for half, code in enumerate((jnp.where(low, even, odd), jnp.where(low, odd, even))):
+                size = jnp.log2(jnp.abs(code)) + SPAN / 2
+                value = jnp.where(code < 0, -size, size)
+                for k in range(4):
+                    part = value[8 * k : 8 * k + 8] * scales[half][k : k + 1]
+                    if half:
+                        part = pltpu.roll(part, 64, 1)
+                    at = slice(16 * s + 8 * half, 16 * s + 8 * half + 8)
+                    out_ref[k, at, columns] = c_ref[k, at, columns] + part
 
 
 def place(gathered, coeffs_in):
-    block = pl.BlockSpec((4, 128, LANES), lambda j: (0, 0, j))
+    block = pl.BlockSpec((4, 128, 4 * LANES), lambda j: (0, 0, j))
     return pl.pallas_call(
         place_kernel,
         out_shape=jax.ShapeDtypeStruct((4, 128, 1024), f32),
-        grid=(8,),
-        in_specs=[pl.BlockSpec((2, 272, LANES), lambda j: (j, 0, 0)), block],
+        grid=(2,),
+        in_specs=[pl.BlockSpec((8, 272, LANES), lambda j: (j, 0, 0)), block],
         out_specs=block,
         compiler_params=pltpu.CompilerParams(vmem_limit_bytes=32 * 2**20),
         name="place",

time: 78.7 us -> 76.9 us (0.977)
  Pallas kernels: 17.4 us -> 15.6 us
    pallas_call x1, Pallas kernels: 3.77 us -> 1.98 us  [place(): pl.pallas_call(place_kernel, out_shape=jax.ShapeDtypeStruct((4, 128, 1024...]
where the time goes in v8:
time: 76.9 us; the launch traced here: 75.9 us
  blocking collectives  30.4 us (40%)
  starting transfers between devices  24.2 us (31%)
  Pallas kernels  15.6 us (20%)
  waiting for transfers between devices  4.58 us (6%)
  local copies, waits for them, and re-layouts  0.93 us (1%)
    all_to_all x1, blocking collectives, per_device(): lax.all_to_all(encode(owned), 'band', split_axis=0, concat_axis=0, tiled=...  23.5 us
    ppermute x7, starting transfers between devices, per_device(): lax.ppermute(tiles[d], 'sub', [(i, (i + d) % 8) for i in range(8)])  10.4 us
    pallas_call x1, Pallas kernels, refine(): pl.pallas_call(refine_kernel, out_shape=jax.ShapeDtypeStruct((32 * 8, LAN...  9.21 us
    all_to_all x1, starting transfers between devices, per_device(): lax.all_to_all(sent, 'band', split_axis=0, concat_axis=0, tiled=True)  8.6 us
    all_to_all x1, blocking collectives, per_device(): lax.all_to_all(new.reshape(8, 4, 8, LANES), 'sub', split_axis=0, concat_a...  6.99 us
    ppermute x1, waiting for transfers between devices, per_device(): below = lax.ppermute(seen, 'sub', [(i + 1, i) for i in range(7)])  3.61 us
    ppermute x1, starting transfers between devices, per_device(): above = lax.ppermute(seen, 'sub', [(i, i + 1) for i in range(7)])  3.31 us
    pallas_call x1, Pallas kernels, pack(): pl.pallas_call(pack_kernel, out_shape=tuple((jax.ShapeDtypeStruct((count,...  2.33 us
  transfers between devices with their start and end apart: 10, of which 3 were waited for; matrix products, arithmetic and copies ran while one was open for 0% of the time, Pallas kernels for 3%

profile of v8, /device:TPU:1, one launch (start us, length us, event | category | flops | bytes accessed | tf_op | source)
XLA Modules:
  0.0 75.9 jit_solution(1207608907997377384)
XLA Ops:
  0.0 1.9 %spread.1 = f32[16,16,256]{2,1,0:T(8,128)} custom-call(bf16[14,4,256]{2,1,0:T(4,128)(2,1)} %hs_ref.1, f32[9,14,9]{2,1,0:T(8,128)} %bitcast.7, bf16[14,32]{1,0:T(8,128)(2,1)} %basis_ref.1, bf16[8,14]{1,0:T(8,128)(2,1)} %response_ref.1), custom_call_target="tpu_custom_call" | custom-call | flops 1000000 | bytes 1000000 | tf_op jit(solution)/shard_map/spread/pallas_call | solution.py:292
  1.9 8.6 %all-to-all-start = ((f32[16,16,256]{2,1,0:T(8,128)}), f32[16,16,256]{2,1,0:T(8,128)S(1)}, u32[]{:S(2)}, u32[]{:S(2)}) async-start(f32[16,16,256]{2,1,0:T(8,128)} %spread.1), calls=%async_computation | async-start | bytes 524288 | tf_op jit(solution)/shard_map/all_to_all | solution.py:372
  10.5 2.3 %pack.1 = (f32[320,128]{1,0:T(8,128)}, f32[256,128]{1,0:T(8,128)}, f32[192,128]{1,0:T(8,128)}, f32[192,128]{1,0:T(8,128)}, f32[192,128]{1,0:T(8,128)}, /*index=5...) custom-call(s32[1]{0:T(128)} %bitcast.pos_ref, f32[4,128,1024]{2,1,0:T(8,128)} %c_ref.1, f32[4,128,1024]{2,1,0:T(8,128)} %c_ref.1, ...), custom_call_target="tpu_custom_call" | custom-call | flops 100000000 | bytes 1600000 | tf_op jit(solution)/shard_map/pack/pallas_call | solution.py:249
  12.8 1.2 %collective-permute-start.1 = (f32[192,128]{1,0:T(8,128)}, f32[192,128]{1,0:T(8,128)S(1)}, u32[]{:S(2)}, u32[]{:S(2)}) collective-permute-start(f32[192,128]{1,0:T(8,128)} %get-tuple-element.15), channel_id=1, source_target_pairs={{0,32},{16,48},{32,64},{48,80},{64,96},{80,112},{96,0},{112,16},{1... | collective-permute-start | bytes 294920 | tf_op jit(solution)/shard_map/ppermute | solution.py:375
  14.0 3.6 %collective-permute-start.2 = (f32[192,128]{1,0:T(8,128)}, f32[192,128]{1,0:T(8,128)S(1)}, u32[]{:S(2)}, u32[]{:S(2)}) collective-permute-start(f32[192,128]{1,0:T(8,128)} %get-tuple-element.16), channel_id=1, source_target_pairs={{0,48},{16,64},{32,80},{48,96},{64,112},{80,0},{96,16},{112,32},{1... | collective-permute-start | bytes 294920 | tf_op jit(solution)/shard_map/ppermute | solution.py:375
  17.6 0.5 collective-permute-start.3
  18.1 1.0 %collective-permute-start.4 = (f32[192,128]{1,0:T(8,128)}, f32[192,128]{1,0:T(8,128)S(1)}, u32[]{:S(2)}, u32[]{:S(2)}) collective-permute-start(f32[192,128]{1,0:T(8,128)} %get-tuple-element.18), channel_id=1, source_target_pairs={{0,80},{16,96},{32,112},{48,0},{64,16},{80,32},{96,48},{112,64},{1... | collective-permute-start | bytes 294920 | tf_op jit(solution)/shard_map/ppermute | solution.py:375
  19.1 1.3 %collective-permute-start = (f32[256,128]{1,0:T(8,128)}, f32[256,128]{1,0:T(8,128)S(1)}, u32[]{:S(2)}, u32[]{:S(2)}) collective-permute-start(f32[256,128]{1,0:T(8,128)} %get-tuple-element.14), channel_id=1, source_target_pairs={{0,16},{16,32},{32,48},{48,64},{64,80},{80,96},{96,112},{112,0},{1... | collective-permute-start | bytes 393224 | tf_op jit(solution)/shard_map/ppermute | solution.py:375
  20.4 0.0 collective-permute-done.1.refs_2_
  20.4 0.5 collective-permute-start.6
  21.0 0.4 collective-permute-done.2.refs_3_
  21.3 2.3 %collective-permute-start.5 = (f32[192,128]{1,0:T(8,128)}, f32[192,128]{1,0:T(8,128)S(1)}, u32[]{:S(2)}, u32[]{:S(2)}) collective-permute-start(f32[192,128]{1,0:T(8,128)} %get-tuple-element.19), channel_id=1, source_target_pairs={{0,96},{16,112},{32,0},{48,16},{64,32},{80,48},{96,64},{112,80},{1... | collective-permute-start | bytes 294920 | tf_op jit(solution)/shard_map/ppermute | solution.py:375
  23.6 0.0 all-to-all-done
  23.6 0.6 collective-permute-done.3.refs_4_
  24.2 3.3 %collective-permute-start.7 = (bf16[256,128]{1,0:T(8,128)(2,1)S(1)}, bf16[256,128]{1,0:T(8,128)(2,1)S(1)}, u32[]{:S(2)}, u32[]{:S(2)}) collective-permute-start(bf16[256,128]{1,0:T(8,128)(2,1)S(1)} %slice.7), channel_id=1, source_target_pairs={{0,16},{16,32},{32,48},{48,64},{64,80},{80,96},{96,112},{1,17},{17... | collective-permute-start | bytes 196616 | tf_op jit(solution)/shard_map/ppermute | solution.py:378
  27.5 0.0 collective-permute-done.4.refs_5_
  27.5 1.9 %collective-permute-start.8 = (bf16[256,128]{1,0:T(8,128)(2,1)S(1)}, bf16[256,128]{1,0:T(8,128)(2,1)S(1)}, u32[]{:S(2)}, u32[]{:S(2)}) collective-permute-start(bf16[256,128]{1,0:T(8,128)(2,1)S(1)} %slice.7), channel_id=1, source_target_pairs={{16,0},{32,16},{48,32},{64,48},{80,64},{96,80},{112,96},{17,1},{33... | collective-permute-start | bytes 196616 | tf_op jit(solution)/shard_map/ppermute | solution.py:379
  29.4 0.0 collective-permute-done.5.refs_6_
  29.4 0.0 collective-permute-done.refs_1_
  29.4 0.0 collective-permute-done.6.refs_7_
  29.5 0.0 collective-permute-done.7.refs_9_
  29.5 3.6 %collective-permute-done.8.refs_10_ = bf16[256,128]{1,0:T(8,128)(2,1)S(1)} collective-permute-done((bf16[256,128]{1,0:T(8,128)(2,1)S(1)}, bf16[256,128]{1,0:T(8,128)(2,1)S(1)}, u32[]{:S(2)}, u32[]{:S(2)}) %collective-permute-start.8) | collective-permute-done | bytes 65568 | tf_op jit(solution)/shard_map/ppermute | solution.py:379
  33.1 0.0 copy-start.1
  33.1 0.9 %copy-done.1 = f32[320,128]{1,0:T(8,128)S(1)} copy-done((f32[320,128]{1,0:T(8,128)S(1)}, f32[320,128]{1,0:T(8,128)}, u32[]{:S(2)}) %copy-start.1) | copy-done | bytes 163864
  34.0 9.2 %refine.1 = f32[256,128]{1,0:T(8,128)S(1)} custom-call(s32[1]{0:T(128)} %bitcast.pos_ref, f32[320,128]{1,0:T(8,128)S(1)} %copy-done.1, f32[256,128]{1,0:T(8,128)S(1)} %collective-permute-done.refs_1_, f32[192,128]{1,0:T(8,128)S(1)} %collective-permute-done.1.refs_2_, f32[192,128]{1,0:T(8,128)S(1)} %collective-permute-done.2.refs_3_, ...), custom_call_target="tpu_custom_call" | custom-call | flops 400000000 | bytes 2000000 | tf_op jit(solution)/shard_map/refine/pallas_call | solution.py:174
  43.2 0.0 copy-start
  43.2 7.0 %all_to_all.15.d_ref = f32[8,4,8,128]{3,2,1,0:T(8,128)S(1)} all-to-all(f32[8,4,8,128]{3,2,1,0:T(8,128)S(1)} %bitcast.6), channel_id=1, replica_groups=mesh['sub'=8,'band'=16] {'sub'}, dimensions={0} | all-to-all | bytes 262144 | tf_op jit(solution)/shard_map/all_to_all | solution.py:381
  50.2 0.2 encode.1
  50.4 23.5 %all_to_all.16.g_ref = bf16[16,272,128]{2,1,0:T(8,128)(2,1)S(1)} all-to-all(bf16[16,272,128]{2,1,0:T(8,128)(2,1)S(1)} %encode.1), channel_id=1, replica_groups=mesh['sub'=8,'band'=16] {'band'}, dimensions={0} | all-to-all | bytes 2228224 | tf_op jit(solution)/shard_map/all_to_all | solution.py:382
  73.9 0.0 copy-done
  73.9 2.0 %place.1 = f32[4,128,1024]{2,1,0:T(8,128)} custom-call(bf16[16,272,128]{2,1,0:T(8,128)(2,1)S(1)} %all_to_all.16.g_ref, f32[4,128,1024]{2,1,0:T(8,128)S(1)} %copy-done), custom_call_target="tpu_custom_call" | custom-call | tf_op jit(solution)/shard_map/place/pallas_call | solution.py:358
  (1 shorter events, 0.0 us)
Async XLA Ops:
  1.9 21.7 %all-to-all-start = ((f32[16,16,256]{2,1,0:T(8,128)}), f32[16,16,256]{2,1,0:T(8,128)S(1)}, u32[]{:S(2)}, u32[]{:S(2)}) async-start(f32[16,16,256]{2,1,0:T(8,128)} %spread.1), calls=%async_computation | async-start | bytes 524288 | tf_op jit(solution)/shard_map/all_to_all | solution.py:372
  12.8 7.6 %collective-permute-start.1 = (f32[192,128]{1,0:T(8,128)}, f32[192,128]{1,0:T(8,128)S(1)}, u32[]{:S(2)}, u32[]{:S(2)}) collective-permute-start(f32[192,128]{1,0:T(8,128)} %get-tuple-element.15), channel_id=1, source_target_pairs={{0,32},{16,48},{32,64},{48,80},{64,96},{80,112},{96,0},{112,16},{1... | collective-permute-start | bytes 294920 | tf_op jit(solution)/shard_map/ppermute | solution.py:375
  14.0 7.3 %collective-permute-start.2 = (f32[192,128]{1,0:T(8,128)}, f32[192,128]{1,0:T(8,128)S(1)}, u32[]{:S(2)}, u32[]{:S(2)}) collective-permute-start(f32[192,128]{1,0:T(8,128)} %get-tuple-element.16), channel_id=1, source_target_pairs={{0,48},{16,64},{32,80},{48,96},{64,112},{80,0},{96,16},{112,32},{1... | collective-permute-start | bytes 294920 | tf_op jit(solution)/shard_map/ppermute | solution.py:375
  17.6 6.6 %collective-permute-start.3 = (f32[192,128]{1,0:T(8,128)}, f32[192,128]{1,0:T(8,128)S(1)}, u32[]{:S(2)}, u32[]{:S(2)}) collective-permute-start(f32[192,128]{1,0:T(8,128)} %get-tuple-element.17), channel_id=1, source_target_pairs={{0,64},{16,80},{32,96},{48,112},{64,0},{80,16},{96,32},{112,48},{1... | collective-permute-start | bytes 294920 | tf_op jit(solution)/shard_map/ppermute | solution.py:375
  18.1 9.4 %collective-permute-start.4 = (f32[192,128]{1,0:T(8,128)}, f32[192,128]{1,0:T(8,128)S(1)}, u32[]{:S(2)}, u32[]{:S(2)}) collective-permute-start(f32[192,128]{1,0:T(8,128)} %get-tuple-element.18), channel_id=1, source_target_pairs={{0,80},{16,96},{32,112},{48,0},{64,16},{80,32},{96,48},{112,64},{1... | collective-permute-start | bytes 294920 | tf_op jit(solution)/shard_map/ppermute | solution.py:375
  19.1 10.3 %collective-permute-start = (f32[256,128]{1,0:T(8,128)}, f32[256,128]{1,0:T(8,128)S(1)}, u32[]{:S(2)}, u32[]{:S(2)}) collective-permute-start(f32[256,128]{1,0:T(8,128)} %get-tuple-element.14), channel_id=1, source_target_pairs={{0,16},{16,32},{32,48},{48,64},{64,80},{80,96},{96,112},{112,0},{1... | collective-permute-start | bytes 393224 | tf_op jit(solution)/shard_map/ppermute | solution.py:375
  20.4 9.0 %collective-permute-start.6 = (f32[256,128]{1,0:T(8,128)}, f32[256,128]{1,0:T(8,128)S(1)}, u32[]{:S(2)}, u32[]{:S(2)}) collective-permute-start(f32[256,128]{1,0:T(8,128)} %get-tuple-element.20), channel_id=1, source_target_pairs={{0,112},{16,0},{32,16},{48,32},{64,48},{80,64},{96,80},{112,96},{1... | collective-permute-start | bytes 393224 | tf_op jit(solution)/shard_map/ppermute | solution.py:375
  21.3 8.1 %collective-permute-start.5 = (f32[192,128]{1,0:T(8,128)}, f32[192,128]{1,0:T(8,128)S(1)}, u32[]{:S(2)}, u32[]{:S(2)}) collective-permute-start(f32[192,128]{1,0:T(8,128)} %get-tuple-element.19), channel_id=1, source_target_pairs={{0,96},{16,112},{32,0},{48,16},{64,32},{80,48},{96,64},{112,80},{1... | collective-permute-start | bytes 294920 | tf_op jit(solution)/shard_map/ppermute | solution.py:375
  24.2 5.3 %collective-permute-start.7 = (bf16[256,128]{1,0:T(8,128)(2,1)S(1)}, bf16[256,128]{1,0:T(8,128)(2,1)S(1)}, u32[]{:S(2)}, u32[]{:S(2)}) collective-permute-start(bf16[256,128]{1,0:T(8,128)(2,1)S(1)} %slice.7), channel_id=1, source_target_pairs={{0,16},{16,32},{32,48},{48,64},{64,80},{80,96},{96,112},{1,17},{17... | collective-permute-start | bytes 196616 | tf_op jit(solution)/shard_map/ppermute | solution.py:378
  27.5 5.6 %collective-permute-start.8 = (bf16[256,128]{1,0:T(8,128)(2,1)S(1)}, bf16[256,128]{1,0:T(8,128)(2,1)S(1)}, u32[]{:S(2)}, u32[]{:S(2)}) collective-permute-start(bf16[256,128]{1,0:T(8,128)(2,1)S(1)} %slice.7), channel_id=1, source_target_pairs={{16,0},{32,16},{48,32},{64,48},{80,64},{96,80},{112,96},{17,1},{33... | collective-permute-start | bytes 196616 | tf_op jit(solution)/shard_map/ppermute | solution.py:379
  33.1 0.9 %copy-start.1 = (f32[320,128]{1,0:T(8,128)S(1)}, f32[320,128]{1,0:T(8,128)}, u32[]{:S(2)}) copy-start(f32[320,128]{1,0:T(8,128)} %get-tuple-element.13.refs_0_) | copy-start | bytes 491524
  43.2 30.7 %copy-start = (f32[4,128,1024]{2,1,0:T(8,128)S(1)}, f32[4,128,1024]{2,1,0:T(8,128)}, u32[]{:S(2)}) copy-start(f32[4,128,1024]{2,1,0:T(8,128)} %c_ref.1) | copy-start | bytes 6291460

commit v9 on v8

--- a/solution.py
+++ b/solution.py
@@ -26,17 +26,21 @@
 
 
 def refine_kernel(pos_ref, *refs):
-    tiles = refs[:8]
-    hp_ref, above_ref, below_ref, out_ref, c_ref, ms_ref, m0, m1, f0, f1, b0, b1, c1_ref, g_ref, hs0, hs1, w0, w1 = refs[8:]
+    mine_ref, other_ref, hp_ref, seen_ref, above_ref, below_ref, out_ref, c_ref, ms_ref, m0, m1, f0, f1, b0, b1, c1_ref, g_ref, hs0, hs1, w0, w1 = refs
     s = pos_ref[0] // 16
     b = pos_ref[0] % 16
-    for d in range(8):
-        at = pl.multiple_of((s + 8 - d) % 8 * (4 * CROWS), 4 * CROWS)
-        c_ref[pl.ds(at, 4 * CROWS), :] = tiles[d][0 : 4 * CROWS]
+    core = s % 2
+    for d in range(4):
+        chip = (s // 2 + 4 - d) % 4
+        mine = pl.multiple_of((2 * chip + core) * (4 * CROWS), 4 * CROWS)
+        theirs = pl.multiple_of((2 * chip + 1 - core) * (4 * CROWS), 4 * CROWS)
+        c_ref[pl.ds(mine, 4 * CROWS), :] = mine_ref[d * 4 * CROWS : (d + 1) * 4 * CROWS]
+        c_ref[pl.ds(theirs, 4 * CROWS), :] = other_ref[d * 4 * CROWS : (d + 1) * 4 * CROWS]
     for k in range(8):
-        ms_ref[32 * k : 32 * k + 8, :] = tiles[1][4 * CROWS + 8 * k : 4 * CROWS + 8 * k + 8]
-        ms_ref[32 * k + 8 : 32 * k + 24, :] = tiles[0][4 * CROWS + 16 * k : 4 * CROWS + 16 * k + 16]
-        ms_ref[32 * k + 24 : 32 * k + 32, :] = tiles[7][4 * CROWS + 8 * k : 4 * CROWS + 8 * k + 8]
+        at = slice(256 + 16 * k, 272 + 16 * k)
+        ms_ref[32 * k : 32 * k + 8, :] = above_ref[at, :].astype(f32)[8:16]
+        ms_ref[32 * k + 8 : 32 * k + 24, :] = seen_ref[at, :].astype(f32)
+        ms_ref[32 * k + 24 : 32 * k + 32, :] = below_ref[at, :].astype(f32)[0:8]
     bk = (b0, b1)
     m = (m0, m1)
     f = (f0, f1)
@@ -169,12 +173,12 @@
         out_ref[pl.ds(r, 32, stride=8), :] = total
 
 
-def refine(pos, tiles, hp, above, below):
+def refine(pos, mine, other, hp, seen, above, below):
     vmem = pl.BlockSpec(memory_space=pltpu.VMEM)
     return pl.pallas_call(
         refine_kernel,
         out_shape=jax.ShapeDtypeStruct((32 * 8, LANES), f32),
-        in_specs=[pl.BlockSpec(memory_space=pltpu.SMEM)] + [vmem] * 11,
+        in_specs=[pl.BlockSpec(memory_space=pltpu.SMEM)] + [vmem] * 6,
         out_specs=vmem,
         scratch_shapes=[
             pltpu.VMEM((32 * CROWS, LANES), f32),
@@ -195,12 +199,11 @@
         compiler_params=pltpu.CompilerParams(vmem_limit_bytes=40 * 2**20),
         cost_estimate=pl.CostEstimate(flops=400_000_000, bytes_accessed=2_000_000, transcendentals=0),
         name="refine",
-    )(pos, *tiles, hp, above, below)
+    )(pos, mine, other, hp, seen, above, below)
 
 
 def pack_kernel(pos_ref, ca_ref, cb_ref, ma_ref, mb_ref, *rest_refs):
-    tile_refs = rest_refs[:8]
-    wide_ref = rest_refs[8]
+    near_ref, wide_ref = rest_refs[4:]
     s = pos_ref[0] // 16
     b = pos_ref[0] % 16
     off = jnp.where(b % 2 == 0, 112, 48)
@@ -214,11 +217,7 @@
     ms = jnp.where(first, ma_ref[...].reshape(128, LANES).astype(f32), mb_ref[...].reshape(128, LANES).astype(f32))
     ms = jnp.where(keep, ms, 0.0).astype(bf16)
     ms = jnp.dot(ms, order, preferred_element_type=f32)
-    tile_refs[0][4 * CROWS : 4 * CROWS + 128] = ms
-    for k in range(8):
-        at = slice(4 * CROWS + 8 * k, 4 * CROWS + 8 * k + 8)
-        tile_refs[1][at] = ms[16 * k + 8 : 16 * k + 16]
-        tile_refs[7][at] = ms[16 * k : 16 * k + 8]
+    near_ref[...] = ms.astype(bf16)
     edge = jnp.zeros((16, LANES), f32)
     for k in range(4):
         rest = jnp.where(keep, jnp.where(first, ca_ref[k], cb_ref[k]), 0.0)
@@ -231,11 +230,10 @@
         wide_ref[k, 0:16] = edge
         wide_ref[k, 16:144] = total
         wide_ref[k, 144:160] = edge
-    for d in range(8):
-        t = (s + d) % 8
-        at = pl.ds(pl.multiple_of(16 * t, 16), CROWS)
+    for d in range(4):
+        at = pl.ds(pl.multiple_of(32 * ((s // 2 + d) % 4), 32), 64)
         for k in range(4):
-            tile_refs[d][k * CROWS : k * CROWS + CROWS] = wide_ref[k, at, :]
+            rest_refs[d][64 * k : 64 * k + 64] = wide_ref[k, at, :]
 
 
 def pack(pos, coeffs_in, ms_image):
@@ -245,10 +243,9 @@
     def high(i, p):
         return (0, 0, jnp.minimum((p[0] % 16 + 1) // 2, 7))
 
-    rows = [4 * CROWS + {0: 128, 1: 64, 7: 64}.get(d, 0) for d in range(8)]
     return pl.pallas_call(
         pack_kernel,
-        out_shape=tuple(jax.ShapeDtypeStruct((count, LANES), f32) for count in rows),
+        out_shape=(jax.ShapeDtypeStruct((256, LANES), f32),) * 4 + (jax.ShapeDtypeStruct((128, LANES), bf16),),
         grid_spec=pltpu.PrefetchScalarGridSpec(
             num_scalar_prefetch=1,
             grid=(1,),
@@ -258,7 +255,8 @@
                 pl.BlockSpec((8, 16, LANES), low),
                 pl.BlockSpec((8, 16, LANES), high),
             ],
-            out_specs=tuple(pl.BlockSpec((count, LANES), lambda i, p: (0, 0)) for count in rows),
+            out_specs=(pl.BlockSpec((256, LANES), lambda i, p: (0, 0)),) * 4
+            + (pl.BlockSpec((128, LANES), lambda i, p: (0, 0)),),
             scratch_shapes=[pltpu.VMEM((4, 160, LANES), f32)],
         ),
         compiler_params=pltpu.CompilerParams(vmem_limit_bytes=60 * 2**20),
@@ -298,6 +296,28 @@
         cost_estimate=pl.CostEstimate(flops=1_000_000, bytes_accessed=1_000_000, transcendentals=0),
         name="spread",
     )(hs_image, kernels, basis, response)
+
+
+def hand_kernel(pos_ref, r0, r1, r2, r3, mine_ref, other_ref):
+    skip = 16 * (pos_ref[0] // 16 % 2)
+    for d, region in enumerate((r0, r1, r2, r3)):
+        for k in range(4):
+            at = CROWS * (4 * d + k)
+            mine_ref[at : at + CROWS] = region[pl.ds(pl.multiple_of(64 * k + skip, 16), CROWS), :]
+            other_ref[at : at + CROWS] = region[pl.ds(pl.multiple_of(64 * k + 16 - skip, 16), CROWS), :]
+
+
+def hand(pos, tiles):
+    vmem = pl.BlockSpec(memory_space=pltpu.VMEM)
+    return pl.pallas_call(
+        hand_kernel,
+        out_shape=(jax.ShapeDtypeStruct((16 * CROWS, LANES), f32),) * 2,
+        in_specs=[pl.BlockSpec(memory_space=pltpu.SMEM)] + [vmem] * 4,
+        out_specs=(vmem, vmem),
+        compiler_params=pltpu.CompilerParams(vmem_limit_bytes=16 * 2**20),
+        cost_estimate=pl.CostEstimate(flops=1_000_000, bytes_accessed=800_000, transcendentals=0),
+        name="hand",
+    )(pos, *tiles)
 
 
 def encode_kernel(d_ref, out_ref):
@@ -370,14 +390,16 @@
     pos = (lax.axis_index("sub") * 16 + lax.axis_index("band")).astype(jnp.int32).reshape(1)
     sent = spread(hs_image, kernels.transpose(1, 0, 2), basis, response)
     hp = lax.all_to_all(sent, "band", split_axis=0, concat_axis=0, tiled=True).reshape(256, 256)
-    tiles = pack(pos, coeffs_in, ms_image)
+    *tiles, near = pack(pos, coeffs_in, ms_image)
     tiles = [tiles[0]] + [
-        lax.ppermute(tiles[d], "sub", [(i, (i + d) % 8) for i in range(8)]) for d in range(1, 8)
+        lax.ppermute(tiles[d], "sub", [(i, (i + 2 * d) % 8) for i in range(8)]) for d in range(1, 4)
     ]
-    seen = hp[:, 0:128].astype(bf16)
+    mine, other = hand(pos, tiles)
+    other = lax.ppermute(other, "sub", [(i, i ^ 1) for i in range(8)])
+    seen = jnp.concatenate([hp[:, 0:128].astype(bf16), near], axis=0)
     above = lax.ppermute(seen, "sub", [(i, i + 1) for i in range(7)])
     below = lax.ppermute(seen, "sub", [(i + 1, i) for i in range(7)])
-    new = refine(pos, tiles, hp, above, below)
+    new = refine(pos, mine, other, hp, seen, above, below)
     owned = lax.all_to_all(new.reshape(8, 4, 8, LANES), "sub", split_axis=0, concat_axis=0, tiled=True)
     gathered = lax.all_to_all(encode(owned), "band", split_axis=0, concat_axis=0, tiled=True)
     return place(gathered, coeffs_in)

time: 76.9 us -> 76 us (0.988)
  starting transfers between devices: 24.2 us -> 22.1 us
  waiting for transfers between devices: 4.58 us -> 6.42 us
  blocking collectives: 30.4 us -> 29.1 us
  other arithmetic: 0 us -> 0.77 us
    all_to_all x1, waiting for transfers between devices: 0.01 us -> 4.79 us  [per_device(): lax.all_to_all(sent, 'band', split_axis=0, concat_axis=0, tiled=True)]
    all_to_all x1, blocking collectives: 23.5 us -> 19.4 us  [per_device(): lax.all_to_all(encode(owned), 'band', split_axis=0, concat_axis=0, tiled=...]
    ppermute x1, waiting for transfers between devices: 3.61 us -> 0.36 us  [per_device(): below = lax.ppermute(seen, 'sub', [(i + 1, i) for i in range(7)])]
    ppermute x7 -> x4, starting transfers between devices: 10.4 us -> 7.52 us  [the longest x3 5.64 us: per_device(): lax.ppermute(tiles[d], 'sub', [(i, (i + 2 * d) % 8) for i in range(8)])]
    ppermute x1, starting transfers between devices: 1.92 us -> 4.72 us  [per_device(): below = lax.ppermute(seen, 'sub', [(i + 1, i) for i in range(7)])]
    all_to_all x1, blocking collectives: 6.99 us -> 9.71 us  [per_device(): lax.all_to_all(new.reshape(8, 4, 8, LANES), 'sub', split_axis=0, concat_a...]
    ppermute x1, waiting for transfers between devices: 0.01 us -> 1.26 us  [per_device(): above = lax.ppermute(seen, 'sub', [(i, i + 1) for i in range(7)])]
    ppermute x1, starting transfers between devices: 3.31 us -> 2.12 us  [per_device(): above = lax.ppermute(seen, 'sub', [(i, i + 1) for i in range(7)])]
  transfers between devices with their start and end apart: 10 -> 7, of which waited for: 3 -> 3; matrix products, arithmetic and copies ran while one was open for 0% -> 1% of each run, Pallas kernels for 3% -> 3%
where the time goes in v9:
time: 76 us; the launch traced here: 74.8 us
  blocking collectives  29.1 us (38%)
  starting transfers between devices  22.1 us (29%)
  Pallas kernels  15.5 us (20%)
  waiting for transfers between devices  6.42 us (8%)
  local copies, waits for them, and re-layouts  0.91 us (1%)
  other arithmetic  0.77 us (1%)
    all_to_all x1, blocking collectives, per_device(): lax.all_to_all(encode(owned), 'band', split_axis=0, concat_axis=0, tiled=...  19.4 us
    all_to_all x1, blocking collectives, per_device(): lax.all_to_all(new.reshape(8, 4, 8, LANES), 'sub', split_axis=0, concat_a...  9.71 us
    pallas_call x1, Pallas kernels, refine(): pl.pallas_call(refine_kernel, out_shape=jax.ShapeDtypeStruct((32 * 8, LAN...  9.22 us
    all_to_all x1, starting transfers between devices, per_device(): lax.all_to_all(sent, 'band', split_axis=0, concat_axis=0, tiled=True)  7.73 us
    ppermute x3, starting transfers between devices, per_device(): lax.ppermute(tiles[d], 'sub', [(i, (i + 2 * d) % 8) for i in range(8)])  5.64 us
    all_to_all x1, waiting for transfers between devices, per_device(): lax.all_to_all(sent, 'band', split_axis=0, concat_axis=0, tiled=True)  4.79 us
    ppermute x1, starting transfers between devices, per_device(): below = lax.ppermute(seen, 'sub', [(i + 1, i) for i in range(7)])  4.72 us
    pallas_call x1, Pallas kernels, pack(): pl.pallas_call(pack_kernel, out_shape=(jax.ShapeDtypeStruct((256, LANES),...  2.18 us
  transfers between devices with their start and end apart: 7, of which 3 were waited for; matrix products, arithmetic and copies ran while one was open for 1% of the time, Pallas kernels for 3%

profile of v9, /device:TPU:1, one launch (start us, length us, event | category | flops | bytes accessed | tf_op | source)
XLA Modules:
  0.0 74.8 jit_solution(17721979155441145106)
XLA Ops:
  0.0 2.2 %pack.1 = (f32[256,128]{1,0:T(8,128)}, f32[256,128]{1,0:T(8,128)}, f32[256,128]{1,0:T(8,128)}, f32[256,128]{1,0:T(8,128)}, bf16[128,128]{1,0:T(8,128)(2,1)}) custom-call(s32[1]{0:T(128)} %bitcast.pos_ref, f32[4,128,1024]{2,1,0:T(8,128)} %c_ref.1, f32[4,128,1024]{2,1,0:T(8,128)} %c_ref.1, bf16[8,16,1024]{2,1,0:T(8,128)(2,1)} %mb_ref.1, ...), custom_call_target="tpu_custom_call" | custom-call | flops 100000000 | bytes 1600000 | tf_op jit(solution)/shard_map/pack/pallas_call | solution.py:246
  2.2 2.0 %collective-permute-start = (f32[256,128]{1,0:T(8,128)}, f32[256,128]{1,0:T(8,128)S(1)}, u32[]{:S(2)}, u32[]{:S(2)}) collective-permute-start(f32[256,128]{1,0:T(8,128)} %get-tuple-element.13), channel_id=1, source_target_pairs={{0,32},{16,48},{32,64},{48,80},{64,96},{80,112},{96,0},{112,16},{1... | collective-permute-start | bytes 393224 | tf_op jit(solution)/shard_map/ppermute | solution.py:395
  4.2 2.4 %collective-permute-start.1 = (f32[256,128]{1,0:T(8,128)}, f32[256,128]{1,0:T(8,128)S(1)}, u32[]{:S(2)}, u32[]{:S(2)}) collective-permute-start(f32[256,128]{1,0:T(8,128)} %get-tuple-element.14), channel_id=1, source_target_pairs={{0,64},{16,80},{32,96},{48,112},{64,0},{80,16},{96,32},{112,48},{1... | collective-permute-start | bytes 393224 | tf_op jit(solution)/shard_map/ppermute | solution.py:395
  6.7 1.2 %collective-permute-start.2 = (f32[256,128]{1,0:T(8,128)}, f32[256,128]{1,0:T(8,128)S(1)}, u32[]{:S(2)}, u32[]{:S(2)}) collective-permute-start(f32[256,128]{1,0:T(8,128)} %get-tuple-element.15), channel_id=1, source_target_pairs={{0,96},{16,112},{32,0},{48,16},{64,32},{80,48},{96,64},{112,80},{1... | collective-permute-start | bytes 393224 | tf_op jit(solution)/shard_map/ppermute | solution.py:395
  7.8 1.9 %spread.1 = f32[16,16,256]{2,1,0:T(8,128)} custom-call(bf16[14,4,256]{2,1,0:T(4,128)(2,1)} %hs_ref.1, f32[9,14,9]{2,1,0:T(8,128)} %bitcast.7, bf16[14,32]{1,0:T(8,128)(2,1)} %basis_ref.1, bf16[8,14]{1,0:T(8,128)(2,1)} %response_ref.1), custom_call_target="tpu_custom_call" | custom-call | flops 1000000 | bytes 1000000 | tf_op jit(solution)/shard_map/spread/pallas_call | solution.py:290
  9.7 7.7 %all-to-all-start = ((f32[16,16,256]{2,1,0:T(8,128)}), f32[16,16,256]{2,1,0:T(8,128)S(1)}, u32[]{:S(2)}, u32[]{:S(2)}) async-start(f32[16,16,256]{2,1,0:T(8,128)} %spread.1), calls=%async_computation | async-start | bytes 524288 | tf_op jit(solution)/shard_map/all_to_all | solution.py:392
  17.4 0.0 collective-permute-done.r1
  17.4 0.0 collective-permute-done.1.r2
  17.4 0.0 collective-permute-done.2.r3
  17.5 0.0 copy-start.1
  17.5 0.9 %copy-done.1 = f32[256,128]{1,0:T(8,128)S(1)} copy-done((f32[256,128]{1,0:T(8,128)S(1)}, f32[256,128]{1,0:T(8,128)}, u32[]{:S(2)}) %copy-start.1) | copy-done | bytes 131096
  18.4 0.1 hand.1
  18.4 1.9 %collective-permute-start.3 = (f32[768,128]{1,0:T(8,128)S(1)}, f32[768,128]{1,0:T(8,128)S(1)}, u32[]{:S(2)}, u32[]{:S(2)}) collective-permute-start(f32[768,128]{1,0:T(8,128)S(1)} %get-tuple-element.17), channel_id=1, source_target_pairs={{0,16},{16,0},{32,48},{48,32},{64,80},{80,64},{96,112},{112,96},{1... | collective-permute-start | bytes 1179656 | tf_op jit(solution)/shard_map/ppermute | solution.py:398
  20.3 4.8 %all-to-all-done = f32[16,16,256]{2,1,0:T(8,128)S(1)} async-done(((f32[16,16,256]{2,1,0:T(8,128)}), f32[16,16,256]{2,1,0:T(8,128)S(1)}, u32[]{:S(2)}, u32[]{:S(2)}) %all-to-all-start) | async-done | bytes 262176 | tf_op jit(solution)/shard_map/all_to_all | solution.py:392
  25.1 0.8 %pad_maximum_fusion.refs_3_ = bf16[384,128]{1,0:T(8,128)(2,1)S(1)} fusion(bf16[128,128]{1,0:T(8,128)(2,1)} %get-tuple-element.18, bf16[256,128]{1,0:T(8,128)(2,1)S(1)} %slice.7), kind=kLoop, calls=%fused_computation.1 | loop fusion | flops 196608 | bytes 196608 | tf_op jit(solution)/shard_map/concatenate | solution.py:399
  25.9 4.7 %collective-permute-start.5 = (bf16[384,128]{1,0:T(8,128)(2,1)S(1)}, bf16[384,128]{1,0:T(8,128)(2,1)S(1)}, u32[]{:S(2)}, u32[]{:S(2)}) collective-permute-start(bf16[384,128]{1,0:T(8,128)(2,1)S(1)} %pad_maximum_fusion.refs_3_), channel_id=1, source_target_pairs={{16,0},{32,16},{48,32},{64,48},{80,64},{96,80},{112,96},{17,1},{33... | collective-permute-start | bytes 294920 | tf_op jit(solution)/shard_map/ppermute | solution.py:401
  30.6 2.1 %collective-permute-start.4 = (bf16[384,128]{1,0:T(8,128)(2,1)S(1)}, bf16[384,128]{1,0:T(8,128)(2,1)S(1)}, u32[]{:S(2)}, u32[]{:S(2)}) collective-permute-start(bf16[384,128]{1,0:T(8,128)(2,1)S(1)} %pad_maximum_fusion.refs_3_), channel_id=1, source_target_pairs={{0,16},{16,32},{32,48},{48,64},{64,80},{80,96},{96,112},{1,17},{17... | collective-permute-start | bytes 294920 | tf_op jit(solution)/shard_map/ppermute | solution.py:400
  32.7 0.4 collective-permute-done.5.refs_5_
  33.1 1.3 %collective-permute-done.4.refs_4_ = bf16[384,128]{1,0:T(8,128)(2,1)S(1)} collective-permute-done((bf16[384,128]{1,0:T(8,128)(2,1)S(1)}, bf16[384,128]{1,0:T(8,128)(2,1)S(1)}, u32[]{:S(2)}, u32[]{:S(2)}) %collective-permute-start.4) | collective-permute-done | bytes 98336 | tf_op jit(solution)/shard_map/ppermute | solution.py:400
  34.3 0.0 collective-permute-done.3.refs_1_
  34.3 9.2 %refine.1 = f32[256,128]{1,0:T(8,128)S(1)} custom-call(s32[1]{0:T(128)} %bitcast.pos_ref, f32[768,128]{1,0:T(8,128)S(1)} %get-tuple-element.16.refs_0_, f32[768,128]{1,0:T(8,128)S(1)} %collective-permute-done.3.refs_1_, f32[256,256]{1,0:T(8,128)S(1)} %bitcast.5, bf16[384,128]{1,0:T(8,128)(2,1)S(1)} %pad_maximum_fusion.refs_3_, ...), custom_call_target="tpu_custom_call" | custom-call | flops 400000000 | bytes 2000000 | tf_op jit(solution)/shard_map/refine/pallas_call | solution.py:178
  43.6 0.0 copy-start
  43.6 9.7 %all_to_all.15.d_ref = f32[8,4,8,128]{3,2,1,0:T(8,128)S(1)} all-to-all(f32[8,4,8,128]{3,2,1,0:T(8,128)S(1)} %bitcast.6), channel_id=1, replica_groups=mesh['sub'=8,'band'=16] {'sub'}, dimensions={0} | all-to-all | bytes 262144 | tf_op jit(solution)/shard_map/all_to_all | solution.py:403
  53.3 0.2 encode.1
  53.5 19.4 %all_to_all.16.g_ref = bf16[16,272,128]{2,1,0:T(8,128)(2,1)S(1)} all-to-all(bf16[16,272,128]{2,1,0:T(8,128)(2,1)S(1)} %encode.1), channel_id=1, replica_groups=mesh['sub'=8,'band'=16] {'band'}, dimensions={0} | all-to-all | bytes 2228224 | tf_op jit(solution)/shard_map/all_to_all | solution.py:404
  72.9 0.0 copy-done
  72.9 2.0 %place.1 = f32[4,128,1024]{2,1,0:T(8,128)} custom-call(bf16[16,272,128]{2,1,0:T(8,128)(2,1)S(1)} %all_to_all.16.g_ref, f32[4,128,1024]{2,1,0:T(8,128)S(1)} %copy-done), custom_call_target="tpu_custom_call" | custom-call | tf_op jit(solution)/shard_map/place/pallas_call | solution.py:378
  (1 shorter events, 0.0 us)
Async XLA Ops:
  2.2 15.2 %collective-permute-start = (f32[256,128]{1,0:T(8,128)}, f32[256,128]{1,0:T(8,128)S(1)}, u32[]{:S(2)}, u32[]{:S(2)}) collective-permute-start(f32[256,128]{1,0:T(8,128)} %get-tuple-element.13), channel_id=1, source_target_pairs={{0,32},{16,48},{32,64},{48,80},{64,96},{80,112},{96,0},{112,16},{1... | collective-permute-start | bytes 393224 | tf_op jit(solution)/shard_map/ppermute | solution.py:395
  4.2 13.2 %collective-permute-start.1 = (f32[256,128]{1,0:T(8,128)}, f32[256,128]{1,0:T(8,128)S(1)}, u32[]{:S(2)}, u32[]{:S(2)}) collective-permute-start(f32[256,128]{1,0:T(8,128)} %get-tuple-element.14), channel_id=1, source_target_pairs={{0,64},{16,80},{32,96},{48,112},{64,0},{80,16},{96,32},{112,48},{1... | collective-permute-start | bytes 393224 | tf_op jit(solution)/shard_map/ppermute | solution.py:395
  6.7 10.8 %collective-permute-start.2 = (f32[256,128]{1,0:T(8,128)}, f32[256,128]{1,0:T(8,128)S(1)}, u32[]{:S(2)}, u32[]{:S(2)}) collective-permute-start(f32[256,128]{1,0:T(8,128)} %get-tuple-element.15), channel_id=1, source_target_pairs={{0,96},{16,112},{32,0},{48,16},{64,32},{80,48},{96,64},{112,80},{1... | collective-permute-start | bytes 393224 | tf_op jit(solution)/shard_map/ppermute | solution.py:395
  9.7 15.4 %all-to-all-start = ((f32[16,16,256]{2,1,0:T(8,128)}), f32[16,16,256]{2,1,0:T(8,128)S(1)}, u32[]{:S(2)}, u32[]{:S(2)}) async-start(f32[16,16,256]{2,1,0:T(8,128)} %spread.1), calls=%async_computation | async-start | bytes 524288 | tf_op jit(solution)/shard_map/all_to_all | solution.py:392
  17.5 0.9 %copy-start.1 = (f32[256,128]{1,0:T(8,128)S(1)}, f32[256,128]{1,0:T(8,128)}, u32[]{:S(2)}) copy-start(f32[256,128]{1,0:T(8,128)} %get-tuple-element.12.r0) | copy-start | bytes 393220
  18.4 15.9 %collective-permute-start.3 = (f32[768,128]{1,0:T(8,128)S(1)}, f32[768,128]{1,0:T(8,128)S(1)}, u32[]{:S(2)}, u32[]{:S(2)}) collective-permute-start(f32[768,128]{1,0:T(8,128)S(1)} %get-tuple-element.17), channel_id=1, source_target_pairs={{0,16},{16,0},{32,48},{48,32},{64,80},{80,64},{96,112},{112,96},{1... | collective-permute-start | bytes 1179656 | tf_op jit(solution)/shard_map/ppermute | solution.py:398
  25.9 7.2 %collective-permute-start.5 = (bf16[384,128]{1,0:T(8,128)(2,1)S(1)}, bf16[384,128]{1,0:T(8,128)(2,1)S(1)}, u32[]{:S(2)}, u32[]{:S(2)}) collective-permute-start(bf16[384,128]{1,0:T(8,128)(2,1)S(1)} %pad_maximum_fusion.refs_3_), channel_id=1, source_target_pairs={{16,0},{32,16},{48,32},{64,48},{80,64},{96,80},{112,96},{17,1},{33... | collective-permute-start | bytes 294920 | tf_op jit(solution)/shard_map/ppermute | solution.py:401
  30.6 3.7 %collective-permute-start.4 = (bf16[384,128]{1,0:T(8,128)(2,1)S(1)}, bf16[384,128]{1,0:T(8,128)(2,1)S(1)}, u32[]{:S(2)}, u32[]{:S(2)}) collective-permute-start(bf16[384,128]{1,0:T(8,128)(2,1)S(1)} %pad_maximum_fusion.refs_3_), channel_id=1, source_target_pairs={{0,16},{16,32},{32,48},{48,64},{64,80},{80,96},{96,112},{1,17},{17... | collective-permute-start | bytes 294920 | tf_op jit(solution)/shard_map/ppermute | solution.py:400
  43.6 29.3 %copy-start = (f32[4,128,1024]{2,1,0:T(8,128)S(1)}, f32[4,128,1024]{2,1,0:T(8,128)}, u32[]{:S(2)}) copy-start(f32[4,128,1024]{2,1,0:T(8,128)} %c_ref.1) | copy-start | bytes 6291460

commit v10 on v9

--- a/solution.py
+++ b/solution.py
@@ -389,11 +389,13 @@
 def per_device(coeffs_in, basis, kernels, response, hs_image, ms_image):
     pos = (lax.axis_index("sub") * 16 + lax.axis_index("band")).astype(jnp.int32).reshape(1)
     sent = spread(hs_image, kernels.transpose(1, 0, 2), basis, response)
+    sent, pos = lax.optimization_barrier((sent, pos))
     hp = lax.all_to_all(sent, "band", split_axis=0, concat_axis=0, tiled=True).reshape(256, 256)
     *tiles, near = pack(pos, coeffs_in, ms_image)
     tiles = [tiles[0]] + [
         lax.ppermute(tiles[d], "sub", [(i, (i + 2 * d) % 8) for i in range(8)]) for d in range(1, 4)
     ]
+    hp, *tiles = lax.optimization_barrier((hp, *tiles))
     mine, other = hand(pos, tiles)
     other = lax.ppermute(other, "sub", [(i, i ^ 1) for i in range(8)])
     seen = jnp.concatenate([hp[:, 0:128].astype(bf16), near], axis=0)

time: 76 us -> 79.2 us (1.042)
  blocking collectives: 29.1 us -> 33.8 us
  starting transfers between devices: 22.1 us -> 20.8 us
    all_to_all x1, waiting for transfers between devices: 4.79 us -> 0.01 us  [per_device(): lax.all_to_all(sent, 'band', split_axis=0, concat_axis=0, tiled=True)]
    ppermute x3, waiting for transfers between devices: 0.01 us -> 4.58 us  [per_device(): lax.ppermute(tiles[d], 'sub', [(i, (i + 2 * d) % 8) for i in range(8)])]
    all_to_all x1, blocking collectives: 19.4 us -> 23.1 us  [per_device(): lax.all_to_all(encode(owned), 'band', split_axis=0, concat_axis=0, tiled=...]
    ppermute x1, starting transfers between devices: 4.72 us -> 1.92 us  [per_device(): below = lax.ppermute(seen, 'sub', [(i + 1, i) for i in range(7)])]
    ppermute x1, starting transfers between devices: 2.12 us -> 3.64 us  [per_device(): above = lax.ppermute(seen, 'sub', [(i, i + 1) for i in range(7)])]
    all_to_all x1, blocking collectives: 9.71 us -> 10.6 us  [per_device(): lax.all_to_all(new.reshape(8, 4, 8, LANES), 'sub', split_axis=0, concat_a...]
    all_to_all x1, starting transfers between devices: 7.73 us -> 8.6 us  [per_device(): lax.all_to_all(sent, 'band', split_axis=0, concat_axis=0, tiled=True)]
    ppermute x3, starting transfers between devices: 5.64 us -> 4.81 us  [per_device(): lax.ppermute(tiles[d], 'sub', [(i, (i + 2 * d) % 8) for i in range(8)])]
  transfers between devices with their start and end apart: 7 -> 7, of which waited for: 3 -> 5; matrix products, arithmetic and copies ran while one was open for 1% -> 1% of each run, Pallas kernels for 3% -> 3%
where the time goes in v10:
time: 79.2 us; the launch traced here: 78 us
  blocking collectives  33.8 us (43%)
  starting transfers between devices  20.8 us (26%)
  Pallas kernels  15.5 us (20%)
  waiting for transfers between devices  6.2 us (8%)
  local copies, waits for them, and re-layouts  0.92 us (1%)
    all_to_all x1, blocking collectives, per_device(): lax.all_to_all(encode(owned), 'band', split_axis=0, concat_axis=0, tiled=...  23.1 us
    all_to_all x1, blocking collectives, per_device(): lax.all_to_all(new.reshape(8, 4, 8, LANES), 'sub', split_axis=0, concat_a...  10.6 us
    pallas_call x1, Pallas kernels, refine(): pl.pallas_call(refine_kernel, out_shape=jax.ShapeDtypeStruct((32 * 8, LAN...  9.22 us
    all_to_all x1, starting transfers between devices, per_device(): lax.all_to_all(sent, 'band', split_axis=0, concat_axis=0, tiled=True)  8.6 us
    ppermute x3, starting transfers between devices, per_device(): lax.ppermute(tiles[d], 'sub', [(i, (i + 2 * d) % 8) for i in range(8)])  4.81 us
    ppermute x3, waiting for transfers between devices, per_device(): lax.ppermute(tiles[d], 'sub', [(i, (i + 2 * d) % 8) for i in range(8)])  4.58 us
    ppermute x1, starting transfers between devices, per_device(): above = lax.ppermute(seen, 'sub', [(i, i + 1) for i in range(7)])  3.64 us
    pallas_call x1, Pallas kernels, pack(): pl.pallas_call(pack_kernel, out_shape=(jax.ShapeDtypeStruct((256, LANES),...  2.2 us
  transfers between devices with their start and end apart: 7, of which 5 were waited for; matrix products, arithmetic and copies ran while one was open for 1% of the time, Pallas kernels for 3%

profile of v10, /device:TPU:1, one launch (start us, length us, event | category | flops | bytes accessed | tf_op | source)
XLA Modules:
  0.0 78.0 jit_solution(7785682120079268429)
XLA Ops:
  0.0 1.9 %spread.1 = f32[16,16,256]{2,1,0:T(8,128)} custom-call(bf16[14,4,256]{2,1,0:T(4,128)(2,1)} %hs_ref.1, f32[9,14,9]{2,1,0:T(8,128)} %bitcast.7, bf16[14,32]{1,0:T(8,128)(2,1)} %basis_ref.1, bf16[8,14]{1,0:T(8,128)(2,1)} %response_ref.1), custom_call_target="tpu_custom_call" | custom-call | flops 1000000 | bytes 1000000 | tf_op jit(solution)/shard_map/spread/pallas_call | solution.py:290
  1.9 8.6 %all-to-all-start = ((f32[16,16,256]{2,1,0:T(8,128)}), f32[16,16,256]{2,1,0:T(8,128)S(1)}, u32[]{:S(2)}, u32[]{:S(2)}) async-start(f32[16,16,256]{2,1,0:T(8,128)} %spread.1), calls=%async_computation | async-start | bytes 524288 | tf_op jit(solution)/shard_map/all_to_all | solution.py:393
  10.5 2.2 %pack.1 = (f32[256,128]{1,0:T(8,128)}, f32[256,128]{1,0:T(8,128)}, f32[256,128]{1,0:T(8,128)}, f32[256,128]{1,0:T(8,128)}, bf16[128,128]{1,0:T(8,128)(2,1)}) custom-call(s32[1]{0:T(128)} %bitcast.1.pos_ref, f32[4,128,1024]{2,1,0:T(8,128)} %c_ref.1, f32[4,128,1024]{2,1,0:T(8,128)} %c_ref.1, bf16[8,16,1024]{2,1,0:T(8,128)(2,1)} %mb_ref.1, ...), custom_call_target="tpu_custom_call" | custom-call | flops 100000000 | bytes 1600000 | tf_op jit(solution)/shard_map/pack/pallas_call | solution.py:246
  12.7 1.2 %collective-permute-start = (f32[256,128]{1,0:T(8,128)}, f32[256,128]{1,0:T(8,128)S(1)}, u32[]{:S(2)}, u32[]{:S(2)}) collective-permute-start(f32[256,128]{1,0:T(8,128)} %get-tuple-element.22), channel_id=1, source_target_pairs={{0,32},{16,48},{32,64},{48,80},{64,96},{80,112},{96,0},{112,16},{1... | collective-permute-start | bytes 393224 | tf_op jit(solution)/shard_map/ppermute | solution.py:396
  13.9 2.4 %collective-permute-start.1 = (f32[256,128]{1,0:T(8,128)}, f32[256,128]{1,0:T(8,128)S(1)}, u32[]{:S(2)}, u32[]{:S(2)}) collective-permute-start(f32[256,128]{1,0:T(8,128)} %get-tuple-element.23), channel_id=1, source_target_pairs={{0,64},{16,80},{32,96},{48,112},{64,0},{80,16},{96,32},{112,48},{1... | collective-permute-start | bytes 393224 | tf_op jit(solution)/shard_map/ppermute | solution.py:396
  16.3 1.1 %collective-permute-start.2 = (f32[256,128]{1,0:T(8,128)}, f32[256,128]{1,0:T(8,128)S(1)}, u32[]{:S(2)}, u32[]{:S(2)}) collective-permute-start(f32[256,128]{1,0:T(8,128)} %get-tuple-element.24), channel_id=1, source_target_pairs={{0,96},{16,112},{32,0},{48,16},{64,32},{80,48},{96,64},{112,80},{1... | collective-permute-start | bytes 393224 | tf_op jit(solution)/shard_map/ppermute | solution.py:396
  17.5 0.7 collective-permute-done.r1
  18.2 3.4 %collective-permute-done.1.r2 = f32[256,128]{1,0:T(8,128)S(1)} collective-permute-done((f32[256,128]{1,0:T(8,128)}, f32[256,128]{1,0:T(8,128)S(1)}, u32[]{:S(2)}, u32[]{:S(2)}) %collective-permute-start.1) | collective-permute-done | bytes 131104 | tf_op jit(solution)/shard_map/ppermute | solution.py:396
  21.6 0.4 collective-permute-done.2.r3
  22.1 0.0 all-to-all-done
  22.1 0.0 copy-start.1
  22.1 0.9 %copy-done.1 = f32[256,128]{1,0:T(8,128)S(1)} copy-done((f32[256,128]{1,0:T(8,128)S(1)}, f32[256,128]{1,0:T(8,128)}, u32[]{:S(2)}) %copy-start.1) | copy-done | bytes 131096
  23.0 0.1 hand.1
  23.0 1.8 %collective-permute-start.3 = (f32[768,128]{1,0:T(8,128)S(1)}, f32[768,128]{1,0:T(8,128)S(1)}, u32[]{:S(2)}, u32[]{:S(2)}) collective-permute-start(f32[768,128]{1,0:T(8,128)S(1)} %get-tuple-element.30), channel_id=1, source_target_pairs={{0,16},{16,0},{32,48},{48,32},{64,80},{80,64},{96,112},{112,96},{1... | collective-permute-start | bytes 1179656 | tf_op jit(solution)/shard_map/ppermute | solution.py:400
  24.9 0.8 pad_maximum_fusion.refs_3_
  25.6 1.9 %collective-permute-start.5 = (bf16[384,128]{1,0:T(8,128)(2,1)S(1)}, bf16[384,128]{1,0:T(8,128)(2,1)S(1)}, u32[]{:S(2)}, u32[]{:S(2)}) collective-permute-start(bf16[384,128]{1,0:T(8,128)(2,1)S(1)} %pad_maximum_fusion.refs_3_), channel_id=1, source_target_pairs={{16,0},{32,16},{48,32},{64,48},{80,64},{96,80},{112,96},{17,1},{33... | collective-permute-start | bytes 294920 | tf_op jit(solution)/shard_map/ppermute | solution.py:403
  27.6 3.6 %collective-permute-start.4 = (bf16[384,128]{1,0:T(8,128)(2,1)S(1)}, bf16[384,128]{1,0:T(8,128)(2,1)S(1)}, u32[]{:S(2)}, u32[]{:S(2)}) collective-permute-start(bf16[384,128]{1,0:T(8,128)(2,1)S(1)} %pad_maximum_fusion.refs_3_), channel_id=1, source_target_pairs={{0,16},{16,32},{32,48},{48,64},{64,80},{80,96},{96,112},{1,17},{17... | collective-permute-start | bytes 294920 | tf_op jit(solution)/shard_map/ppermute | solution.py:402
  31.2 0.4 collective-permute-done.5.refs_5_
  31.6 1.3 %collective-permute-done.4.refs_4_ = bf16[384,128]{1,0:T(8,128)(2,1)S(1)} collective-permute-done((bf16[384,128]{1,0:T(8,128)(2,1)S(1)}, bf16[384,128]{1,0:T(8,128)(2,1)S(1)}, u32[]{:S(2)}, u32[]{:S(2)}) %collective-permute-start.4) | collective-permute-done | bytes 98336 | tf_op jit(solution)/shard_map/ppermute | solution.py:402
  32.8 0.0 collective-permute-done.3.refs_1_
  32.8 9.2 %refine.1 = f32[256,128]{1,0:T(8,128)S(1)} custom-call(s32[1]{0:T(128)} %bitcast.1.pos_ref, f32[768,128]{1,0:T(8,128)S(1)} %get-tuple-element.29.refs_0_, f32[768,128]{1,0:T(8,128)S(1)} %collective-permute-done.3.refs_1_, f32[256,256]{1,0:T(8,128)S(1)} %bitcast.5, bf16[384,128]{1,0:T(8,128)(2,1)S(1)} %pad_maximum_fusion.refs_3_, ...), custom_call_target="tpu_custom_call" | custom-call | flops 400000000 | bytes 2000000 | tf_op jit(solution)/shard_map/refine/pallas_call | solution.py:178
  42.0 0.0 copy-start
  42.0 10.6 %all_to_all.15.d_ref = f32[8,4,8,128]{3,2,1,0:T(8,128)S(1)} all-to-all(f32[8,4,8,128]{3,2,1,0:T(8,128)S(1)} %bitcast.6), channel_id=1, replica_groups=mesh['sub'=8,'band'=16] {'sub'}, dimensions={0} | all-to-all | bytes 262144 | tf_op jit(solution)/shard_map/all_to_all | solution.py:405
  52.7 0.2 encode.1
  52.9 23.1 %all_to_all.16.g_ref = bf16[16,272,128]{2,1,0:T(8,128)(2,1)S(1)} all-to-all(bf16[16,272,128]{2,1,0:T(8,128)(2,1)S(1)} %encode.1), channel_id=1, replica_groups=mesh['sub'=8,'band'=16] {'band'}, dimensions={0} | all-to-all | bytes 2228224 | tf_op jit(solution)/shard_map/all_to_all | solution.py:406
  76.1 0.0 copy-done
  76.1 2.0 %place.1 = f32[4,128,1024]{2,1,0:T(8,128)} custom-call(bf16[16,272,128]{2,1,0:T(8,128)(2,1)S(1)} %all_to_all.16.g_ref, f32[4,128,1024]{2,1,0:T(8,128)S(1)} %copy-done), custom_call_target="tpu_custom_call" | custom-call | tf_op jit(solution)/shard_map/place/pallas_call | solution.py:378
  (1 shorter events, 0.0 us)
Async XLA Ops:
  1.9 20.2 %all-to-all-start = ((f32[16,16,256]{2,1,0:T(8,128)}), f32[16,16,256]{2,1,0:T(8,128)S(1)}, u32[]{:S(2)}, u32[]{:S(2)}) async-start(f32[16,16,256]{2,1,0:T(8,128)} %spread.1), calls=%async_computation | async-start | bytes 524288 | tf_op jit(solution)/shard_map/all_to_all | solution.py:393
  12.7 5.5 %collective-permute-start = (f32[256,128]{1,0:T(8,128)}, f32[256,128]{1,0:T(8,128)S(1)}, u32[]{:S(2)}, u32[]{:S(2)}) collective-permute-start(f32[256,128]{1,0:T(8,128)} %get-tuple-element.22), channel_id=1, source_target_pairs={{0,32},{16,48},{32,64},{48,80},{64,96},{80,112},{96,0},{112,16},{1... | collective-permute-start | bytes 393224 | tf_op jit(solution)/shard_map/ppermute | solution.py:396
  13.9 7.7 %collective-permute-start.1 = (f32[256,128]{1,0:T(8,128)}, f32[256,128]{1,0:T(8,128)S(1)}, u32[]{:S(2)}, u32[]{:S(2)}) collective-permute-start(f32[256,128]{1,0:T(8,128)} %get-tuple-element.23), channel_id=1, source_target_pairs={{0,64},{16,80},{32,96},{48,112},{64,0},{80,16},{96,32},{112,48},{1... | collective-permute-start | bytes 393224 | tf_op jit(solution)/shard_map/ppermute | solution.py:396
  16.3 5.7 %collective-permute-start.2 = (f32[256,128]{1,0:T(8,128)}, f32[256,128]{1,0:T(8,128)S(1)}, u32[]{:S(2)}, u32[]{:S(2)}) collective-permute-start(f32[256,128]{1,0:T(8,128)} %get-tuple-element.24), channel_id=1, source_target_pairs={{0,96},{16,112},{32,0},{48,16},{64,32},{80,48},{96,64},{112,80},{1... | collective-permute-start | bytes 393224 | tf_op jit(solution)/shard_map/ppermute | solution.py:396
  22.1 0.9 %copy-start.1 = (f32[256,128]{1,0:T(8,128)S(1)}, f32[256,128]{1,0:T(8,128)}, u32[]{:S(2)}) copy-start(f32[256,128]{1,0:T(8,128)} %get-tuple-element.25.r0) | copy-start | bytes 393220
  23.0 9.8 %collective-permute-start.3 = (f32[768,128]{1,0:T(8,128)S(1)}, f32[768,128]{1,0:T(8,128)S(1)}, u32[]{:S(2)}, u32[]{:S(2)}) collective-permute-start(f32[768,128]{1,0:T(8,128)S(1)} %get-tuple-element.30), channel_id=1, source_target_pairs={{0,16},{16,0},{32,48},{48,32},{64,80},{80,64},{96,112},{112,96},{1... | collective-permute-start | bytes 1179656 | tf_op jit(solution)/shard_map/ppermute | solution.py:400
  25.6 5.9 %collective-permute-start.5 = (bf16[384,128]{1,0:T(8,128)(2,1)S(1)}, bf16[384,128]{1,0:T(8,128)(2,1)S(1)}, u32[]{:S(2)}, u32[]{:S(2)}) collective-permute-start(bf16[384,128]{1,0:T(8,128)(2,1)S(1)} %pad_maximum_fusion.refs_3_), channel_id=1, source_target_pairs={{16,0},{32,16},{48,32},{64,48},{80,64},{96,80},{112,96},{17,1},{33... | collective-permute-start | bytes 294920 | tf_op jit(solution)/shard_map/ppermute | solution.py:403
  27.6 5.3 %collective-permute-start.4 = (bf16[384,128]{1,0:T(8,128)(2,1)S(1)}, bf16[384,128]{1,0:T(8,128)(2,1)S(1)}, u32[]{:S(2)}, u32[]{:S(2)}) collective-permute-start(bf16[384,128]{1,0:T(8,128)(2,1)S(1)} %pad_maximum_fusion.refs_3_), channel_id=1, source_target_pairs={{0,16},{16,32},{32,48},{48,64},{64,80},{80,96},{96,112},{1,17},{17... | collective-permute-start | bytes 294920 | tf_op jit(solution)/shard_map/ppermute | solution.py:402
  42.0 34.0 %copy-start = (f32[4,128,1024]{2,1,0:T(8,128)S(1)}, f32[4,128,1024]{2,1,0:T(8,128)}, u32[]{:S(2)}) copy-start(f32[4,128,1024]{2,1,0:T(8,128)} %c_ref.1) | copy-start | bytes 6291460

commit v11 on v10

--- a/solution.py
+++ b/solution.py
@@ -395,12 +395,12 @@
     tiles = [tiles[0]] + [
         lax.ppermute(tiles[d], "sub", [(i, (i + 2 * d) % 8) for i in range(8)]) for d in range(1, 4)
     ]
-    hp, *tiles = lax.optimization_barrier((hp, *tiles))
-    mine, other = hand(pos, tiles)
-    other = lax.ppermute(other, "sub", [(i, i ^ 1) for i in range(8)])
     seen = jnp.concatenate([hp[:, 0:128].astype(bf16), near], axis=0)
     above = lax.ppermute(seen, "sub", [(i, i + 1) for i in range(7)])
     below = lax.ppermute(seen, "sub", [(i + 1, i) for i in range(7)])
+    above, below, *tiles = lax.optimization_barrier((above, below, *tiles))
+    mine, other = hand(pos, tiles)
+    other = lax.ppermute(other, "sub", [(i, i ^ 1) for i in range(8)])
     new = refine(pos, mine, other, hp, seen, above, below)
     owned = lax.all_to_all(new.reshape(8, 4, 8, LANES), "sub", split_axis=0, concat_axis=0, tiled=True)
     gathered = lax.all_to_all(encode(owned), "band", split_axis=0, concat_axis=0, tiled=True)

time: 79.2 us -> 74.2 us (0.937)
  blocking collectives: 33.8 us -> 31.4 us
  waiting for transfers between devices: 6.2 us -> 3.83 us
    ppermute x3, waiting for transfers between devices: 4.58 us -> 0.01 us  [per_device(): lax.ppermute(tiles[d], 'sub', [(i, (i + 2 * d) % 8) for i in range(8)])]
    all_to_all x1, blocking collectives: 23.1 us -> 20.6 us  [per_device(): lax.all_to_all(encode(owned), 'band', split_axis=0, concat_axis=0, tiled=...]
    ppermute x1, starting transfers between devices: 1.92 us -> 4 us  [per_device(): below = lax.ppermute(seen, 'sub', [(i + 1, i) for i in range(7)])]
    ppermute x1, starting transfers between devices: 1.82 us -> 0.09 us  [per_device(): other = lax.ppermute(other, 'sub', [(i, i ^ 1) for i in range(8)])]
    ppermute x1, waiting for transfers between devices: 0.01 us -> 1.71 us  [per_device(): other = lax.ppermute(other, 'sub', [(i, i ^ 1) for i in range(8)])]
  transfers between devices with their start and end apart: 7 -> 7, of which waited for: 5 -> 4; matrix products, arithmetic and copies ran while one was open for 1% -> 1% of each run, Pallas kernels for 3% -> 3%
where the time goes in v11:
time: 74.2 us; the launch traced here: 73 us
  blocking collectives  31.4 us (42%)
  starting transfers between devices  20.5 us (28%)
  Pallas kernels  15.5 us (21%)
  waiting for transfers between devices  3.83 us (5%)
  local copies, waits for them, and re-layouts  0.92 us (1%)
  other arithmetic  0.77 us (1%)
    all_to_all x1, blocking collectives, per_device(): lax.all_to_all(encode(owned), 'band', split_axis=0, concat_axis=0, tiled=...  20.6 us
    all_to_all x1, blocking collectives, per_device(): lax.all_to_all(new.reshape(8, 4, 8, LANES), 'sub', split_axis=0, concat_a...  10.8 us
    pallas_call x1, Pallas kernels, refine(): pl.pallas_call(refine_kernel, out_shape=jax.ShapeDtypeStruct((32 * 8, LAN...  9.21 us
    all_to_all x1, starting transfers between devices, per_device(): lax.all_to_all(sent, 'band', split_axis=0, concat_axis=0, tiled=True)  8.6 us
    ppermute x3, starting transfers between devices, per_device(): lax.ppermute(tiles[d], 'sub', [(i, (i + 2 * d) % 8) for i in range(8)])  4.81 us
    ppermute x1, starting transfers between devices, per_device(): below = lax.ppermute(seen, 'sub', [(i + 1, i) for i in range(7)])  4 us
    ppermute x1, starting transfers between devices, per_device(): above = lax.ppermute(seen, 'sub', [(i, i + 1) for i in range(7)])  3.02 us
    pallas_call x1, Pallas kernels, pack(): pl.pallas_call(pack_kernel, out_shape=(jax.ShapeDtypeStruct((256, LANES),...  2.2 us
  transfers between devices with their start and end apart: 7, of which 4 were waited for; matrix products, arithmetic and copies ran while one was open for 1% of the time, Pallas kernels for 3%

profile of v11, /device:TPU:1, one launch (start us, length us, event | category | flops | bytes accessed | tf_op | source)
XLA Modules:
  0.0 73.0 jit_solution(909755574855949656)
XLA Ops:
  0.0 1.9 %spread.1 = f32[16,16,256]{2,1,0:T(8,128)} custom-call(bf16[14,4,256]{2,1,0:T(4,128)(2,1)} %hs_ref.1, f32[9,14,9]{2,1,0:T(8,128)} %bitcast.7, bf16[14,32]{1,0:T(8,128)(2,1)} %basis_ref.1, bf16[8,14]{1,0:T(8,128)(2,1)} %response_ref.1), custom_call_target="tpu_custom_call" | custom-call | flops 1000000 | bytes 1000000 | tf_op jit(solution)/shard_map/spread/pallas_call | solution.py:290
  1.9 8.6 %all-to-all-start = ((f32[16,16,256]{2,1,0:T(8,128)}), f32[16,16,256]{2,1,0:T(8,128)S(1)}, u32[]{:S(2)}, u32[]{:S(2)}) async-start(f32[16,16,256]{2,1,0:T(8,128)} %spread.1), calls=%async_computation | async-start | bytes 524288 | tf_op jit(solution)/shard_map/all_to_all | solution.py:393
  10.5 2.2 %pack.1 = (f32[256,128]{1,0:T(8,128)}, f32[256,128]{1,0:T(8,128)}, f32[256,128]{1,0:T(8,128)}, f32[256,128]{1,0:T(8,128)}, bf16[128,128]{1,0:T(8,128)(2,1)}) custom-call(s32[1]{0:T(128)} %bitcast.1.pos_ref, f32[4,128,1024]{2,1,0:T(8,128)} %c_ref.1, f32[4,128,1024]{2,1,0:T(8,128)} %c_ref.1, bf16[8,16,1024]{2,1,0:T(8,128)(2,1)} %mb_ref.1, ...), custom_call_target="tpu_custom_call" | custom-call | flops 100000000 | bytes 1600000 | tf_op jit(solution)/shard_map/pack/pallas_call | solution.py:246
  12.7 1.2 %collective-permute-start.2 = (f32[256,128]{1,0:T(8,128)}, f32[256,128]{1,0:T(8,128)S(1)}, u32[]{:S(2)}, u32[]{:S(2)}) collective-permute-start(f32[256,128]{1,0:T(8,128)} %get-tuple-element.24), channel_id=1, source_target_pairs={{0,32},{16,48},{32,64},{48,80},{64,96},{80,112},{96,0},{112,16},{1... | collective-permute-start | bytes 393224 | tf_op jit(solution)/shard_map/ppermute | solution.py:396
  13.9 2.4 %collective-permute-start.3 = (f32[256,128]{1,0:T(8,128)}, f32[256,128]{1,0:T(8,128)S(1)}, u32[]{:S(2)}, u32[]{:S(2)}) collective-permute-start(f32[256,128]{1,0:T(8,128)} %get-tuple-element.25), channel_id=1, source_target_pairs={{0,64},{16,80},{32,96},{48,112},{64,0},{80,16},{96,32},{112,48},{1... | collective-permute-start | bytes 393224 | tf_op jit(solution)/shard_map/ppermute | solution.py:396
  16.3 1.1 %collective-permute-start.4 = (f32[256,128]{1,0:T(8,128)}, f32[256,128]{1,0:T(8,128)S(1)}, u32[]{:S(2)}, u32[]{:S(2)}) collective-permute-start(f32[256,128]{1,0:T(8,128)} %get-tuple-element.26), channel_id=1, source_target_pairs={{0,96},{16,112},{32,0},{48,16},{64,32},{80,48},{96,64},{112,80},{1... | collective-permute-start | bytes 393224 | tf_op jit(solution)/shard_map/ppermute | solution.py:396
  17.5 0.5 all-to-all-done
  18.0 0.8 %pad_maximum_fusion.refs_3_ = bf16[384,128]{1,0:T(8,128)(2,1)S(1)} fusion(bf16[128,128]{1,0:T(8,128)(2,1)} %get-tuple-element.22, bf16[256,128]{1,0:T(8,128)(2,1)S(1)} %slice.7), kind=kLoop, calls=%fused_computation.1 | loop fusion | flops 196608 | bytes 196608 | tf_op jit(solution)/shard_map/concatenate | solution.py:398
  18.8 4.0 %collective-permute-start.1 = (bf16[384,128]{1,0:T(8,128)(2,1)S(1)}, bf16[384,128]{1,0:T(8,128)(2,1)S(1)}, u32[]{:S(2)}, u32[]{:S(2)}) collective-permute-start(bf16[384,128]{1,0:T(8,128)(2,1)S(1)} %pad_maximum_fusion.refs_3_), channel_id=1, source_target_pairs={{16,0},{32,16},{48,32},{64,48},{80,64},{96,80},{112,96},{17,1},{33... | collective-permute-start | bytes 294920 | tf_op jit(solution)/shard_map/ppermute | solution.py:400
  22.8 3.0 %collective-permute-start = (bf16[384,128]{1,0:T(8,128)(2,1)S(1)}, bf16[384,128]{1,0:T(8,128)(2,1)S(1)}, u32[]{:S(2)}, u32[]{:S(2)}) collective-permute-start(bf16[384,128]{1,0:T(8,128)(2,1)S(1)} %pad_maximum_fusion.refs_3_), channel_id=1, source_target_pairs={{0,16},{16,32},{32,48},{48,64},{64,80},{80,96},{96,112},{1,17},{17... | collective-permute-start | bytes 294920 | tf_op jit(solution)/shard_map/ppermute | solution.py:399
  25.8 0.0 collective-permute-done.2.r1
  25.8 0.0 collective-permute-done.3.r2
  25.9 0.0 collective-permute-done.4.r3
  25.9 0.3 collective-permute-done.1.refs_5_
  26.2 1.3 %collective-permute-done.refs_4_ = bf16[384,128]{1,0:T(8,128)(2,1)S(1)} collective-permute-done((bf16[384,128]{1,0:T(8,128)(2,1)S(1)}, bf16[384,128]{1,0:T(8,128)(2,1)S(1)}, u32[]{:S(2)}, u32[]{:S(2)}) %collective-permute-start) | collective-permute-done | bytes 98336 | tf_op jit(solution)/shard_map/ppermute | solution.py:399
  27.4 0.0 copy-start.1
  27.4 0.9 %copy-done.1 = f32[256,128]{1,0:T(8,128)S(1)} copy-done((f32[256,128]{1,0:T(8,128)S(1)}, f32[256,128]{1,0:T(8,128)}, u32[]{:S(2)}) %copy-start.1) | copy-done | bytes 131096
  28.4 0.1 hand.1
  28.4 0.1 collective-permute-start.5
  28.5 1.7 %collective-permute-done.5.refs_1_ = f32[768,128]{1,0:T(8,128)S(1)} collective-permute-done((f32[768,128]{1,0:T(8,128)S(1)}, f32[768,128]{1,0:T(8,128)S(1)}, u32[]{:S(2)}, u32[]{:S(2)}) %collective-permute-start.5) | collective-permute-done | bytes 393248 | tf_op jit(solution)/shard_map/ppermute | solution.py:403
  30.2 9.2 %refine.1 = f32[256,128]{1,0:T(8,128)S(1)} custom-call(s32[1]{0:T(128)} %bitcast.1.pos_ref, f32[768,128]{1,0:T(8,128)S(1)} %get-tuple-element.31.refs_0_, f32[768,128]{1,0:T(8,128)S(1)} %collective-permute-done.5.refs_1_, f32[256,256]{1,0:T(8,128)S(1)} %bitcast.5, bf16[384,128]{1,0:T(8,128)(2,1)S(1)} %pad_maximum_fusion.refs_3_, ...), custom_call_target="tpu_custom_call" | custom-call | flops 400000000 | bytes 2000000 | tf_op jit(solution)/shard_map/refine/pallas_call | solution.py:178
  39.4 0.0 copy-start
  39.4 10.8 %all_to_all.15.d_ref = f32[8,4,8,128]{3,2,1,0:T(8,128)S(1)} all-to-all(f32[8,4,8,128]{3,2,1,0:T(8,128)S(1)} %bitcast.6), channel_id=1, replica_groups=mesh['sub'=8,'band'=16] {'sub'}, dimensions={0} | all-to-all | bytes 262144 | tf_op jit(solution)/shard_map/all_to_all | solution.py:405
  50.2 0.2 encode.1
  50.5 20.6 %all_to_all.16.g_ref = bf16[16,272,128]{2,1,0:T(8,128)(2,1)S(1)} all-to-all(bf16[16,272,128]{2,1,0:T(8,128)(2,1)S(1)} %encode.1), channel_id=1, replica_groups=mesh['sub'=8,'band'=16] {'band'}, dimensions={0} | all-to-all | bytes 2228224 | tf_op jit(solution)/shard_map/all_to_all | solution.py:406
  71.1 0.0 copy-done
  71.1 2.0 %place.1 = f32[4,128,1024]{2,1,0:T(8,128)} custom-call(bf16[16,272,128]{2,1,0:T(8,128)(2,1)S(1)} %all_to_all.16.g_ref, f32[4,128,1024]{2,1,0:T(8,128)S(1)} %copy-done), custom_call_target="tpu_custom_call" | custom-call | tf_op jit(solution)/shard_map/place/pallas_call | solution.py:378
  (1 shorter events, 0.0 us)
Async XLA Ops:
  1.9 16.1 %all-to-all-start = ((f32[16,16,256]{2,1,0:T(8,128)}), f32[16,16,256]{2,1,0:T(8,128)S(1)}, u32[]{:S(2)}, u32[]{:S(2)}) async-start(f32[16,16,256]{2,1,0:T(8,128)} %spread.1), calls=%async_computation | async-start | bytes 524288 | tf_op jit(solution)/shard_map/all_to_all | solution.py:393
  12.7 13.2 %collective-permute-start.2 = (f32[256,128]{1,0:T(8,128)}, f32[256,128]{1,0:T(8,128)S(1)}, u32[]{:S(2)}, u32[]{:S(2)}) collective-permute-start(f32[256,128]{1,0:T(8,128)} %get-tuple-element.24), channel_id=1, source_target_pairs={{0,32},{16,48},{32,64},{48,80},{64,96},{80,112},{96,0},{112,16},{1... | collective-permute-start | bytes 393224 | tf_op jit(solution)/shard_map/ppermute | solution.py:396
  13.9 12.0 %collective-permute-start.3 = (f32[256,128]{1,0:T(8,128)}, f32[256,128]{1,0:T(8,128)S(1)}, u32[]{:S(2)}, u32[]{:S(2)}) collective-permute-start(f32[256,128]{1,0:T(8,128)} %get-tuple-element.25), channel_id=1, source_target_pairs={{0,64},{16,80},{32,96},{48,112},{64,0},{80,16},{96,32},{112,48},{1... | collective-permute-start | bytes 393224 | tf_op jit(solution)/shard_map/ppermute | solution.py:396
  16.3 9.5 %collective-permute-start.4 = (f32[256,128]{1,0:T(8,128)}, f32[256,128]{1,0:T(8,128)S(1)}, u32[]{:S(2)}, u32[]{:S(2)}) collective-permute-start(f32[256,128]{1,0:T(8,128)} %get-tuple-element.26), channel_id=1, source_target_pairs={{0,96},{16,112},{32,0},{48,16},{64,32},{80,48},{96,64},{112,80},{1... | collective-permute-start | bytes 393224 | tf_op jit(solution)/shard_map/ppermute | solution.py:396
  18.8 7.4 %collective-permute-start.1 = (bf16[384,128]{1,0:T(8,128)(2,1)S(1)}, bf16[384,128]{1,0:T(8,128)(2,1)S(1)}, u32[]{:S(2)}, u32[]{:S(2)}) collective-permute-start(bf16[384,128]{1,0:T(8,128)(2,1)S(1)} %pad_maximum_fusion.refs_3_), channel_id=1, source_target_pairs={{16,0},{32,16},{48,32},{64,48},{80,64},{96,80},{112,96},{17,1},{33... | collective-permute-start | bytes 294920 | tf_op jit(solution)/shard_map/ppermute | solution.py:400
  22.8 4.6 %collective-permute-start = (bf16[384,128]{1,0:T(8,128)(2,1)S(1)}, bf16[384,128]{1,0:T(8,128)(2,1)S(1)}, u32[]{:S(2)}, u32[]{:S(2)}) collective-permute-start(bf16[384,128]{1,0:T(8,128)(2,1)S(1)} %pad_maximum_fusion.refs_3_), channel_id=1, source_target_pairs={{0,16},{16,32},{32,48},{48,64},{64,80},{80,96},{96,112},{1,17},{17... | collective-permute-start | bytes 294920 | tf_op jit(solution)/shard_map/ppermute | solution.py:399
  27.4 0.9 %copy-start.1 = (f32[256,128]{1,0:T(8,128)S(1)}, f32[256,128]{1,0:T(8,128)}, u32[]{:S(2)}) copy-start(f32[256,128]{1,0:T(8,128)} %get-tuple-element.27.r0) | copy-start | bytes 393220
  28.4 1.8 %collective-permute-start.5 = (f32[768,128]{1,0:T(8,128)S(1)}, f32[768,128]{1,0:T(8,128)S(1)}, u32[]{:S(2)}, u32[]{:S(2)}) collective-permute-start(f32[768,128]{1,0:T(8,128)S(1)} %get-tuple-element.32), channel_id=1, source_target_pairs={{0,16},{16,0},{32,48},{48,32},{64,80},{80,64},{96,112},{112,96},{1... | collective-permute-start | bytes 1179656 | tf_op jit(solution)/shard_map/ppermute | solution.py:403
  39.4 31.6 %copy-start = (f32[4,128,1024]{2,1,0:T(8,128)S(1)}, f32[4,128,1024]{2,1,0:T(8,128)}, u32[]{:S(2)}) copy-start(f32[4,128,1024]{2,1,0:T(8,128)} %c_ref.1) | copy-start | bytes 6291460

commit v12 on v11

--- a/solution.py
+++ b/solution.py
@@ -26,7 +26,7 @@
 
 
 def refine_kernel(pos_ref, *refs):
-    mine_ref, other_ref, hp_ref, seen_ref, above_ref, below_ref, out_ref, c_ref, ms_ref, m0, m1, f0, f1, b0, b1, c1_ref, g_ref, hs0, hs1, w0, w1 = refs
+    mine_ref, other_ref, hp_ref, seen_ref, cross_ref, out_ref, c_ref, ms_ref, m0, m1, f0, f1, b0, b1, c1_ref, g_ref, hs0, hs1, w0, w1 = refs
     s = pos_ref[0] // 16
     b = pos_ref[0] % 16
     core = s % 2
@@ -36,11 +36,18 @@
         theirs = pl.multiple_of((2 * chip + 1 - core) * (4 * CROWS), 4 * CROWS)
         c_ref[pl.ds(mine, 4 * CROWS), :] = mine_ref[d * 4 * CROWS : (d + 1) * 4 * CROWS]
         c_ref[pl.ds(theirs, 4 * CROWS), :] = other_ref[d * 4 * CROWS : (d + 1) * 4 * CROWS]
+
+    def neighbours(low, high):
+        theirs = other_ref[16 * CROWS + low : 16 * CROWS + high]
+        across = cross_ref[low:high].astype(f32)
+        flag = jnp.zeros((high - low, LANES), jnp.int32) + core
+        return jnp.where(flag == 0, across, theirs), jnp.where(flag == 0, theirs, across)
+
+    ms_above, ms_below = neighbours(256, 384)
     for k in range(8):
-        at = slice(256 + 16 * k, 272 + 16 * k)
-        ms_ref[32 * k : 32 * k + 8, :] = above_ref[at, :].astype(f32)[8:16]
-        ms_ref[32 * k + 8 : 32 * k + 24, :] = seen_ref[at, :].astype(f32)
-        ms_ref[32 * k + 24 : 32 * k + 32, :] = below_ref[at, :].astype(f32)[0:8]
+        ms_ref[32 * k : 32 * k + 8, :] = ms_above[16 * k + 8 : 16 * k + 16]
+        ms_ref[32 * k + 8 : 32 * k + 24, :] = seen_ref[256 + 16 * k : 272 + 16 * k].astype(f32)
+        ms_ref[32 * k + 24 : 32 * k + 32, :] = ms_below[16 * k : 16 * k + 8]
     bk = (b0, b1)
     m = (m0, m1)
     f = (f0, f1)
@@ -48,9 +55,10 @@
     w = (w0, w1)
     for h in range(2):
         at = slice(h * 128, h * 128 + 128)
-        hst[h][0:72, :] = above_ref[at, :].astype(f32).T[24:96]
+        above, below = neighbours(h * 128, h * 128 + 128)
+        hst[h][0:72, :] = above.T[24:96]
         hst[h][72:168, :] = hp_ref[at, 0:128].T[0:96]
-        hst[h][168:240, :] = below_ref[at, :].astype(f32).T[0:72]
+        hst[h][168:240, :] = below.T[0:72]
         w[h][...] = hp_ref[at, 128:256].T
     basis = jnp.concatenate([w0[81:113, :], w1[81:113, :]], axis=1).astype(bf16)
     response = jnp.concatenate([w0[113:121, :], w1[113:121, :]], axis=1).astype(bf16)
@@ -173,12 +181,12 @@
         out_ref[pl.ds(r, 32, stride=8), :] = total
 
 
-def refine(pos, mine, other, hp, seen, above, below):
+def refine(pos, mine, other, hp, seen, cross):
     vmem = pl.BlockSpec(memory_space=pltpu.VMEM)
     return pl.pallas_call(
         refine_kernel,
         out_shape=jax.ShapeDtypeStruct((32 * 8, LANES), f32),
-        in_specs=[pl.BlockSpec(memory_space=pltpu.SMEM)] + [vmem] * 6,
+        in_specs=[pl.BlockSpec(memory_space=pltpu.SMEM)] + [vmem] * 5,
         out_specs=vmem,
         scratch_shapes=[
             pltpu.VMEM((32 * CROWS, LANES), f32),
@@ -199,7 +207,7 @@
         compiler_params=pltpu.CompilerParams(vmem_limit_bytes=40 * 2**20),
         cost_estimate=pl.CostEstimate(flops=400_000_000, bytes_accessed=2_000_000, transcendentals=0),
         name="refine",
-    )(pos, mine, other, hp, seen, above, below)
+    )(pos, mine, other, hp, seen, cross)
 
 
 def pack_kernel(pos_ref, ca_ref, cb_ref, ma_ref, mb_ref, *rest_refs):
@@ -298,7 +306,8 @@
     )(hs_image, kernels, basis, response)
 
 
-def hand_kernel(pos_ref, r0, r1, r2, r3, mine_ref, other_ref):
+def hand_kernel(pos_ref, r0, r1, r2, r3, seen_ref, mine_ref, other_ref):
+    other_ref[16 * CROWS : 16 * CROWS + 384] = seen_ref[...].astype(f32)
     skip = 16 * (pos_ref[0] // 16 % 2)
     for d, region in enumerate((r0, r1, r2, r3)):
         for k in range(4):
@@ -307,17 +316,20 @@
             other_ref[at : at + CROWS] = region[pl.ds(pl.multiple_of(64 * k + 16 - skip, 16), CROWS), :]
 
 
-def hand(pos, tiles):
+def hand(pos, tiles, seen):
     vmem = pl.BlockSpec(memory_space=pltpu.VMEM)
     return pl.pallas_call(
         hand_kernel,
-        out_shape=(jax.ShapeDtypeStruct((16 * CROWS, LANES), f32),) * 2,
-        in_specs=[pl.BlockSpec(memory_space=pltpu.SMEM)] + [vmem] * 4,
+        out_shape=(
+            jax.ShapeDtypeStruct((16 * CROWS, LANES), f32),
+            jax.ShapeDtypeStruct((16 * CROWS + 384, LANES), f32),
+        ),
+        in_specs=[pl.BlockSpec(memory_space=pltpu.SMEM)] + [vmem] * 5,
         out_specs=(vmem, vmem),
         compiler_params=pltpu.CompilerParams(vmem_limit_bytes=16 * 2**20),
         cost_estimate=pl.CostEstimate(flops=1_000_000, bytes_accessed=800_000, transcendentals=0),
         name="hand",
-    )(pos, *tiles)
+    )(pos, *tiles, seen)
 
 
 def encode_kernel(d_ref, out_ref):
@@ -396,12 +408,11 @@
         lax.ppermute(tiles[d], "sub", [(i, (i + 2 * d) % 8) for i in range(8)]) for d in range(1, 4)
     ]
     seen = jnp.concatenate([hp[:, 0:128].astype(bf16), near], axis=0)
-    above = lax.ppermute(seen, "sub", [(i, i + 1) for i in range(7)])
-    below = lax.ppermute(seen, "sub", [(i + 1, i) for i in range(7)])
-    above, below, *tiles = lax.optimization_barrier((above, below, *tiles))
-    mine, other = hand(pos, tiles)
+    cross = lax.ppermute(seen, "sub", [(1, 2), (2, 1), (3, 4), (4, 3), (5, 6), (6, 5)])
+    cross, *tiles = lax.optimization_barrier((cross, *tiles))
+    mine, other = hand(pos, tiles, seen)
     other = lax.ppermute(other, "sub", [(i, i ^ 1) for i in range(8)])
-    new = refine(pos, mine, other, hp, seen, above, below)
+    new = refine(pos, mine, other, hp, seen, cross)
     owned = lax.all_to_all(new.reshape(8, 4, 8, LANES), "sub", split_axis=0, concat_axis=0, tiled=True)
     gathered = lax.all_to_all(encode(owned), "band", split_axis=0, concat_axis=0, tiled=True)
     return place(gathered, coeffs_in)

time: 74.2 us -> 72.2 us (0.973)
  starting transfers between devices: 20.5 us -> 18.6 us
  blocking collectives: 31.4 us -> 30.4 us
  waiting for transfers between devices: 3.83 us -> 4.78 us
    ppermute x2 -> x1, starting transfers between devices: 7.02 us -> 5.1 us  [per_device(): lax.ppermute(seen, 'sub', [(1, 2), (2, 1), (3, 4), (4, 3), (5, 6), (6, 5)])]
    ppermute x2 -> x1, waiting for transfers between devices: 1.59 us -> 2.25 us  [per_device(): lax.ppermute(seen, 'sub', [(1, 2), (2, 1), (3, 4), (4, 3), (5, 6), (6, 5)])]
  transfers between devices with their start and end apart: 7 -> 6, of which waited for: 4 -> 3; matrix products, arithmetic and copies ran while one was open for 1% -> 1% of each run, Pallas kernels for 3% -> 3%
where the time goes in v12:
time: 72.2 us; the launch traced here: 71.1 us
  blocking collectives  30.4 us (42%)
  starting transfers between devices  18.6 us (26%)
  Pallas kernels  15.5 us (21%)
  waiting for transfers between devices  4.78 us (7%)
  local copies, waits for them, and re-layouts  0.92 us (1%)
  other arithmetic  0.77 us (1%)
    all_to_all x1, blocking collectives, per_device(): lax.all_to_all(encode(owned), 'band', split_axis=0, concat_axis=0, tiled=...  20.3 us
    all_to_all x1, blocking collectives, per_device(): lax.all_to_all(new.reshape(8, 4, 8, LANES), 'sub', split_axis=0, concat_a...  10.1 us
    pallas_call x1, Pallas kernels, refine(): pl.pallas_call(refine_kernel, out_shape=jax.ShapeDtypeStruct((32 * 8, LAN...  9.21 us
    all_to_all x1, starting transfers between devices, per_device(): lax.all_to_all(sent, 'band', split_axis=0, concat_axis=0, tiled=True)  8.6 us
    ppermute x1, starting transfers between devices, per_device(): lax.ppermute(seen, 'sub', [(1, 2), (2, 1), (3, 4), (4, 3), (5, 6), (6, 5)])  5.1 us
    ppermute x3, starting transfers between devices, per_device(): lax.ppermute(tiles[d], 'sub', [(i, (i + 2 * d) % 8) for i in range(8)])  4.81 us
    ppermute x1, waiting for transfers between devices, per_device(): lax.ppermute(seen, 'sub', [(1, 2), (2, 1), (3, 4), (4, 3), (5, 6), (6, 5)])  2.25 us
    pallas_call x1, Pallas kernels, pack(): pl.pallas_call(pack_kernel, out_shape=(jax.ShapeDtypeStruct((256, LANES),...  2.2 us
  transfers between devices with their start and end apart: 6, of which 3 were waited for; matrix products, arithmetic and copies ran while one was open for 1% of the time, Pallas kernels for 3%

profile of v12, /device:TPU:1, one launch (start us, length us, event | category | flops | bytes accessed | tf_op | source)
XLA Modules:
  0.0 71.1 jit_solution(5486334147325339068)
XLA Ops:
  0.0 1.9 %spread.1 = f32[16,16,256]{2,1,0:T(8,128)} custom-call(bf16[14,4,256]{2,1,0:T(4,128)(2,1)} %hs_ref.1, f32[9,14,9]{2,1,0:T(8,128)} %bitcast.7, bf16[14,32]{1,0:T(8,128)(2,1)} %basis_ref.1, bf16[8,14]{1,0:T(8,128)(2,1)} %response_ref.1), custom_call_target="tpu_custom_call" | custom-call | flops 1000000 | bytes 1000000 | tf_op jit(solution)/shard_map/spread/pallas_call | solution.py:298
  1.9 8.6 %all-to-all-start = ((f32[16,16,256]{2,1,0:T(8,128)}), f32[16,16,256]{2,1,0:T(8,128)S(1)}, u32[]{:S(2)}, u32[]{:S(2)}) async-start(f32[16,16,256]{2,1,0:T(8,128)} %spread.1), calls=%async_computation | async-start | bytes 524288 | tf_op jit(solution)/shard_map/all_to_all | solution.py:405
  10.5 2.2 %pack.1 = (f32[256,128]{1,0:T(8,128)}, f32[256,128]{1,0:T(8,128)}, f32[256,128]{1,0:T(8,128)}, f32[256,128]{1,0:T(8,128)}, bf16[128,128]{1,0:T(8,128)(2,1)}) custom-call(s32[1]{0:T(128)} %bitcast.1.pos_ref, f32[4,128,1024]{2,1,0:T(8,128)} %c_ref.1, f32[4,128,1024]{2,1,0:T(8,128)} %c_ref.1, bf16[8,16,1024]{2,1,0:T(8,128)(2,1)} %mb_ref.1, ...), custom_call_target="tpu_custom_call" | custom-call | flops 100000000 | bytes 1600000 | tf_op jit(solution)/shard_map/pack/pallas_call | solution.py:254
  12.7 1.2 %collective-permute-start.1 = (f32[256,128]{1,0:T(8,128)}, f32[256,128]{1,0:T(8,128)S(1)}, u32[]{:S(2)}, u32[]{:S(2)}) collective-permute-start(f32[256,128]{1,0:T(8,128)} %get-tuple-element.23), channel_id=1, source_target_pairs={{0,32},{16,48},{32,64},{48,80},{64,96},{80,112},{96,0},{112,16},{1... | collective-permute-start | bytes 393224 | tf_op jit(solution)/shard_map/ppermute | solution.py:408
  13.9 2.4 %collective-permute-start.2 = (f32[256,128]{1,0:T(8,128)}, f32[256,128]{1,0:T(8,128)S(1)}, u32[]{:S(2)}, u32[]{:S(2)}) collective-permute-start(f32[256,128]{1,0:T(8,128)} %get-tuple-element.24), channel_id=1, source_target_pairs={{0,64},{16,80},{32,96},{48,112},{64,0},{80,16},{96,32},{112,48},{1... | collective-permute-start | bytes 393224 | tf_op jit(solution)/shard_map/ppermute | solution.py:408
  16.3 1.1 %collective-permute-start.3 = (f32[256,128]{1,0:T(8,128)}, f32[256,128]{1,0:T(8,128)S(1)}, u32[]{:S(2)}, u32[]{:S(2)}) collective-permute-start(f32[256,128]{1,0:T(8,128)} %get-tuple-element.25), channel_id=1, source_target_pairs={{0,96},{16,112},{32,0},{48,16},{64,32},{80,48},{96,64},{112,80},{1... | collective-permute-start | bytes 393224 | tf_op jit(solution)/shard_map/ppermute | solution.py:408
  17.5 0.5 all-to-all-done
  18.0 0.8 %pad_maximum_fusion.seen_ref.refs_3_ = bf16[384,128]{1,0:T(8,128)(2,1)S(1)} fusion(bf16[128,128]{1,0:T(8,128)(2,1)} %get-tuple-element.21, bf16[256,128]{1,0:T(8,128)(2,1)S(1)} %slice.7), kind=kLoop, calls=%fused_computation.1 | loop fusion | flops 196608 | bytes 196608 | tf_op jit(solution)/shard_map/concatenate | solution.py:410
  18.8 5.1 %collective-permute-start = (bf16[384,128]{1,0:T(8,128)(2,1)S(1)}, bf16[384,128]{1,0:T(8,128)(2,1)S(1)}, u32[]{:S(2)}, u32[]{:S(2)}) collective-permute-start(bf16[384,128]{1,0:T(8,128)(2,1)S(1)} %pad_maximum_fusion.seen_ref.refs_3_), channel_id=1, source_target_pairs={{16,32},{32,16},{48,64},{64,48},{80,96},{96,80},{17,33},{33,17},{4... | collective-permute-start | bytes 294920 | tf_op jit(solution)/shard_map/ppermute | solution.py:411
  23.9 0.0 collective-permute-done.1.r1
  23.9 0.0 collective-permute-done.2.r2
  23.9 0.0 collective-permute-done.3.r3
  23.9 2.3 %collective-permute-done.refs_4_ = bf16[384,128]{1,0:T(8,128)(2,1)S(1)} collective-permute-done((bf16[384,128]{1,0:T(8,128)(2,1)S(1)}, bf16[384,128]{1,0:T(8,128)(2,1)S(1)}, u32[]{:S(2)}, u32[]{:S(2)}) %collective-permute-start) | collective-permute-done | bytes 98336 | tf_op jit(solution)/shard_map/ppermute | solution.py:411
  26.2 0.0 copy-start.1
  26.2 0.9 %copy-done.1 = f32[256,128]{1,0:T(8,128)S(1)} copy-done((f32[256,128]{1,0:T(8,128)S(1)}, f32[256,128]{1,0:T(8,128)}, u32[]{:S(2)}) %copy-start.1) | copy-done | bytes 131096
  27.1 0.1 hand.1
  27.2 0.1 collective-permute-start.4
  27.3 2.0 %collective-permute-done.4.refs_1_ = f32[1152,128]{1,0:T(8,128)S(1)} collective-permute-done((f32[1152,128]{1,0:T(8,128)S(1)}, f32[1152,128]{1,0:T(8,128)S(1)}, u32[]{:S(2)}, u32[]{:S(2)}) %collective-permute-start.4) | collective-permute-done | bytes 589856 | tf_op jit(solution)/shard_map/ppermute | solution.py:414
  29.2 9.2 %refine.1 = f32[256,128]{1,0:T(8,128)S(1)} custom-call(s32[1]{0:T(128)} %bitcast.1.pos_ref, f32[768,128]{1,0:T(8,128)S(1)} %get-tuple-element.30.refs_0_, f32[1152,128]{1,0:T(8,128)S(1)} %collective-permute-done.4.refs_1_, f32[256,256]{1,0:T(8,128)S(1)} %bitcast.5, bf16[384,128]{1,0:T(8,128)(2,1)S(1)} %pad_maximum_fusion.seen_ref.refs_3_, ...), custom_call_target="tpu_custom_call" | custom-call | flops 400000000 | bytes 2000000 | tf_op jit(solution)/shard_map/refine/pallas_call | solution.py:186
  38.5 0.0 copy-start
  38.5 10.1 %all_to_all.15.d_ref = f32[8,4,8,128]{3,2,1,0:T(8,128)S(1)} all-to-all(f32[8,4,8,128]{3,2,1,0:T(8,128)S(1)} %bitcast.6), channel_id=1, replica_groups=mesh['sub'=8,'band'=16] {'sub'}, dimensions={0} | all-to-all | bytes 262144 | tf_op jit(solution)/shard_map/all_to_all | solution.py:416
  48.6 0.2 encode.1
  48.8 20.3 %all_to_all.16.g_ref = bf16[16,272,128]{2,1,0:T(8,128)(2,1)S(1)} all-to-all(bf16[16,272,128]{2,1,0:T(8,128)(2,1)S(1)} %encode.1), channel_id=1, replica_groups=mesh['sub'=8,'band'=16] {'band'}, dimensions={0} | all-to-all | bytes 2228224 | tf_op jit(solution)/shard_map/all_to_all | solution.py:417
  69.1 0.0 copy-done
  69.1 2.0 %place.1 = f32[4,128,1024]{2,1,0:T(8,128)} custom-call(bf16[16,272,128]{2,1,0:T(8,128)(2,1)S(1)} %all_to_all.16.g_ref, f32[4,128,1024]{2,1,0:T(8,128)S(1)} %copy-done), custom_call_target="tpu_custom_call" | custom-call | tf_op jit(solution)/shard_map/place/pallas_call | solution.py:390
  (1 shorter events, 0.0 us)
Async XLA Ops:
  1.9 16.1 %all-to-all-start = ((f32[16,16,256]{2,1,0:T(8,128)}), f32[16,16,256]{2,1,0:T(8,128)S(1)}, u32[]{:S(2)}, u32[]{:S(2)}) async-start(f32[16,16,256]{2,1,0:T(8,128)} %spread.1), calls=%async_computation | async-start | bytes 524288 | tf_op jit(solution)/shard_map/all_to_all | solution.py:405
  12.7 11.2 %collective-permute-start.1 = (f32[256,128]{1,0:T(8,128)}, f32[256,128]{1,0:T(8,128)S(1)}, u32[]{:S(2)}, u32[]{:S(2)}) collective-permute-start(f32[256,128]{1,0:T(8,128)} %get-tuple-element.23), channel_id=1, source_target_pairs={{0,32},{16,48},{32,64},{48,80},{64,96},{80,112},{96,0},{112,16},{1... | collective-permute-start | bytes 393224 | tf_op jit(solution)/shard_map/ppermute | solution.py:408
  13.9 10.0 %collective-permute-start.2 = (f32[256,128]{1,0:T(8,128)}, f32[256,128]{1,0:T(8,128)S(1)}, u32[]{:S(2)}, u32[]{:S(2)}) collective-permute-start(f32[256,128]{1,0:T(8,128)} %get-tuple-element.24), channel_id=1, source_target_pairs={{0,64},{16,80},{32,96},{48,112},{64,0},{80,16},{96,32},{112,48},{1... | collective-permute-start | bytes 393224 | tf_op jit(solution)/shard_map/ppermute | solution.py:408
  16.3 7.6 %collective-permute-start.3 = (f32[256,128]{1,0:T(8,128)}, f32[256,128]{1,0:T(8,128)S(1)}, u32[]{:S(2)}, u32[]{:S(2)}) collective-permute-start(f32[256,128]{1,0:T(8,128)} %get-tuple-element.25), channel_id=1, source_target_pairs={{0,96},{16,112},{32,0},{48,16},{64,32},{80,48},{96,64},{112,80},{1... | collective-permute-start | bytes 393224 | tf_op jit(solution)/shard_map/ppermute | solution.py:408
  18.8 7.4 %collective-permute-start = (bf16[384,128]{1,0:T(8,128)(2,1)S(1)}, bf16[384,128]{1,0:T(8,128)(2,1)S(1)}, u32[]{:S(2)}, u32[]{:S(2)}) collective-permute-start(bf16[384,128]{1,0:T(8,128)(2,1)S(1)} %pad_maximum_fusion.seen_ref.refs_3_), channel_id=1, source_target_pairs={{16,32},{32,16},{48,64},{64,48},{80,96},{96,80},{17,33},{33,17},{4... | collective-permute-start | bytes 294920 | tf_op jit(solution)/shard_map/ppermute | solution.py:411
  26.2 0.9 %copy-start.1 = (f32[256,128]{1,0:T(8,128)S(1)}, f32[256,128]{1,0:T(8,128)}, u32[]{:S(2)}) copy-start(f32[256,128]{1,0:T(8,128)} %get-tuple-element.26.r0) | copy-start | bytes 393220
  27.2 2.1 %collective-permute-start.4 = (f32[1152,128]{1,0:T(8,128)S(1)}, f32[1152,128]{1,0:T(8,128)S(1)}, u32[]{:S(2)}, u32[]{:S(2)}) collective-permute-start(f32[1152,128]{1,0:T(8,128)S(1)} %get-tuple-element.31), channel_id=1, source_target_pairs={{0,16},{16,0},{32,48},{48,32},{64,80},{80,64},{96,112},{112,96},{1... | collective-permute-start | bytes 1769480 | tf_op jit(solution)/shard_map/ppermute | solution.py:414
  38.5 30.7 %copy-start = (f32[4,128,1024]{2,1,0:T(8,128)S(1)}, f32[4,128,1024]{2,1,0:T(8,128)}, u32[]{:S(2)}) copy-start(f32[4,128,1024]{2,1,0:T(8,128)} %c_ref.1) | copy-start | bytes 6291460

commit v13 on v12

--- a/solution.py
+++ b/solution.py
@@ -210,8 +210,29 @@
     )(pos, mine, other, hp, seen, cross)
 
 
-def pack_kernel(pos_ref, ca_ref, cb_ref, ma_ref, mb_ref, *rest_refs):
-    near_ref, wide_ref = rest_refs[4:]
+def spread(hs_ref, k_ref, basis_ref, response_ref, sent_ref):
+    lane = lax.broadcasted_iota(jnp.int32, (1, LANES), 1)
+    hs = hs_ref[...].astype(f32)
+    rows = [jnp.concatenate([hs[:, i, :], jnp.zeros((2, 256), f32)], axis=0) for i in range(4)]
+    sent_ref[0, :, 128:256] = jnp.zeros((16, 128), f32)
+    for a in range(9):
+        sent_ref[0, 0:14, 128 + 9 * a : 137 + 9 * a] = k_ref[a]
+    sent_ref[0, 0:14, 209:241] = basis_ref[...].astype(f32)
+    sent_ref[0, 0:14, 241:249] = response_ref[...].astype(f32).T
+    params = sent_ref[0, :, 128:256]
+    for t in range(16):
+        total = jnp.zeros((16, LANES), f32)
+        for i in range(4):
+            moved = pltpu.roll(rows[i], (24 * i + 3 - 16 * t) % 256, 1)[:, 0:128]
+            total = jnp.where((lane >= 24 * i) & (lane < 24 * i + 24), moved, total)
+        sent_ref[t, :, 0:128] = total
+        if t:
+            sent_ref[t, :, 128:256] = params
+
+
+def pack_kernel(pos_ref, ca_ref, cb_ref, ma_ref, mb_ref, hs_ref, k_ref, basis_ref, response_ref, *rest_refs):
+    spread(hs_ref, k_ref, basis_ref, response_ref, rest_refs[5])
+    near_ref, _, wide_ref = rest_refs[4:]
     s = pos_ref[0] // 16
     b = pos_ref[0] % 16
     off = jnp.where(b % 2 == 0, 112, 48)
@@ -244,7 +265,7 @@
             rest_refs[d][64 * k : 64 * k + 64] = wide_ref[k, at, :]
 
 
-def pack(pos, coeffs_in, ms_image):
+def pack(pos, coeffs_in, ms_image, hs_image, kernels, basis, response):
     def low(i, p):
         return (0, 0, jnp.maximum((p[0] % 16 + 1) // 2 - 1, 0))
 
@@ -253,7 +274,10 @@
 
     return pl.pallas_call(
         pack_kernel,
-        out_shape=(jax.ShapeDtypeStruct((256, LANES), f32),) * 4 + (jax.ShapeDtypeStruct((128, LANES), bf16),),
+        out_shape=(jax.ShapeDtypeStruct((256, LANES), f32),) * 4 + (
+            jax.ShapeDtypeStruct((128, LANES), bf16),
+            jax.ShapeDtypeStruct((16, 16, 256), f32),
+        ),
         grid_spec=pltpu.PrefetchScalarGridSpec(
             num_scalar_prefetch=1,
             grid=(1,),
@@ -262,48 +286,22 @@
                 pl.BlockSpec((4, 128, LANES), high),
                 pl.BlockSpec((8, 16, LANES), low),
                 pl.BlockSpec((8, 16, LANES), high),
+                pl.BlockSpec((14, 4, 256), lambda i, p: (0, 0, 0)),
+                pl.BlockSpec((9, 14, 9), lambda i, p: (0, 0, 0)),
+                pl.BlockSpec((14, 32), lambda i, p: (0, 0)),
+                pl.BlockSpec((8, 14), lambda i, p: (0, 0)),
             ],
             out_specs=(pl.BlockSpec((256, LANES), lambda i, p: (0, 0)),) * 4
-            + (pl.BlockSpec((128, LANES), lambda i, p: (0, 0)),),
+            + (
+                pl.BlockSpec((128, LANES), lambda i, p: (0, 0)),
+                pl.BlockSpec((16, 16, 256), lambda i, p: (0, 0, 0)),
+            ),
             scratch_shapes=[pltpu.VMEM((4, 160, LANES), f32)],
         ),
         compiler_params=pltpu.CompilerParams(vmem_limit_bytes=60 * 2**20),
         cost_estimate=pl.CostEstimate(flops=100_000_000, bytes_accessed=1_600_000, transcendentals=0),
         name="pack",
-    )(pos, coeffs_in, coeffs_in, ms_image, ms_image)
-
-
-def spread_kernel(hs_ref, k_ref, basis_ref, response_ref, sent_ref):
-    lane = lax.broadcasted_iota(jnp.int32, (1, LANES), 1)
-    hs = hs_ref[...].astype(f32)
-    rows = [jnp.concatenate([hs[:, i, :], jnp.zeros((2, 256), f32)], axis=0) for i in range(4)]
-    sent_ref[0, :, 128:256] = jnp.zeros((16, 128), f32)
-    for a in range(9):
-        sent_ref[0, 0:14, 128 + 9 * a : 137 + 9 * a] = k_ref[a]
-    sent_ref[0, 0:14, 209:241] = basis_ref[...].astype(f32)
-    sent_ref[0, 0:14, 241:249] = response_ref[...].astype(f32).T
-    params = sent_ref[0, :, 128:256]
-    for t in range(16):
-        total = jnp.zeros((16, LANES), f32)
-        for i in range(4):
-            moved = pltpu.roll(rows[i], (24 * i + 3 - 16 * t) % 256, 1)[:, 0:128]
-            total = jnp.where((lane >= 24 * i) & (lane < 24 * i + 24), moved, total)
-        sent_ref[t, :, 0:128] = total
-        if t:
-            sent_ref[t, :, 128:256] = params
-
-
-def spread(hs_image, kernels, basis, response):
-    vmem = pl.BlockSpec(memory_space=pltpu.VMEM)
-    return pl.pallas_call(
-        spread_kernel,
-        out_shape=jax.ShapeDtypeStruct((16, 16, 256), f32),
-        in_specs=[vmem] * 4,
-        out_specs=vmem,
-        compiler_params=pltpu.CompilerParams(vmem_limit_bytes=60 * 2**20),
-        cost_estimate=pl.CostEstimate(flops=1_000_000, bytes_accessed=1_000_000, transcendentals=0),
-        name="spread",
-    )(hs_image, kernels, basis, response)
+    )(pos, coeffs_in, coeffs_in, ms_image, ms_image, hs_image, kernels, basis, response)
 
 
 def hand_kernel(pos_ref, r0, r1, r2, r3, seen_ref, mine_ref, other_ref):
@@ -400,10 +398,8 @@
 
 def per_device(coeffs_in, basis, kernels, response, hs_image, ms_image):
     pos = (lax.axis_index("sub") * 16 + lax.axis_index("band")).astype(jnp.int32).reshape(1)
-    sent = spread(hs_image, kernels.transpose(1, 0, 2), basis, response)
-    sent, pos = lax.optimization_barrier((sent, pos))
+    *tiles, near, sent = pack(pos, coeffs_in, ms_image, hs_image, kernels.transpose(1, 0, 2), basis, response)
     hp = lax.all_to_all(sent, "band", split_axis=0, concat_axis=0, tiled=True).reshape(256, 256)
-    *tiles, near = pack(pos, coeffs_in, ms_image)
     tiles = [tiles[0]] + [
         lax.ppermute(tiles[d], "sub", [(i, (i + 2 * d) % 8) for i in range(8)]) for d in range(1, 4)
     ]

time: 72.2 us -> 71.6 us (level)
  waiting for transfers between devices: 4.78 us -> 6.91 us
  Pallas kernels: 15.5 us -> 13.8 us
  blocking collectives: 30.4 us -> 29.5 us
    all_to_all x1, waiting for transfers between devices: 0.52 us -> 2.66 us  [per_device(): lax.all_to_all(sent, 'band', split_axis=0, concat_axis=0, tiled=True)]
    pallas_call x1 -> x0, Pallas kernels: 1.86 us -> none  [spread(): pl.pallas_call(spread_kernel, out_shape=jax.ShapeDtypeStruct((16, 16, 256...]
    all_to_all x1, blocking collectives: 20.3 us -> 19.4 us  [per_device(): lax.all_to_all(encode(owned), 'band', split_axis=0, concat_axis=0, tiled=...]
  transfers between devices with their start and end apart: 6 -> 6, of which waited for: 3 -> 3; matrix products, arithmetic and copies ran while one was open for 1% -> 1% of each run, Pallas kernels for 3% -> 0%
where the time goes in v13:
time: 71.6 us; the launch traced here: 70.6 us
  blocking collectives  29.5 us (41%)
  starting transfers between devices  18.7 us (26%)
  Pallas kernels  13.8 us (19%)
  waiting for transfers between devices  6.91 us (10%)
  local copies, waits for them, and re-layouts  0.92 us (1%)
  other arithmetic  0.77 us (1%)
    all_to_all x1, blocking collectives, per_device(): lax.all_to_all(encode(owned), 'band', split_axis=0, concat_axis=0, tiled=...  19.4 us
    all_to_all x1, blocking collectives, per_device(): lax.all_to_all(new.reshape(8, 4, 8, LANES), 'sub', split_axis=0, concat_a...  10.1 us
    pallas_call x1, Pallas kernels, refine(): pl.pallas_call(refine_kernel, out_shape=jax.ShapeDtypeStruct((32 * 8, LAN...  9.21 us
    all_to_all x1, starting transfers between devices, per_device(): lax.all_to_all(sent, 'band', split_axis=0, concat_axis=0, tiled=True)  8.6 us
    ppermute x1, starting transfers between devices, per_device(): lax.ppermute(seen, 'sub', [(1, 2), (2, 1), (3, 4), (4, 3), (5, 6), (6, 5)])  5.09 us
    ppermute x3, starting transfers between devices, per_device(): lax.ppermute(tiles[d], 'sub', [(i, (i + 2 * d) % 8) for i in range(8)])  4.88 us
    all_to_all x1, waiting for transfers between devices, per_device(): lax.all_to_all(sent, 'band', split_axis=0, concat_axis=0, tiled=True)  2.66 us
    pallas_call x1, Pallas kernels, pack(): pl.pallas_call(pack_kernel, out_shape=(jax.ShapeDtypeStruct((256, LANES),...  2.29 us
  transfers between devices with their start and end apart: 6, of which 3 were waited for; matrix products, arithmetic and copies ran while one was open for 1% of the time, Pallas kernels for 0%

profile of v13, /device:TPU:1, one launch (start us, length us, event | category | flops | bytes accessed | tf_op | source)
XLA Modules:
  0.0 70.6 jit_solution(14419080002607901201)
XLA Ops:
  0.0 2.3 %pack.1 = (f32[256,128]{1,0:T(8,128)}, f32[256,128]{1,0:T(8,128)}, f32[256,128]{1,0:T(8,128)}, f32[256,128]{1,0:T(8,128)}, bf16[128,128]{1,0:T(8,128)(2,1)}, /*index=5*/f32[16,16,256]{2,1,0:T(8,128)}) custom-call(s32[1]{0:T(128)} %bitcast.pos_ref, f32[4,128,1024]{2,1,0:T(8,128)} %c_ref.1, f32[4,128,1024]{2,1,0:T(8,128)} %c_ref.1, ...), custom_call_target="tpu_custom_call" | custom-call | flops 100000000 | bytes 1600000 | tf_op jit(solution)/shard_map/pack/pallas_call | solution.py:275
  2.3 8.6 %all-to-all-start = ((f32[16,16,256]{2,1,0:T(8,128)}), f32[16,16,256]{2,1,0:T(8,128)S(1)}, u32[]{:S(2)}, u32[]{:S(2)}) async-start(f32[16,16,256]{2,1,0:T(8,128)} %get-tuple-element.18), calls=%async_computation | async-start | bytes 524288 | tf_op jit(solution)/shard_map/all_to_all | solution.py:402
  10.9 1.3 %collective-permute-start.1 = (f32[256,128]{1,0:T(8,128)}, f32[256,128]{1,0:T(8,128)S(1)}, u32[]{:S(2)}, u32[]{:S(2)}) collective-permute-start(f32[256,128]{1,0:T(8,128)} %get-tuple-element.21), channel_id=1, source_target_pairs={{0,32},{16,48},{32,64},{48,80},{64,96},{80,112},{96,0},{112,16},{1... | collective-permute-start | bytes 393224 | tf_op jit(solution)/shard_map/ppermute | solution.py:404
  12.2 2.5 %collective-permute-start.2 = (f32[256,128]{1,0:T(8,128)}, f32[256,128]{1,0:T(8,128)S(1)}, u32[]{:S(2)}, u32[]{:S(2)}) collective-permute-start(f32[256,128]{1,0:T(8,128)} %get-tuple-element.22), channel_id=1, source_target_pairs={{0,64},{16,80},{32,96},{48,112},{64,0},{80,16},{96,32},{112,48},{1... | collective-permute-start | bytes 393224 | tf_op jit(solution)/shard_map/ppermute | solution.py:404
  14.6 1.2 %collective-permute-start.3 = (f32[256,128]{1,0:T(8,128)}, f32[256,128]{1,0:T(8,128)S(1)}, u32[]{:S(2)}, u32[]{:S(2)}) collective-permute-start(f32[256,128]{1,0:T(8,128)} %get-tuple-element.23), channel_id=1, source_target_pairs={{0,96},{16,112},{32,0},{48,16},{64,32},{80,48},{96,64},{112,80},{1... | collective-permute-start | bytes 393224 | tf_op jit(solution)/shard_map/ppermute | solution.py:404
  15.8 2.7 %all-to-all-done = f32[16,16,256]{2,1,0:T(8,128)S(1)} async-done(((f32[16,16,256]{2,1,0:T(8,128)}), f32[16,16,256]{2,1,0:T(8,128)S(1)}, u32[]{:S(2)}, u32[]{:S(2)}) %all-to-all-start) | async-done | bytes 262176 | tf_op jit(solution)/shard_map/all_to_all | solution.py:402
  18.5 0.8 %pad_maximum_fusion.seen_ref.refs_3_ = bf16[384,128]{1,0:T(8,128)(2,1)S(1)} fusion(bf16[128,128]{1,0:T(8,128)(2,1)} %get-tuple-element.19, bf16[256,128]{1,0:T(8,128)(2,1)S(1)} %slice.7), kind=kLoop, calls=%fused_computation.1 | loop fusion | flops 196608 | bytes 196608 | tf_op jit(solution)/shard_map/concatenate | solution.py:406
  19.2 5.1 %collective-permute-start = (bf16[384,128]{1,0:T(8,128)(2,1)S(1)}, bf16[384,128]{1,0:T(8,128)(2,1)S(1)}, u32[]{:S(2)}, u32[]{:S(2)}) collective-permute-start(bf16[384,128]{1,0:T(8,128)(2,1)S(1)} %pad_maximum_fusion.seen_ref.refs_3_), channel_id=1, source_target_pairs={{16,32},{32,16},{48,64},{64,48},{80,96},{96,80},{17,33},{33,17},{4... | collective-permute-start | bytes 294920 | tf_op jit(solution)/shard_map/ppermute | solution.py:407
  24.3 0.0 collective-permute-done.1.r1
  24.3 0.0 collective-permute-done.2.r2
  24.3 0.0 collective-permute-done.3.r3
  24.4 2.3 %collective-permute-done.refs_4_ = bf16[384,128]{1,0:T(8,128)(2,1)S(1)} collective-permute-done((bf16[384,128]{1,0:T(8,128)(2,1)S(1)}, bf16[384,128]{1,0:T(8,128)(2,1)S(1)}, u32[]{:S(2)}, u32[]{:S(2)}) %collective-permute-start) | collective-permute-done | bytes 98336 | tf_op jit(solution)/shard_map/ppermute | solution.py:407
  26.6 0.0 copy-start.1
  26.6 0.9 %copy-done.1 = f32[256,128]{1,0:T(8,128)S(1)} copy-done((f32[256,128]{1,0:T(8,128)S(1)}, f32[256,128]{1,0:T(8,128)}, u32[]{:S(2)}) %copy-start.1) | copy-done | bytes 131096
  27.5 0.1 hand.1
  27.6 0.1 collective-permute-start.4
  27.7 2.0 %collective-permute-done.4.refs_1_ = f32[1152,128]{1,0:T(8,128)S(1)} collective-permute-done((f32[1152,128]{1,0:T(8,128)S(1)}, f32[1152,128]{1,0:T(8,128)S(1)}, u32[]{:S(2)}, u32[]{:S(2)}) %collective-permute-start.4) | collective-permute-done | bytes 589856 | tf_op jit(solution)/shard_map/ppermute | solution.py:410
  29.7 9.2 %refine.1 = f32[256,128]{1,0:T(8,128)S(1)} custom-call(s32[1]{0:T(128)} %bitcast.pos_ref, f32[768,128]{1,0:T(8,128)S(1)} %get-tuple-element.28.refs_0_, f32[1152,128]{1,0:T(8,128)S(1)} %collective-permute-done.4.refs_1_, f32[256,256]{1,0:T(8,128)S(1)} %bitcast.5, bf16[384,128]{1,0:T(8,128)(2,1)S(1)} %pad_maximum_fusion.seen_ref.refs_3_, ...), custom_call_target="tpu_custom_call" | custom-call | flops 400000000 | bytes 2000000 | tf_op jit(solution)/shard_map/refine/pallas_call | solution.py:186
  38.9 0.0 copy-start
  38.9 10.1 %all_to_all.15.d_ref = f32[8,4,8,128]{3,2,1,0:T(8,128)S(1)} all-to-all(f32[8,4,8,128]{3,2,1,0:T(8,128)S(1)} %bitcast.6), channel_id=1, replica_groups=mesh['sub'=8,'band'=16] {'sub'}, dimensions={0} | all-to-all | bytes 262144 | tf_op jit(solution)/shard_map/all_to_all | solution.py:412
  49.0 0.2 encode.1
  49.2 19.4 %all_to_all.16.g_ref = bf16[16,272,128]{2,1,0:T(8,128)(2,1)S(1)} all-to-all(bf16[16,272,128]{2,1,0:T(8,128)(2,1)S(1)} %encode.1), channel_id=1, replica_groups=mesh['sub'=8,'band'=16] {'band'}, dimensions={0} | all-to-all | bytes 2228224 | tf_op jit(solution)/shard_map/all_to_all | solution.py:413
  68.6 0.0 copy-done
  68.6 2.0 %place.1 = f32[4,128,1024]{2,1,0:T(8,128)} custom-call(bf16[16,272,128]{2,1,0:T(8,128)(2,1)S(1)} %all_to_all.16.g_ref, f32[4,128,1024]{2,1,0:T(8,128)S(1)} %copy-done), custom_call_target="tpu_custom_call" | custom-call | tf_op jit(solution)/shard_map/place/pallas_call | solution.py:388
  (1 shorter events, 0.0 us)
Async XLA Ops:
  2.3 16.2 %all-to-all-start = ((f32[16,16,256]{2,1,0:T(8,128)}), f32[16,16,256]{2,1,0:T(8,128)S(1)}, u32[]{:S(2)}, u32[]{:S(2)}) async-start(f32[16,16,256]{2,1,0:T(8,128)} %get-tuple-element.18), calls=%async_computation | async-start | bytes 524288 | tf_op jit(solution)/shard_map/all_to_all | solution.py:402
  10.9 13.4 %collective-permute-start.1 = (f32[256,128]{1,0:T(8,128)}, f32[256,128]{1,0:T(8,128)S(1)}, u32[]{:S(2)}, u32[]{:S(2)}) collective-permute-start(f32[256,128]{1,0:T(8,128)} %get-tuple-element.21), channel_id=1, source_target_pairs={{0,32},{16,48},{32,64},{48,80},{64,96},{80,112},{96,0},{112,16},{1... | collective-permute-start | bytes 393224 | tf_op jit(solution)/shard_map/ppermute | solution.py:404
  12.2 12.2 %collective-permute-start.2 = (f32[256,128]{1,0:T(8,128)}, f32[256,128]{1,0:T(8,128)S(1)}, u32[]{:S(2)}, u32[]{:S(2)}) collective-permute-start(f32[256,128]{1,0:T(8,128)} %get-tuple-element.22), channel_id=1, source_target_pairs={{0,64},{16,80},{32,96},{48,112},{64,0},{80,16},{96,32},{112,48},{1... | collective-permute-start | bytes 393224 | tf_op jit(solution)/shard_map/ppermute | solution.py:404
  14.6 9.7 %collective-permute-start.3 = (f32[256,128]{1,0:T(8,128)}, f32[256,128]{1,0:T(8,128)S(1)}, u32[]{:S(2)}, u32[]{:S(2)}) collective-permute-start(f32[256,128]{1,0:T(8,128)} %get-tuple-element.23), channel_id=1, source_target_pairs={{0,96},{16,112},{32,0},{48,16},{64,32},{80,48},{96,64},{112,80},{1... | collective-permute-start | bytes 393224 | tf_op jit(solution)/shard_map/ppermute | solution.py:404
  19.2 7.4 %collective-permute-start = (bf16[384,128]{1,0:T(8,128)(2,1)S(1)}, bf16[384,128]{1,0:T(8,128)(2,1)S(1)}, u32[]{:S(2)}, u32[]{:S(2)}) collective-permute-start(bf16[384,128]{1,0:T(8,128)(2,1)S(1)} %pad_maximum_fusion.seen_ref.refs_3_), channel_id=1, source_target_pairs={{16,32},{32,16},{48,64},{64,48},{80,96},{96,80},{17,33},{33,17},{4... | collective-permute-start | bytes 294920 | tf_op jit(solution)/shard_map/ppermute | solution.py:407
  26.6 0.9 %copy-start.1 = (f32[256,128]{1,0:T(8,128)S(1)}, f32[256,128]{1,0:T(8,128)}, u32[]{:S(2)}) copy-start(f32[256,128]{1,0:T(8,128)} %get-tuple-element.24.r0) | copy-start | bytes 393220
  27.6 2.1 %collective-permute-start.4 = (f32[1152,128]{1,0:T(8,128)S(1)}, f32[1152,128]{1,0:T(8,128)S(1)}, u32[]{:S(2)}, u32[]{:S(2)}) collective-permute-start(f32[1152,128]{1,0:T(8,128)S(1)} %get-tuple-element.29), channel_id=1, source_target_pairs={{0,16},{16,0},{32,48},{48,32},{64,80},{80,64},{96,112},{112,96},{1... | collective-permute-start | bytes 1769480 | tf_op jit(solution)/shard_map/ppermute | solution.py:410
  38.9 29.7 %copy-start = (f32[4,128,1024]{2,1,0:T(8,128)S(1)}, f32[4,128,1024]{2,1,0:T(8,128)}, u32[]{:S(2)}) copy-start(f32[4,128,1024]{2,1,0:T(8,128)} %c_ref.1) | copy-start | bytes 6291460

commit v14 on v13

--- a/solution.py
+++ b/solution.py
@@ -304,6 +304,22 @@
     )(pos, coeffs_in, coeffs_in, ms_image, ms_image, hs_image, kernels, basis, response)
 
 
+def hold_kernel(region_ref, out_ref):
+    out_ref[...] = region_ref[...]
+
+
+def hold(region):
+    vmem = pl.BlockSpec(memory_space=pltpu.VMEM)
+    return pl.pallas_call(
+        hold_kernel,
+        out_shape=jax.ShapeDtypeStruct(region.shape, region.dtype),
+        in_specs=[vmem],
+        out_specs=vmem,
+        compiler_params=pltpu.CompilerParams(vmem_limit_bytes=16 * 2**20),
+        name="hold",
+    )(region)
+
+
 def hand_kernel(pos_ref, r0, r1, r2, r3, seen_ref, mine_ref, other_ref):
     other_ref[16 * CROWS : 16 * CROWS + 384] = seen_ref[...].astype(f32)
     skip = 16 * (pos_ref[0] // 16 % 2)
@@ -403,6 +419,7 @@
     tiles = [tiles[0]] + [
         lax.ppermute(tiles[d], "sub", [(i, (i + 2 * d) % 8) for i in range(8)]) for d in range(1, 4)
     ]
+    tiles[0], near = lax.optimization_barrier((hold(tiles[0]), near))
     seen = jnp.concatenate([hp[:, 0:128].astype(bf16), near], axis=0)
     cross = lax.ppermute(seen, "sub", [(1, 2), (2, 1), (3, 4), (4, 3), (5, 6), (6, 5)])
     cross, *tiles = lax.optimization_barrier((cross, *tiles))

time: 71.6 us -> 70.7 us (0.987)
  waiting for transfers between devices: 6.91 us -> 6 us
    all_to_all x1, waiting for transfers between devices: 2.66 us -> 1.74 us  [per_device(): lax.all_to_all(sent, 'band', split_axis=0, concat_axis=0, tiled=True)]
where the time goes in v14:
time: 70.7 us; the launch traced here: 69.7 us
  blocking collectives  29.5 us (42%)
  starting transfers between devices  18.7 us (26%)
  Pallas kernels  13.8 us (20%)
  waiting for transfers between devices  6 us (8%)
  local copies, waits for them, and re-layouts  0.92 us (1%)
  other arithmetic  0.77 us (1%)
    all_to_all x1, blocking collectives, per_device(): lax.all_to_all(encode(owned), 'band', split_axis=0, concat_axis=0, tiled=...  19.4 us
    all_to_all x1, blocking collectives, per_device(): lax.all_to_all(new.reshape(8, 4, 8, LANES), 'sub', split_axis=0, concat_a...  10.1 us
    pallas_call x1, Pallas kernels, refine(): pl.pallas_call(refine_kernel, out_shape=jax.ShapeDtypeStruct((32 * 8, LAN...  9.2 us
    all_to_all x1, starting transfers between devices, per_device(): lax.all_to_all(sent, 'band', split_axis=0, concat_axis=0, tiled=True)  8.6 us
    ppermute x1, starting transfers between devices, per_device(): lax.ppermute(seen, 'sub', [(1, 2), (2, 1), (3, 4), (4, 3), (5, 6), (6, 5)])  5.09 us
    ppermute x3, starting transfers between devices, per_device(): lax.ppermute(tiles[d], 'sub', [(i, (i + 2 * d) % 8) for i in range(8)])  4.88 us
    pallas_call x1, Pallas kernels, pack(): pl.pallas_call(pack_kernel, out_shape=(jax.ShapeDtypeStruct((256, LANES),...  2.29 us
    ppermute x1, waiting for transfers between devices, per_device(): lax.ppermute(seen, 'sub', [(1, 2), (2, 1), (3, 4), (4, 3), (5, 6), (6, 5)])  2.25 us
  transfers between devices with their start and end apart: 6, of which 3 were waited for; matrix products, arithmetic and copies ran while one was open for 1% of the time, Pallas kernels for 0%

profile of v14, /device:TPU:1, one launch (start us, length us, event | category | flops | bytes accessed | tf_op | source)
XLA Modules:
  0.0 69.7 jit_solution(9980507899311666539)
XLA Ops:
  0.0 2.3 %pack.1 = (f32[256,128]{1,0:T(8,128)}, f32[256,128]{1,0:T(8,128)}, f32[256,128]{1,0:T(8,128)}, f32[256,128]{1,0:T(8,128)}, bf16[128,128]{1,0:T(8,128)(2,1)}, /*index=5*/f32[16,16,256]{2,1,0:T(8,128)}) custom-call(s32[1]{0:T(128)} %bitcast.pos_ref, f32[4,128,1024]{2,1,0:T(8,128)} %c_ref.1, f32[4,128,1024]{2,1,0:T(8,128)} %c_ref.1, ...), custom_call_target="tpu_custom_call" | custom-call | flops 100000000 | bytes 1600000 | tf_op jit(solution)/shard_map/pack/pallas_call | solution.py:275
  2.3 8.6 %all-to-all-start = ((f32[16,16,256]{2,1,0:T(8,128)}), f32[16,16,256]{2,1,0:T(8,128)S(1)}, u32[]{:S(2)}, u32[]{:S(2)}) async-start(f32[16,16,256]{2,1,0:T(8,128)} %get-tuple-element.20), calls=%async_computation | async-start | bytes 524288 | tf_op jit(solution)/shard_map/all_to_all | solution.py:418
  10.9 1.3 %collective-permute-start.1 = (f32[256,128]{1,0:T(8,128)}, f32[256,128]{1,0:T(8,128)S(1)}, u32[]{:S(2)}, u32[]{:S(2)}) collective-permute-start(f32[256,128]{1,0:T(8,128)} %get-tuple-element.25), channel_id=1, source_target_pairs={{0,32},{16,48},{32,64},{48,80},{64,96},{80,112},{96,0},{112,16},{1... | collective-permute-start | bytes 393224 | tf_op jit(solution)/shard_map/ppermute | solution.py:420
  12.2 2.5 %collective-permute-start.2 = (f32[256,128]{1,0:T(8,128)}, f32[256,128]{1,0:T(8,128)S(1)}, u32[]{:S(2)}, u32[]{:S(2)}) collective-permute-start(f32[256,128]{1,0:T(8,128)} %get-tuple-element.26), channel_id=1, source_target_pairs={{0,64},{16,80},{32,96},{48,112},{64,0},{80,16},{96,32},{112,48},{1... | collective-permute-start | bytes 393224 | tf_op jit(solution)/shard_map/ppermute | solution.py:420
  14.6 1.2 %collective-permute-start.3 = (f32[256,128]{1,0:T(8,128)}, f32[256,128]{1,0:T(8,128)S(1)}, u32[]{:S(2)}, u32[]{:S(2)}) collective-permute-start(f32[256,128]{1,0:T(8,128)} %get-tuple-element.27), channel_id=1, source_target_pairs={{0,96},{16,112},{32,0},{48,16},{64,32},{80,48},{96,64},{112,80},{1... | collective-permute-start | bytes 393224 | tf_op jit(solution)/shard_map/ppermute | solution.py:420
  15.8 0.0 copy-start.1
  15.8 0.9 %copy-done.1 = f32[256,128]{1,0:T(8,128)S(1)} copy-done((f32[256,128]{1,0:T(8,128)S(1)}, f32[256,128]{1,0:T(8,128)}, u32[]{:S(2)}) %copy-start.1) | copy-done | bytes 131096
  16.7 1.7 %all-to-all-done = f32[16,16,256]{2,1,0:T(8,128)S(1)} async-done(((f32[16,16,256]{2,1,0:T(8,128)}), f32[16,16,256]{2,1,0:T(8,128)S(1)}, u32[]{:S(2)}, u32[]{:S(2)}) %all-to-all-start) | async-done | bytes 262176 | tf_op jit(solution)/shard_map/all_to_all | solution.py:418
  18.5 0.8 %pad_maximum_fusion.seen_ref.refs_3_ = bf16[384,128]{1,0:T(8,128)(2,1)S(1)} fusion(bf16[128,128]{1,0:T(8,128)(2,1)} %get-tuple-element.23, bf16[256,128]{1,0:T(8,128)(2,1)S(1)} %slice.7), kind=kLoop, calls=%fused_computation.1 | loop fusion | flops 196608 | bytes 196608 | tf_op jit(solution)/shard_map/concatenate | solution.py:423
  19.2 5.1 %collective-permute-start = (bf16[384,128]{1,0:T(8,128)(2,1)S(1)}, bf16[384,128]{1,0:T(8,128)(2,1)S(1)}, u32[]{:S(2)}, u32[]{:S(2)}) collective-permute-start(bf16[384,128]{1,0:T(8,128)(2,1)S(1)} %pad_maximum_fusion.seen_ref.refs_3_), channel_id=1, source_target_pairs={{16,32},{32,16},{48,64},{64,48},{80,96},{96,80},{17,33},{33,17},{4... | collective-permute-start | bytes 294920 | tf_op jit(solution)/shard_map/ppermute | solution.py:424
  24.3 0.0 collective-permute-done.1.r1
  24.3 0.0 collective-permute-done.2.r2
  24.3 0.0 collective-permute-done.3.r3
  24.4 2.3 %collective-permute-done.refs_4_ = bf16[384,128]{1,0:T(8,128)(2,1)S(1)} collective-permute-done((bf16[384,128]{1,0:T(8,128)(2,1)S(1)}, bf16[384,128]{1,0:T(8,128)(2,1)S(1)}, u32[]{:S(2)}, u32[]{:S(2)}) %collective-permute-start) | collective-permute-done | bytes 98336 | tf_op jit(solution)/shard_map/ppermute | solution.py:424
  26.6 0.1 hand.1
  26.7 0.1 collective-permute-start.4
  26.8 2.0 %collective-permute-done.4.refs_1_ = f32[1152,128]{1,0:T(8,128)S(1)} collective-permute-done((f32[1152,128]{1,0:T(8,128)S(1)}, f32[1152,128]{1,0:T(8,128)S(1)}, u32[]{:S(2)}, u32[]{:S(2)}) %collective-permute-start.4) | collective-permute-done | bytes 589856 | tf_op jit(solution)/shard_map/ppermute | solution.py:427
  28.8 9.2 %refine.1 = f32[256,128]{1,0:T(8,128)S(1)} custom-call(s32[1]{0:T(128)} %bitcast.pos_ref, f32[768,128]{1,0:T(8,128)S(1)} %get-tuple-element.32.refs_0_, f32[1152,128]{1,0:T(8,128)S(1)} %collective-permute-done.4.refs_1_, f32[256,256]{1,0:T(8,128)S(1)} %bitcast.5, bf16[384,128]{1,0:T(8,128)(2,1)S(1)} %pad_maximum_fusion.seen_ref.refs_3_, ...), custom_call_target="tpu_custom_call" | custom-call | flops 400000000 | bytes 2000000 | tf_op jit(solution)/shard_map/refine/pallas_call | solution.py:186
  38.0 0.0 copy-start
  38.0 10.1 %all_to_all.15.d_ref = f32[8,4,8,128]{3,2,1,0:T(8,128)S(1)} all-to-all(f32[8,4,8,128]{3,2,1,0:T(8,128)S(1)} %bitcast.6), channel_id=1, replica_groups=mesh['sub'=8,'band'=16] {'sub'}, dimensions={0} | all-to-all | bytes 262144 | tf_op jit(solution)/shard_map/all_to_all | solution.py:429
  48.1 0.2 encode.1
  48.3 19.4 %all_to_all.16.g_ref = bf16[16,272,128]{2,1,0:T(8,128)(2,1)S(1)} all-to-all(bf16[16,272,128]{2,1,0:T(8,128)(2,1)S(1)} %encode.1), channel_id=1, replica_groups=mesh['sub'=8,'band'=16] {'band'}, dimensions={0} | all-to-all | bytes 2228224 | tf_op jit(solution)/shard_map/all_to_all | solution.py:430
  67.7 0.0 copy-done
  67.7 2.0 %place.1 = f32[4,128,1024]{2,1,0:T(8,128)} custom-call(bf16[16,272,128]{2,1,0:T(8,128)(2,1)S(1)} %all_to_all.16.g_ref, f32[4,128,1024]{2,1,0:T(8,128)S(1)} %copy-done), custom_call_target="tpu_custom_call" | custom-call | tf_op jit(solution)/shard_map/place/pallas_call | solution.py:404
  (2 shorter events, 0.0 us)
Async XLA Ops:
  2.3 16.2 %all-to-all-start = ((f32[16,16,256]{2,1,0:T(8,128)}), f32[16,16,256]{2,1,0:T(8,128)S(1)}, u32[]{:S(2)}, u32[]{:S(2)}) async-start(f32[16,16,256]{2,1,0:T(8,128)} %get-tuple-element.20), calls=%async_computation | async-start | bytes 524288 | tf_op jit(solution)/shard_map/all_to_all | solution.py:418
  10.9 13.4 %collective-permute-start.1 = (f32[256,128]{1,0:T(8,128)}, f32[256,128]{1,0:T(8,128)S(1)}, u32[]{:S(2)}, u32[]{:S(2)}) collective-permute-start(f32[256,128]{1,0:T(8,128)} %get-tuple-element.25), channel_id=1, source_target_pairs={{0,32},{16,48},{32,64},{48,80},{64,96},{80,112},{96,0},{112,16},{1... | collective-permute-start | bytes 393224 | tf_op jit(solution)/shard_map/ppermute | solution.py:420
  12.2 12.2 %collective-permute-start.2 = (f32[256,128]{1,0:T(8,128)}, f32[256,128]{1,0:T(8,128)S(1)}, u32[]{:S(2)}, u32[]{:S(2)}) collective-permute-start(f32[256,128]{1,0:T(8,128)} %get-tuple-element.26), channel_id=1, source_target_pairs={{0,64},{16,80},{32,96},{48,112},{64,0},{80,16},{96,32},{112,48},{1... | collective-permute-start | bytes 393224 | tf_op jit(solution)/shard_map/ppermute | solution.py:420
  14.6 9.7 %collective-permute-start.3 = (f32[256,128]{1,0:T(8,128)}, f32[256,128]{1,0:T(8,128)S(1)}, u32[]{:S(2)}, u32[]{:S(2)}) collective-permute-start(f32[256,128]{1,0:T(8,128)} %get-tuple-element.27), channel_id=1, source_target_pairs={{0,96},{16,112},{32,0},{48,16},{64,32},{80,48},{96,64},{112,80},{1... | collective-permute-start | bytes 393224 | tf_op jit(solution)/shard_map/ppermute | solution.py:420
  15.8 0.9 %copy-start.1 = (f32[256,128]{1,0:T(8,128)S(1)}, f32[256,128]{1,0:T(8,128)}, u32[]{:S(2)}) copy-start(f32[256,128]{1,0:T(8,128)} %get-tuple-element.21.region_ref) | copy-start | bytes 393220
  19.2 7.4 %collective-permute-start = (bf16[384,128]{1,0:T(8,128)(2,1)S(1)}, bf16[384,128]{1,0:T(8,128)(2,1)S(1)}, u32[]{:S(2)}, u32[]{:S(2)}) collective-permute-start(bf16[384,128]{1,0:T(8,128)(2,1)S(1)} %pad_maximum_fusion.seen_ref.refs_3_), channel_id=1, source_target_pairs={{16,32},{32,16},{48,64},{64,48},{80,96},{96,80},{17,33},{33,17},{4... | collective-permute-start | bytes 294920 | tf_op jit(solution)/shard_map/ppermute | solution.py:424
  26.7 2.1 %collective-permute-start.4 = (f32[1152,128]{1,0:T(8,128)S(1)}, f32[1152,128]{1,0:T(8,128)S(1)}, u32[]{:S(2)}, u32[]{:S(2)}) collective-permute-start(f32[1152,128]{1,0:T(8,128)S(1)} %get-tuple-element.33), channel_id=1, source_target_pairs={{0,16},{16,0},{32,48},{48,32},{64,80},{80,64},{96,112},{112,96},{1... | collective-permute-start | bytes 1769480 | tf_op jit(solution)/shard_map/ppermute | solution.py:427
  38.0 29.7 %copy-start = (f32[4,128,1024]{2,1,0:T(8,128)S(1)}, f32[4,128,1024]{2,1,0:T(8,128)}, u32[]{:S(2)}) copy-start(f32[4,128,1024]{2,1,0:T(8,128)} %c_ref.1) | copy-start | bytes 6291460

commit v15 on v14

--- a/solution.py
+++ b/solution.py
@@ -422,7 +422,6 @@
     tiles[0], near = lax.optimization_barrier((hold(tiles[0]), near))
     seen = jnp.concatenate([hp[:, 0:128].astype(bf16), near], axis=0)
     cross = lax.ppermute(seen, "sub", [(1, 2), (2, 1), (3, 4), (4, 3), (5, 6), (6, 5)])
-    cross, *tiles = lax.optimization_barrier((cross, *tiles))
     mine, other = hand(pos, tiles, seen)
     other = lax.ppermute(other, "sub", [(i, i ^ 1) for i in range(8)])
     new = refine(pos, mine, other, hp, seen, cross)

time: 70.7 us -> 73 us (1.033)
  blocking collectives: 29.5 us -> 32.4 us
    all_to_all x1, blocking collectives: 19.4 us -> 23.1 us  [per_device(): lax.all_to_all(encode(owned), 'band', split_axis=0, concat_axis=0, tiled=...]
    ppermute x1, starting transfers between devices: 5.09 us -> 2.86 us  [per_device(): lax.ppermute(seen, 'sub', [(1, 2), (2, 1), (3, 4), (4, 3), (5, 6), (6, 5)])]
    ppermute x1, waiting for transfers between devices: 1.99 us -> 0.01 us  [per_device(): other = lax.ppermute(other, 'sub', [(i, i ^ 1) for i in range(8)])]
    ppermute x1, starting transfers between devices: 0.09 us -> 1.82 us  [per_device(): other = lax.ppermute(other, 'sub', [(i, i ^ 1) for i in range(8)])]
    ppermute x3, waiting for transfers between devices: 0.01 us -> 1.12 us  [per_device(): lax.ppermute(tiles[d], 'sub', [(i, (i + 2 * d) % 8) for i in range(8)])]
    all_to_all x1, blocking collectives: 10.1 us -> 9.25 us  [per_device(): lax.all_to_all(new.reshape(8, 4, 8, LANES), 'sub', split_axis=0, concat_a...]
    ppermute x1, waiting for transfers between devices: 2.25 us -> 3.05 us  [per_device(): lax.ppermute(seen, 'sub', [(1, 2), (2, 1), (3, 4), (4, 3), (5, 6), (6, 5)])]
  transfers between devices with their start and end apart: 6 -> 6, of which waited for: 3 -> 4; matrix products, arithmetic and copies ran while one was open for 1% -> 1% of each run, Pallas kernels for 0% -> 0%
where the time goes in v15:
time: 73 us; the launch traced here: 72 us
  blocking collectives  32.4 us (44%)
  starting transfers between devices  18.2 us (25%)
  Pallas kernels  13.8 us (19%)
  waiting for transfers between devices  5.92 us (8%)
  local copies, waits for them, and re-layouts  0.92 us (1%)
  other arithmetic  0.77 us (1%)
    all_to_all x1, blocking collectives, per_device(): lax.all_to_all(encode(owned), 'band', split_axis=0, concat_axis=0, tiled=...  23.1 us
    all_to_all x1, blocking collectives, per_device(): lax.all_to_all(new.reshape(8, 4, 8, LANES), 'sub', split_axis=0, concat_a...  9.25 us
    pallas_call x1, Pallas kernels, refine(): pl.pallas_call(refine_kernel, out_shape=jax.ShapeDtypeStruct((32 * 8, LAN...  9.21 us
    all_to_all x1, starting transfers between devices, per_device(): lax.all_to_all(sent, 'band', split_axis=0, concat_axis=0, tiled=True)  8.6 us
    ppermute x3, starting transfers between devices, per_device(): lax.ppermute(tiles[d], 'sub', [(i, (i + 2 * d) % 8) for i in range(8)])  4.88 us
    ppermute x1, waiting for transfers between devices, per_device(): lax.ppermute(seen, 'sub', [(1, 2), (2, 1), (3, 4), (4, 3), (5, 6), (6, 5)])  3.05 us
    ppermute x1, starting transfers between devices, per_device(): lax.ppermute(seen, 'sub', [(1, 2), (2, 1), (3, 4), (4, 3), (5, 6), (6, 5)])  2.86 us
    pallas_call x1, Pallas kernels, pack(): pl.pallas_call(pack_kernel, out_shape=(jax.ShapeDtypeStruct((256, LANES),...  2.29 us
  transfers between devices with their start and end apart: 6, of which 4 were waited for; matrix products, arithmetic and copies ran while one was open for 1% of the time, Pallas kernels for 0%

profile of v15, /device:TPU:1, one launch (start us, length us, event | category | flops | bytes accessed | tf_op | source)
XLA Modules:
  0.0 72.0 jit_solution(13947395355326740419)
XLA Ops:
  0.0 2.3 %pack.1 = (f32[256,128]{1,0:T(8,128)}, f32[256,128]{1,0:T(8,128)}, f32[256,128]{1,0:T(8,128)}, f32[256,128]{1,0:T(8,128)}, bf16[128,128]{1,0:T(8,128)(2,1)}, /*index=5*/f32[16,16,256]{2,1,0:T(8,128)}) custom-call(s32[1]{0:T(128)} %bitcast.pos_ref, f32[4,128,1024]{2,1,0:T(8,128)} %c_ref.1, f32[4,128,1024]{2,1,0:T(8,128)} %c_ref.1, ...), custom_call_target="tpu_custom_call" | custom-call | flops 100000000 | bytes 1600000 | tf_op jit(solution)/shard_map/pack/pallas_call | solution.py:275
  2.3 8.6 %all-to-all-start = ((f32[16,16,256]{2,1,0:T(8,128)}), f32[16,16,256]{2,1,0:T(8,128)S(1)}, u32[]{:S(2)}, u32[]{:S(2)}) async-start(f32[16,16,256]{2,1,0:T(8,128)} %get-tuple-element.21), calls=%async_computation | async-start | bytes 524288 | tf_op jit(solution)/shard_map/all_to_all | solution.py:418
  10.9 1.3 %collective-permute-start = (f32[256,128]{1,0:T(8,128)}, f32[256,128]{1,0:T(8,128)S(1)}, u32[]{:S(2)}, u32[]{:S(2)}) collective-permute-start(f32[256,128]{1,0:T(8,128)} %get-tuple-element.18), channel_id=1, source_target_pairs={{0,32},{16,48},{32,64},{48,80},{64,96},{80,112},{96,0},{112,16},{1... | collective-permute-start | bytes 393224 | tf_op jit(solution)/shard_map/ppermute | solution.py:420
  12.2 2.5 %collective-permute-start.1 = (f32[256,128]{1,0:T(8,128)}, f32[256,128]{1,0:T(8,128)S(1)}, u32[]{:S(2)}, u32[]{:S(2)}) collective-permute-start(f32[256,128]{1,0:T(8,128)} %get-tuple-element.19), channel_id=1, source_target_pairs={{0,64},{16,80},{32,96},{48,112},{64,0},{80,16},{96,32},{112,48},{1... | collective-permute-start | bytes 393224 | tf_op jit(solution)/shard_map/ppermute | solution.py:420
  14.6 1.2 %collective-permute-start.2 = (f32[256,128]{1,0:T(8,128)}, f32[256,128]{1,0:T(8,128)S(1)}, u32[]{:S(2)}, u32[]{:S(2)}) collective-permute-start(f32[256,128]{1,0:T(8,128)} %get-tuple-element.20), channel_id=1, source_target_pairs={{0,96},{16,112},{32,0},{48,16},{64,32},{80,48},{96,64},{112,80},{1... | collective-permute-start | bytes 393224 | tf_op jit(solution)/shard_map/ppermute | solution.py:420
  15.8 0.0 copy-start.1
  15.8 0.9 %copy-done.1 = f32[256,128]{1,0:T(8,128)S(1)} copy-done((f32[256,128]{1,0:T(8,128)S(1)}, f32[256,128]{1,0:T(8,128)}, u32[]{:S(2)}) %copy-start.1) | copy-done | bytes 131096
  16.7 1.7 %all-to-all-done = f32[16,16,256]{2,1,0:T(8,128)S(1)} async-done(((f32[16,16,256]{2,1,0:T(8,128)}), f32[16,16,256]{2,1,0:T(8,128)S(1)}, u32[]{:S(2)}, u32[]{:S(2)}) %all-to-all-start) | async-done | bytes 262176 | tf_op jit(solution)/shard_map/all_to_all | solution.py:418
  18.5 0.8 %pad_maximum_fusion.seen_ref.refs_3_ = bf16[384,128]{1,0:T(8,128)(2,1)S(1)} fusion(bf16[128,128]{1,0:T(8,128)(2,1)} %get-tuple-element.22, bf16[256,128]{1,0:T(8,128)(2,1)S(1)} %slice.7), kind=kLoop, calls=%fused_computation.1 | loop fusion | flops 196608 | bytes 196608 | tf_op jit(solution)/shard_map/concatenate | solution.py:423
  19.2 0.0 collective-permute-done.r1
  19.2 0.9 %collective-permute-done.1.r2 = f32[256,128]{1,0:T(8,128)S(1)} collective-permute-done((f32[256,128]{1,0:T(8,128)}, f32[256,128]{1,0:T(8,128)S(1)}, u32[]{:S(2)}, u32[]{:S(2)}) %collective-permute-start.1) | collective-permute-done | bytes 131104 | tf_op jit(solution)/shard_map/ppermute | solution.py:420
  20.1 0.2 collective-permute-done.2.r3
  20.3 0.1 hand.1
  20.4 1.8 %collective-permute-start.3 = (f32[1152,128]{1,0:T(8,128)S(1)}, f32[1152,128]{1,0:T(8,128)S(1)}, u32[]{:S(2)}, u32[]{:S(2)}) collective-permute-start(f32[1152,128]{1,0:T(8,128)S(1)} %get-tuple-element.24), channel_id=1, source_target_pairs={{0,16},{16,0},{32,48},{48,32},{64,80},{80,64},{96,112},{112,96},{1... | collective-permute-start | bytes 1769480 | tf_op jit(solution)/shard_map/ppermute | solution.py:426
  22.2 2.9 %collective-permute-start.4 = (bf16[384,128]{1,0:T(8,128)(2,1)S(1)}, bf16[384,128]{1,0:T(8,128)(2,1)S(1)}, u32[]{:S(2)}, u32[]{:S(2)}) collective-permute-start(bf16[384,128]{1,0:T(8,128)(2,1)S(1)} %pad_maximum_fusion.seen_ref.refs_3_), channel_id=1, source_target_pairs={{16,32},{32,16},{48,64},{64,48},{80,96},{96,80},{17,33},{33,17},{4... | collective-permute-start | bytes 294920 | tf_op jit(solution)/shard_map/ppermute | solution.py:424
  25.1 3.1 %collective-permute-done.4.refs_4_ = bf16[384,128]{1,0:T(8,128)(2,1)S(1)} collective-permute-done((bf16[384,128]{1,0:T(8,128)(2,1)S(1)}, bf16[384,128]{1,0:T(8,128)(2,1)S(1)}, u32[]{:S(2)}, u32[]{:S(2)}) %collective-permute-start.4) | collective-permute-done | bytes 98336 | tf_op jit(solution)/shard_map/ppermute | solution.py:424
  28.2 0.0 collective-permute-done.3.refs_1_
  28.2 9.2 %refine.1 = f32[256,128]{1,0:T(8,128)S(1)} custom-call(s32[1]{0:T(128)} %bitcast.pos_ref, f32[768,128]{1,0:T(8,128)S(1)} %get-tuple-element.23.refs_0_, f32[1152,128]{1,0:T(8,128)S(1)} %collective-permute-done.3.refs_1_, f32[256,256]{1,0:T(8,128)S(1)} %bitcast.5, bf16[384,128]{1,0:T(8,128)(2,1)S(1)} %pad_maximum_fusion.seen_ref.refs_3_, ...), custom_call_target="tpu_custom_call" | custom-call | flops 400000000 | bytes 2000000 | tf_op jit(solution)/shard_map/refine/pallas_call | solution.py:186
  37.4 0.0 copy-start
  37.4 9.3 %all_to_all.15.d_ref = f32[8,4,8,128]{3,2,1,0:T(8,128)S(1)} all-to-all(f32[8,4,8,128]{3,2,1,0:T(8,128)S(1)} %bitcast.6), channel_id=1, replica_groups=mesh['sub'=8,'band'=16] {'sub'}, dimensions={0} | all-to-all | bytes 262144 | tf_op jit(solution)/shard_map/all_to_all | solution.py:428
  46.6 0.2 encode.1
  46.9 23.1 %all_to_all.16.g_ref = bf16[16,272,128]{2,1,0:T(8,128)(2,1)S(1)} all-to-all(bf16[16,272,128]{2,1,0:T(8,128)(2,1)S(1)} %encode.1), channel_id=1, replica_groups=mesh['sub'=8,'band'=16] {'band'}, dimensions={0} | all-to-all | bytes 2228224 | tf_op jit(solution)/shard_map/all_to_all | solution.py:429
  70.0 0.0 copy-done
  70.0 2.0 %place.1 = f32[4,128,1024]{2,1,0:T(8,128)} custom-call(bf16[16,272,128]{2,1,0:T(8,128)(2,1)S(1)} %all_to_all.16.g_ref, f32[4,128,1024]{2,1,0:T(8,128)S(1)} %copy-done), custom_call_target="tpu_custom_call" | custom-call | tf_op jit(solution)/shard_map/place/pallas_call | solution.py:404
  (2 shorter events, 0.0 us)
Async XLA Ops:
  2.3 16.2 %all-to-all-start = ((f32[16,16,256]{2,1,0:T(8,128)}), f32[16,16,256]{2,1,0:T(8,128)S(1)}, u32[]{:S(2)}, u32[]{:S(2)}) async-start(f32[16,16,256]{2,1,0:T(8,128)} %get-tuple-element.21), calls=%async_computation | async-start | bytes 524288 | tf_op jit(solution)/shard_map/all_to_all | solution.py:418
  10.9 8.3 %collective-permute-start = (f32[256,128]{1,0:T(8,128)}, f32[256,128]{1,0:T(8,128)S(1)}, u32[]{:S(2)}, u32[]{:S(2)}) collective-permute-start(f32[256,128]{1,0:T(8,128)} %get-tuple-element.18), channel_id=1, source_target_pairs={{0,32},{16,48},{32,64},{48,80},{64,96},{80,112},{96,0},{112,16},{1... | collective-permute-start | bytes 393224 | tf_op jit(solution)/shard_map/ppermute | solution.py:420
  12.2 8.0 %collective-permute-start.1 = (f32[256,128]{1,0:T(8,128)}, f32[256,128]{1,0:T(8,128)S(1)}, u32[]{:S(2)}, u32[]{:S(2)}) collective-permute-start(f32[256,128]{1,0:T(8,128)} %get-tuple-element.19), channel_id=1, source_target_pairs={{0,64},{16,80},{32,96},{48,112},{64,0},{80,16},{96,32},{112,48},{1... | collective-permute-start | bytes 393224 | tf_op jit(solution)/shard_map/ppermute | solution.py:420
  14.6 5.7 %collective-permute-start.2 = (f32[256,128]{1,0:T(8,128)}, f32[256,128]{1,0:T(8,128)S(1)}, u32[]{:S(2)}, u32[]{:S(2)}) collective-permute-start(f32[256,128]{1,0:T(8,128)} %get-tuple-element.20), channel_id=1, source_target_pairs={{0,96},{16,112},{32,0},{48,16},{64,32},{80,48},{96,64},{112,80},{1... | collective-permute-start | bytes 393224 | tf_op jit(solution)/shard_map/ppermute | solution.py:420
  15.8 0.9 %copy-start.1 = (f32[256,128]{1,0:T(8,128)S(1)}, f32[256,128]{1,0:T(8,128)}, u32[]{:S(2)}) copy-start(f32[256,128]{1,0:T(8,128)} %get-tuple-element.15.region_ref) | copy-start | bytes 393220
  20.4 7.8 %collective-permute-start.3 = (f32[1152,128]{1,0:T(8,128)S(1)}, f32[1152,128]{1,0:T(8,128)S(1)}, u32[]{:S(2)}, u32[]{:S(2)}) collective-permute-start(f32[1152,128]{1,0:T(8,128)S(1)} %get-tuple-element.24), channel_id=1, source_target_pairs={{0,16},{16,0},{32,48},{48,32},{64,80},{80,64},{96,112},{112,96},{1... | collective-permute-start | bytes 1769480 | tf_op jit(solution)/shard_map/ppermute | solution.py:426
  22.2 5.9 %collective-permute-start.4 = (bf16[384,128]{1,0:T(8,128)(2,1)S(1)}, bf16[384,128]{1,0:T(8,128)(2,1)S(1)}, u32[]{:S(2)}, u32[]{:S(2)}) collective-permute-start(bf16[384,128]{1,0:T(8,128)(2,1)S(1)} %pad_maximum_fusion.seen_ref.refs_3_), channel_id=1, source_target_pairs={{16,32},{32,16},{48,64},{64,48},{80,96},{96,80},{17,33},{33,17},{4... | collective-permute-start | bytes 294920 | tf_op jit(solution)/shard_map/ppermute | solution.py:424
  37.4 32.6 %copy-start = (f32[4,128,1024]{2,1,0:T(8,128)S(1)}, f32[4,128,1024]{2,1,0:T(8,128)}, u32[]{:S(2)}) copy-start(f32[4,128,1024]{2,1,0:T(8,128)} %c_ref.1) | copy-start | bytes 6291460

commit v16 on v14

--- a/solution.py
+++ b/solution.py
@@ -26,7 +26,7 @@
 
 
 def refine_kernel(pos_ref, *refs):
-    mine_ref, other_ref, hp_ref, seen_ref, cross_ref, out_ref, c_ref, ms_ref, m0, m1, f0, f1, b0, b1, c1_ref, g_ref, hs0, hs1, w0, w1 = refs
+    mine_ref, other_ref, w_ref, own_ref, seen_ref, cross_ref, out_ref, c_ref, ms_ref, m0, m1, f0, f1, b0, b1, c1_ref, g_ref, hs0, hs1 = refs
     s = pos_ref[0] // 16
     b = pos_ref[0] % 16
     core = s % 2
@@ -52,16 +52,14 @@
     m = (m0, m1)
     f = (f0, f1)
     hst = (hs0, hs1)
-    w = (w0, w1)
+    w = (w_ref.at[0], w_ref.at[1])
     for h in range(2):
-        at = slice(h * 128, h * 128 + 128)
         above, below = neighbours(h * 128, h * 128 + 128)
         hst[h][0:72, :] = above.T[24:96]
-        hst[h][72:168, :] = hp_ref[at, 0:128].T[0:96]
+        hst[h][72:168, :] = own_ref[h]
         hst[h][168:240, :] = below.T[0:72]
-        w[h][...] = hp_ref[at, 128:256].T
-    basis = jnp.concatenate([w0[81:113, :], w1[81:113, :]], axis=1).astype(bf16)
-    response = jnp.concatenate([w0[113:121, :], w1[113:121, :]], axis=1).astype(bf16)
+    basis = jnp.concatenate([w_ref[0, 81:113], w_ref[1, 81:113]], axis=1).astype(bf16)
+    response = jnp.concatenate([w_ref[0, 113:121], w_ref[1, 113:121]], axis=1).astype(bf16)
     combined = lax.dot_general(response, basis, (((1,), (1,)), ((), ())), preferred_element_type=f32).astype(bf16)
     lane = lax.broadcasted_iota(jnp.int32, (1, LANES), 1)
     group = lane % 32
@@ -181,12 +179,12 @@
         out_ref[pl.ds(r, 32, stride=8), :] = total
 
 
-def refine(pos, mine, other, hp, seen, cross):
+def refine(pos, mine, other, w, own, seen, cross):
     vmem = pl.BlockSpec(memory_space=pltpu.VMEM)
     return pl.pallas_call(
         refine_kernel,
         out_shape=jax.ShapeDtypeStruct((32 * 8, LANES), f32),
-        in_specs=[pl.BlockSpec(memory_space=pltpu.SMEM)] + [vmem] * 5,
+        in_specs=[pl.BlockSpec(memory_space=pltpu.SMEM)] + [vmem] * 6,
         out_specs=vmem,
         scratch_shapes=[
             pltpu.VMEM((32 * CROWS, LANES), f32),
@@ -201,13 +199,11 @@
             pltpu.VMEM((MROWS * 32, LANES), f32),
             pltpu.VMEM((256, LANES), f32),
             pltpu.VMEM((256, LANES), f32),
-            pltpu.VMEM((LANES, LANES), f32),
-            pltpu.VMEM((LANES, LANES), f32),
         ],
         compiler_params=pltpu.CompilerParams(vmem_limit_bytes=40 * 2**20),
         cost_estimate=pl.CostEstimate(flops=400_000_000, bytes_accessed=2_000_000, transcendentals=0),
         name="refine",
-    )(pos, mine, other, hp, seen, cross)
+    )(pos, mine, other, w, own, seen, cross)
 
 
 def spread(hs_ref, k_ref, basis_ref, response_ref, sent_ref):
@@ -304,6 +300,26 @@
     )(pos, coeffs_in, coeffs_in, ms_image, ms_image, hs_image, kernels, basis, response)
 
 
+def turn_kernel(hp_ref, w_ref, own_ref):
+    for h in range(2):
+        at = slice(h * 128, h * 128 + 128)
+        w_ref[h] = hp_ref[at, 128:256].T
+        own_ref[h] = hp_ref[at, 0:128].T[0:96]
+
+
+def turn(hp):
+    vmem = pl.BlockSpec(memory_space=pltpu.VMEM)
+    return pl.pallas_call(
+        turn_kernel,
+        out_shape=(jax.ShapeDtypeStruct((2, 128, LANES), f32), jax.ShapeDtypeStruct((2, 96, LANES), f32)),
+        in_specs=[vmem],
+        out_specs=(vmem, vmem),
+        compiler_params=pltpu.CompilerParams(vmem_limit_bytes=16 * 2**20),
+        cost_estimate=pl.CostEstimate(flops=1_000_000, bytes_accessed=20_000_000, transcendentals=0),
+        name="turn",
+    )(hp)
+
+
 def hold_kernel(region_ref, out_ref):
     out_ref[...] = region_ref[...]
 
@@ -425,7 +441,8 @@
     cross, *tiles = lax.optimization_barrier((cross, *tiles))
     mine, other = hand(pos, tiles, seen)
     other = lax.ppermute(other, "sub", [(i, i ^ 1) for i in range(8)])
-    new = refine(pos, mine, other, hp, seen, cross)
+    w, own = turn(hp)
+    new = refine(pos, mine, other, w, own, seen, cross)
     owned = lax.all_to_all(new.reshape(8, 4, 8, LANES), "sub", split_axis=0, concat_axis=0, tiled=True)
     gathered = lax.all_to_all(encode(owned), "band", split_axis=0, concat_axis=0, tiled=True)
     return place(gathered, coeffs_in)

time: 70.7 us -> 70.8 us (level)
  no operation moved by 1% of the time
where the time goes in v16:
time: 70.8 us; the launch traced here: 69.7 us
  blocking collectives  29.5 us (42%)
  starting transfers between devices  18.7 us (26%)
  Pallas kernels  13.9 us (20%)
  waiting for transfers between devices  5.87 us (8%)
  local copies, waits for them, and re-layouts  0.92 us (1%)
  other arithmetic  0.77 us (1%)
    all_to_all x1, blocking collectives, per_device(): lax.all_to_all(encode(owned), 'band', split_axis=0, concat_axis=0, tiled=...  19.4 us
    all_to_all x1, blocking collectives, per_device(): lax.all_to_all(new.reshape(8, 4, 8, LANES), 'sub', split_axis=0, concat_a...  10.1 us
    pallas_call x1, Pallas kernels, refine(): pl.pallas_call(refine_kernel, out_shape=jax.ShapeDtypeStruct((32 * 8, LAN...  9.27 us
    all_to_all x1, starting transfers between devices, per_device(): lax.all_to_all(sent, 'band', split_axis=0, concat_axis=0, tiled=True)  8.6 us
    ppermute x1, starting transfers between devices, per_device(): lax.ppermute(seen, 'sub', [(1, 2), (2, 1), (3, 4), (4, 3), (5, 6), (6, 5)])  5.09 us
    ppermute x3, starting transfers between devices, per_device(): lax.ppermute(tiles[d], 'sub', [(i, (i + 2 * d) % 8) for i in range(8)])  4.88 us
    pallas_call x1, Pallas kernels, pack(): pl.pallas_call(pack_kernel, out_shape=(jax.ShapeDtypeStruct((256, LANES),...  2.28 us
    ppermute x1, waiting for transfers between devices, per_device(): lax.ppermute(seen, 'sub', [(1, 2), (2, 1), (3, 4), (4, 3), (5, 6), (6, 5)])  2.25 us
  transfers between devices with their start and end apart: 6, of which 3 were waited for; matrix products, arithmetic and copies ran while one was open for 1% of the time, Pallas kernels for 0%

profile of v16, /device:TPU:1, one launch (start us, length us, event | category | flops | bytes accessed | tf_op | source)
XLA Modules:
  0.0 69.7 jit_solution(8457669792382704930)
XLA Ops:
  0.0 2.3 %pack.1 = (f32[256,128]{1,0:T(8,128)}, f32[256,128]{1,0:T(8,128)}, f32[256,128]{1,0:T(8,128)}, f32[256,128]{1,0:T(8,128)}, bf16[128,128]{1,0:T(8,128)(2,1)}, /*index=5*/f32[16,16,256]{2,1,0:T(8,128)}) custom-call(s32[1]{0:T(128)} %bitcast.pos_ref, f32[4,128,1024]{2,1,0:T(8,128)} %c_ref.1, f32[4,128,1024]{2,1,0:T(8,128)} %c_ref.1, ...), custom_call_target="tpu_custom_call" | custom-call | flops 100000000 | bytes 1600000 | tf_op jit(solution)/shard_map/pack/pallas_call | solution.py:271
  2.3 8.6 %all-to-all-start = ((f32[16,16,256]{2,1,0:T(8,128)}), f32[16,16,256]{2,1,0:T(8,128)S(1)}, u32[]{:S(2)}, u32[]{:S(2)}) async-start(f32[16,16,256]{2,1,0:T(8,128)} %get-tuple-element.22), calls=%async_computation | async-start | bytes 524288 | tf_op jit(solution)/shard_map/all_to_all | solution.py:434
  10.9 1.3 %collective-permute-start.1 = (f32[256,128]{1,0:T(8,128)}, f32[256,128]{1,0:T(8,128)S(1)}, u32[]{:S(2)}, u32[]{:S(2)}) collective-permute-start(f32[256,128]{1,0:T(8,128)} %get-tuple-element.27), channel_id=1, source_target_pairs={{0,32},{16,48},{32,64},{48,80},{64,96},{80,112},{96,0},{112,16},{1... | collective-permute-start | bytes 393224 | tf_op jit(solution)/shard_map/ppermute | solution.py:436
  12.2 2.5 %collective-permute-start.2 = (f32[256,128]{1,0:T(8,128)}, f32[256,128]{1,0:T(8,128)S(1)}, u32[]{:S(2)}, u32[]{:S(2)}) collective-permute-start(f32[256,128]{1,0:T(8,128)} %get-tuple-element.28), channel_id=1, source_target_pairs={{0,64},{16,80},{32,96},{48,112},{64,0},{80,16},{96,32},{112,48},{1... | collective-permute-start | bytes 393224 | tf_op jit(solution)/shard_map/ppermute | solution.py:436
  14.6 1.2 %collective-permute-start.3 = (f32[256,128]{1,0:T(8,128)}, f32[256,128]{1,0:T(8,128)S(1)}, u32[]{:S(2)}, u32[]{:S(2)}) collective-permute-start(f32[256,128]{1,0:T(8,128)} %get-tuple-element.29), channel_id=1, source_target_pairs={{0,96},{16,112},{32,0},{48,16},{64,32},{80,48},{96,64},{112,80},{1... | collective-permute-start | bytes 393224 | tf_op jit(solution)/shard_map/ppermute | solution.py:436
  15.8 0.0 copy-start.1
  15.8 0.9 %copy-done.1 = f32[256,128]{1,0:T(8,128)S(1)} copy-done((f32[256,128]{1,0:T(8,128)S(1)}, f32[256,128]{1,0:T(8,128)}, u32[]{:S(2)}) %copy-start.1) | copy-done | bytes 131096
  16.7 1.7 %all-to-all-done = f32[16,16,256]{2,1,0:T(8,128)S(1)} async-done(((f32[16,16,256]{2,1,0:T(8,128)}), f32[16,16,256]{2,1,0:T(8,128)S(1)}, u32[]{:S(2)}, u32[]{:S(2)}) %all-to-all-start) | async-done | bytes 262176 | tf_op jit(solution)/shard_map/all_to_all | solution.py:434
  18.5 0.8 %pad_maximum_fusion.seen_ref.refs_4_ = bf16[384,128]{1,0:T(8,128)(2,1)S(1)} fusion(bf16[128,128]{1,0:T(8,128)(2,1)} %get-tuple-element.25, bf16[256,128]{1,0:T(8,128)(2,1)S(1)} %slice.7), kind=kLoop, calls=%fused_computation.1 | loop fusion | flops 196608 | bytes 196608 | tf_op jit(solution)/shard_map/concatenate | solution.py:439
  19.2 5.1 %collective-permute-start = (bf16[384,128]{1,0:T(8,128)(2,1)S(1)}, bf16[384,128]{1,0:T(8,128)(2,1)S(1)}, u32[]{:S(2)}, u32[]{:S(2)}) collective-permute-start(bf16[384,128]{1,0:T(8,128)(2,1)S(1)} %pad_maximum_fusion.seen_ref.refs_4_), channel_id=1, source_target_pairs={{16,32},{32,16},{48,64},{64,48},{80,96},{96,80},{17,33},{33,17},{4... | collective-permute-start | bytes 294920 | tf_op jit(solution)/shard_map/ppermute | solution.py:440
  24.3 0.0 collective-permute-done.1.r1
  24.3 0.0 collective-permute-done.2.r2
  24.3 0.0 collective-permute-done.3.r3
  24.3 2.3 %collective-permute-done.refs_5_ = bf16[384,128]{1,0:T(8,128)(2,1)S(1)} collective-permute-done((bf16[384,128]{1,0:T(8,128)(2,1)S(1)}, bf16[384,128]{1,0:T(8,128)(2,1)S(1)}, u32[]{:S(2)}, u32[]{:S(2)}) %collective-permute-start) | collective-permute-done | bytes 98336 | tf_op jit(solution)/shard_map/ppermute | solution.py:440
  26.6 0.1 hand.1
  26.7 0.1 collective-permute-start.4
  26.8 0.1 turn.1
  26.9 1.9 %collective-permute-done.4.refs_1_ = f32[1152,128]{1,0:T(8,128)S(1)} collective-permute-done((f32[1152,128]{1,0:T(8,128)S(1)}, f32[1152,128]{1,0:T(8,128)S(1)}, u32[]{:S(2)}, u32[]{:S(2)}) %collective-permute-start.4) | collective-permute-done | bytes 589856 | tf_op jit(solution)/shard_map/ppermute | solution.py:443
  28.8 9.3 %refine.1 = f32[256,128]{1,0:T(8,128)S(1)} custom-call(s32[1]{0:T(128)} %bitcast.pos_ref, f32[768,128]{1,0:T(8,128)S(1)} %get-tuple-element.34.refs_0_, f32[1152,128]{1,0:T(8,128)S(1)} %collective-permute-done.4.refs_1_, f32[2,128,128]{2,1,0:T(8,128)S(1)} %get-tuple-element.36.refs_2_, f32[2,96,128]{2,1,0:T(8,128)S(1)} %get-tuple-element.37.refs_3_, ...), custom_call_target="tpu_custom_call" | custom-call | flops 400000000 | bytes 2000000 | tf_op jit(solution)/shard_map/refine/pallas_call | solution.py:184
  38.0 0.0 copy-start
  38.0 10.1 %all_to_all.15.d_ref = f32[8,4,8,128]{3,2,1,0:T(8,128)S(1)} all-to-all(f32[8,4,8,128]{3,2,1,0:T(8,128)S(1)} %bitcast.6), channel_id=1, replica_groups=mesh['sub'=8,'band'=16] {'sub'}, dimensions={0} | all-to-all | bytes 262144 | tf_op jit(solution)/shard_map/all_to_all | solution.py:446
  48.2 0.2 encode.1
  48.4 19.4 %all_to_all.16.g_ref = bf16[16,272,128]{2,1,0:T(8,128)(2,1)S(1)} all-to-all(bf16[16,272,128]{2,1,0:T(8,128)(2,1)S(1)} %encode.1), channel_id=1, replica_groups=mesh['sub'=8,'band'=16] {'band'}, dimensions={0} | all-to-all | bytes 2228224 | tf_op jit(solution)/shard_map/all_to_all | solution.py:447
  67.8 0.0 copy-done
  67.8 2.0 %place.1 = f32[4,128,1024]{2,1,0:T(8,128)} custom-call(bf16[16,272,128]{2,1,0:T(8,128)(2,1)S(1)} %all_to_all.16.g_ref, f32[4,128,1024]{2,1,0:T(8,128)S(1)} %copy-done), custom_call_target="tpu_custom_call" | custom-call | tf_op jit(solution)/shard_map/place/pallas_call | solution.py:420
  (2 shorter events, 0.0 us)
Async XLA Ops:
  2.3 16.2 %all-to-all-start = ((f32[16,16,256]{2,1,0:T(8,128)}), f32[16,16,256]{2,1,0:T(8,128)S(1)}, u32[]{:S(2)}, u32[]{:S(2)}) async-start(f32[16,16,256]{2,1,0:T(8,128)} %get-tuple-element.22), calls=%async_computation | async-start | bytes 524288 | tf_op jit(solution)/shard_map/all_to_all | solution.py:434
  10.9 13.4 %collective-permute-start.1 = (f32[256,128]{1,0:T(8,128)}, f32[256,128]{1,0:T(8,128)S(1)}, u32[]{:S(2)}, u32[]{:S(2)}) collective-permute-start(f32[256,128]{1,0:T(8,128)} %get-tuple-element.27), channel_id=1, source_target_pairs={{0,32},{16,48},{32,64},{48,80},{64,96},{80,112},{96,0},{112,16},{1... | collective-permute-start | bytes 393224 | tf_op jit(solution)/shard_map/ppermute | solution.py:436
  12.2 12.2 %collective-permute-start.2 = (f32[256,128]{1,0:T(8,128)}, f32[256,128]{1,0:T(8,128)S(1)}, u32[]{:S(2)}, u32[]{:S(2)}) collective-permute-start(f32[256,128]{1,0:T(8,128)} %get-tuple-element.28), channel_id=1, source_target_pairs={{0,64},{16,80},{32,96},{48,112},{64,0},{80,16},{96,32},{112,48},{1... | collective-permute-start | bytes 393224 | tf_op jit(solution)/shard_map/ppermute | solution.py:436
  14.6 9.7 %collective-permute-start.3 = (f32[256,128]{1,0:T(8,128)}, f32[256,128]{1,0:T(8,128)S(1)}, u32[]{:S(2)}, u32[]{:S(2)}) collective-permute-start(f32[256,128]{1,0:T(8,128)} %get-tuple-element.29), channel_id=1, source_target_pairs={{0,96},{16,112},{32,0},{48,16},{64,32},{80,48},{96,64},{112,80},{1... | collective-permute-start | bytes 393224 | tf_op jit(solution)/shard_map/ppermute | solution.py:436
  15.8 0.9 %copy-start.1 = (f32[256,128]{1,0:T(8,128)S(1)}, f32[256,128]{1,0:T(8,128)}, u32[]{:S(2)}) copy-start(f32[256,128]{1,0:T(8,128)} %get-tuple-element.23.region_ref) | copy-start | bytes 393220
  19.2 7.4 %collective-permute-start = (bf16[384,128]{1,0:T(8,128)(2,1)S(1)}, bf16[384,128]{1,0:T(8,128)(2,1)S(1)}, u32[]{:S(2)}, u32[]{:S(2)}) collective-permute-start(bf16[384,128]{1,0:T(8,128)(2,1)S(1)} %pad_maximum_fusion.seen_ref.refs_4_), channel_id=1, source_target_pairs={{16,32},{32,16},{48,64},{64,48},{80,96},{96,80},{17,33},{33,17},{4... | collective-permute-start | bytes 294920 | tf_op jit(solution)/shard_map/ppermute | solution.py:440
  26.7 2.1 %collective-permute-start.4 = (f32[1152,128]{1,0:T(8,128)S(1)}, f32[1152,128]{1,0:T(8,128)S(1)}, u32[]{:S(2)}, u32[]{:S(2)}) collective-permute-start(f32[1152,128]{1,0:T(8,128)S(1)} %get-tuple-element.35), channel_id=1, source_target_pairs={{0,16},{16,0},{32,48},{48,32},{64,80},{80,64},{96,112},{112,96},{1... | collective-permute-start | bytes 1769480 | tf_op jit(solution)/shard_map/ppermute | solution.py:443
  38.0 29.7 %copy-start = (f32[4,128,1024]{2,1,0:T(8,128)S(1)}, f32[4,128,1024]{2,1,0:T(8,128)}, u32[]{:S(2)}) copy-start(f32[4,128,1024]{2,1,0:T(8,128)} %c_ref.1) | copy-start | bytes 6291460

commit v17 on v14

--- a/solution.py
+++ b/solution.py
@@ -231,8 +231,8 @@
 
 
 def pack_kernel(pos_ref, ca_ref, cb_ref, ma_ref, mb_ref, hs_ref, k_ref, basis_ref, response_ref, *rest_refs):
-    spread(hs_ref, k_ref, basis_ref, response_ref, rest_refs[5])
-    near_ref, _, wide_ref = rest_refs[4:]
+    spread(hs_ref, k_ref, basis_ref, response_ref, rest_refs[4])
+    wide_ref = rest_refs[5]
     s = pos_ref[0] // 16
     b = pos_ref[0] % 16
     off = jnp.where(b % 2 == 0, 112, 48)
@@ -246,7 +246,7 @@
     ms = jnp.where(first, ma_ref[...].reshape(128, LANES).astype(f32), mb_ref[...].reshape(128, LANES).astype(f32))
     ms = jnp.where(keep, ms, 0.0).astype(bf16)
     ms = jnp.dot(ms, order, preferred_element_type=f32)
-    near_ref[...] = ms.astype(bf16)
+    rest_refs[0][256:384] = ms
     edge = jnp.zeros((16, LANES), f32)
     for k in range(4):
         rest = jnp.where(keep, jnp.where(first, ca_ref[k], cb_ref[k]), 0.0)
@@ -274,10 +274,9 @@
 
     return pl.pallas_call(
         pack_kernel,
-        out_shape=(jax.ShapeDtypeStruct((256, LANES), f32),) * 4 + (
-            jax.ShapeDtypeStruct((128, LANES), bf16),
-            jax.ShapeDtypeStruct((16, 16, 256), f32),
-        ),
+        out_shape=(jax.ShapeDtypeStruct((384, LANES), f32),)
+        + (jax.ShapeDtypeStruct((256, LANES), f32),) * 3
+        + (jax.ShapeDtypeStruct((16, 16, 256), f32),),
         grid_spec=pltpu.PrefetchScalarGridSpec(
             num_scalar_prefetch=1,
             grid=(1,),
@@ -291,11 +290,9 @@
                 pl.BlockSpec((14, 32), lambda i, p: (0, 0)),
                 pl.BlockSpec((8, 14), lambda i, p: (0, 0)),
             ],
-            out_specs=(pl.BlockSpec((256, LANES), lambda i, p: (0, 0)),) * 4
-            + (
-                pl.BlockSpec((128, LANES), lambda i, p: (0, 0)),
-                pl.BlockSpec((16, 16, 256), lambda i, p: (0, 0, 0)),
-            ),
+            out_specs=(pl.BlockSpec((384, LANES), lambda i, p: (0, 0)),)
+            + (pl.BlockSpec((256, LANES), lambda i, p: (0, 0)),) * 3
+            + (pl.BlockSpec((16, 16, 256), lambda i, p: (0, 0, 0)),),
             scratch_shapes=[pltpu.VMEM((4, 160, LANES), f32)],
         ),
         compiler_params=pltpu.CompilerParams(vmem_limit_bytes=60 * 2**20),
@@ -304,20 +301,38 @@
     )(pos, coeffs_in, coeffs_in, ms_image, ms_image, hs_image, kernels, basis, response)
 
 
-def hold_kernel(region_ref, out_ref):
-    out_ref[...] = region_ref[...]
+def hold_kernel(region_ref, out_ref, near_ref):
+    out_ref[...] = region_ref[0:256]
+    near_ref[...] = region_ref[256:384].astype(bf16)
 
 
 def hold(region):
     vmem = pl.BlockSpec(memory_space=pltpu.VMEM)
     return pl.pallas_call(
         hold_kernel,
-        out_shape=jax.ShapeDtypeStruct(region.shape, region.dtype),
+        out_shape=(jax.ShapeDtypeStruct((256, LANES), f32), jax.ShapeDtypeStruct((128, LANES), bf16)),
         in_specs=[vmem],
-        out_specs=vmem,
+        out_specs=(vmem, vmem),
         compiler_params=pltpu.CompilerParams(vmem_limit_bytes=16 * 2**20),
         name="hold",
     )(region)
+
+
+def join_kernel(hp_ref, near_ref, seen_ref):
+    seen_ref[0:256] = hp_ref[:, 0:128].astype(bf16)
+    seen_ref[256:384] = near_ref[...]
+
+
+def join(hp, near):
+    vmem = pl.BlockSpec(memory_space=pltpu.VMEM)
+    return pl.pallas_call(
+        join_kernel,
+        out_shape=jax.ShapeDtypeStruct((384, LANES), bf16),
+        in_specs=[vmem] * 2,
+        out_specs=vmem,
+        compiler_params=pltpu.CompilerParams(vmem_limit_bytes=16 * 2**20),
+        name="join",
+    )(hp, near)
 
 
 def hand_kernel(pos_ref, r0, r1, r2, r3, seen_ref, mine_ref, other_ref):
@@ -414,13 +429,13 @@
 
 def per_device(coeffs_in, basis, kernels, response, hs_image, ms_image):
     pos = (lax.axis_index("sub") * 16 + lax.axis_index("band")).astype(jnp.int32).reshape(1)
-    *tiles, near, sent = pack(pos, coeffs_in, ms_image, hs_image, kernels.transpose(1, 0, 2), basis, response)
+    *tiles, sent = pack(pos, coeffs_in, ms_image, hs_image, kernels.transpose(1, 0, 2), basis, response)
     hp = lax.all_to_all(sent, "band", split_axis=0, concat_axis=0, tiled=True).reshape(256, 256)
     tiles = [tiles[0]] + [
         lax.ppermute(tiles[d], "sub", [(i, (i + 2 * d) % 8) for i in range(8)]) for d in range(1, 4)
     ]
-    tiles[0], near = lax.optimization_barrier((hold(tiles[0]), near))
-    seen = jnp.concatenate([hp[:, 0:128].astype(bf16), near], axis=0)
+    tiles[0], near = hold(tiles[0])
+    seen = join(hp, near)
     cross = lax.ppermute(seen, "sub", [(1, 2), (2, 1), (3, 4), (4, 3), (5, 6), (6, 5)])
     cross, *tiles = lax.optimization_barrier((cross, *tiles))
     mine, other = hand(pos, tiles, seen)

time: 70.7 us -> 69.9 us (0.989)
  other arithmetic: 0.77 us -> 0 us
    concatenate x1 -> x0, other arithmetic: 0.77 us -> none  [per_device(): seen = jnp.concatenate([hp[:, 0:128].astype(bf16), near], axis=0)]
    pallas_call x2 -> x3, Pallas kernels: 2.3 us -> 2.31 us  [the longest x1 2.29 us: pack(): pl.pallas_call(pack_kernel, out_shape=(jax.ShapeDtypeStruct((384, LANES),...]
  transfers between devices with their start and end apart: 6 -> 6, of which waited for: 3 -> 3; matrix products, arithmetic and copies ran while one was open for 1% -> 0% of each run, Pallas kernels for 0% -> 0%
where the time goes in v17:
time: 69.9 us; the launch traced here: 68.9 us
  blocking collectives  29.5 us (42%)
  starting transfers between devices  18.7 us (27%)
  Pallas kernels  13.8 us (20%)
  waiting for transfers between devices  5.97 us (9%)
  local copies, waits for them, and re-layouts  0.93 us (1%)
    all_to_all x1, blocking collectives, per_device(): lax.all_to_all(encode(owned), 'band', split_axis=0, concat_axis=0, tiled=...  19.4 us
    all_to_all x1, blocking collectives, per_device(): lax.all_to_all(new.reshape(8, 4, 8, LANES), 'sub', split_axis=0, concat_a...  10.1 us
    pallas_call x1, Pallas kernels, refine(): pl.pallas_call(refine_kernel, out_shape=jax.ShapeDtypeStruct((32 * 8, LAN...  9.2 us
    all_to_all x1, starting transfers between devices, per_device(): lax.all_to_all(sent, 'band', split_axis=0, concat_axis=0, tiled=True)  8.6 us
    ppermute x1, starting transfers between devices, per_device(): lax.ppermute(seen, 'sub', [(1, 2), (2, 1), (3, 4), (4, 3), (5, 6), (6, 5)])  5.1 us
    ppermute x3, starting transfers between devices, per_device(): lax.ppermute(tiles[d], 'sub', [(i, (i + 2 * d) % 8) for i in range(8)])  4.88 us
    pallas_call x1, Pallas kernels, pack(): pl.pallas_call(pack_kernel, out_shape=(jax.ShapeDtypeStruct((384, LANES),...  2.29 us
    ppermute x1, waiting for transfers between devices, per_device(): lax.ppermute(seen, 'sub', [(1, 2), (2, 1), (3, 4), (4, 3), (5, 6), (6, 5)])  2.25 us
  transfers between devices with their start and end apart: 6, of which 3 were waited for; matrix products, arithmetic and copies ran while one was open for 0% of the time, Pallas kernels for 0%

profile of v17, /device:TPU:1, one launch (start us, length us, event | category | flops | bytes accessed | tf_op | source)
XLA Modules:
  0.0 68.9 jit_solution(3283134211208910625)
XLA Ops:
  0.0 2.3 %pack.1 = (f32[384,128]{1,0:T(8,128)}, f32[256,128]{1,0:T(8,128)}, f32[256,128]{1,0:T(8,128)}, f32[256,128]{1,0:T(8,128)}, f32[16,16,256]{2,1,0:T(8,128)}) custom-call(s32[1]{0:T(128)} %bitcast.pos_ref, f32[4,128,1024]{2,1,0:T(8,128)} %c_ref.1, f32[4,128,1024]{2,1,0:T(8,128)} %c_ref.1, bf16[8,16,1024]{2,1,0:T(8,128)(2,1)} %mb_ref.1, ...), custom_call_target="tpu_custom_call" | custom-call | flops 100000000 | bytes 1600000 | tf_op jit(solution)/shard_map/pack/pallas_call | solution.py:275
  2.3 8.6 %all-to-all-start = ((f32[16,16,256]{2,1,0:T(8,128)}), f32[16,16,256]{2,1,0:T(8,128)S(1)}, u32[]{:S(2)}, u32[]{:S(2)}) async-start(f32[16,16,256]{2,1,0:T(8,128)} %get-tuple-element.19), calls=%async_computation | async-start | bytes 524288 | tf_op jit(solution)/shard_map/all_to_all | solution.py:433
  10.9 1.3 %collective-permute-start.1 = (f32[256,128]{1,0:T(8,128)}, f32[256,128]{1,0:T(8,128)S(1)}, u32[]{:S(2)}, u32[]{:S(2)}) collective-permute-start(f32[256,128]{1,0:T(8,128)} %get-tuple-element.23), channel_id=1, source_target_pairs={{0,32},{16,48},{32,64},{48,80},{64,96},{80,112},{96,0},{112,16},{1... | collective-permute-start | bytes 393224 | tf_op jit(solution)/shard_map/ppermute | solution.py:435
  12.2 2.4 %collective-permute-start.2 = (f32[256,128]{1,0:T(8,128)}, f32[256,128]{1,0:T(8,128)S(1)}, u32[]{:S(2)}, u32[]{:S(2)}) collective-permute-start(f32[256,128]{1,0:T(8,128)} %get-tuple-element.24), channel_id=1, source_target_pairs={{0,64},{16,80},{32,96},{48,112},{64,0},{80,16},{96,32},{112,48},{1... | collective-permute-start | bytes 393224 | tf_op jit(solution)/shard_map/ppermute | solution.py:435
  14.6 1.2 %collective-permute-start.3 = (f32[256,128]{1,0:T(8,128)}, f32[256,128]{1,0:T(8,128)S(1)}, u32[]{:S(2)}, u32[]{:S(2)}) collective-permute-start(f32[256,128]{1,0:T(8,128)} %get-tuple-element.25), channel_id=1, source_target_pairs={{0,96},{16,112},{32,0},{48,16},{64,32},{80,48},{96,64},{112,80},{1... | collective-permute-start | bytes 393224 | tf_op jit(solution)/shard_map/ppermute | solution.py:435
  15.8 0.0 copy-start.1
  15.8 0.9 %copy-done.1 = f32[384,128]{1,0:T(8,128)S(1)} copy-done((f32[384,128]{1,0:T(8,128)S(1)}, f32[384,128]{1,0:T(8,128)}, u32[]{:S(2)}) %copy-start.1) | copy-done | bytes 196632
  16.7 1.7 %all-to-all-done = f32[16,16,256]{2,1,0:T(8,128)S(1)} async-done(((f32[16,16,256]{2,1,0:T(8,128)}), f32[16,16,256]{2,1,0:T(8,128)S(1)}, u32[]{:S(2)}, u32[]{:S(2)}) %all-to-all-start) | async-done | bytes 262176 | tf_op jit(solution)/shard_map/all_to_all | solution.py:433
  18.5 5.1 %collective-permute-start = (bf16[384,128]{1,0:T(8,128)(2,1)S(1)}, bf16[384,128]{1,0:T(8,128)(2,1)S(1)}, u32[]{:S(2)}, u32[]{:S(2)}) collective-permute-start(bf16[384,128]{1,0:T(8,128)(2,1)S(1)} %join.1.seen_ref.refs_3_), channel_id=1, source_target_pairs={{16,32},{32,16},{48,64},{64,48},{80,96},{96,80},{17,33},{33,17},{4... | collective-permute-start | bytes 294920 | tf_op jit(solution)/shard_map/ppermute | solution.py:439
  23.6 0.0 collective-permute-done.1.r1
  23.6 0.0 collective-permute-done.2.r2
  23.6 0.0 collective-permute-done.3.r3
  23.6 2.3 %collective-permute-done.refs_4_ = bf16[384,128]{1,0:T(8,128)(2,1)S(1)} collective-permute-done((bf16[384,128]{1,0:T(8,128)(2,1)S(1)}, bf16[384,128]{1,0:T(8,128)(2,1)S(1)}, u32[]{:S(2)}, u32[]{:S(2)}) %collective-permute-start) | collective-permute-done | bytes 98336 | tf_op jit(solution)/shard_map/ppermute | solution.py:439
  25.9 0.1 hand.1
  25.9 0.1 collective-permute-start.4
  26.0 2.0 %collective-permute-done.4.refs_1_ = f32[1152,128]{1,0:T(8,128)S(1)} collective-permute-done((f32[1152,128]{1,0:T(8,128)S(1)}, f32[1152,128]{1,0:T(8,128)S(1)}, u32[]{:S(2)}, u32[]{:S(2)}) %collective-permute-start.4) | collective-permute-done | bytes 589856 | tf_op jit(solution)/shard_map/ppermute | solution.py:442
  28.0 9.2 %refine.1 = f32[256,128]{1,0:T(8,128)S(1)} custom-call(s32[1]{0:T(128)} %bitcast.pos_ref, f32[768,128]{1,0:T(8,128)S(1)} %get-tuple-element.30.refs_0_, f32[1152,128]{1,0:T(8,128)S(1)} %collective-permute-done.4.refs_1_, f32[256,256]{1,0:T(8,128)S(1)} %bitcast.5, bf16[384,128]{1,0:T(8,128)(2,1)S(1)} %join.1.seen_ref.refs_3_, ...), custom_call_target="tpu_custom_call" | custom-call | flops 400000000 | bytes 2000000 | tf_op jit(solution)/shard_map/refine/pallas_call | solution.py:186
  37.2 0.0 copy-start
  37.2 10.1 %all_to_all.15.d_ref = f32[8,4,8,128]{3,2,1,0:T(8,128)S(1)} all-to-all(f32[8,4,8,128]{3,2,1,0:T(8,128)S(1)} %bitcast.6), channel_id=1, replica_groups=mesh['sub'=8,'band'=16] {'sub'}, dimensions={0} | all-to-all | bytes 262144 | tf_op jit(solution)/shard_map/all_to_all | solution.py:444
  47.4 0.2 encode.1
  47.6 19.4 %all_to_all.16.g_ref = bf16[16,272,128]{2,1,0:T(8,128)(2,1)S(1)} all-to-all(bf16[16,272,128]{2,1,0:T(8,128)(2,1)S(1)} %encode.1), channel_id=1, replica_groups=mesh['sub'=8,'band'=16] {'band'}, dimensions={0} | all-to-all | bytes 2228224 | tf_op jit(solution)/shard_map/all_to_all | solution.py:445
  66.9 0.0 copy-done
  66.9 2.0 %place.1 = f32[4,128,1024]{2,1,0:T(8,128)} custom-call(bf16[16,272,128]{2,1,0:T(8,128)(2,1)S(1)} %all_to_all.16.g_ref, f32[4,128,1024]{2,1,0:T(8,128)S(1)} %copy-done), custom_call_target="tpu_custom_call" | custom-call | tf_op jit(solution)/shard_map/place/pallas_call | solution.py:419
  (2 shorter events, 0.0 us)
Async XLA Ops:
  2.3 16.2 %all-to-all-start = ((f32[16,16,256]{2,1,0:T(8,128)}), f32[16,16,256]{2,1,0:T(8,128)S(1)}, u32[]{:S(2)}, u32[]{:S(2)}) async-start(f32[16,16,256]{2,1,0:T(8,128)} %get-tuple-element.19), calls=%async_computation | async-start | bytes 524288 | tf_op jit(solution)/shard_map/all_to_all | solution.py:433
  10.9 12.7 %collective-permute-start.1 = (f32[256,128]{1,0:T(8,128)}, f32[256,128]{1,0:T(8,128)S(1)}, u32[]{:S(2)}, u32[]{:S(2)}) collective-permute-start(f32[256,128]{1,0:T(8,128)} %get-tuple-element.23), channel_id=1, source_target_pairs={{0,32},{16,48},{32,64},{48,80},{64,96},{80,112},{96,0},{112,16},{1... | collective-permute-start | bytes 393224 | tf_op jit(solution)/shard_map/ppermute | solution.py:435
  12.2 11.4 %collective-permute-start.2 = (f32[256,128]{1,0:T(8,128)}, f32[256,128]{1,0:T(8,128)S(1)}, u32[]{:S(2)}, u32[]{:S(2)}) collective-permute-start(f32[256,128]{1,0:T(8,128)} %get-tuple-element.24), channel_id=1, source_target_pairs={{0,64},{16,80},{32,96},{48,112},{64,0},{80,16},{96,32},{112,48},{1... | collective-permute-start | bytes 393224 | tf_op jit(solution)/shard_map/ppermute | solution.py:435
  14.6 9.0 %collective-permute-start.3 = (f32[256,128]{1,0:T(8,128)}, f32[256,128]{1,0:T(8,128)S(1)}, u32[]{:S(2)}, u32[]{:S(2)}) collective-permute-start(f32[256,128]{1,0:T(8,128)} %get-tuple-element.25), channel_id=1, source_target_pairs={{0,96},{16,112},{32,0},{48,16},{64,32},{80,48},{96,64},{112,80},{1... | collective-permute-start | bytes 393224 | tf_op jit(solution)/shard_map/ppermute | solution.py:435
  15.8 0.9 %copy-start.1 = (f32[384,128]{1,0:T(8,128)S(1)}, f32[384,128]{1,0:T(8,128)}, u32[]{:S(2)}) copy-start(f32[384,128]{1,0:T(8,128)} %get-tuple-element.20.region_ref) | copy-start | bytes 589828
  18.5 7.4 %collective-permute-start = (bf16[384,128]{1,0:T(8,128)(2,1)S(1)}, bf16[384,128]{1,0:T(8,128)(2,1)S(1)}, u32[]{:S(2)}, u32[]{:S(2)}) collective-permute-start(bf16[384,128]{1,0:T(8,128)(2,1)S(1)} %join.1.seen_ref.refs_3_), channel_id=1, source_target_pairs={{16,32},{32,16},{48,64},{64,48},{80,96},{96,80},{17,33},{33,17},{4... | collective-permute-start | bytes 294920 | tf_op jit(solution)/shard_map/ppermute | solution.py:439
  25.9 2.1 %collective-permute-start.4 = (f32[1152,128]{1,0:T(8,128)S(1)}, f32[1152,128]{1,0:T(8,128)S(1)}, u32[]{:S(2)}, u32[]{:S(2)}) collective-permute-start(f32[1152,128]{1,0:T(8,128)S(1)} %get-tuple-element.31), channel_id=1, source_target_pairs={{0,16},{16,0},{32,48},{48,32},{64,80},{80,64},{96,112},{112,96},{1... | collective-permute-start | bytes 1769480 | tf_op jit(solution)/shard_map/ppermute | solution.py:442
  37.2 29.7 %copy-start = (f32[4,128,1024]{2,1,0:T(8,128)S(1)}, f32[4,128,1024]{2,1,0:T(8,128)}, u32[]{:S(2)}) copy-start(f32[4,128,1024]{2,1,0:T(8,128)} %c_ref.1) | copy-start | bytes 6291460

commit v18 on v17

--- a/solution.py
+++ b/solution.py
@@ -104,10 +104,10 @@
             seen = hst[h][pl.ds(pl.multiple_of(n * JCOLS, 8), JCOLS), :]
             f[h][pl.ds(pl.multiple_of(8 + n * JCOLS, 8), JCOLS), :] = jnp.where(inside, seen - blurred, 0.0)
 
-    def back_rows(u):
+    def back_rows(u, first=0, count=JCOLS, phases=4):
         for h in range(2):
-            win = [[f[h][pl.ds(8 + (u - t) * JCOLS - tt, JCOLS), :] for tt in range(3)] for t in range(3)]
-            for p in range(4):
+            win = [[f[h][pl.ds(8 + (u - t) * JCOLS + first - tt, count), :] for tt in range(3)] for t in range(3)]
+            for p in range(phases):
                 for q in range(4):
                     total = None
                     for t in range(3):
@@ -117,8 +117,8 @@
                             tap = (p + 4 * t) * 9 + q + 4 * tt
                             term = w[h][tap : tap + 1, :] * win[t][tt]
                             total = term if total is None else total + term
-                    at = pl.multiple_of((4 * u - 8 + p) * LANES + 32 * q, 32)
-                    bk[h][pl.ds(at, JCOLS), :] = rounded(total)
+                    at = (4 * u - 8 + p) * LANES + 32 * q + first
+                    bk[h][pl.ds(at, count), :] = rounded(total)
 
     def hs_gradient(row, rows):
         at = pl.ds((row - 8) * LANES, rows * LANES)
@@ -141,7 +141,8 @@
         if 1 <= block < 5:
             ms_gradient(block * 8, value)
     loop(0, IROWS, blur_row)
-    loop(2, 10, back_rows)
+    loop(2, 9, back_rows)
+    back_rows(9, phases=1)
     for block in range(1, 5):
         grad = hs_gradient(block * 8, 8)
         values = []
@@ -158,7 +159,7 @@
         if 2 <= block < 4:
             ms_gradient(block * 8, value)
     loop(2, 8, blur_row)
-    loop(4, 8, back_rows)
+    loop(4, 8, lambda u: back_rows(u, 4, 16))
     place_at = lax.broadcasted_iota(jnp.int32, (LANES, LANES), 1)
     take = lax.broadcasted_iota(jnp.int32, (LANES, LANES), 0)
     shift = 4 * (take % 32) + take // 32 - 16

time: 69.9 us -> 69.6 us (level)
  no operation moved by 1% of the time
where the time goes in v18:
time: 69.6 us; the launch traced here: 68.6 us
  blocking collectives  29.5 us (42%)
  starting transfers between devices  18.7 us (27%)
  Pallas kernels  13.4 us (19%)
  waiting for transfers between devices  5.97 us (9%)
  local copies, waits for them, and re-layouts  0.93 us (1%)
    all_to_all x1, blocking collectives, per_device(): lax.all_to_all(encode(owned), 'band', split_axis=0, concat_axis=0, tiled=...  19.4 us
    all_to_all x1, blocking collectives, per_device(): lax.all_to_all(new.reshape(8, 4, 8, LANES), 'sub', split_axis=0, concat_a...  10.1 us
    pallas_call x1, Pallas kernels, refine(): pl.pallas_call(refine_kernel, out_shape=jax.ShapeDtypeStruct((32 * 8, LAN...  8.86 us
    all_to_all x1, starting transfers between devices, per_device(): lax.all_to_all(sent, 'band', split_axis=0, concat_axis=0, tiled=True)  8.6 us
    ppermute x1, starting transfers between devices, per_device(): lax.ppermute(seen, 'sub', [(1, 2), (2, 1), (3, 4), (4, 3), (5, 6), (6, 5)])  5.1 us
    ppermute x3, starting transfers between devices, per_device(): lax.ppermute(tiles[d], 'sub', [(i, (i + 2 * d) % 8) for i in range(8)])  4.88 us
    pallas_call x1, Pallas kernels, pack(): pl.pallas_call(pack_kernel, out_shape=(jax.ShapeDtypeStruct((384, LANES),...  2.29 us
    ppermute x1, waiting for transfers between devices, per_device(): lax.ppermute(seen, 'sub', [(1, 2), (2, 1), (3, 4), (4, 3), (5, 6), (6, 5)])  2.25 us
  transfers between devices with their start and end apart: 6, of which 3 were waited for; matrix products, arithmetic and copies ran while one was open for 0% of the time, Pallas kernels for 0%

profile of v18, /device:TPU:1, one launch (start us, length us, event | category | flops | bytes accessed | tf_op | source)
XLA Modules:
  0.0 68.6 jit_solution(11476200432549266698)
XLA Ops:
  0.0 2.3 %pack.1 = (f32[384,128]{1,0:T(8,128)}, f32[256,128]{1,0:T(8,128)}, f32[256,128]{1,0:T(8,128)}, f32[256,128]{1,0:T(8,128)}, f32[16,16,256]{2,1,0:T(8,128)}) custom-call(s32[1]{0:T(128)} %bitcast.pos_ref, f32[4,128,1024]{2,1,0:T(8,128)} %c_ref.1, f32[4,128,1024]{2,1,0:T(8,128)} %c_ref.1, bf16[8,16,1024]{2,1,0:T(8,128)(2,1)} %mb_ref.1, ...), custom_call_target="tpu_custom_call" | custom-call | flops 100000000 | bytes 1600000 | tf_op jit(solution)/shard_map/pack/pallas_call | solution.py:276
  2.3 8.6 %all-to-all-start = ((f32[16,16,256]{2,1,0:T(8,128)}), f32[16,16,256]{2,1,0:T(8,128)S(1)}, u32[]{:S(2)}, u32[]{:S(2)}) async-start(f32[16,16,256]{2,1,0:T(8,128)} %get-tuple-element.19), calls=%async_computation | async-start | bytes 524288 | tf_op jit(solution)/shard_map/all_to_all | solution.py:434
  10.9 1.3 %collective-permute-start.1 = (f32[256,128]{1,0:T(8,128)}, f32[256,128]{1,0:T(8,128)S(1)}, u32[]{:S(2)}, u32[]{:S(2)}) collective-permute-start(f32[256,128]{1,0:T(8,128)} %get-tuple-element.23), channel_id=1, source_target_pairs={{0,32},{16,48},{32,64},{48,80},{64,96},{80,112},{96,0},{112,16},{1... | collective-permute-start | bytes 393224 | tf_op jit(solution)/shard_map/ppermute | solution.py:436
  12.2 2.4 %collective-permute-start.2 = (f32[256,128]{1,0:T(8,128)}, f32[256,128]{1,0:T(8,128)S(1)}, u32[]{:S(2)}, u32[]{:S(2)}) collective-permute-start(f32[256,128]{1,0:T(8,128)} %get-tuple-element.24), channel_id=1, source_target_pairs={{0,64},{16,80},{32,96},{48,112},{64,0},{80,16},{96,32},{112,48},{1... | collective-permute-start | bytes 393224 | tf_op jit(solution)/shard_map/ppermute | solution.py:436
  14.6 1.2 %collective-permute-start.3 = (f32[256,128]{1,0:T(8,128)}, f32[256,128]{1,0:T(8,128)S(1)}, u32[]{:S(2)}, u32[]{:S(2)}) collective-permute-start(f32[256,128]{1,0:T(8,128)} %get-tuple-element.25), channel_id=1, source_target_pairs={{0,96},{16,112},{32,0},{48,16},{64,32},{80,48},{96,64},{112,80},{1... | collective-permute-start | bytes 393224 | tf_op jit(solution)/shard_map/ppermute | solution.py:436
  15.8 0.0 copy-start.1
  15.8 0.9 %copy-done.1 = f32[384,128]{1,0:T(8,128)S(1)} copy-done((f32[384,128]{1,0:T(8,128)S(1)}, f32[384,128]{1,0:T(8,128)}, u32[]{:S(2)}) %copy-start.1) | copy-done | bytes 196632
  16.7 1.7 %all-to-all-done = f32[16,16,256]{2,1,0:T(8,128)S(1)} async-done(((f32[16,16,256]{2,1,0:T(8,128)}), f32[16,16,256]{2,1,0:T(8,128)S(1)}, u32[]{:S(2)}, u32[]{:S(2)}) %all-to-all-start) | async-done | bytes 262176 | tf_op jit(solution)/shard_map/all_to_all | solution.py:434
  18.5 5.1 %collective-permute-start = (bf16[384,128]{1,0:T(8,128)(2,1)S(1)}, bf16[384,128]{1,0:T(8,128)(2,1)S(1)}, u32[]{:S(2)}, u32[]{:S(2)}) collective-permute-start(bf16[384,128]{1,0:T(8,128)(2,1)S(1)} %join.1.seen_ref.refs_3_), channel_id=1, source_target_pairs={{16,32},{32,16},{48,64},{64,48},{80,96},{96,80},{17,33},{33,17},{4... | collective-permute-start | bytes 294920 | tf_op jit(solution)/shard_map/ppermute | solution.py:440
  23.6 0.0 collective-permute-done.1.r1
  23.6 0.0 collective-permute-done.2.r2
  23.6 0.0 collective-permute-done.3.r3
  23.6 2.3 %collective-permute-done.refs_4_ = bf16[384,128]{1,0:T(8,128)(2,1)S(1)} collective-permute-done((bf16[384,128]{1,0:T(8,128)(2,1)S(1)}, bf16[384,128]{1,0:T(8,128)(2,1)S(1)}, u32[]{:S(2)}, u32[]{:S(2)}) %collective-permute-start) | collective-permute-done | bytes 98336 | tf_op jit(solution)/shard_map/ppermute | solution.py:440
  25.9 0.1 hand.1
  25.9 0.1 collective-permute-start.4
  26.0 2.0 %collective-permute-done.4.refs_1_ = f32[1152,128]{1,0:T(8,128)S(1)} collective-permute-done((f32[1152,128]{1,0:T(8,128)S(1)}, f32[1152,128]{1,0:T(8,128)S(1)}, u32[]{:S(2)}, u32[]{:S(2)}) %collective-permute-start.4) | collective-permute-done | bytes 589856 | tf_op jit(solution)/shard_map/ppermute | solution.py:443
  28.0 8.9 %refine.1 = f32[256,128]{1,0:T(8,128)S(1)} custom-call(s32[1]{0:T(128)} %bitcast.pos_ref, f32[768,128]{1,0:T(8,128)S(1)} %get-tuple-element.30.refs_0_, f32[1152,128]{1,0:T(8,128)S(1)} %collective-permute-done.4.refs_1_, f32[256,256]{1,0:T(8,128)S(1)} %bitcast.5, bf16[384,128]{1,0:T(8,128)(2,1)S(1)} %join.1.seen_ref.refs_3_, ...), custom_call_target="tpu_custom_call" | custom-call | flops 400000000 | bytes 2000000 | tf_op jit(solution)/shard_map/refine/pallas_call | solution.py:187
  36.9 0.0 copy-start
  36.9 10.1 %all_to_all.15.d_ref = f32[8,4,8,128]{3,2,1,0:T(8,128)S(1)} all-to-all(f32[8,4,8,128]{3,2,1,0:T(8,128)S(1)} %bitcast.6), channel_id=1, replica_groups=mesh['sub'=8,'band'=16] {'sub'}, dimensions={0} | all-to-all | bytes 262144 | tf_op jit(solution)/shard_map/all_to_all | solution.py:445
  47.0 0.2 encode.1
  47.2 19.4 %all_to_all.16.g_ref = bf16[16,272,128]{2,1,0:T(8,128)(2,1)S(1)} all-to-all(bf16[16,272,128]{2,1,0:T(8,128)(2,1)S(1)} %encode.1), channel_id=1, replica_groups=mesh['sub'=8,'band'=16] {'band'}, dimensions={0} | all-to-all | bytes 2228224 | tf_op jit(solution)/shard_map/all_to_all | solution.py:446
  66.6 0.0 copy-done
  66.6 2.0 %place.1 = f32[4,128,1024]{2,1,0:T(8,128)} custom-call(bf16[16,272,128]{2,1,0:T(8,128)(2,1)S(1)} %all_to_all.16.g_ref, f32[4,128,1024]{2,1,0:T(8,128)S(1)} %copy-done), custom_call_target="tpu_custom_call" | custom-call | tf_op jit(solution)/shard_map/place/pallas_call | solution.py:420
  (2 shorter events, 0.0 us)
Async XLA Ops:
  2.3 16.2 %all-to-all-start = ((f32[16,16,256]{2,1,0:T(8,128)}), f32[16,16,256]{2,1,0:T(8,128)S(1)}, u32[]{:S(2)}, u32[]{:S(2)}) async-start(f32[16,16,256]{2,1,0:T(8,128)} %get-tuple-element.19), calls=%async_computation | async-start | bytes 524288 | tf_op jit(solution)/shard_map/all_to_all | solution.py:434
  10.9 12.7 %collective-permute-start.1 = (f32[256,128]{1,0:T(8,128)}, f32[256,128]{1,0:T(8,128)S(1)}, u32[]{:S(2)}, u32[]{:S(2)}) collective-permute-start(f32[256,128]{1,0:T(8,128)} %get-tuple-element.23), channel_id=1, source_target_pairs={{0,32},{16,48},{32,64},{48,80},{64,96},{80,112},{96,0},{112,16},{1... | collective-permute-start | bytes 393224 | tf_op jit(solution)/shard_map/ppermute | solution.py:436
  12.2 11.4 %collective-permute-start.2 = (f32[256,128]{1,0:T(8,128)}, f32[256,128]{1,0:T(8,128)S(1)}, u32[]{:S(2)}, u32[]{:S(2)}) collective-permute-start(f32[256,128]{1,0:T(8,128)} %get-tuple-element.24), channel_id=1, source_target_pairs={{0,64},{16,80},{32,96},{48,112},{64,0},{80,16},{96,32},{112,48},{1... | collective-permute-start | bytes 393224 | tf_op jit(solution)/shard_map/ppermute | solution.py:436
  14.6 9.0 %collective-permute-start.3 = (f32[256,128]{1,0:T(8,128)}, f32[256,128]{1,0:T(8,128)S(1)}, u32[]{:S(2)}, u32[]{:S(2)}) collective-permute-start(f32[256,128]{1,0:T(8,128)} %get-tuple-element.25), channel_id=1, source_target_pairs={{0,96},{16,112},{32,0},{48,16},{64,32},{80,48},{96,64},{112,80},{1... | collective-permute-start | bytes 393224 | tf_op jit(solution)/shard_map/ppermute | solution.py:436
  15.8 0.9 %copy-start.1 = (f32[384,128]{1,0:T(8,128)S(1)}, f32[384,128]{1,0:T(8,128)}, u32[]{:S(2)}) copy-start(f32[384,128]{1,0:T(8,128)} %get-tuple-element.20.region_ref) | copy-start | bytes 589828
  18.5 7.4 %collective-permute-start = (bf16[384,128]{1,0:T(8,128)(2,1)S(1)}, bf16[384,128]{1,0:T(8,128)(2,1)S(1)}, u32[]{:S(2)}, u32[]{:S(2)}) collective-permute-start(bf16[384,128]{1,0:T(8,128)(2,1)S(1)} %join.1.seen_ref.refs_3_), channel_id=1, source_target_pairs={{16,32},{32,16},{48,64},{64,48},{80,96},{96,80},{17,33},{33,17},{4... | collective-permute-start | bytes 294920 | tf_op jit(solution)/shard_map/ppermute | solution.py:440
  25.9 2.1 %collective-permute-start.4 = (f32[1152,128]{1,0:T(8,128)S(1)}, f32[1152,128]{1,0:T(8,128)S(1)}, u32[]{:S(2)}, u32[]{:S(2)}) collective-permute-start(f32[1152,128]{1,0:T(8,128)S(1)} %get-tuple-element.31), channel_id=1, source_target_pairs={{0,16},{16,0},{32,48},{48,32},{64,80},{80,64},{96,112},{112,96},{1... | collective-permute-start | bytes 1769480 | tf_op jit(solution)/shard_map/ppermute | solution.py:443
  36.9 29.7 %copy-start = (f32[4,128,1024]{2,1,0:T(8,128)S(1)}, f32[4,128,1024]{2,1,0:T(8,128)}, u32[]{:S(2)}) copy-start(f32[4,128,1024]{2,1,0:T(8,128)} %c_ref.1) | copy-start | bytes 6291460

commit v19 on v18

--- a/solution.py
+++ b/solution.py
@@ -336,7 +336,7 @@
     )(hp, near)
 
 
-def hand_kernel(pos_ref, r0, r1, r2, r3, seen_ref, mine_ref, other_ref):
+def hand_kernel(pos_ref, r0, r2, r1, r3, seen_ref, mine_ref, other_ref):
     other_ref[16 * CROWS : 16 * CROWS + 384] = seen_ref[...].astype(f32)
     skip = 16 * (pos_ref[0] // 16 % 2)
     for d, region in enumerate((r0, r1, r2, r3)):
@@ -359,7 +359,7 @@
         compiler_params=pltpu.CompilerParams(vmem_limit_bytes=16 * 2**20),
         cost_estimate=pl.CostEstimate(flops=1_000_000, bytes_accessed=800_000, transcendentals=0),
         name="hand",
-    )(pos, *tiles, seen)
+    )(pos, tiles[0], tiles[2], tiles[1], tiles[3], seen)
 
 
 def encode_kernel(d_ref, out_ref):
@@ -432,9 +432,8 @@
     pos = (lax.axis_index("sub") * 16 + lax.axis_index("band")).astype(jnp.int32).reshape(1)
     *tiles, sent = pack(pos, coeffs_in, ms_image, hs_image, kernels.transpose(1, 0, 2), basis, response)
     hp = lax.all_to_all(sent, "band", split_axis=0, concat_axis=0, tiled=True).reshape(256, 256)
-    tiles = [tiles[0]] + [
-        lax.ppermute(tiles[d], "sub", [(i, (i + 2 * d) % 8) for i in range(8)]) for d in range(1, 4)
-    ]
+    for d in (2, 1, 3):
+        tiles[d] = lax.ppermute(tiles[d], "sub", [(i, (i + 2 * d) % 8) for i in range(8)])
     tiles[0], near = hold(tiles[0])
     seen = join(hp, near)
     cross = lax.ppermute(seen, "sub", [(1, 2), (2, 1), (3, 4), (4, 3), (5, 6), (6, 5)])

time: 69.6 us -> 69.6 us (level)
  no operation moved by 1% of the time
where the time goes in v19:
time: 69.6 us; the launch traced here: 68.6 us
  blocking collectives  29.5 us (42%)
  starting transfers between devices  18.7 us (27%)
  Pallas kernels  13.4 us (19%)
  waiting for transfers between devices  5.97 us (9%)
  local copies, waits for them, and re-layouts  0.93 us (1%)
    all_to_all x1, blocking collectives, per_device(): lax.all_to_all(encode(owned), 'band', split_axis=0, concat_axis=0, tiled=...  19.4 us
    all_to_all x1, blocking collectives, per_device(): lax.all_to_all(new.reshape(8, 4, 8, LANES), 'sub', split_axis=0, concat_a...  10.1 us
    pallas_call x1, Pallas kernels, refine(): pl.pallas_call(refine_kernel, out_shape=jax.ShapeDtypeStruct((32 * 8, LAN...  8.86 us
    all_to_all x1, starting transfers between devices, per_device(): lax.all_to_all(sent, 'band', split_axis=0, concat_axis=0, tiled=True)  8.6 us
    ppermute x1, starting transfers between devices, per_device(): lax.ppermute(seen, 'sub', [(1, 2), (2, 1), (3, 4), (4, 3), (5, 6), (6, 5)])  5.1 us
    ppermute x3, starting transfers between devices, per_device(): lax.ppermute(tiles[d], 'sub', [(i, (i + 2 * d) % 8) for i in range(8)])  4.88 us
    pallas_call x1, Pallas kernels, pack(): pl.pallas_call(pack_kernel, out_shape=(jax.ShapeDtypeStruct((384, LANES),...  2.29 us
    ppermute x1, waiting for transfers between devices, per_device(): lax.ppermute(seen, 'sub', [(1, 2), (2, 1), (3, 4), (4, 3), (5, 6), (6, 5)])  2.25 us
  transfers between devices with their start and end apart: 6, of which 3 were waited for; matrix products, arithmetic and copies ran while one was open for 0% of the time, Pallas kernels for 0%

profile of v19, /device:TPU:1, one launch (start us, length us, event | category | flops | bytes accessed | tf_op | source)
XLA Modules:
  0.0 68.6 jit_solution(17885831616607562438)
XLA Ops:
  0.0 2.3 %pack.1 = (f32[384,128]{1,0:T(8,128)}, f32[256,128]{1,0:T(8,128)}, f32[256,128]{1,0:T(8,128)}, f32[256,128]{1,0:T(8,128)}, f32[16,16,256]{2,1,0:T(8,128)}) custom-call(s32[1]{0:T(128)} %bitcast.pos_ref, f32[4,128,1024]{2,1,0:T(8,128)} %c_ref.1, f32[4,128,1024]{2,1,0:T(8,128)} %c_ref.1, bf16[8,16,1024]{2,1,0:T(8,128)(2,1)} %mb_ref.1, ...), custom_call_target="tpu_custom_call" | custom-call | flops 100000000 | bytes 1600000 | tf_op jit(solution)/shard_map/pack/pallas_call | solution.py:276
  2.3 8.6 %all-to-all-start = ((f32[16,16,256]{2,1,0:T(8,128)}), f32[16,16,256]{2,1,0:T(8,128)S(1)}, u32[]{:S(2)}, u32[]{:S(2)}) async-start(f32[16,16,256]{2,1,0:T(8,128)} %get-tuple-element.19), calls=%async_computation | async-start | bytes 524288 | tf_op jit(solution)/shard_map/all_to_all | solution.py:434
  10.9 1.3 %collective-permute-start.1 = (f32[256,128]{1,0:T(8,128)}, f32[256,128]{1,0:T(8,128)S(1)}, u32[]{:S(2)}, u32[]{:S(2)}) collective-permute-start(f32[256,128]{1,0:T(8,128)} %get-tuple-element.23), channel_id=1, source_target_pairs={{0,32},{16,48},{32,64},{48,80},{64,96},{80,112},{96,0},{112,16},{1... | collective-permute-start | bytes 393224 | tf_op jit(solution)/shard_map/ppermute | solution.py:436
  12.2 2.4 %collective-permute-start.2 = (f32[256,128]{1,0:T(8,128)}, f32[256,128]{1,0:T(8,128)S(1)}, u32[]{:S(2)}, u32[]{:S(2)}) collective-permute-start(f32[256,128]{1,0:T(8,128)} %get-tuple-element.24), channel_id=1, source_target_pairs={{0,64},{16,80},{32,96},{48,112},{64,0},{80,16},{96,32},{112,48},{1... | collective-permute-start | bytes 393224 | tf_op jit(solution)/shard_map/ppermute | solution.py:436
  14.6 1.2 %collective-permute-start.3 = (f32[256,128]{1,0:T(8,128)}, f32[256,128]{1,0:T(8,128)S(1)}, u32[]{:S(2)}, u32[]{:S(2)}) collective-permute-start(f32[256,128]{1,0:T(8,128)} %get-tuple-element.25), channel_id=1, source_target_pairs={{0,96},{16,112},{32,0},{48,16},{64,32},{80,48},{96,64},{112,80},{1... | collective-permute-start | bytes 393224 | tf_op jit(solution)/shard_map/ppermute | solution.py:436
  15.8 0.0 copy-start.1
  15.8 0.9 %copy-done.1 = f32[384,128]{1,0:T(8,128)S(1)} copy-done((f32[384,128]{1,0:T(8,128)S(1)}, f32[384,128]{1,0:T(8,128)}, u32[]{:S(2)}) %copy-start.1) | copy-done | bytes 196632
  16.7 1.7 %all-to-all-done = f32[16,16,256]{2,1,0:T(8,128)S(1)} async-done(((f32[16,16,256]{2,1,0:T(8,128)}), f32[16,16,256]{2,1,0:T(8,128)S(1)}, u32[]{:S(2)}, u32[]{:S(2)}) %all-to-all-start) | async-done | bytes 262176 | tf_op jit(solution)/shard_map/all_to_all | solution.py:434
  18.5 5.1 %collective-permute-start = (bf16[384,128]{1,0:T(8,128)(2,1)S(1)}, bf16[384,128]{1,0:T(8,128)(2,1)S(1)}, u32[]{:S(2)}, u32[]{:S(2)}) collective-permute-start(bf16[384,128]{1,0:T(8,128)(2,1)S(1)} %join.1.seen_ref.refs_3_), channel_id=1, source_target_pairs={{16,32},{32,16},{48,64},{64,48},{80,96},{96,80},{17,33},{33,17},{4... | collective-permute-start | bytes 294920 | tf_op jit(solution)/shard_map/ppermute | solution.py:439
  23.6 0.0 collective-permute-done.1.r1
  23.6 0.0 collective-permute-done.2.r2
  23.6 0.0 collective-permute-done.3.r3
  23.6 2.3 %collective-permute-done.refs_4_ = bf16[384,128]{1,0:T(8,128)(2,1)S(1)} collective-permute-done((bf16[384,128]{1,0:T(8,128)(2,1)S(1)}, bf16[384,128]{1,0:T(8,128)(2,1)S(1)}, u32[]{:S(2)}, u32[]{:S(2)}) %collective-permute-start) | collective-permute-done | bytes 98336 | tf_op jit(solution)/shard_map/ppermute | solution.py:439
  25.9 0.1 hand.1
  25.9 0.1 collective-permute-start.4
  26.0 2.0 %collective-permute-done.4.refs_1_ = f32[1152,128]{1,0:T(8,128)S(1)} collective-permute-done((f32[1152,128]{1,0:T(8,128)S(1)}, f32[1152,128]{1,0:T(8,128)S(1)}, u32[]{:S(2)}, u32[]{:S(2)}) %collective-permute-start.4) | collective-permute-done | bytes 589856 | tf_op jit(solution)/shard_map/ppermute | solution.py:442
  28.0 8.9 %refine.1 = f32[256,128]{1,0:T(8,128)S(1)} custom-call(s32[1]{0:T(128)} %bitcast.pos_ref, f32[768,128]{1,0:T(8,128)S(1)} %get-tuple-element.30.refs_0_, f32[1152,128]{1,0:T(8,128)S(1)} %collective-permute-done.4.refs_1_, f32[256,256]{1,0:T(8,128)S(1)} %bitcast.5, bf16[384,128]{1,0:T(8,128)(2,1)S(1)} %join.1.seen_ref.refs_3_, ...), custom_call_target="tpu_custom_call" | custom-call | flops 400000000 | bytes 2000000 | tf_op jit(solution)/shard_map/refine/pallas_call | solution.py:187
  36.9 0.0 copy-start
  36.9 10.1 %all_to_all.15.d_ref = f32[8,4,8,128]{3,2,1,0:T(8,128)S(1)} all-to-all(f32[8,4,8,128]{3,2,1,0:T(8,128)S(1)} %bitcast.6), channel_id=1, replica_groups=mesh['sub'=8,'band'=16] {'sub'}, dimensions={0} | all-to-all | bytes 262144 | tf_op jit(solution)/shard_map/all_to_all | solution.py:444
  47.0 0.2 encode.1
  47.2 19.4 %all_to_all.16.g_ref = bf16[16,272,128]{2,1,0:T(8,128)(2,1)S(1)} all-to-all(bf16[16,272,128]{2,1,0:T(8,128)(2,1)S(1)} %encode.1), channel_id=1, replica_groups=mesh['sub'=8,'band'=16] {'band'}, dimensions={0} | all-to-all | bytes 2228224 | tf_op jit(solution)/shard_map/all_to_all | solution.py:445
  66.6 0.0 copy-done
  66.6 2.0 %place.1 = f32[4,128,1024]{2,1,0:T(8,128)} custom-call(bf16[16,272,128]{2,1,0:T(8,128)(2,1)S(1)} %all_to_all.16.g_ref, f32[4,128,1024]{2,1,0:T(8,128)S(1)} %copy-done), custom_call_target="tpu_custom_call" | custom-call | tf_op jit(solution)/shard_map/place/pallas_call | solution.py:420
  (2 shorter events, 0.0 us)
Async XLA Ops:
  2.3 16.2 %all-to-all-start = ((f32[16,16,256]{2,1,0:T(8,128)}), f32[16,16,256]{2,1,0:T(8,128)S(1)}, u32[]{:S(2)}, u32[]{:S(2)}) async-start(f32[16,16,256]{2,1,0:T(8,128)} %get-tuple-element.19), calls=%async_computation | async-start | bytes 524288 | tf_op jit(solution)/shard_map/all_to_all | solution.py:434
  10.9 12.7 %collective-permute-start.1 = (f32[256,128]{1,0:T(8,128)}, f32[256,128]{1,0:T(8,128)S(1)}, u32[]{:S(2)}, u32[]{:S(2)}) collective-permute-start(f32[256,128]{1,0:T(8,128)} %get-tuple-element.23), channel_id=1, source_target_pairs={{0,32},{16,48},{32,64},{48,80},{64,96},{80,112},{96,0},{112,16},{1... | collective-permute-start | bytes 393224 | tf_op jit(solution)/shard_map/ppermute | solution.py:436
  12.2 11.4 %collective-permute-start.2 = (f32[256,128]{1,0:T(8,128)}, f32[256,128]{1,0:T(8,128)S(1)}, u32[]{:S(2)}, u32[]{:S(2)}) collective-permute-start(f32[256,128]{1,0:T(8,128)} %get-tuple-element.24), channel_id=1, source_target_pairs={{0,64},{16,80},{32,96},{48,112},{64,0},{80,16},{96,32},{112,48},{1... | collective-permute-start | bytes 393224 | tf_op jit(solution)/shard_map/ppermute | solution.py:436
  14.6 9.0 %collective-permute-start.3 = (f32[256,128]{1,0:T(8,128)}, f32[256,128]{1,0:T(8,128)S(1)}, u32[]{:S(2)}, u32[]{:S(2)}) collective-permute-start(f32[256,128]{1,0:T(8,128)} %get-tuple-element.25), channel_id=1, source_target_pairs={{0,96},{16,112},{32,0},{48,16},{64,32},{80,48},{96,64},{112,80},{1... | collective-permute-start | bytes 393224 | tf_op jit(solution)/shard_map/ppermute | solution.py:436
  15.8 0.9 %copy-start.1 = (f32[384,128]{1,0:T(8,128)S(1)}, f32[384,128]{1,0:T(8,128)}, u32[]{:S(2)}) copy-start(f32[384,128]{1,0:T(8,128)} %get-tuple-element.20.region_ref) | copy-start | bytes 589828
  18.5 7.4 %collective-permute-start = (bf16[384,128]{1,0:T(8,128)(2,1)S(1)}, bf16[384,128]{1,0:T(8,128)(2,1)S(1)}, u32[]{:S(2)}, u32[]{:S(2)}) collective-permute-start(bf16[384,128]{1,0:T(8,128)(2,1)S(1)} %join.1.seen_ref.refs_3_), channel_id=1, source_target_pairs={{16,32},{32,16},{48,64},{64,48},{80,96},{96,80},{17,33},{33,17},{4... | collective-permute-start | bytes 294920 | tf_op jit(solution)/shard_map/ppermute | solution.py:439
  25.9 2.1 %collective-permute-start.4 = (f32[1152,128]{1,0:T(8,128)S(1)}, f32[1152,128]{1,0:T(8,128)S(1)}, u32[]{:S(2)}, u32[]{:S(2)}) collective-permute-start(f32[1152,128]{1,0:T(8,128)S(1)} %get-tuple-element.31), channel_id=1, source_target_pairs={{0,16},{16,0},{32,48},{48,32},{64,80},{80,64},{96,112},{112,96},{1... | collective-permute-start | bytes 1769480 | tf_op jit(solution)/shard_map/ppermute | solution.py:442
  36.9 29.7 %copy-start = (f32[4,128,1024]{2,1,0:T(8,128)S(1)}, f32[4,128,1024]{2,1,0:T(8,128)}, u32[]{:S(2)}) copy-start(f32[4,128,1024]{2,1,0:T(8,128)} %c_ref.1) | copy-start | bytes 6291460

commit v20 on v18

--- a/solution.py
+++ b/solution.py
@@ -416,12 +416,12 @@
 
 
 def place(gathered, coeffs_in):
-    block = pl.BlockSpec((4, 128, 4 * LANES), lambda j: (0, 0, j))
+    block = pl.BlockSpec((4, 128, 8 * LANES), lambda j: (0, 0, j))
     return pl.pallas_call(
         place_kernel,
         out_shape=jax.ShapeDtypeStruct((4, 128, 1024), f32),
-        grid=(2,),
-        in_specs=[pl.BlockSpec((8, 272, LANES), lambda j: (j, 0, 0)), block],
+        grid=(1,),
+        in_specs=[pl.BlockSpec((16, 272, LANES), lambda j: (j, 0, 0)), block],
         out_specs=block,
         compiler_params=pltpu.CompilerParams(vmem_limit_bytes=32 * 2**20),
         name="place",

time: 69.6 us -> 69.7 us (level)
  no operation moved by 1% of the time
where the time goes in v20:
time: 69.7 us; the launch traced here: 68.7 us
  blocking collectives  29.5 us (42%)
  starting transfers between devices  18.7 us (27%)
  Pallas kernels  13.5 us (19%)
  waiting for transfers between devices  5.97 us (9%)
  local copies, waits for them, and re-layouts  0.93 us (1%)
    all_to_all x1, blocking collectives, per_device(): lax.all_to_all(encode(owned), 'band', split_axis=0, concat_axis=0, tiled=...  19.4 us
    all_to_all x1, blocking collectives, per_device(): lax.all_to_all(new.reshape(8, 4, 8, LANES), 'sub', split_axis=0, concat_a...  10.1 us
    pallas_call x1, Pallas kernels, refine(): pl.pallas_call(refine_kernel, out_shape=jax.ShapeDtypeStruct((32 * 8, LAN...  8.86 us
    all_to_all x1, starting transfers between devices, per_device(): lax.all_to_all(sent, 'band', split_axis=0, concat_axis=0, tiled=True)  8.6 us
    ppermute x1, starting transfers between devices, per_device(): lax.ppermute(seen, 'sub', [(1, 2), (2, 1), (3, 4), (4, 3), (5, 6), (6, 5)])  5.1 us
    ppermute x3, starting transfers between devices, per_device(): lax.ppermute(tiles[d], 'sub', [(i, (i + 2 * d) % 8) for i in range(8)])  4.88 us
    pallas_call x1, Pallas kernels, pack(): pl.pallas_call(pack_kernel, out_shape=(jax.ShapeDtypeStruct((384, LANES),...  2.29 us
    ppermute x1, waiting for transfers between devices, per_device(): lax.ppermute(seen, 'sub', [(1, 2), (2, 1), (3, 4), (4, 3), (5, 6), (6, 5)])  2.25 us
  transfers between devices with their start and end apart: 6, of which 3 were waited for; matrix products, arithmetic and copies ran while one was open for 0% of the time, Pallas kernels for 0%

profile of v20, /device:TPU:1, one launch (start us, length us, event | category | flops | bytes accessed | tf_op | source)
XLA Modules:
  0.0 68.7 jit_solution(16433409050072339657)
XLA Ops:
  0.0 2.3 %pack.1 = (f32[384,128]{1,0:T(8,128)}, f32[256,128]{1,0:T(8,128)}, f32[256,128]{1,0:T(8,128)}, f32[256,128]{1,0:T(8,128)}, f32[16,16,256]{2,1,0:T(8,128)}) custom-call(s32[1]{0:T(128)} %bitcast.pos_ref, f32[4,128,1024]{2,1,0:T(8,128)} %c_ref.1, f32[4,128,1024]{2,1,0:T(8,128)} %c_ref.1, bf16[8,16,1024]{2,1,0:T(8,128)(2,1)} %mb_ref.1, ...), custom_call_target="tpu_custom_call" | custom-call | flops 100000000 | bytes 1600000 | tf_op jit(solution)/shard_map/pack/pallas_call | solution.py:276
  2.3 8.6 %all-to-all-start = ((f32[16,16,256]{2,1,0:T(8,128)}), f32[16,16,256]{2,1,0:T(8,128)S(1)}, u32[]{:S(2)}, u32[]{:S(2)}) async-start(f32[16,16,256]{2,1,0:T(8,128)} %get-tuple-element.19), calls=%async_computation | async-start | bytes 524288 | tf_op jit(solution)/shard_map/all_to_all | solution.py:434
  10.9 1.3 %collective-permute-start.1 = (f32[256,128]{1,0:T(8,128)}, f32[256,128]{1,0:T(8,128)S(1)}, u32[]{:S(2)}, u32[]{:S(2)}) collective-permute-start(f32[256,128]{1,0:T(8,128)} %get-tuple-element.23), channel_id=1, source_target_pairs={{0,32},{16,48},{32,64},{48,80},{64,96},{80,112},{96,0},{112,16},{1... | collective-permute-start | bytes 393224 | tf_op jit(solution)/shard_map/ppermute | solution.py:436
  12.2 2.4 %collective-permute-start.2 = (f32[256,128]{1,0:T(8,128)}, f32[256,128]{1,0:T(8,128)S(1)}, u32[]{:S(2)}, u32[]{:S(2)}) collective-permute-start(f32[256,128]{1,0:T(8,128)} %get-tuple-element.24), channel_id=1, source_target_pairs={{0,64},{16,80},{32,96},{48,112},{64,0},{80,16},{96,32},{112,48},{1... | collective-permute-start | bytes 393224 | tf_op jit(solution)/shard_map/ppermute | solution.py:436
  14.6 1.2 %collective-permute-start.3 = (f32[256,128]{1,0:T(8,128)}, f32[256,128]{1,0:T(8,128)S(1)}, u32[]{:S(2)}, u32[]{:S(2)}) collective-permute-start(f32[256,128]{1,0:T(8,128)} %get-tuple-element.25), channel_id=1, source_target_pairs={{0,96},{16,112},{32,0},{48,16},{64,32},{80,48},{96,64},{112,80},{1... | collective-permute-start | bytes 393224 | tf_op jit(solution)/shard_map/ppermute | solution.py:436
  15.8 0.0 copy-start.1
  15.8 0.9 %copy-done.1 = f32[384,128]{1,0:T(8,128)S(1)} copy-done((f32[384,128]{1,0:T(8,128)S(1)}, f32[384,128]{1,0:T(8,128)}, u32[]{:S(2)}) %copy-start.1) | copy-done | bytes 196632
  16.7 1.7 %all-to-all-done = f32[16,16,256]{2,1,0:T(8,128)S(1)} async-done(((f32[16,16,256]{2,1,0:T(8,128)}), f32[16,16,256]{2,1,0:T(8,128)S(1)}, u32[]{:S(2)}, u32[]{:S(2)}) %all-to-all-start) | async-done | bytes 262176 | tf_op jit(solution)/shard_map/all_to_all | solution.py:434
  18.5 5.1 %collective-permute-start = (bf16[384,128]{1,0:T(8,128)(2,1)S(1)}, bf16[384,128]{1,0:T(8,128)(2,1)S(1)}, u32[]{:S(2)}, u32[]{:S(2)}) collective-permute-start(bf16[384,128]{1,0:T(8,128)(2,1)S(1)} %join.1.seen_ref.refs_3_), channel_id=1, source_target_pairs={{16,32},{32,16},{48,64},{64,48},{80,96},{96,80},{17,33},{33,17},{4... | collective-permute-start | bytes 294920 | tf_op jit(solution)/shard_map/ppermute | solution.py:440
  23.6 0.0 collective-permute-done.1.r1
  23.6 0.0 collective-permute-done.2.r2
  23.6 0.0 collective-permute-done.3.r3
  23.6 2.3 %collective-permute-done.refs_4_ = bf16[384,128]{1,0:T(8,128)(2,1)S(1)} collective-permute-done((bf16[384,128]{1,0:T(8,128)(2,1)S(1)}, bf16[384,128]{1,0:T(8,128)(2,1)S(1)}, u32[]{:S(2)}, u32[]{:S(2)}) %collective-permute-start) | collective-permute-done | bytes 98336 | tf_op jit(solution)/shard_map/ppermute | solution.py:440
  25.9 0.1 hand.1
  25.9 0.1 collective-permute-start.4
  26.0 2.0 %collective-permute-done.4.refs_1_ = f32[1152,128]{1,0:T(8,128)S(1)} collective-permute-done((f32[1152,128]{1,0:T(8,128)S(1)}, f32[1152,128]{1,0:T(8,128)S(1)}, u32[]{:S(2)}, u32[]{:S(2)}) %collective-permute-start.4) | collective-permute-done | bytes 589856 | tf_op jit(solution)/shard_map/ppermute | solution.py:443
  28.0 8.9 %refine.1 = f32[256,128]{1,0:T(8,128)S(1)} custom-call(s32[1]{0:T(128)} %bitcast.pos_ref, f32[768,128]{1,0:T(8,128)S(1)} %get-tuple-element.30.refs_0_, f32[1152,128]{1,0:T(8,128)S(1)} %collective-permute-done.4.refs_1_, f32[256,256]{1,0:T(8,128)S(1)} %bitcast.5, bf16[384,128]{1,0:T(8,128)(2,1)S(1)} %join.1.seen_ref.refs_3_, ...), custom_call_target="tpu_custom_call" | custom-call | flops 400000000 | bytes 2000000 | tf_op jit(solution)/shard_map/refine/pallas_call | solution.py:187
  36.9 0.0 copy-start
  36.9 10.1 %all_to_all.15.d_ref = f32[8,4,8,128]{3,2,1,0:T(8,128)S(1)} all-to-all(f32[8,4,8,128]{3,2,1,0:T(8,128)S(1)} %bitcast.6), channel_id=1, replica_groups=mesh['sub'=8,'band'=16] {'sub'}, dimensions={0} | all-to-all | bytes 262144 | tf_op jit(solution)/shard_map/all_to_all | solution.py:445
  47.0 0.2 encode.1
  47.2 19.4 %all_to_all.16.g_ref = bf16[16,272,128]{2,1,0:T(8,128)(2,1)S(1)} all-to-all(bf16[16,272,128]{2,1,0:T(8,128)(2,1)S(1)} %encode.1), channel_id=1, replica_groups=mesh['sub'=8,'band'=16] {'band'}, dimensions={0} | all-to-all | bytes 2228224 | tf_op jit(solution)/shard_map/all_to_all | solution.py:446
  66.6 0.0 copy-done
  66.6 2.1 %place.1 = f32[4,128,1024]{2,1,0:T(8,128)} custom-call(bf16[16,272,128]{2,1,0:T(8,128)(2,1)S(1)} %all_to_all.16.g_ref, f32[4,128,1024]{2,1,0:T(8,128)S(1)} %copy-done), custom_call_target="tpu_custom_call" | custom-call | tf_op jit(solution)/shard_map/place/pallas_call | solution.py:420
  (2 shorter events, 0.0 us)
Async XLA Ops:
  2.3 16.2 %all-to-all-start = ((f32[16,16,256]{2,1,0:T(8,128)}), f32[16,16,256]{2,1,0:T(8,128)S(1)}, u32[]{:S(2)}, u32[]{:S(2)}) async-start(f32[16,16,256]{2,1,0:T(8,128)} %get-tuple-element.19), calls=%async_computation | async-start | bytes 524288 | tf_op jit(solution)/shard_map/all_to_all | solution.py:434
  10.9 12.7 %collective-permute-start.1 = (f32[256,128]{1,0:T(8,128)}, f32[256,128]{1,0:T(8,128)S(1)}, u32[]{:S(2)}, u32[]{:S(2)}) collective-permute-start(f32[256,128]{1,0:T(8,128)} %get-tuple-element.23), channel_id=1, source_target_pairs={{0,32},{16,48},{32,64},{48,80},{64,96},{80,112},{96,0},{112,16},{1... | collective-permute-start | bytes 393224 | tf_op jit(solution)/shard_map/ppermute | solution.py:436
  12.2 11.4 %collective-permute-start.2 = (f32[256,128]{1,0:T(8,128)}, f32[256,128]{1,0:T(8,128)S(1)}, u32[]{:S(2)}, u32[]{:S(2)}) collective-permute-start(f32[256,128]{1,0:T(8,128)} %get-tuple-element.24), channel_id=1, source_target_pairs={{0,64},{16,80},{32,96},{48,112},{64,0},{80,16},{96,32},{112,48},{1... | collective-permute-start | bytes 393224 | tf_op jit(solution)/shard_map/ppermute | solution.py:436
  14.6 9.0 %collective-permute-start.3 = (f32[256,128]{1,0:T(8,128)}, f32[256,128]{1,0:T(8,128)S(1)}, u32[]{:S(2)}, u32[]{:S(2)}) collective-permute-start(f32[256,128]{1,0:T(8,128)} %get-tuple-element.25), channel_id=1, source_target_pairs={{0,96},{16,112},{32,0},{48,16},{64,32},{80,48},{96,64},{112,80},{1... | collective-permute-start | bytes 393224 | tf_op jit(solution)/shard_map/ppermute | solution.py:436
  15.8 0.9 %copy-start.1 = (f32[384,128]{1,0:T(8,128)S(1)}, f32[384,128]{1,0:T(8,128)}, u32[]{:S(2)}) copy-start(f32[384,128]{1,0:T(8,128)} %get-tuple-element.20.region_ref) | copy-start | bytes 589828
  18.5 7.4 %collective-permute-start = (bf16[384,128]{1,0:T(8,128)(2,1)S(1)}, bf16[384,128]{1,0:T(8,128)(2,1)S(1)}, u32[]{:S(2)}, u32[]{:S(2)}) collective-permute-start(bf16[384,128]{1,0:T(8,128)(2,1)S(1)} %join.1.seen_ref.refs_3_), channel_id=1, source_target_pairs={{16,32},{32,16},{48,64},{64,48},{80,96},{96,80},{17,33},{33,17},{4... | collective-permute-start | bytes 294920 | tf_op jit(solution)/shard_map/ppermute | solution.py:440
  25.9 2.1 %collective-permute-start.4 = (f32[1152,128]{1,0:T(8,128)S(1)}, f32[1152,128]{1,0:T(8,128)S(1)}, u32[]{:S(2)}, u32[]{:S(2)}) collective-permute-start(f32[1152,128]{1,0:T(8,128)S(1)} %get-tuple-element.31), channel_id=1, source_target_pairs={{0,16},{16,0},{32,48},{48,32},{64,80},{80,64},{96,112},{112,96},{1... | collective-permute-start | bytes 1769480 | tf_op jit(solution)/shard_map/ppermute | solution.py:443
  36.9 29.7 %copy-start = (f32[4,128,1024]{2,1,0:T(8,128)S(1)}, f32[4,128,1024]{2,1,0:T(8,128)}, u32[]{:S(2)}) copy-start(f32[4,128,1024]{2,1,0:T(8,128)} %c_ref.1) | copy-start | bytes 6291460

commit v21 on v18

--- a/solution.py
+++ b/solution.py
@@ -423,7 +423,7 @@
         grid=(2,),
         in_specs=[pl.BlockSpec((8, 272, LANES), lambda j: (j, 0, 0)), block],
         out_specs=block,
-        compiler_params=pltpu.CompilerParams(vmem_limit_bytes=32 * 2**20),
+        compiler_params=pltpu.CompilerParams(vmem_limit_bytes=60 * 2**20),
         name="place",
     )(gathered, coeffs_in)
 

time: 69.6 us -> 71.4 us (1.026)
  Pallas kernels: 13.4 us -> 14.7 us
    pallas_call x1, Pallas kernels: 1.98 us -> 3.28 us  [place(): pl.pallas_call(place_kernel, out_shape=jax.ShapeDtypeStruct((4, 128, 1024...]
    all_to_all x1, blocking collectives: 19.4 us -> 20.2 us  [per_device(): lax.all_to_all(encode(owned), 'band', split_axis=0, concat_axis=0, tiled=...]
where the time goes in v21:
time: 71.4 us; the launch traced here: 70.6 us
  blocking collectives  30.2 us (42%)
  starting transfers between devices  18.7 us (26%)
  Pallas kernels  14.7 us (21%)
  waiting for transfers between devices  5.97 us (8%)
  local copies, waits for them, and re-layouts  0.93 us (1%)
    all_to_all x1, blocking collectives, per_device(): lax.all_to_all(encode(owned), 'band', split_axis=0, concat_axis=0, tiled=...  20.2 us
    all_to_all x1, blocking collectives, per_device(): lax.all_to_all(new.reshape(8, 4, 8, LANES), 'sub', split_axis=0, concat_a...  10 us
    pallas_call x1, Pallas kernels, refine(): pl.pallas_call(refine_kernel, out_shape=jax.ShapeDtypeStruct((32 * 8, LAN...  8.86 us
    all_to_all x1, starting transfers between devices, per_device(): lax.all_to_all(sent, 'band', split_axis=0, concat_axis=0, tiled=True)  8.6 us
    ppermute x1, starting transfers between devices, per_device(): lax.ppermute(seen, 'sub', [(1, 2), (2, 1), (3, 4), (4, 3), (5, 6), (6, 5)])  5.1 us
    ppermute x3, starting transfers between devices, per_device(): lax.ppermute(tiles[d], 'sub', [(i, (i + 2 * d) % 8) for i in range(8)])  4.88 us
    pallas_call x1, Pallas kernels, place(): pl.pallas_call(place_kernel, out_shape=jax.ShapeDtypeStruct((4, 128, 1024...  3.28 us
    pallas_call x1, Pallas kernels, pack(): pl.pallas_call(pack_kernel, out_shape=(jax.ShapeDtypeStruct((384, LANES),...  2.29 us
  transfers between devices with their start and end apart: 6, of which 3 were waited for; matrix products, arithmetic and copies ran while one was open for 0% of the time, Pallas kernels for 0%

profile of v21, /device:TPU:1, one launch (start us, length us, event | category | flops | bytes accessed | tf_op | source)
XLA Modules:
  0.0 70.6 jit_solution(16140102246019592201)
XLA Ops:
  0.0 2.3 %pack.1 = (f32[384,128]{1,0:T(8,128)}, f32[256,128]{1,0:T(8,128)}, f32[256,128]{1,0:T(8,128)}, f32[256,128]{1,0:T(8,128)}, f32[16,16,256]{2,1,0:T(8,128)}) custom-call(s32[1]{0:T(128)} %bitcast.pos_ref, f32[4,128,1024]{2,1,0:T(8,128)} %c_ref.1, f32[4,128,1024]{2,1,0:T(8,128)} %c_ref.1, bf16[8,16,1024]{2,1,0:T(8,128)(2,1)} %mb_ref.1, ...), custom_call_target="tpu_custom_call" | custom-call | flops 100000000 | bytes 1600000 | tf_op jit(solution)/shard_map/pack/pallas_call | solution.py:276
  2.3 8.6 %all-to-all-start = ((f32[16,16,256]{2,1,0:T(8,128)}), f32[16,16,256]{2,1,0:T(8,128)S(1)}, u32[]{:S(2)}, u32[]{:S(2)}) async-start(f32[16,16,256]{2,1,0:T(8,128)} %get-tuple-element.19), calls=%async_computation | async-start | bytes 524288 | tf_op jit(solution)/shard_map/all_to_all | solution.py:434
  10.9 1.3 %collective-permute-start.1 = (f32[256,128]{1,0:T(8,128)}, f32[256,128]{1,0:T(8,128)S(1)}, u32[]{:S(2)}, u32[]{:S(2)}) collective-permute-start(f32[256,128]{1,0:T(8,128)} %get-tuple-element.23), channel_id=1, source_target_pairs={{0,32},{16,48},{32,64},{48,80},{64,96},{80,112},{96,0},{112,16},{1... | collective-permute-start | bytes 393224 | tf_op jit(solution)/shard_map/ppermute | solution.py:436
  12.2 2.4 %collective-permute-start.2 = (f32[256,128]{1,0:T(8,128)}, f32[256,128]{1,0:T(8,128)S(1)}, u32[]{:S(2)}, u32[]{:S(2)}) collective-permute-start(f32[256,128]{1,0:T(8,128)} %get-tuple-element.24), channel_id=1, source_target_pairs={{0,64},{16,80},{32,96},{48,112},{64,0},{80,16},{96,32},{112,48},{1... | collective-permute-start | bytes 393224 | tf_op jit(solution)/shard_map/ppermute | solution.py:436
  14.6 1.2 %collective-permute-start.3 = (f32[256,128]{1,0:T(8,128)}, f32[256,128]{1,0:T(8,128)S(1)}, u32[]{:S(2)}, u32[]{:S(2)}) collective-permute-start(f32[256,128]{1,0:T(8,128)} %get-tuple-element.25), channel_id=1, source_target_pairs={{0,96},{16,112},{32,0},{48,16},{64,32},{80,48},{96,64},{112,80},{1... | collective-permute-start | bytes 393224 | tf_op jit(solution)/shard_map/ppermute | solution.py:436
  15.8 0.0 copy-start
  15.8 0.9 %copy-done = f32[384,128]{1,0:T(8,128)S(1)} copy-done((f32[384,128]{1,0:T(8,128)S(1)}, f32[384,128]{1,0:T(8,128)}, u32[]{:S(2)}) %copy-start) | copy-done | bytes 196632
  16.7 1.7 %all-to-all-done = f32[16,16,256]{2,1,0:T(8,128)S(1)} async-done(((f32[16,16,256]{2,1,0:T(8,128)}), f32[16,16,256]{2,1,0:T(8,128)S(1)}, u32[]{:S(2)}, u32[]{:S(2)}) %all-to-all-start) | async-done | bytes 262176 | tf_op jit(solution)/shard_map/all_to_all | solution.py:434
  18.5 5.1 %collective-permute-start = (bf16[384,128]{1,0:T(8,128)(2,1)S(1)}, bf16[384,128]{1,0:T(8,128)(2,1)S(1)}, u32[]{:S(2)}, u32[]{:S(2)}) collective-permute-start(bf16[384,128]{1,0:T(8,128)(2,1)S(1)} %join.1.seen_ref.refs_3_), channel_id=1, source_target_pairs={{16,32},{32,16},{48,64},{64,48},{80,96},{96,80},{17,33},{33,17},{4... | collective-permute-start | bytes 294920 | tf_op jit(solution)/shard_map/ppermute | solution.py:440
  23.6 0.0 collective-permute-done.1.r1
  23.6 0.0 collective-permute-done.2.r2
  23.6 0.0 collective-permute-done.3.r3
  23.6 2.3 %collective-permute-done.refs_4_ = bf16[384,128]{1,0:T(8,128)(2,1)S(1)} collective-permute-done((bf16[384,128]{1,0:T(8,128)(2,1)S(1)}, bf16[384,128]{1,0:T(8,128)(2,1)S(1)}, u32[]{:S(2)}, u32[]{:S(2)}) %collective-permute-start) | collective-permute-done | bytes 98336 | tf_op jit(solution)/shard_map/ppermute | solution.py:440
  25.9 0.1 hand.1
  25.9 0.1 collective-permute-start.4
  26.0 2.0 %collective-permute-done.4.refs_1_ = f32[1152,128]{1,0:T(8,128)S(1)} collective-permute-done((f32[1152,128]{1,0:T(8,128)S(1)}, f32[1152,128]{1,0:T(8,128)S(1)}, u32[]{:S(2)}, u32[]{:S(2)}) %collective-permute-start.4) | collective-permute-done | bytes 589856 | tf_op jit(solution)/shard_map/ppermute | solution.py:443
  28.0 8.9 %refine.1 = f32[256,128]{1,0:T(8,128)S(1)} custom-call(s32[1]{0:T(128)} %bitcast.pos_ref, f32[768,128]{1,0:T(8,128)S(1)} %get-tuple-element.30.refs_0_, f32[1152,128]{1,0:T(8,128)S(1)} %collective-permute-done.4.refs_1_, f32[256,256]{1,0:T(8,128)S(1)} %bitcast.5, bf16[384,128]{1,0:T(8,128)(2,1)S(1)} %join.1.seen_ref.refs_3_, ...), custom_call_target="tpu_custom_call" | custom-call | flops 400000000 | bytes 2000000 | tf_op jit(solution)/shard_map/refine/pallas_call | solution.py:187
  36.9 10.0 %all_to_all.15.d_ref = f32[8,4,8,128]{3,2,1,0:T(8,128)S(1)} all-to-all(f32[8,4,8,128]{3,2,1,0:T(8,128)S(1)} %bitcast.6), channel_id=1, replica_groups=mesh['sub'=8,'band'=16] {'sub'}, dimensions={0} | all-to-all | bytes 262144 | tf_op jit(solution)/shard_map/all_to_all | solution.py:445
  46.9 0.2 encode.1
  47.1 20.2 %all_to_all.16.g_ref = bf16[16,272,128]{2,1,0:T(8,128)(2,1)} all-to-all(bf16[16,272,128]{2,1,0:T(8,128)(2,1)S(1)} %encode.1), channel_id=1, replica_groups=mesh['sub'=8,'band'=16] {'band'}, dimensions={0} | all-to-all | bytes 2228224 | tf_op jit(solution)/shard_map/all_to_all | solution.py:446
  67.3 3.3 %place.1 = f32[4,128,1024]{2,1,0:T(8,128)} custom-call(bf16[16,272,128]{2,1,0:T(8,128)(2,1)} %all_to_all.16.g_ref, f32[4,128,1024]{2,1,0:T(8,128)} %c_ref.1), custom_call_target="tpu_custom_call" | custom-call | tf_op jit(solution)/shard_map/place/pallas_call | solution.py:420
  (2 shorter events, 0.0 us)
Async XLA Ops:
  2.3 16.2 %all-to-all-start = ((f32[16,16,256]{2,1,0:T(8,128)}), f32[16,16,256]{2,1,0:T(8,128)S(1)}, u32[]{:S(2)}, u32[]{:S(2)}) async-start(f32[16,16,256]{2,1,0:T(8,128)} %get-tuple-element.19), calls=%async_computation | async-start | bytes 524288 | tf_op jit(solution)/shard_map/all_to_all | solution.py:434
  10.9 12.7 %collective-permute-start.1 = (f32[256,128]{1,0:T(8,128)}, f32[256,128]{1,0:T(8,128)S(1)}, u32[]{:S(2)}, u32[]{:S(2)}) collective-permute-start(f32[256,128]{1,0:T(8,128)} %get-tuple-element.23), channel_id=1, source_target_pairs={{0,32},{16,48},{32,64},{48,80},{64,96},{80,112},{96,0},{112,16},{1... | collective-permute-start | bytes 393224 | tf_op jit(solution)/shard_map/ppermute | solution.py:436
  12.2 11.4 %collective-permute-start.2 = (f32[256,128]{1,0:T(8,128)}, f32[256,128]{1,0:T(8,128)S(1)}, u32[]{:S(2)}, u32[]{:S(2)}) collective-permute-start(f32[256,128]{1,0:T(8,128)} %get-tuple-element.24), channel_id=1, source_target_pairs={{0,64},{16,80},{32,96},{48,112},{64,0},{80,16},{96,32},{112,48},{1... | collective-permute-start | bytes 393224 | tf_op jit(solution)/shard_map/ppermute | solution.py:436
  14.6 9.0 %collective-permute-start.3 = (f32[256,128]{1,0:T(8,128)}, f32[256,128]{1,0:T(8,128)S(1)}, u32[]{:S(2)}, u32[]{:S(2)}) collective-permute-start(f32[256,128]{1,0:T(8,128)} %get-tuple-element.25), channel_id=1, source_target_pairs={{0,96},{16,112},{32,0},{48,16},{64,32},{80,48},{96,64},{112,80},{1... | collective-permute-start | bytes 393224 | tf_op jit(solution)/shard_map/ppermute | solution.py:436
  15.8 0.9 %copy-start = (f32[384,128]{1,0:T(8,128)S(1)}, f32[384,128]{1,0:T(8,128)}, u32[]{:S(2)}) copy-start(f32[384,128]{1,0:T(8,128)} %get-tuple-element.20.region_ref) | copy-start | bytes 589828
  18.5 7.4 %collective-permute-start = (bf16[384,128]{1,0:T(8,128)(2,1)S(1)}, bf16[384,128]{1,0:T(8,128)(2,1)S(1)}, u32[]{:S(2)}, u32[]{:S(2)}) collective-permute-start(bf16[384,128]{1,0:T(8,128)(2,1)S(1)} %join.1.seen_ref.refs_3_), channel_id=1, source_target_pairs={{16,32},{32,16},{48,64},{64,48},{80,96},{96,80},{17,33},{33,17},{4... | collective-permute-start | bytes 294920 | tf_op jit(solution)/shard_map/ppermute | solution.py:440
  25.9 2.1 %collective-permute-start.4 = (f32[1152,128]{1,0:T(8,128)S(1)}, f32[1152,128]{1,0:T(8,128)S(1)}, u32[]{:S(2)}, u32[]{:S(2)}) collective-permute-start(f32[1152,128]{1,0:T(8,128)S(1)} %get-tuple-element.31), channel_id=1, source_target_pairs={{0,16},{16,0},{32,48},{48,32},{64,80},{80,64},{96,112},{112,96},{1... | collective-permute-start | bytes 1769480 | tf_op jit(solution)/shard_map/ppermute | solution.py:443
